TPU v7x, 32 devices: a whole 2x2x4 slice. The times are simulated.
32 devices in a mesh: past: 8 (over y, x, core), second: 4 (over z).
Axes of the slice: x: 2, y: 2, z: 4, core: 2. Of those that a mesh axis runs over, the one named last changes fastest.
Arguments:
- g_hist: bfloat16 [16384, 4096], P('past', 'second'), may hold values from -6 to 6
- sigma_hist: bfloat16 [1024, 16384], P(None, 'past'), may hold values from -0.0625 to 0.0625
- volterra: bfloat16 [2, 512, 1024], replicated, may hold values from -0.1875 to 0.1875
- sigma_edge: bfloat16 [512, 4096], P(None, 'second'), may hold values from -6 to 6
- coupling: float32 [32, 4096], P(None, 'second'), may hold values from 0.3 to 3
Outputs:
- g_new: bfloat16 [1024, 4096], P(None, 'second')
- sigma_new: bfloat16 [1024, 4096], P(None, 'second')
All inputs are finite; a program needn't handle non-finite values.
Results may differ from a plain program's by a relative error of at most 0.0059.
Values may be sent and summed in bfloat16 or wider, within the bound.
No kernel may reach another device: no remote copies, remote signals or barrier semaphores. Data moves between devices by JAX's collectives and lax.ppermute only.
A program may use at most 64 MiB of HBM per device.

v0:
```python
import jax
import jax.numpy as jnp
from jax import lax
from jax.sharding import PartitionSpec as P

N = 32
BLK = 16
NB = 2


def per_device(g_hist, sigma_hist, volterra, sigma_edge, coupling):
    rows = BLK * N
    columns = g_hist.shape[1]
    count_all = rows * columns * lax.axis_size("second")
    prev = sigma_edge
    g_blocks = []
    s_blocks = []
    for block in range(NB):
        sig_rows = sigma_hist[block * rows : (block + 1) * rows, :]
        w_memory = volterra[block][:, :rows]
        w_sigma = volterra[block][:, rows:]
        start_value = jnp.dot(w_sigma, prev, preferred_element_type=jnp.float32)
        partial_sum = jnp.dot(sig_rows, g_hist, preferred_element_type=jnp.float32)
        memory = lax.psum(partial_sum, "past").astype(jnp.bfloat16)
        gnew = start_value + jnp.dot(w_memory, memory, preferred_element_type=jnp.float32)
        cubic = gnew.reshape(BLK, N, columns) ** 3 * coupling[None]
        local_sq = jnp.sum(cubic * cubic)
        total_sq = lax.psum(local_sq, "second")
        meansq = total_sq / count_all
        sigma = (cubic / jnp.sqrt(meansq + 1e-06)).reshape(rows, columns).astype(jnp.bfloat16)
        g_blocks.append(gnew.astype(jnp.bfloat16))
        s_blocks.append(sigma)
        prev = sigma
    return (jnp.concatenate(g_blocks, axis=0), jnp.concatenate(s_blocks, axis=0))


def solution(mesh):
    return jax.shard_map(
        per_device,
        mesh=mesh,
        in_specs=(P("past", "second"), P(None, "past"), P(), P(None, "second"), P(None, "second")),
        out_specs=(P(None, "second"), P(None, "second")),
        check_vma=False,
    )
```

profile of v0, /device:TPU:0, one launch (start us, length us, event | category | flops | bytes accessed | tf_op | source)
XLA Modules:
  0.0 139.3 jit_solution(4706337641651526923)
XLA Ops:
  0.6 0.0 copy-start
  0.6 0.0 copy-start.9
  0.7 0.0 copy-start.8
  0.7 6.6 %fusion = f32[512,1024]{1,0:T(8,128)} fusion(bf16[2048,1024]{1,0:T(8,128)(2,1)} %param.5, bf16[1024,2048]{1,0:T(8,128)(2,1)} %param.6), kind=kOutput, calls=%fused_computation.10 | convolution fusion | flops 2147483648 | bytes 8388608 | tf_op jit(solution)/shard_map/dot_general | solution.py:23
  7.3 0.0 copy-done.9
  7.3 0.0 copy-done.8
  7.3 3.7 %fusion.2 = f32[512,1024]{1,0:T(8,128)} fusion(bf16[2048,1024]{1,0:T(8,128)(2,1)S(1)} %copy-done.8, bf16[1024,2048]{1,0:T(8,128)(2,1)S(1)} %copy-done.9), kind=kOutput, calls=%fused_computation.14 | convolution fusion | flops 2147483648 | bytes 8388608 | tf_op jit(solution)/shard_map/dot_general | solution.py:23
  11.0 0.0 copy-start.5
  11.0 89.8 %all-reduce.2 = (bf16[512,1024]{1,0:T(8,128)(2,1)}, bf16[512,1024]{1,0:T(8,128)(2,1)}) all-reduce(f32[512,1024]{1,0:T(8,128)} %fusion.2, f32[512,1024]{1,0:T(8,128)} %fusion), channel_id=1, replica_groups=mesh['past'=8,'second'=4] {'past'}, use_global_device_ids=true, to_apply=%region_0.0 | all-reduce | flops 1048576 | bytes 6291456 | tf_op jit(solution)/shard_map/psum | solution.py:24
  100.7 0.0 copy-done.5
  100.7 1.1 slice_bitcast_fusion
  101.9 0.0 copy-start.4
  101.9 0.0 copy-start.7
  101.9 0.0 copy-done
  101.9 0.7 fusion.10
  102.6 0.2 copy-done.4
  102.8 0.4 copy-done.7
  103.2 1.6 %multiply_reduce_fusion.1 = (f32[]{:T(128)}, f32[512,1024]{1,0:T(8,128)S(1)}) fusion(f32[32,1024]{1,0:T(8,128)S(1)} %copy-done.4, f32[512,1024]{1,0:T(8,128)S(1)} %fusion.10, bf16[512,1024]{1,0:T(8,128)(2,1)S(1)} %copy-done.7, bf16[512,1024]{1,0:T(8,128)(2,1)S(1)} %get-tuple-element.7), kind=kOutput, calls=%fused_computation.13 | convolution fusion | flops 540016640 | bytes 5898244 | tf_op jit(solution)/shard_map/dot_general | solution.py:25
  104.7 12.6 %psum.29 = f32[]{:T(128)} all-reduce(f32[]{:T(128)} %get-tuple-element.8), channel_id=1, replica_groups=mesh['past'=8,'second'=4] {'second'}, use_global_device_ids=true, to_apply=%region_2.0 | all-reduce | flops 1 | bytes 8 | tf_op jit(solution)/shard_map/psum | solution.py:28
  118.0 0.0 copy-start.3
  118.0 1.4 %fusion.12 = (bf16[512,1024]{1,0:T(8,128)(2,1)}, bf16[512,1024]{1,0:T(8,128)(2,1)S(1)}) fusion(f32[512,1024]{1,0:T(8,128)S(1)} %get-tuple-element.9, f32[]{:T(128)S(6)} %sqrt.6, f32[32,1024]{1,0:T(8,128)S(1)} %copy-done.4), kind=kLoop, calls=%fused_computation.27 | loop fusion | flops 3145728 | bytes 4325380 | tf_op jit(solution)/shard_map/convert_element_type | solution.py:31
  119.4 0.0 copy-done.3
  119.4 0.7 fusion.7
  120.1 0.9 copy-done.6
  121.0 1.7 %bitcast_convert_fusion = (bf16[512,1024]{1,0:T(8,128)(2,1)}, f32[1024,512]{0,1:T(8,128)S(1)}) fusion(f32[1024,512]{0,1:T(8,128)S(1)} %fusion.7, bf16[512,1024]{1,0:T(8,128)(2,1)S(1)} %copy-done.6, bf16[512,1024]{1,0:T(8,128)(2,1)S(1)} %copy-done.3), kind=kOutput, calls=%fused_computation.6 | convolution fusion | flops 537919488 | bytes 6815744 | tf_op jit(solution)/shard_map/dot_general | solution.py:25
  122.7 0.0 copy-done.1
  122.7 1.1 multiply_reduce_fusion
  123.9 9.0 %psum.31 = f32[]{:T(128)} all-reduce(f32[]{:T(128)} %multiply_reduce_fusion), channel_id=1, replica_groups=mesh['past'=8,'second'=4] {'second'}, use_global_device_ids=true, to_apply=%region_5.0 | all-reduce | flops 1 | bytes 8 | tf_op jit(solution)/shard_map/psum | solution.py:28
  133.5 3.0 %pad_maximum_fusion = bf16[1024,1024]{1,0:T(8,128)(2,1)} fusion(bf16[512,1024]{1,0:T(8,128)(2,1)} %get-tuple-element.10, bf16[512,1024]{1,0:T(8,128)(2,1)} %get-tuple-element.4), kind=kLoop, calls=%fused_computation.4 | loop fusion | flops 4194304 | bytes 4194304 | tf_op jit(solution)/shard_map/concatenate | solution.py:34
  136.6 0.3 divide_convert_fusion
  136.9 0.9 copy-done.2
  137.8 1.5 %pad_maximum_fusion.1 = bf16[1024,1024]{1,0:T(8,128)(2,1)} fusion(bf16[512,1024]{1,0:T(8,128)(2,1)S(1)} %divide_convert_fusion, bf16[512,1024]{1,0:T(8,128)(2,1)S(1)} %copy-done.2), kind=kLoop, calls=%fused_computation.5 | loop fusion | flops 4194304 | bytes 4194304 | tf_op jit(solution)/shard_map/concatenate | solution.py:34
  (3 shorter events, 0.0 us)
Async XLA Ops:
  0.6 101.2 %copy-start = (bf16[512,1024]{1,0:T(8,128)(2,1)S(1)}, bf16[512,1024]{1,0:T(8,128)(2,1)}, u32[]{:S(2)}) copy-start(bf16[512,1024]{1,0:T(8,128)(2,1)} %param.8) | copy-start | bytes 3145732
  0.6 6.6 %copy-start.9 = (bf16[1024,2048]{1,0:T(8,128)(2,1)S(1)}, bf16[1024,2048]{1,0:T(8,128)(2,1)}, u32[]{:S(2)}) copy-start(bf16[1024,2048]{1,0:T(8,128)(2,1)} %param.6) | copy-start | bytes 12582916
  0.7 6.6 %copy-start.8 = (bf16[2048,1024]{1,0:T(8,128)(2,1)S(1)}, bf16[2048,1024]{1,0:T(8,128)(2,1)}, u32[]{:S(2)}) copy-start(bf16[2048,1024]{1,0:T(8,128)(2,1)} %param.5) | copy-start | bytes 12582916
  11.0 89.8 %copy-start.5 = (bf16[2,512,1024]{2,1,0:T(8,128)(2,1)S(1)}, bf16[2,512,1024]{2,1,0:T(8,128)(2,1)}, u32[]{:S(2)}) copy-start(bf16[2,512,1024]{2,1,0:T(8,128)(2,1)} %param.7) | copy-start | bytes 6291460
  101.9 0.9 copy-start.4
  101.9 1.3 copy-start.7
  118.0 1.4 %copy-start.3 = (bf16[512,1024]{1,0:T(8,128)(2,1)S(1)}, bf16[512,1024]{1,0:T(8,128)(2,1)}, u32[]{:S(2)}) copy-start(bf16[512,1024]{1,0:T(8,128)(2,1)} %get-tuple-element.6) | copy-start | bytes 3145732
  119.4 3.3 %copy-start.1 = (bf16[512,1024]{1,0:T(8,128)(2,1)}, bf16[512,1024]{1,0:T(8,128)(2,1)S(1)}, u32[]{:S(2)}) copy-start(bf16[512,1024]{1,0:T(8,128)(2,1)S(1)} %get-tuple-element.5) | copy-start | bytes 3145732
  119.4 1.6 %copy-start.6 = (bf16[512,1024]{1,0:T(8,128)(2,1)S(1)}, bf16[512,1024]{1,0:T(8,128)(2,1)}, u32[]{:S(2)}) copy-start(bf16[512,1024]{1,0:T(8,128)(2,1)} %get-tuple-element.3) | copy-start | bytes 3145732
  136.6 1.2 copy-start.2
where the time goes:
time: 140 us; the launch traced here: 139 us
  blocking collectives  111 us (79%)
  matrix products  15 us (11%)
  other arithmetic  7.42 us (5%)
  local copies, waits for them, and re-layouts  3.51 us (3%)
  between operations  2.08 us (1%)
    psum x1, blocking collectives, per_device(): memory = lax.psum(partial_sum, 'past').astype(jnp.bfloat16)  89.8 us
    psum x2, blocking collectives, per_device(): total_sq = lax.psum(local_sq, 'second')  21.5 us
    dot_general x2, matrix products, per_device(): partial_sum = jnp.dot(sig_rows, g_hist, preferred_element_type=jnp.float32)  10.3 us
    dot_general x2, matrix products, per_device(): jnp.dot(w_memory, memory, preferred_element_type=jnp.float32)  3.25 us
    concatenate x1, other arithmetic, per_device(): jnp.concatenate(g_blocks, axis=0)  3.03 us

commit v1 on v0

v1 whole, which is shorter than its diff:
```python
import functools

import jax
import jax.numpy as jnp
from jax import lax
from jax.experimental import pallas as pl
from jax.experimental.pallas import tpu as pltpu
from jax.sharding import PartitionSpec as P

VMEM = 48 * 1024 * 1024
F32 = jnp.float32
BF16 = jnp.bfloat16


def log2(n):
    bits = n.bit_length() - 1
    assert n == 1 << bits
    return bits


def level_bits(size, depth):
    bits = list(range(log2(size)))
    return bits, bits[:1] + bits[1:depth][::-1] + bits[depth:]


def reverse_bits(value, bits):
    result = value * 0
    for i in range(bits):
        result = result | (((value >> i) & 1) << (bits - 1 - i))
    return result


class Order:
    def __init__(self, depth):
        self.depth, self.half = depth, 1 << (depth - 1)

    def own(self, me):
        return reverse_bits(me, self.depth)

    def kept(self, me, j):
        return self.own(me) ^ jnp.where(me % 2 == 1, reverse_bits(j, self.depth - 1), j)

    def sent(self, me, j):
        return self.own(me) ^ self.half ^ jnp.where(me % 2 == 1, j, reverse_bits(j, self.depth - 1))

    def place(self, me, block):
        apart = block ^ self.own(me)
        low, top = apart & (self.half - 1), apart & self.half
        turned = (me + top // self.half) % 2 == 1
        return top + jnp.where(turned, reverse_bits(low, self.depth - 1), low)


def partial_kernel(count, me, sigma, *refs):
    parts, out, total = refs[:count], refs[count], refs[count + 1]
    step = pl.program_id(0)
    right = jnp.concatenate([part[...] for part in parts], axis=1)
    product = jnp.dot(sigma[...], right, preferred_element_type=F32)

    @pl.when(step == 0)
    def _():
        total[...] = product

    @pl.when(step > 0)
    def _():
        total[...] += product

    @pl.when(step == pl.num_programs(0) - 1)
    def _():
        out[...] = total[...].astype(out.dtype)


def partial_product(me, sigma_hist, g_hist, block, rows, blocks_of, count, width, dtype):
    depth = g_hist.shape[0]
    chunk = depth // 4
    columns = count * width

    def part(j):
        return pl.BlockSpec((chunk, width), lambda k, me: (k, blocks_of(me[0], j)))

    return pl.pallas_call(
        functools.partial(partial_kernel, count),
        grid_spec=pltpu.PrefetchScalarGridSpec(
            num_scalar_prefetch=1,
            grid=(depth // chunk,),
            in_specs=[pl.BlockSpec((rows, chunk), lambda k, me: (block, k))]
            + [part(j) for j in range(count)],
            out_specs=pl.BlockSpec((rows, columns), lambda k, me: (0, 0)),
            scratch_shapes=[pltpu.VMEM((rows, columns), F32)],
        ),
        out_shape=jax.ShapeDtypeStruct((rows, columns), dtype),
        compiler_params=pltpu.CompilerParams(vmem_limit_bytes=VMEM),
        cost_estimate=pl.CostEstimate(
            flops=2 * rows * depth * columns, bytes_accessed=2 * depth * (rows + columns), transcendentals=0
        ),
        name="partial_product",
    )(me, sigma_hist, *[g_hist] * count)


def cubed(g, coupling):
    orbitals = coupling.shape[0]
    g3 = g.reshape(g.shape[0] // orbitals, orbitals, g.shape[1])
    return (g3 * g3 * g3 * coupling[None]).reshape(g.shape)


def fold_rows(x):
    return jnp.sum(x.reshape(x.shape[0] // 8, 8, x.shape[1]), axis=0)


def scale_of(squares, count):
    return 1.0 / jnp.sqrt(jnp.sum(squares) / count + 1e-06)


def own_first_kernel(me, memory, w, prev, coupling, cubic, squares):
    rows = memory.shape[0]
    g = jnp.dot(w[0, :, :rows], memory[...], preferred_element_type=F32)
    g += jnp.dot(w[0, :, rows:], prev[...], preferred_element_type=F32)
    c = cubed(g, coupling[...])
    cubic[...] = c
    squares[...] = fold_rows(c * c)


def own_next_kernel(count_all, me, memory, w, prev_cubic, prev_squares, coupling, cubic, squares):
    rows = memory.shape[0]
    prev = (prev_cubic[...] * scale_of(prev_squares[...], count_all)).astype(BF16)
    g = jnp.dot(w[0, :, :rows], memory[...], preferred_element_type=F32)
    g += jnp.dot(w[0, :, rows:], prev, preferred_element_type=F32)
    c = cubed(g, coupling[...])
    cubic[...] = c
    squares[...] = fold_rows(c * c)


def own_columns(me, order, memory, volterra, block, prev, prev_squares, coupling, count_all):
    rows, width = memory.shape
    full = lambda shape: pl.BlockSpec(shape, lambda i, me: (0, 0))
    w_spec = pl.BlockSpec((1, rows, 2 * rows), lambda i, me: (block, 0, 0))
    coupling_spec = pl.BlockSpec((coupling.shape[0], width), lambda i, me: (0, order.own(me[0])))
    if prev_squares is None:
        kernel = own_first_kernel
        in_specs = [full((rows, width)), w_spec, pl.BlockSpec((rows, width), lambda i, me: (0, order.own(me[0])))]
        operands = [memory, volterra, prev]
    else:
        kernel = functools.partial(own_next_kernel, count_all)
        in_specs = [full((rows, width)), w_spec, full((rows, width)), full(prev_squares.shape)]
        operands = [memory, volterra, prev, prev_squares]
    return pl.pallas_call(
        kernel,
        grid_spec=pltpu.PrefetchScalarGridSpec(
            num_scalar_prefetch=1,
            grid=(1,),
            in_specs=in_specs + [coupling_spec],
            out_specs=[full((rows, width)), full((8, width))],
        ),
        out_shape=[jax.ShapeDtypeStruct((rows, width), F32), jax.ShapeDtypeStruct((8, width), F32)],
        compiler_params=pltpu.CompilerParams(vmem_limit_bytes=VMEM),
        cost_estimate=pl.CostEstimate(
            flops=4 * rows * rows * width, bytes_accessed=4 * rows * rows + 8 * rows * width, transcendentals=0
        ),
        name="own_columns",
    )(me, *operands, coupling)


def finish_kernel(count_all, first, last, me, left, right, w, prev, squares, coupling, *refs):
    refs = list(refs)
    w_next = None if last else refs.pop(0)
    refs = refs if first else refs[2:]
    g_out, s_out = refs[:2]
    rows = left.shape[0]
    memory = jnp.concatenate([left[...], right[...]], axis=1)
    g = jnp.dot(w[0, :, :rows], memory, preferred_element_type=F32)
    if first:
        g += jnp.dot(w[0, :, rows:], prev[...], preferred_element_type=F32)
    else:
        g += prev[...]
    g_out[...] = g.astype(BF16)
    sigma = (cubed(g, coupling[...]) * scale_of(squares[...], count_all)).astype(BF16)
    s_out[...] = sigma
    if not last:
        refs[2][...] = jnp.dot(w_next[0, :, rows:], sigma, preferred_element_type=F32)


def finish(me, order, memory, volterra, block, prev, squares, coupling, outs, count_all, width):
    rows, columns = memory.shape
    blocks = volterra.shape[0]
    pair = 2 * width
    first, last = block == 0, block == blocks - 1
    place = lambda side: pl.BlockSpec((rows, width), lambda q, me: (0, order.place(me[0], 2 * q + side)))
    w_spec = lambda k: pl.BlockSpec((1, rows, 2 * rows), lambda q, me: (k, 0, 0))
    straight = lambda size, row=0: pl.BlockSpec((size, pair), lambda q, me: (row, q))
    operands = [memory, memory, volterra, prev, squares, coupling]
    in_specs = [
        place(0),
        place(1),
        w_spec(block),
        straight(rows),
        pl.BlockSpec(squares.shape, lambda q, me: (0, 0)),
        straight(coupling.shape[0]),
    ]
    out_specs = [straight(rows, block)] * 2
    out_shape = [jax.ShapeDtypeStruct((blocks * rows, columns), BF16)] * 2
    aliases = {}
    if not last:
        operands.append(volterra)
        in_specs.append(w_spec(block + 1))
        out_specs.append(straight(rows))
        out_shape.append(jax.ShapeDtypeStruct((rows, columns), F32))
    if not first:
        aliases = {1 + len(operands): 0, 2 + len(operands): 1}
        operands += outs
        in_specs += [pl.BlockSpec(memory_space=pl.ANY)] * 2
    return pl.pallas_call(
        functools.partial(finish_kernel, count_all, first, last),
        grid_spec=pltpu.PrefetchScalarGridSpec(
            num_scalar_prefetch=1, grid=(columns // pair,), in_specs=in_specs, out_specs=out_specs
        ),
        out_shape=out_shape,
        input_output_aliases=aliases,
        compiler_params=pltpu.CompilerParams(vmem_limit_bytes=VMEM),
        cost_estimate=pl.CostEstimate(
            flops=4 * rows * rows * columns, bytes_accessed=4 * rows * rows + 6 * rows * columns, transcendentals=0
        ),
        name="finish_block",
    )(me, *operands)


def per_device(past, second, g_hist, sigma_hist, volterra, sigma_edge, coupling):
    blocks, rows = volterra.shape[:2]
    columns = g_hist.shape[1]
    count_all = rows * columns * second
    depth = min(log2(past), log2(max(columns // 128, 2)))
    width = columns >> depth
    even, odd = level_bits(past, depth)
    order = Order(depth)
    me = lax.axis_index("past").astype(jnp.int32).reshape(1)

    def swap(x, level):
        pairs = [(d, d ^ (1 << (odd if d % 2 else even)[level])) for d in range(past)]
        return lax.ppermute(x, "past", pairs)

    def reduced(block):
        send = partial_product(me, sigma_hist, g_hist, block, rows, order.sent, order.half, width, BF16)
        arrived = swap(send, 0)
        total = partial_product(me, sigma_hist, g_hist, block, rows, order.kept, order.half, width, F32)
        for level in range(1, depth):
            kept = total.shape[1] // 2
            send = (total[:, kept:] + arrived[:, kept:].astype(F32)).astype(BF16)
            total = total[:, :kept] + arrived[:, :kept].astype(F32)
            arrived = swap(send, level)
        total = total + arrived.astype(F32)
        for level in range(depth, len(even)):
            rounded = total.astype(BF16)
            total = rounded.astype(F32) + swap(rounded, level).astype(F32)
        return total.astype(BF16)

    def gathered(piece):
        for level in reversed(range(depth)):
            piece = jnp.concatenate([piece, swap(piece, level)], axis=1)
        return piece

    def summed(squares):
        for level in range(log2(second)):
            squares = squares + lax.ppermute(squares, "second", [(d, d ^ (1 << level)) for d in range(second)])
        for level in range(depth):
            squares = squares + swap(squares, level)
        return squares

    own, whole, squares = [], [], []
    cubic, total = sigma_edge, None
    for block in range(blocks):
        own.append(reduced(block))
    for block in range(blocks):
        cubic, local = own_columns(me, order, own[block], volterra, block, cubic, total, coupling, count_all)
        total = summed(local)
        squares.append(total)
        whole.append(gathered(own[block]))
    outs, start = None, sigma_edge
    for block in range(blocks):
        results = finish(
            me, order, whole[block], volterra, block, start, squares[block], coupling, outs, count_all, width
        )
        outs = results[:2]
        start = results[2] if block < blocks - 1 else None
    return tuple(outs)


def solution(mesh):
    return jax.shard_map(
        functools.partial(per_device, mesh.shape["past"], mesh.shape["second"]),
        mesh=mesh,
        in_specs=(P("past", "second"), P(None, "past"), P(), P(None, "second"), P(None, "second")),
        out_specs=(P(None, "second"), P(None, "second")),
        check_vma=False,
    )
```

time: 140 us -> 96.3 us (0.69)
  blocking collectives: 111 us -> 0 us
  starting transfers between devices: 0 us -> 32.9 us
  waiting for transfers between devices: 0 us -> 29.7 us
  Pallas kernels: 0 us -> 28 us
  matrix products: 15 us -> 0 us
  other arithmetic: 7.42 us -> 0.82 us
    psum x3 -> x0, blocking collectives: 111 us -> none  [the longest x1 89.8 us: per_device(): memory = lax.psum(partial_sum, 'past').astype(jnp.bfloat16)]
    ppermute x0 -> x22, starting transfers between devices: none -> 32.9 us  [the longest x18 22.8 us: swap(): return lax.ppermute(x, 'past', pairs)]
    ppermute x0 -> x22, waiting for transfers between devices: none -> 29.7 us  [the longest x18 23.3 us: swap(): return lax.ppermute(x, 'past', pairs)]
    pallas_call x0 -> x8, Pallas kernels: none -> 28 us  [the longest x4 16.6 us: partial_product(): pl.pallas_call(functools.partial(partial_kernel, count), grid_spec=pltpu....]
    dot_general x6 -> x0, matrix products: 15 us -> none  [the longest x2 10.3 us: per_device(): partial_sum = jnp.dot(sig_rows, g_hist, preferred_element_type=jnp.float32)]
    concatenate x2 -> x6, other arithmetic: 4.52 us -> 0.41 us  [gathered(): piece = jnp.concatenate([piece, swap(piece, level)], axis=1)]
    unnamed x20 -> x10, local copies, waits for them, and re-layouts: 2.37 us -> 3.66 us
  transfers between devices with their start and end apart: 0 -> 22, of which waited for: 0 -> 15; matrix products, arithmetic and copies ran while one was open for 0% -> 1% of each run, Pallas kernels for 0% -> 22%
where the time goes in v1:
time: 96.3 us; the launch traced here: 95.9 us
  starting transfers between devices  32.9 us (34%)
  waiting for transfers between devices  29.7 us (31%)
  Pallas kernels  28 us (29%)
  local copies, waits for them, and re-layouts  3.66 us (4%)
    ppermute x18, waiting for transfers between devices, swap(): return lax.ppermute(x, 'past', pairs)  23.3 us
    ppermute x18, starting transfers between devices, swap(): return lax.ppermute(x, 'past', pairs)  22.8 us
    pallas_call x4, Pallas kernels, partial_product(): pl.pallas_call(functools.partial(partial_kernel, count), grid_spec=pltpu....  16.6 us
    ppermute x4, starting transfers between devices, summed(): lax.ppermute(squares, 'second', [(d, d ^ 1 << level) for d in range(secon...  10 us
    pallas_call x2, Pallas kernels, finish(): pl.pallas_call(functools.partial(finish_kernel, count_all, first, last),...  9.61 us
    ppermute x4, waiting for transfers between devices, summed(): lax.ppermute(squares, 'second', [(d, d ^ 1 << level) for d in range(secon...  6.45 us
    unnamed x10, local copies, waits for them, and re-layouts  3.66 us
  transfers between devices with their start and end apart: 22, of which 15 were waited for; matrix products, arithmetic and copies ran while one was open for 1% of the time, Pallas kernels for 22%

profile of v1, /device:TPU:0, one launch (start us, length us, event | category | flops | bytes accessed | tf_op | source)
XLA Modules:
  0.0 95.9 jit_solution(3752183051355717495)
XLA Ops:
  0.6 2.2 %copy-done = bf16[1024,2048]{1,0:T(8,128)(2,1)S(1)} copy-done((bf16[1024,2048]{1,0:T(8,128)(2,1)S(1)}, bf16[1024,2048]{1,0:T(8,128)(2,1)}, u32[]{:S(2)}) %copy-start) | copy-done | bytes 4194328
  2.8 4.1 %partial_product.7 = bf16[512,512]{1,0:T(8,128)(2,1)S(1)} custom-call(s32[1]{0:T(128)} %bitcast.me, bf16[1024,2048]{1,0:T(8,128)(2,1)S(1)} %copy-done, bf16[2048,1024]{1,0:T(8,128)(2,1)} %refs_3_.7, bf16[2048,1024]{1,0:T(8,128)(2,1)} %refs_3_.7, bf16[2048,1024]{1,0:T(8,128)(2,1)} %refs_3_.7, bf16[2048,1024]{1,0:T(8,128)(2,1)} %refs_3_.7), custom_call_target="tpu_custom_call" | custom-call | flops 1073741824 | bytes 4194304 | tf_op jit(solution)/shard_map/partial_product/pallas_call | solution.py:80
  7.5 4.1 %partial_product.5 = bf16[512,512]{1,0:T(8,128)(2,1)S(1)} custom-call(s32[1]{0:T(128)} %bitcast.me, bf16[1024,2048]{1,0:T(8,128)(2,1)S(1)} %copy-done, bf16[2048,1024]{1,0:T(8,128)(2,1)} %refs_3_.7, bf16[2048,1024]{1,0:T(8,128)(2,1)} %refs_3_.7, bf16[2048,1024]{1,0:T(8,128)(2,1)} %refs_3_.7, bf16[2048,1024]{1,0:T(8,128)(2,1)} %refs_3_.7), custom_call_target="tpu_custom_call" | custom-call | flops 1073741824 | bytes 4194304 | tf_op jit(solution)/shard_map/partial_product/pallas_call | solution.py:80
  11.7 4.1 %partial_product.4 = f32[512,512]{1,0:T(8,128)S(1)} custom-call(s32[1]{0:T(128)} %bitcast.me, bf16[1024,2048]{1,0:T(8,128)(2,1)S(1)} %copy-done, bf16[2048,1024]{1,0:T(8,128)(2,1)} %refs_3_.7, bf16[2048,1024]{1,0:T(8,128)(2,1)} %refs_3_.7, bf16[2048,1024]{1,0:T(8,128)(2,1)} %refs_3_.7, bf16[2048,1024]{1,0:T(8,128)(2,1)} %refs_3_.7), custom_call_target="tpu_custom_call" | custom-call | flops 1073741824 | bytes 4194304 | tf_op jit(solution)/shard_map/partial_product/pallas_call | solution.py:80
  15.9 4.2 %partial_product.6 = f32[512,512]{1,0:T(8,128)S(1)} custom-call(s32[1]{0:T(128)} %bitcast.me, bf16[1024,2048]{1,0:T(8,128)(2,1)S(1)} %copy-done, bf16[2048,1024]{1,0:T(8,128)(2,1)} %refs_3_.7, bf16[2048,1024]{1,0:T(8,128)(2,1)} %refs_3_.7, bf16[2048,1024]{1,0:T(8,128)(2,1)} %refs_3_.7, bf16[2048,1024]{1,0:T(8,128)(2,1)} %refs_3_.7), custom_call_target="tpu_custom_call" | custom-call | flops 1073741824 | bytes 4194304 | tf_op jit(solution)/shard_map/partial_product/pallas_call | solution.py:80
  20.2 3.0 %collective-permute-start.7 = (bf16[512,256]{1,0:T(8,128)(2,1)S(1)}, bf16[512,256]{1,0:T(8,128)(2,1)S(1)}, u32[]{:S(2)}, u32[]{:S(2)}) collective-permute-start(bf16[512,256]{1,0:T(8,128)(2,1)S(1)} %get-tuple-element.14), channel_id=1, source_target_pairs={{0,8},{4,20},{8,0},{12,28},{16,24},{20,4},{24,16},{28,12},{1,9},{5... | collective-permute-start | bytes 786440 | tf_op jit(solution)/shard_map/ppermute | solution.py:237
  23.4 4.1 %collective-permute-done.7 = bf16[512,256]{1,0:T(8,128)(2,1)S(1)} collective-permute-done((bf16[512,256]{1,0:T(8,128)(2,1)S(1)}, bf16[512,256]{1,0:T(8,128)(2,1)S(1)}, u32[]{:S(2)}, u32[]{:S(2)}) %collective-permute-start.7) | collective-permute-done | bytes 262176 | tf_op jit(solution)/shard_map/ppermute | solution.py:237
  27.6 2.1 %collective-permute-start.8 = (bf16[512,128]{1,0:T(8,128)(2,1)S(1)}, bf16[512,128]{1,0:T(8,128)(2,1)S(1)}, u32[]{:S(2)}, u32[]{:S(2)}) collective-permute-start(bf16[512,128]{1,0:T(8,128)(2,1)S(1)} %fusion.2), channel_id=1, source_target_pairs={{0,16},{4,12},{8,24},{12,4},{16,0},{20,28},{24,8},{28,20},{1,17},{... | collective-permute-start | bytes 393224 | tf_op jit(solution)/shard_map/ppermute | solution.py:237
  31.0 2.4 %collective-permute-start.2 = (bf16[512,128]{1,0:T(8,128)(2,1)S(1)}, bf16[512,128]{1,0:T(8,128)(2,1)S(1)}, u32[]{:S(2)}, u32[]{:S(2)}) collective-permute-start(bf16[512,128]{1,0:T(8,128)(2,1)S(1)} %fusion.5), channel_id=1, source_target_pairs={{0,16},{4,12},{8,24},{12,4},{16,0},{20,28},{24,8},{28,20},{1,17},{... | collective-permute-start | bytes 393224 | tf_op jit(solution)/shard_map/ppermute | solution.py:237
  34.8 1.6 %collective-permute-done.2 = bf16[512,128]{1,0:T(8,128)(2,1)S(1)} collective-permute-done((bf16[512,128]{1,0:T(8,128)(2,1)S(1)}, bf16[512,128]{1,0:T(8,128)(2,1)S(1)}, u32[]{:S(2)}, u32[]{:S(2)}) %collective-permute-start.2) | collective-permute-done | bytes 131104 | tf_op jit(solution)/shard_map/ppermute | solution.py:237
  36.4 2.1 %collective-permute-start.3 = (bf16[512,128]{1,0:T(8,128)(2,1)S(1)}, bf16[512,128]{1,0:T(8,128)(2,1)S(1)}, u32[]{:S(2)}, u32[]{:S(2)}) collective-permute-start(bf16[512,128]{1,0:T(8,128)(2,1)S(1)} %fusion.7.memory), channel_id=1, source_target_pairs={{0,16},{4,12},{8,24},{12,4},{16,0},{20,28},{24,8},{28,20},{1,17},{... | collective-permute-start | bytes 393224 | tf_op jit(solution)/shard_map/ppermute | solution.py:237
  40.1 2.7 %collective-permute-done.3 = bf16[512,128]{1,0:T(8,128)(2,1)S(1)} collective-permute-done((bf16[512,128]{1,0:T(8,128)(2,1)S(1)}, bf16[512,128]{1,0:T(8,128)(2,1)S(1)}, u32[]{:S(2)}, u32[]{:S(2)}) %collective-permute-start.3) | collective-permute-done | bytes 131104 | tf_op jit(solution)/shard_map/ppermute | solution.py:237
  42.9 2.1 %collective-permute-start.4 = (bf16[512,256]{1,0:T(8,128)(2,1)S(1)}, bf16[512,256]{1,0:T(8,128)(2,1)S(1)}, u32[]{:S(2)}, u32[]{:S(2)}) collective-permute-start(bf16[512,256]{1,0:T(8,128)(2,1)S(1)} %pad_maximum_fusion.4), channel_id=1, source_target_pairs={{0,8},{4,20},{8,0},{12,28},{16,24},{20,4},{24,16},{28,12},{1,9},{5... | collective-permute-start | bytes 786440 | tf_op jit(solution)/shard_map/ppermute | solution.py:237
  45.1 4.2 %collective-permute-done.4 = bf16[512,256]{1,0:T(8,128)(2,1)S(1)} collective-permute-done((bf16[512,256]{1,0:T(8,128)(2,1)S(1)}, bf16[512,256]{1,0:T(8,128)(2,1)S(1)}, u32[]{:S(2)}, u32[]{:S(2)}) %collective-permute-start.4) | collective-permute-done | bytes 262176 | tf_op jit(solution)/shard_map/ppermute | solution.py:237
  49.9 2.2 %collective-permute-start.12 = (f32[8,128]{1,0:T(8,128)S(1)}, f32[8,128]{1,0:T(8,128)S(1)}, u32[]{:S(2)}, u32[]{:S(2)}) collective-permute-start(f32[8,128]{1,0:T(8,128)S(1)} %get-tuple-element.8), channel_id=1, source_target_pairs={{0,1},{1,0},{2,3},{3,2},{4,5},{5,4},{6,7},{7,6},{8,9},{9,8},{10,11... | collective-permute-start | bytes 12296 | tf_op jit(solution)/shard_map/ppermute | solution.py:261
  52.1 1.6 %collective-permute-done.12 = f32[8,128]{1,0:T(8,128)S(1)} collective-permute-done((f32[8,128]{1,0:T(8,128)S(1)}, f32[8,128]{1,0:T(8,128)S(1)}, u32[]{:S(2)}, u32[]{:S(2)}) %collective-permute-start.12) | collective-permute-done | bytes 4128 | tf_op jit(solution)/shard_map/ppermute | solution.py:261
  53.7 3.0 %collective-permute-start.13 = (f32[8,128]{1,0:T(8,128)S(1)}, f32[8,128]{1,0:T(8,128)S(1)}, u32[]{:S(2)}, u32[]{:S(2)}) collective-permute-start(f32[8,128]{1,0:T(8,128)S(1)} %add.70), channel_id=1, source_target_pairs={{0,2},{1,3},{2,0},{3,1},{4,6},{5,7},{6,4},{7,5},{8,10},{9,11},{10,... | collective-permute-start | bytes 12296 | tf_op jit(solution)/shard_map/ppermute | solution.py:261
  56.7 1.6 %collective-permute-done.13 = f32[8,128]{1,0:T(8,128)S(1)} collective-permute-done((f32[8,128]{1,0:T(8,128)S(1)}, f32[8,128]{1,0:T(8,128)S(1)}, u32[]{:S(2)}, u32[]{:S(2)}) %collective-permute-start.13) | collective-permute-done | bytes 4128 | tf_op jit(solution)/shard_map/ppermute | solution.py:261
  59.5 1.8 %collective-permute-start.15 = (f32[8,128]{1,0:T(8,128)S(1)}, f32[8,128]{1,0:T(8,128)S(1)}, u32[]{:S(2)}, u32[]{:S(2)}) collective-permute-start(f32[8,128]{1,0:T(8,128)S(1)} %add.72), channel_id=1, source_target_pairs={{0,8},{4,20},{8,0},{12,28},{16,24},{20,4},{24,16},{28,12},{1,9},{5... | collective-permute-start | bytes 12296 | tf_op jit(solution)/shard_map/ppermute | solution.py:237
  61.3 1.8 %collective-permute-done.15 = f32[8,128]{1,0:T(8,128)S(1)} collective-permute-done((f32[8,128]{1,0:T(8,128)S(1)}, f32[8,128]{1,0:T(8,128)S(1)}, u32[]{:S(2)}, u32[]{:S(2)}) %collective-permute-start.15) | collective-permute-done | bytes 4128 | tf_op jit(solution)/shard_map/ppermute | solution.py:237
  63.1 1.9 %collective-permute-start.16 = (f32[8,128]{1,0:T(8,128)S(1)}, f32[8,128]{1,0:T(8,128)S(1)}, u32[]{:S(2)}, u32[]{:S(2)}) collective-permute-start(f32[8,128]{1,0:T(8,128)S(1)} %add.73), channel_id=1, source_target_pairs={{0,16},{4,12},{8,24},{12,4},{16,0},{20,28},{24,8},{28,20},{1,17},{... | collective-permute-start | bytes 12296 | tf_op jit(solution)/shard_map/ppermute | solution.py:237
  64.9 1.8 %collective-permute-done.16 = f32[8,128]{1,0:T(8,128)S(1)} collective-permute-done((f32[8,128]{1,0:T(8,128)S(1)}, f32[8,128]{1,0:T(8,128)S(1)}, u32[]{:S(2)}, u32[]{:S(2)}) %collective-permute-start.16) | collective-permute-done | bytes 4128 | tf_op jit(solution)/shard_map/ppermute | solution.py:237
  68.0 1.9 %collective-permute-start.17 = (f32[8,128]{1,0:T(8,128)S(1)}, f32[8,128]{1,0:T(8,128)S(1)}, u32[]{:S(2)}, u32[]{:S(2)}) collective-permute-start(f32[8,128]{1,0:T(8,128)S(1)} %get-tuple-element.11), channel_id=1, source_target_pairs={{0,1},{1,0},{2,3},{3,2},{4,5},{5,4},{6,7},{7,6},{8,9},{9,8},{10,11... | collective-permute-start | bytes 12296 | tf_op jit(solution)/shard_map/ppermute | solution.py:261
  70.0 1.7 %collective-permute-done.17 = f32[8,128]{1,0:T(8,128)S(1)} collective-permute-done((f32[8,128]{1,0:T(8,128)S(1)}, f32[8,128]{1,0:T(8,128)S(1)}, u32[]{:S(2)}, u32[]{:S(2)}) %collective-permute-start.17) | collective-permute-done | bytes 4128 | tf_op jit(solution)/shard_map/ppermute | solution.py:261
  71.6 2.9 %collective-permute-start.18 = (f32[8,128]{1,0:T(8,128)S(1)}, f32[8,128]{1,0:T(8,128)S(1)}, u32[]{:S(2)}, u32[]{:S(2)}) collective-permute-start(f32[8,128]{1,0:T(8,128)S(1)} %add.75), channel_id=1, source_target_pairs={{0,2},{1,3},{2,0},{3,1},{4,6},{5,7},{6,4},{7,5},{8,10},{9,11},{10,... | collective-permute-start | bytes 12296 | tf_op jit(solution)/shard_map/ppermute | solution.py:261
  74.6 1.6 %collective-permute-done.18 = f32[8,128]{1,0:T(8,128)S(1)} collective-permute-done((f32[8,128]{1,0:T(8,128)S(1)}, f32[8,128]{1,0:T(8,128)S(1)}, u32[]{:S(2)}, u32[]{:S(2)}) %collective-permute-start.18) | collective-permute-done | bytes 4128 | tf_op jit(solution)/shard_map/ppermute | solution.py:261
  77.3 1.8 %collective-permute-start.20 = (f32[8,128]{1,0:T(8,128)S(1)}, f32[8,128]{1,0:T(8,128)S(1)}, u32[]{:S(2)}, u32[]{:S(2)}) collective-permute-start(f32[8,128]{1,0:T(8,128)S(1)} %add.77), channel_id=1, source_target_pairs={{0,8},{4,20},{8,0},{12,28},{16,24},{20,4},{24,16},{28,12},{1,9},{5... | collective-permute-start | bytes 12296 | tf_op jit(solution)/shard_map/ppermute | solution.py:237
  79.2 1.8 %collective-permute-done.20 = f32[8,128]{1,0:T(8,128)S(1)} collective-permute-done((f32[8,128]{1,0:T(8,128)S(1)}, f32[8,128]{1,0:T(8,128)S(1)}, u32[]{:S(2)}, u32[]{:S(2)}) %collective-permute-start.20) | collective-permute-done | bytes 4128 | tf_op jit(solution)/shard_map/ppermute | solution.py:237
  80.9 1.9 %collective-permute-start.21 = (f32[8,128]{1,0:T(8,128)S(1)}, f32[8,128]{1,0:T(8,128)S(1)}, u32[]{:S(2)}, u32[]{:S(2)}) collective-permute-start(f32[8,128]{1,0:T(8,128)S(1)} %add.78), channel_id=1, source_target_pairs={{0,16},{4,12},{8,24},{12,4},{16,0},{20,28},{24,8},{28,20},{1,17},{... | collective-permute-start | bytes 12296 | tf_op jit(solution)/shard_map/ppermute | solution.py:237
  82.8 1.8 %collective-permute-done.21 = f32[8,128]{1,0:T(8,128)S(1)} collective-permute-done((f32[8,128]{1,0:T(8,128)S(1)}, f32[8,128]{1,0:T(8,128)S(1)}, u32[]{:S(2)}, u32[]{:S(2)}) %collective-permute-start.21) | collective-permute-done | bytes 4128 | tf_op jit(solution)/shard_map/ppermute | solution.py:237
  84.7 6.5 %finish_block.2 = (bf16[1024,1024]{1,0:T(8,128)(2,1)}, bf16[1024,1024]{1,0:T(8,128)(2,1)}, f32[512,1024]{1,0:T(8,128)S(1)}) custom-call(s32[1]{0:T(128)} %bitcast.me, bf16[512,1024]{1,0:T(8,128)(2,1)S(1)} %pad_maximum_fusion.1.left.right, bf16[512,1024]{1,0:T(8,128)(2,1)S(1)} %pad_maximum_fusion.1.left.right, bf16[2,512,1024]{2,1,0:T(8,128)(2,1)} %w.7, ...), custom_call_target="tpu_custom_call" | custom-call | flops 1073741824 | bytes 4194304 | tf_op jit(solution)/shard_map/finish_block/pallas_call | solution.py:210
  92.8 3.1 %finish_block.3 = (bf16[1024,1024]{1,0:T(8,128)(2,1)}, bf16[1024,1024]{1,0:T(8,128)(2,1)}) custom-call(s32[1]{0:T(128)} %bitcast.me, bf16[512,1024]{1,0:T(8,128)(2,1)S(1)} %pad_maximum_fusion.left.right, bf16[512,1024]{1,0:T(8,128)(2,1)S(1)} %pad_maximum_fusion.left.right, ...), custom_call_target="tpu_custom_call", output_to_operand_aliasing={{0}: (7, {}), {1}: (8, {})} | custom-call | flops 1073741824 | bytes 4194304 | tf_op jit(solution)/shard_map/finish_block/pallas_call | solution.py:210
  (52 shorter events, 11.4 us)
Async XLA Ops:
  0.6 2.2 %copy-start = (bf16[1024,2048]{1,0:T(8,128)(2,1)S(1)}, bf16[1024,2048]{1,0:T(8,128)(2,1)}, u32[]{:S(2)}) copy-start(bf16[1024,2048]{1,0:T(8,128)(2,1)} %sigma.7) | copy-start | bytes 12582916
  7.0 13.1 %collective-permute-start.6 = (bf16[512,512]{1,0:T(8,128)(2,1)S(1)}, bf16[512,512]{1,0:T(8,128)(2,1)S(1)}, u32[]{:S(2)}, u32[]{:S(2)}) collective-permute-start(bf16[512,512]{1,0:T(8,128)(2,1)S(1)} %partial_product.7), channel_id=1, source_target_pairs={{0,4},{4,0},{8,12},{12,8},{16,20},{20,16},{24,28},{28,24},{1,5},{5... | collective-permute-start | bytes 1572872 | tf_op jit(solution)/shard_map/ppermute | solution.py:237
  11.6 11.6 %collective-permute-start = (bf16[512,512]{1,0:T(8,128)(2,1)S(1)}, bf16[512,512]{1,0:T(8,128)(2,1)S(1)}, u32[]{:S(2)}, u32[]{:S(2)}) collective-permute-start(bf16[512,512]{1,0:T(8,128)(2,1)S(1)} %partial_product.5), channel_id=1, source_target_pairs={{0,4},{4,0},{8,12},{12,8},{16,20},{20,16},{24,28},{28,24},{1,5},{5... | collective-permute-start | bytes 1572872 | tf_op jit(solution)/shard_map/ppermute | solution.py:237
  20.2 7.4 %collective-permute-start.7 = (bf16[512,256]{1,0:T(8,128)(2,1)S(1)}, bf16[512,256]{1,0:T(8,128)(2,1)S(1)}, u32[]{:S(2)}, u32[]{:S(2)}) collective-permute-start(bf16[512,256]{1,0:T(8,128)(2,1)S(1)} %get-tuple-element.14), channel_id=1, source_target_pairs={{0,8},{4,20},{8,0},{12,28},{16,24},{20,4},{24,16},{28,12},{1,9},{5... | collective-permute-start | bytes 786440 | tf_op jit(solution)/shard_map/ppermute | solution.py:237
  23.3 7.6 %collective-permute-start.1 = (bf16[512,256]{1,0:T(8,128)(2,1)S(1)}, bf16[512,256]{1,0:T(8,128)(2,1)S(1)}, u32[]{:S(2)}, u32[]{:S(2)}) collective-permute-start(bf16[512,256]{1,0:T(8,128)(2,1)S(1)} %get-tuple-element.16), channel_id=1, source_target_pairs={{0,8},{4,20},{8,0},{12,28},{16,24},{20,4},{24,16},{28,12},{1,9},{5... | collective-permute-start | bytes 786440 | tf_op jit(solution)/shard_map/ppermute | solution.py:237
  27.6 5.8 %collective-permute-start.8 = (bf16[512,128]{1,0:T(8,128)(2,1)S(1)}, bf16[512,128]{1,0:T(8,128)(2,1)S(1)}, u32[]{:S(2)}, u32[]{:S(2)}) collective-permute-start(bf16[512,128]{1,0:T(8,128)(2,1)S(1)} %fusion.2), channel_id=1, source_target_pairs={{0,16},{4,12},{8,24},{12,4},{16,0},{20,28},{24,8},{28,20},{1,17},{... | collective-permute-start | bytes 393224 | tf_op jit(solution)/shard_map/ppermute | solution.py:237
  30.9 18.5 %copy-start.1 = (bf16[2,512,1024]{2,1,0:T(8,128)(2,1)S(1)}, bf16[2,512,1024]{2,1,0:T(8,128)(2,1)}, u32[]{:S(2)}) copy-start(bf16[2,512,1024]{2,1,0:T(8,128)(2,1)} %w.7) | copy-start | bytes 6291460
  31.0 18.5 %copy-start.3 = (bf16[512,1024]{1,0:T(8,128)(2,1)S(1)}, bf16[512,1024]{1,0:T(8,128)(2,1)}, u32[]{:S(2)}) copy-start(bf16[512,1024]{1,0:T(8,128)(2,1)} %prev.3) | copy-start | bytes 3145732
  31.0 18.5 %copy-start.4 = (f32[32,1024]{1,0:T(8,128)S(1)}, f32[32,1024]{1,0:T(8,128)}, u32[]{:S(2)}) copy-start(f32[32,1024]{1,0:T(8,128)} %coupling.7) | copy-start | bytes 393220
  31.0 5.4 %collective-permute-start.2 = (bf16[512,128]{1,0:T(8,128)(2,1)S(1)}, bf16[512,128]{1,0:T(8,128)(2,1)S(1)}, u32[]{:S(2)}, u32[]{:S(2)}) collective-permute-start(bf16[512,128]{1,0:T(8,128)(2,1)S(1)} %fusion.5), channel_id=1, source_target_pairs={{0,16},{4,12},{8,24},{12,4},{16,0},{20,28},{24,8},{28,20},{1,17},{... | collective-permute-start | bytes 393224 | tf_op jit(solution)/shard_map/ppermute | solution.py:237
  33.5 5.0 %collective-permute-start.9 = (bf16[512,128]{1,0:T(8,128)(2,1)S(1)}, bf16[512,128]{1,0:T(8,128)(2,1)S(1)}, u32[]{:S(2)}, u32[]{:S(2)}) collective-permute-start(bf16[512,128]{1,0:T(8,128)(2,1)S(1)} %fusion.4.memory), channel_id=1, source_target_pairs={{0,16},{4,12},{8,24},{12,4},{16,0},{20,28},{24,8},{28,20},{1,17},{... | collective-permute-start | bytes 393224 | tf_op jit(solution)/shard_map/ppermute | solution.py:237
  36.4 6.4 %collective-permute-start.3 = (bf16[512,128]{1,0:T(8,128)(2,1)S(1)}, bf16[512,128]{1,0:T(8,128)(2,1)S(1)}, u32[]{:S(2)}, u32[]{:S(2)}) collective-permute-start(bf16[512,128]{1,0:T(8,128)(2,1)S(1)} %fusion.7.memory), channel_id=1, source_target_pairs={{0,16},{4,12},{8,24},{12,4},{16,0},{20,28},{24,8},{28,20},{1,17},{... | collective-permute-start | bytes 393224 | tf_op jit(solution)/shard_map/ppermute | solution.py:237
  38.5 6.4 %collective-permute-start.10 = (bf16[512,256]{1,0:T(8,128)(2,1)S(1)}, bf16[512,256]{1,0:T(8,128)(2,1)S(1)}, u32[]{:S(2)}, u32[]{:S(2)}) collective-permute-start(bf16[512,256]{1,0:T(8,128)(2,1)S(1)} %pad_maximum_fusion.5), channel_id=1, source_target_pairs={{0,8},{4,20},{8,0},{12,28},{16,24},{20,4},{24,16},{28,12},{1,9},{5... | collective-permute-start | bytes 786440 | tf_op jit(solution)/shard_map/ppermute | solution.py:237
  42.9 6.5 %collective-permute-start.4 = (bf16[512,256]{1,0:T(8,128)(2,1)S(1)}, bf16[512,256]{1,0:T(8,128)(2,1)S(1)}, u32[]{:S(2)}, u32[]{:S(2)}) collective-permute-start(bf16[512,256]{1,0:T(8,128)(2,1)S(1)} %pad_maximum_fusion.4), channel_id=1, source_target_pairs={{0,8},{4,20},{8,0},{12,28},{16,24},{20,4},{24,16},{28,12},{1,9},{5... | collective-permute-start | bytes 786440 | tf_op jit(solution)/shard_map/ppermute | solution.py:237
  45.0 39.5 %collective-permute-start.11 = (bf16[512,512]{1,0:T(8,128)(2,1)S(1)}, bf16[512,512]{1,0:T(8,128)(2,1)S(1)}, u32[]{:S(2)}, u32[]{:S(2)}) collective-permute-start(bf16[512,512]{1,0:T(8,128)(2,1)S(1)} %pad_maximum_fusion.3), channel_id=1, source_target_pairs={{0,4},{4,0},{8,12},{12,8},{16,20},{20,16},{24,28},{28,24},{1,5},{5... | collective-permute-start | bytes 1572872 | tf_op jit(solution)/shard_map/ppermute | solution.py:237
  49.4 41.8 %collective-permute-start.5 = (bf16[512,512]{1,0:T(8,128)(2,1)S(1)}, bf16[512,512]{1,0:T(8,128)(2,1)S(1)}, u32[]{:S(2)}, u32[]{:S(2)}) collective-permute-start(bf16[512,512]{1,0:T(8,128)(2,1)S(1)} %pad_maximum_fusion.2), channel_id=1, source_target_pairs={{0,4},{4,0},{8,12},{12,8},{16,20},{20,16},{24,28},{28,24},{1,5},{5... | collective-permute-start | bytes 1572872 | tf_op jit(solution)/shard_map/ppermute | solution.py:237
  49.9 3.8 %collective-permute-start.12 = (f32[8,128]{1,0:T(8,128)S(1)}, f32[8,128]{1,0:T(8,128)S(1)}, u32[]{:S(2)}, u32[]{:S(2)}) collective-permute-start(f32[8,128]{1,0:T(8,128)S(1)} %get-tuple-element.8), channel_id=1, source_target_pairs={{0,1},{1,0},{2,3},{3,2},{4,5},{5,4},{6,7},{7,6},{8,9},{9,8},{10,11... | collective-permute-start | bytes 12296 | tf_op jit(solution)/shard_map/ppermute | solution.py:261
  53.7 4.6 %collective-permute-start.13 = (f32[8,128]{1,0:T(8,128)S(1)}, f32[8,128]{1,0:T(8,128)S(1)}, u32[]{:S(2)}, u32[]{:S(2)}) collective-permute-start(f32[8,128]{1,0:T(8,128)S(1)} %add.70), channel_id=1, source_target_pairs={{0,2},{1,3},{2,0},{3,1},{4,6},{5,7},{6,4},{7,5},{8,10},{9,11},{10,... | collective-permute-start | bytes 12296 | tf_op jit(solution)/shard_map/ppermute | solution.py:261
  58.3 1.2 %collective-permute-start.14 = (f32[8,128]{1,0:T(8,128)S(1)}, f32[8,128]{1,0:T(8,128)S(1)}, u32[]{:S(2)}, u32[]{:S(2)}) collective-permute-start(f32[8,128]{1,0:T(8,128)S(1)} %add.71), channel_id=1, source_target_pairs={{0,4},{4,0},{8,12},{12,8},{16,20},{20,16},{24,28},{28,24},{1,5},{5... | collective-permute-start | bytes 12296 | tf_op jit(solution)/shard_map/ppermute | solution.py:237
  59.5 3.6 %collective-permute-start.15 = (f32[8,128]{1,0:T(8,128)S(1)}, f32[8,128]{1,0:T(8,128)S(1)}, u32[]{:S(2)}, u32[]{:S(2)}) collective-permute-start(f32[8,128]{1,0:T(8,128)S(1)} %add.72), channel_id=1, source_target_pairs={{0,8},{4,20},{8,0},{12,28},{16,24},{20,4},{24,16},{28,12},{1,9},{5... | collective-permute-start | bytes 12296 | tf_op jit(solution)/shard_map/ppermute | solution.py:237
  63.1 3.6 %collective-permute-start.16 = (f32[8,128]{1,0:T(8,128)S(1)}, f32[8,128]{1,0:T(8,128)S(1)}, u32[]{:S(2)}, u32[]{:S(2)}) collective-permute-start(f32[8,128]{1,0:T(8,128)S(1)} %add.73), channel_id=1, source_target_pairs={{0,16},{4,12},{8,24},{12,4},{16,0},{20,28},{24,8},{28,20},{1,17},{... | collective-permute-start | bytes 12296 | tf_op jit(solution)/shard_map/ppermute | solution.py:237
  68.0 3.6 %collective-permute-start.17 = (f32[8,128]{1,0:T(8,128)S(1)}, f32[8,128]{1,0:T(8,128)S(1)}, u32[]{:S(2)}, u32[]{:S(2)}) collective-permute-start(f32[8,128]{1,0:T(8,128)S(1)} %get-tuple-element.11), channel_id=1, source_target_pairs={{0,1},{1,0},{2,3},{3,2},{4,5},{5,4},{6,7},{7,6},{8,9},{9,8},{10,11... | collective-permute-start | bytes 12296 | tf_op jit(solution)/shard_map/ppermute | solution.py:261
  71.6 4.5 %collective-permute-start.18 = (f32[8,128]{1,0:T(8,128)S(1)}, f32[8,128]{1,0:T(8,128)S(1)}, u32[]{:S(2)}, u32[]{:S(2)}) collective-permute-start(f32[8,128]{1,0:T(8,128)S(1)} %add.75), channel_id=1, source_target_pairs={{0,2},{1,3},{2,0},{3,1},{4,6},{5,7},{6,4},{7,5},{8,10},{9,11},{10,... | collective-permute-start | bytes 12296 | tf_op jit(solution)/shard_map/ppermute | solution.py:261
  76.2 1.2 %collective-permute-start.19 = (f32[8,128]{1,0:T(8,128)S(1)}, f32[8,128]{1,0:T(8,128)S(1)}, u32[]{:S(2)}, u32[]{:S(2)}) collective-permute-start(f32[8,128]{1,0:T(8,128)S(1)} %add.76), channel_id=1, source_target_pairs={{0,4},{4,0},{8,12},{12,8},{16,20},{20,16},{24,28},{28,24},{1,5},{5... | collective-permute-start | bytes 12296 | tf_op jit(solution)/shard_map/ppermute | solution.py:237
  77.3 3.6 %collective-permute-start.20 = (f32[8,128]{1,0:T(8,128)S(1)}, f32[8,128]{1,0:T(8,128)S(1)}, u32[]{:S(2)}, u32[]{:S(2)}) collective-permute-start(f32[8,128]{1,0:T(8,128)S(1)} %add.77), channel_id=1, source_target_pairs={{0,8},{4,20},{8,0},{12,28},{16,24},{20,4},{24,16},{28,12},{1,9},{5... | collective-permute-start | bytes 12296 | tf_op jit(solution)/shard_map/ppermute | solution.py:237
  80.9 3.6 %collective-permute-start.21 = (f32[8,128]{1,0:T(8,128)S(1)}, f32[8,128]{1,0:T(8,128)S(1)}, u32[]{:S(2)}, u32[]{:S(2)}) collective-permute-start(f32[8,128]{1,0:T(8,128)S(1)} %add.78), channel_id=1, source_target_pairs={{0,16},{4,12},{8,24},{12,4},{16,0},{20,28},{24,8},{28,20},{1,17},{... | collective-permute-start | bytes 12296 | tf_op jit(solution)/shard_map/ppermute | solution.py:237
  91.2 1.6 %copy-start.2 = (bf16[2,512,1024]{2,1,0:T(8,128)(2,1)S(1)}, bf16[2,512,1024]{2,1,0:T(8,128)(2,1)}, u32[]{:S(2)}) copy-start(bf16[2,512,1024]{2,1,0:T(8,128)(2,1)} %w.7) | copy-start | bytes 6291460

commit v2 on v1

--- a/solution.py
+++ b/solution.py
@@ -43,49 +43,29 @@
     def sent(self, me, j):
         return self.own(me) ^ self.half ^ jnp.where(me % 2 == 1, j, reverse_bits(j, self.depth - 1))
 
-    def place(self, me, block):
-        apart = block ^ self.own(me)
-        low, top = apart & (self.half - 1), apart & self.half
-        turned = (me + top // self.half) % 2 == 1
-        return top + jnp.where(turned, reverse_bits(low, self.depth - 1), low)
-
-
-def partial_kernel(count, me, sigma, *refs):
-    parts, out, total = refs[:count], refs[count], refs[count + 1]
-    step = pl.program_id(0)
-    right = jnp.concatenate([part[...] for part in parts], axis=1)
-    product = jnp.dot(sigma[...], right, preferred_element_type=F32)
-
-    @pl.when(step == 0)
-    def _():
-        total[...] = product
-
-    @pl.when(step > 0)
-    def _():
-        total[...] += product
-
-    @pl.when(step == pl.num_programs(0) - 1)
-    def _():
-        out[...] = total[...].astype(out.dtype)
+    def owner(self, block):
+        return reverse_bits(block, self.depth)
+
+
+def partial_kernel(me, sigma, left, right, out):
+    both = jnp.concatenate([left[...], right[...]], axis=1)
+    out[...] = jnp.dot(sigma[...], both, preferred_element_type=F32).astype(out.dtype)
 
 
 def partial_product(me, sigma_hist, g_hist, block, rows, blocks_of, count, width, dtype):
     depth = g_hist.shape[0]
-    chunk = depth // 4
     columns = count * width
 
-    def part(j):
-        return pl.BlockSpec((chunk, width), lambda k, me: (k, blocks_of(me[0], j)))
+    def part(side):
+        return pl.BlockSpec((depth, width), lambda q, me: (0, blocks_of(me[0], 2 * q + side)))
 
     return pl.pallas_call(
-        functools.partial(partial_kernel, count),
+        partial_kernel,
         grid_spec=pltpu.PrefetchScalarGridSpec(
             num_scalar_prefetch=1,
-            grid=(depth // chunk,),
-            in_specs=[pl.BlockSpec((rows, chunk), lambda k, me: (block, k))]
-            + [part(j) for j in range(count)],
-            out_specs=pl.BlockSpec((rows, columns), lambda k, me: (0, 0)),
-            scratch_shapes=[pltpu.VMEM((rows, columns), F32)],
+            grid=(count // 2,),
+            in_specs=[pl.BlockSpec((rows, depth), lambda q, me: (block, 0)), part(0), part(1)],
+            out_specs=pl.BlockSpec((rows, 2 * width), lambda q, me: (0, q)),
         ),
         out_shape=jax.ShapeDtypeStruct((rows, columns), dtype),
         compiler_params=pltpu.CompilerParams(vmem_limit_bytes=VMEM),
@@ -93,7 +73,7 @@
             flops=2 * rows * depth * columns, bytes_accessed=2 * depth * (rows + columns), transcendentals=0
         ),
         name="partial_product",
-    )(me, sigma_hist, *[g_hist] * count)
+    )(me, sigma_hist, g_hist, g_hist)
 
 
 def cubed(g, coupling):
@@ -140,7 +120,7 @@
         operands = [memory, volterra, prev]
     else:
         kernel = functools.partial(own_next_kernel, count_all)
-        in_specs = [full((rows, width)), w_spec, full((rows, width)), full(prev_squares.shape)]
+        in_specs = [full((rows, width)), w_spec, full((rows, width)), pl.BlockSpec(prev_squares.shape, lambda i, me: (0, 0, 0))]
         operands = [memory, volterra, prev, prev_squares]
     return pl.pallas_call(
         kernel,
@@ -179,11 +159,11 @@
 
 
 def finish(me, order, memory, volterra, block, prev, squares, coupling, outs, count_all, width):
-    rows, columns = memory.shape
+    rows, columns = memory.shape[1], coupling.shape[1]
     blocks = volterra.shape[0]
     pair = 2 * width
     first, last = block == 0, block == blocks - 1
-    place = lambda side: pl.BlockSpec((rows, width), lambda q, me: (0, order.place(me[0], 2 * q + side)))
+    place = lambda side: pl.BlockSpec((None, rows, width), lambda q, me: (order.owner(2 * q + side), 0, 0))
     w_spec = lambda k: pl.BlockSpec((1, rows, 2 * rows), lambda q, me: (k, 0, 0))
     straight = lambda size, row=0: pl.BlockSpec((size, pair), lambda q, me: (row, q))
     operands = [memory, memory, volterra, prev, squares, coupling]
@@ -192,7 +172,7 @@
         place(1),
         w_spec(block),
         straight(rows),
-        pl.BlockSpec(squares.shape, lambda q, me: (0, 0)),
+        pl.BlockSpec(squares.shape, lambda q, me: (0, 0, 0)),
         straight(coupling.shape[0]),
     ]
     out_specs = [straight(rows, block)] * 2
@@ -225,7 +205,7 @@
 def per_device(past, second, g_hist, sigma_hist, volterra, sigma_edge, coupling):
     blocks, rows = volterra.shape[:2]
     columns = g_hist.shape[1]
-    count_all = rows * columns * second
+    count_all = rows * columns * second * (past >> min(log2(past), log2(max(columns // 128, 2))))
     depth = min(log2(past), log2(max(columns // 128, 2)))
     width = columns >> depth
     even, odd = level_bits(past, depth)
@@ -251,27 +231,15 @@
             total = rounded.astype(F32) + swap(rounded, level).astype(F32)
         return total.astype(BF16)
 
-    def gathered(piece):
-        for level in reversed(range(depth)):
-            piece = jnp.concatenate([piece, swap(piece, level)], axis=1)
-        return piece
-
-    def summed(squares):
-        for level in range(log2(second)):
-            squares = squares + lax.ppermute(squares, "second", [(d, d ^ (1 << level)) for d in range(second)])
-        for level in range(depth):
-            squares = squares + swap(squares, level)
-        return squares
-
     own, whole, squares = [], [], []
     cubic, total = sigma_edge, None
     for block in range(blocks):
         own.append(reduced(block))
     for block in range(blocks):
         cubic, local = own_columns(me, order, own[block], volterra, block, cubic, total, coupling, count_all)
-        total = summed(local)
+        total = lax.all_gather(local, ("past", "second"))
         squares.append(total)
-        whole.append(gathered(own[block]))
+        whole.append(lax.all_gather(own[block], "past"))
     outs, start = None, sigma_edge
     for block in range(blocks):
         results = finish(

time: 96.3 us -> 206 us (2.14)
  blocking collectives: 0 us -> 132 us
  starting transfers between devices: 32.9 us -> 9.11 us
  between operations: 0.83 us -> 14.2 us
  waiting for transfers between devices: 29.7 us -> 16.9 us
  Pallas kernels: 28 us -> 21.8 us
  local copies, waits for them, and re-layouts: 3.66 us -> 9.78 us
    all_gather x0 -> x2, blocking collectives: none -> 132 us  [per_device(): total = lax.all_gather(local, ('past', 'second'))]
    ppermute x18 -> x6, starting transfers between devices: 22.8 us -> 9.03 us  [swap(): return lax.ppermute(x, 'past', pairs)]
    ppermute x4 -> x0, starting transfers between devices: 10 us -> none  [summed(): lax.ppermute(squares, 'second', [(d, d ^ 1 << level) for d in range(secon...]
    ppermute x18 -> x6, waiting for transfers between devices: 23.3 us -> 16.8 us  [swap(): return lax.ppermute(x, 'past', pairs)]
    ppermute x4 -> x0, waiting for transfers between devices: 6.45 us -> none  [summed(): lax.ppermute(squares, 'second', [(d, d ^ 1 << level) for d in range(secon...]
    unnamed x10 -> x24, local copies, waits for them, and re-layouts: 3.66 us -> 9.78 us
    pallas_call x4, Pallas kernels: 16.6 us -> 11.2 us  [partial_product(): pl.pallas_call(partial_kernel, grid_spec=pltpu.PrefetchScalarGridSpec(num...]
  transfers between devices with their start and end apart: 22 -> 8, of which waited for: 15 -> 4; matrix products, arithmetic and copies ran while one was open for 1% -> 0% of each run, Pallas kernels for 22% -> 8%
where the time goes in v2:
time: 206 us; the launch traced here: 205 us
  blocking collectives  132 us (64%)
  Pallas kernels  21.8 us (11%)
  waiting for transfers between devices  16.9 us (8%)
  between operations  14.2 us (7%)
  local copies, waits for them, and re-layouts  9.78 us (5%)
  starting transfers between devices  9.11 us (4%)
    all_gather x2, blocking collectives, per_device(): total = lax.all_gather(local, ('past', 'second'))  132 us
    ppermute x6, waiting for transfers between devices, swap(): return lax.ppermute(x, 'past', pairs)  16.8 us
    pallas_call x4, Pallas kernels, partial_product(): pl.pallas_call(partial_kernel, grid_spec=pltpu.PrefetchScalarGridSpec(num...  11.2 us
    unnamed x24, local copies, waits for them, and re-layouts  9.78 us
    ppermute x6, starting transfers between devices, swap(): return lax.ppermute(x, 'past', pairs)  9.03 us
    pallas_call x2, Pallas kernels, finish(): pl.pallas_call(functools.partial(finish_kernel, count_all, first, last),...  8.85 us
  transfers between devices with their start and end apart: 8, of which 4 were waited for; matrix products, arithmetic and copies ran while one was open for 0% of the time, Pallas kernels for 8%

profile of v2, /device:TPU:0, one launch (start us, length us, event | category | flops | bytes accessed | tf_op | source)
XLA Modules:
  0.0 205.3 jit_solution(13781401364230265769)
XLA Ops:
  7.2 0.0 all-gather.9.cloned.1.call-start
  7.2 2.2 %copy-done = bf16[1024,2048]{1,0:T(8,128)(2,1)S(1)} copy-done((bf16[1024,2048]{1,0:T(8,128)(2,1)S(1)}, bf16[1024,2048]{1,0:T(8,128)(2,1)}, u32[]{:S(2)}) %copy-start) | copy-done | bytes 4194328
  9.4 2.8 %partial_product.7 = bf16[512,512]{1,0:T(8,128)(2,1)S(1)} custom-call(s32[1]{0:T(128)} %bitcast.me, bf16[1024,2048]{1,0:T(8,128)(2,1)S(1)} %copy-done, bf16[2048,1024]{1,0:T(8,128)(2,1)} %right.7, bf16[2048,1024]{1,0:T(8,128)(2,1)} %right.7), custom_call_target="tpu_custom_call" | custom-call | flops 1073741824 | bytes 4194304 | tf_op jit(solution)/shard_map/partial_product/pallas_call | solution.py:62
  12.2 0.5 collective-permute-start.3
  12.7 2.8 %partial_product.6 = f32[512,512]{1,0:T(8,128)S(1)} custom-call(s32[1]{0:T(128)} %bitcast.me, bf16[1024,2048]{1,0:T(8,128)(2,1)S(1)} %copy-done, bf16[2048,1024]{1,0:T(8,128)(2,1)} %right.7, bf16[2048,1024]{1,0:T(8,128)(2,1)} %right.7), custom_call_target="tpu_custom_call" | custom-call | flops 1073741824 | bytes 4194304 | tf_op jit(solution)/shard_map/partial_product/pallas_call | solution.py:62
  15.5 0.1 fusion
  15.6 2.6 %collective-permute-start.4 = (bf16[512,256]{1,0:T(8,128)(2,1)S(1)}, bf16[512,256]{1,0:T(8,128)(2,1)S(1)}, u32[]{:S(2)}, u32[]{:S(2)}) collective-permute-start(bf16[512,256]{1,0:T(8,128)(2,1)S(1)} %get-tuple-element.14), channel_id=1, source_target_pairs={{0,8},{4,20},{8,0},{12,28},{16,24},{20,4},{24,16},{28,12},{1,9},{5... | collective-permute-start | bytes 786440 | tf_op jit(solution)/shard_map/ppermute | solution.py:217
  18.2 4.4 %collective-permute-done.4 = bf16[512,256]{1,0:T(8,128)(2,1)S(1)} collective-permute-done((bf16[512,256]{1,0:T(8,128)(2,1)S(1)}, bf16[512,256]{1,0:T(8,128)(2,1)S(1)}, u32[]{:S(2)}, u32[]{:S(2)}) %collective-permute-start.4) | collective-permute-done | bytes 262176 | tf_op jit(solution)/shard_map/ppermute | solution.py:217
  22.6 2.1 %collective-permute-start.5 = (bf16[512,128]{1,0:T(8,128)(2,1)S(1)}, bf16[512,128]{1,0:T(8,128)(2,1)S(1)}, u32[]{:S(2)}, u32[]{:S(2)}) collective-permute-start(bf16[512,128]{1,0:T(8,128)(2,1)S(1)} %fusion.2), channel_id=1, source_target_pairs={{0,16},{4,12},{8,24},{12,4},{16,0},{20,28},{24,8},{28,20},{1,17},{... | collective-permute-start | bytes 393224 | tf_op jit(solution)/shard_map/ppermute | solution.py:217
  24.7 2.9 %collective-permute-done.5 = bf16[512,128]{1,0:T(8,128)(2,1)S(1)} collective-permute-done((bf16[512,128]{1,0:T(8,128)(2,1)S(1)}, bf16[512,128]{1,0:T(8,128)(2,1)S(1)}, u32[]{:S(2)}, u32[]{:S(2)}) %collective-permute-start.5) | collective-permute-done | bytes 131104 | tf_op jit(solution)/shard_map/ppermute | solution.py:217
  27.7 0.7 fusion.4.memory
  28.4 0.0 all-gather.7.cloned.1.call-start
  28.5 2.2 %copy-done.1 = bf16[1024,2048]{1,0:T(8,128)(2,1)S(1)} copy-done((bf16[1024,2048]{1,0:T(8,128)(2,1)S(1)}, bf16[1024,2048]{1,0:T(8,128)(2,1)}, u32[]{:S(2)}) %copy-start.1) | copy-done | bytes 4194328
  30.7 2.8 %partial_product.5 = bf16[512,512]{1,0:T(8,128)(2,1)S(1)} custom-call(s32[1]{0:T(128)} %bitcast.me, bf16[1024,2048]{1,0:T(8,128)(2,1)S(1)} %copy-done.1, bf16[2048,1024]{1,0:T(8,128)(2,1)} %right.7, bf16[2048,1024]{1,0:T(8,128)(2,1)} %right.7), custom_call_target="tpu_custom_call" | custom-call | flops 1073741824 | bytes 4194304 | tf_op jit(solution)/shard_map/partial_product/pallas_call | solution.py:62
  33.4 0.1 collective-permute-start
  33.5 2.8 %partial_product.4 = f32[512,512]{1,0:T(8,128)S(1)} custom-call(s32[1]{0:T(128)} %bitcast.me, bf16[1024,2048]{1,0:T(8,128)(2,1)S(1)} %copy-done.1, bf16[2048,1024]{1,0:T(8,128)(2,1)} %right.7, bf16[2048,1024]{1,0:T(8,128)(2,1)} %right.7), custom_call_target="tpu_custom_call" | custom-call | flops 1073741824 | bytes 4194304 | tf_op jit(solution)/shard_map/partial_product/pallas_call | solution.py:62
  36.4 0.1 fusion.1
  36.5 2.1 collective-permute-start.1
  38.6 5.8 %collective-permute-done.1 = bf16[512,256]{1,0:T(8,128)(2,1)S(1)} collective-permute-done((bf16[512,256]{1,0:T(8,128)(2,1)S(1)}, bf16[512,256]{1,0:T(8,128)(2,1)S(1)}, u32[]{:S(2)}, u32[]{:S(2)}) %collective-permute-start.1) | collective-permute-done | bytes 262176 | tf_op jit(solution)/shard_map/ppermute | solution.py:217
  44.4 1.7 collective-permute-start.2
  46.1 3.7 %collective-permute-done.2 = bf16[512,128]{1,0:T(8,128)(2,1)S(1)} collective-permute-done((bf16[512,128]{1,0:T(8,128)(2,1)S(1)}, bf16[512,128]{1,0:T(8,128)(2,1)S(1)}, u32[]{:S(2)}, u32[]{:S(2)}) %collective-permute-start.2) | collective-permute-done | bytes 131104 | tf_op jit(solution)/shard_map/ppermute | solution.py:217
  49.8 0.7 fusion.7.memory
  50.6 0.5 own_columns.2
  51.1 67.5 %all-gather.2 = f32[256,128]{1,0:T(8,128)S(1)} all-gather(f32[8,128]{1,0:T(8,128)S(1)} %get-tuple-element.8), channel_id=4, replica_groups=mesh['past'=8,'second'=4] {'past','second'}, dimensions={0}, use_global_device_ids=true | all-gather | bytes 135168 | tf_op jit(solution)/shard_map/all_gather | solution.py:240
  118.5 1.4 own_columns.3
  119.9 64.3 %all-gather.3 = f32[256,128]{1,0:T(8,128)S(1)} all-gather(f32[8,128]{1,0:T(8,128)S(1)} %get-tuple-element.11), channel_id=5, replica_groups=mesh['past'=8,'second'=4] {'past','second'}, dimensions={0}, use_global_device_ids=true | all-gather | bytes 135168 | tf_op jit(solution)/shard_map/all_gather | solution.py:240
  184.2 1.2 copy-done.5
  185.4 6.1 %finish_block.2 = (bf16[1024,1024]{1,0:T(8,128)(2,1)}, bf16[1024,1024]{1,0:T(8,128)(2,1)}, f32[512,1024]{1,0:T(8,128)S(1)}) custom-call(s32[1]{0:T(128)} %bitcast.me, bf16[8,512,128]{2,1,0:T(8,128)(2,1)S(1)} %bitcast.5, bf16[8,512,128]{2,1,0:T(8,128)(2,1)S(1)} %bitcast.6, bf16[2,512,1024]{2,1,0:T(8,128)(2,1)} %w.7, bf16[512,1024]{1,0:T(8,128)(2,1)S(1)} %copy-done.4, ...), custom_call_target="tpu_custom_call" | custom-call | flops 1073741824 | bytes 4194304 | tf_op jit(solution)/shard_map/finish_block/pallas_call | solution.py:190
  191.5 1.3 copy-done.8
  192.9 1.2 copy-done.6
  194.1 1.6 copy-done.9
  195.7 2.8 %finish_block.3 = (bf16[1024,1024]{1,0:T(8,128)(2,1)}, bf16[1024,1024]{1,0:T(8,128)(2,1)}) custom-call(s32[1]{0:T(128)} %bitcast.me, bf16[8,512,128]{2,1,0:T(8,128)(2,1)S(1)} %bitcast.7, bf16[8,512,128]{2,1,0:T(8,128)(2,1)S(1)} %bitcast.8, bf16[2,512,1024]{2,1,0:T(8,128)(2,1)S(1)} %copy-done.3, ...), custom_call_target="tpu_custom_call", output_to_operand_aliasing={{0}: (7, {}), {1}: (8, {})} | custom-call | flops 1073741824 | bytes 4194304 | tf_op jit(solution)/shard_map/finish_block/pallas_call | solution.py:190
  (26 shorter events, 0.1 us)
Async XLA Ops:
  7.2 177.1 %all-gather.9.cloned.1.call-start = ((), (), s32[]{:S(2)}) async-start(), calls=%async_computation.1 | async-start | bytes 1179648 | tf_op jit(solution)/shard_map/all_gather | solution.py:242
  7.2 2.2 %copy-start = (bf16[1024,2048]{1,0:T(8,128)(2,1)S(1)}, bf16[1024,2048]{1,0:T(8,128)(2,1)}, u32[]{:S(2)}) copy-start(bf16[1024,2048]{1,0:T(8,128)(2,1)} %sigma.7) | copy-start | bytes 12582916
  12.2 3.3 %collective-permute-start.3 = (bf16[512,512]{1,0:T(8,128)(2,1)S(1)}, bf16[512,512]{1,0:T(8,128)(2,1)S(1)}, u32[]{:S(2)}, u32[]{:S(2)}) collective-permute-start(bf16[512,512]{1,0:T(8,128)(2,1)S(1)} %partial_product.7), channel_id=1, source_target_pairs={{0,4},{4,0},{8,12},{12,8},{16,20},{20,16},{24,28},{28,24},{1,5},{5... | collective-permute-start | bytes 1572872 | tf_op jit(solution)/shard_map/ppermute | solution.py:217
  15.6 6.9 %collective-permute-start.4 = (bf16[512,256]{1,0:T(8,128)(2,1)S(1)}, bf16[512,256]{1,0:T(8,128)(2,1)S(1)}, u32[]{:S(2)}, u32[]{:S(2)}) collective-permute-start(bf16[512,256]{1,0:T(8,128)(2,1)S(1)} %get-tuple-element.14), channel_id=1, source_target_pairs={{0,8},{4,20},{8,0},{12,28},{16,24},{20,4},{24,16},{28,12},{1,9},{5... | collective-permute-start | bytes 786440 | tf_op jit(solution)/shard_map/ppermute | solution.py:217
  22.6 5.1 %collective-permute-start.5 = (bf16[512,128]{1,0:T(8,128)(2,1)S(1)}, bf16[512,128]{1,0:T(8,128)(2,1)S(1)}, u32[]{:S(2)}, u32[]{:S(2)}) collective-permute-start(bf16[512,128]{1,0:T(8,128)(2,1)S(1)} %fusion.2), channel_id=1, source_target_pairs={{0,16},{4,12},{8,24},{12,4},{16,0},{20,28},{24,8},{28,20},{1,17},{... | collective-permute-start | bytes 393224 | tf_op jit(solution)/shard_map/ppermute | solution.py:217
  28.4 164.5 %all-gather.7.cloned.1.call-start = ((), (), s32[]{:S(2)}) async-start(), calls=%async_computation | async-start | bytes 1179648 | tf_op jit(solution)/shard_map/all_gather | solution.py:242
  28.5 2.2 %copy-start.1 = (bf16[1024,2048]{1,0:T(8,128)(2,1)S(1)}, bf16[1024,2048]{1,0:T(8,128)(2,1)}, u32[]{:S(2)}) copy-start(bf16[1024,2048]{1,0:T(8,128)(2,1)} %sigma.7) | copy-start | bytes 12582916
  33.4 3.0 %collective-permute-start = (bf16[512,512]{1,0:T(8,128)(2,1)S(1)}, bf16[512,512]{1,0:T(8,128)(2,1)S(1)}, u32[]{:S(2)}, u32[]{:S(2)}) collective-permute-start(bf16[512,512]{1,0:T(8,128)(2,1)S(1)} %partial_product.5), channel_id=1, source_target_pairs={{0,4},{4,0},{8,12},{12,8},{16,20},{20,16},{24,28},{28,24},{1,5},{5... | collective-permute-start | bytes 1572872 | tf_op jit(solution)/shard_map/ppermute | solution.py:217
  36.4 14.2 %copy-start.2 = (bf16[2,512,1024]{2,1,0:T(8,128)(2,1)S(1)}, bf16[2,512,1024]{2,1,0:T(8,128)(2,1)}, u32[]{:S(2)}) copy-start(bf16[2,512,1024]{2,1,0:T(8,128)(2,1)} %w.7) | copy-start | bytes 6291460
  36.4 14.2 %copy-start.4 = (bf16[512,1024]{1,0:T(8,128)(2,1)S(1)}, bf16[512,1024]{1,0:T(8,128)(2,1)}, u32[]{:S(2)}) copy-start(bf16[512,1024]{1,0:T(8,128)(2,1)} %prev.3) | copy-start | bytes 3145732
  36.4 14.2 %copy-start.7 = (f32[32,1024]{1,0:T(8,128)S(1)}, f32[32,1024]{1,0:T(8,128)}, u32[]{:S(2)}) copy-start(f32[32,1024]{1,0:T(8,128)} %coupling.7) | copy-start | bytes 393220
  36.4 14.2 %copy-start.10 = (bf16[512,128]{1,0:T(8,128)(2,1)S(1)}, bf16[512,128]{1,0:T(8,128)(2,1)}, u32[]{:S(2)}) copy-start(bf16[512,128]{1,0:T(8,128)(2,1)} %fusion.4.memory) | copy-start | bytes 393220
  36.5 7.8 %collective-permute-start.1 = (bf16[512,256]{1,0:T(8,128)(2,1)S(1)}, bf16[512,256]{1,0:T(8,128)(2,1)S(1)}, u32[]{:S(2)}, u32[]{:S(2)}) collective-permute-start(bf16[512,256]{1,0:T(8,128)(2,1)S(1)} %get-tuple-element.16), channel_id=1, source_target_pairs={{0,8},{4,20},{8,0},{12,28},{16,24},{20,4},{24,16},{28,12},{1,9},{5... | collective-permute-start | bytes 786440 | tf_op jit(solution)/shard_map/ppermute | solution.py:217
  44.4 5.4 %collective-permute-start.2 = (bf16[512,128]{1,0:T(8,128)(2,1)S(1)}, bf16[512,128]{1,0:T(8,128)(2,1)S(1)}, u32[]{:S(2)}, u32[]{:S(2)}) collective-permute-start(bf16[512,128]{1,0:T(8,128)(2,1)S(1)} %fusion.5), channel_id=1, source_target_pairs={{0,16},{4,12},{8,24},{12,4},{16,0},{20,28},{24,8},{28,20},{1,17},{... | collective-permute-start | bytes 393224 | tf_op jit(solution)/shard_map/ppermute | solution.py:217
  50.6 67.9 %copy-start.11 = (bf16[512,128]{1,0:T(8,128)(2,1)S(1)}, bf16[512,128]{1,0:T(8,128)(2,1)}, u32[]{:S(2)}) copy-start(bf16[512,128]{1,0:T(8,128)(2,1)} %fusion.7.memory) | copy-start | bytes 393220
  184.2 1.2 copy-start.5
  185.4 7.4 %copy-start.3 = (bf16[2,512,1024]{2,1,0:T(8,128)(2,1)S(1)}, bf16[2,512,1024]{2,1,0:T(8,128)(2,1)}, u32[]{:S(2)}) copy-start(bf16[2,512,1024]{2,1,0:T(8,128)(2,1)} %w.7) | copy-start | bytes 6291460
  191.5 1.3 copy-start.8
  192.9 1.2 copy-start.6
  194.1 1.6 copy-start.9
Sparse Core Ops, SparseCore 0:
  28.5 25.9 all-gather.8
  56.4 23.5 all-gather.6

commit v3 on v0

v3 whole, which is shorter than its diff:
```python
import functools

import jax
import jax.numpy as jnp
from jax import lax
from jax.experimental import pallas as pl
from jax.experimental.pallas import tpu as pltpu
from jax.sharding import Mesh, PartitionSpec as P

VMEM = 48 * 1024 * 1024
F32 = jnp.float32
BF16 = jnp.bfloat16
PAST = ("outer", "chip", "core")


def cost(flops, size):
    return pl.CostEstimate(flops=flops, bytes_accessed=size, transcendentals=0)


def cubed(g, coupling):
    orbitals = coupling.shape[0]
    g3 = g.reshape(g.shape[0] // orbitals, orbitals, g.shape[1])
    return (g3 * g3 * g3 * coupling[None]).reshape(g.shape)


def fold_rows(x):
    return jnp.sum(x.reshape(x.shape[0] // 8, 8, x.shape[1]), axis=0)


def scale_of(squares, count):
    return 1.0 / jnp.sqrt(jnp.sum(squares) / count + 1e-06)


def partial_kernel(core, sigma, g, out):
    width = out.shape[2]
    product = jnp.dot(sigma[...], g[...], preferred_element_type=F32).astype(out.dtype)
    for j in range(out.shape[0]):
        out[j] = product[:, j * width : (j + 1) * width]


def partial_product(core, sigma_hist, g_hist, block, rows, chips, other, dtype):
    depth, columns = g_hist.shape
    width = columns // (2 * chips)
    group = min(chips, 2)
    steps = chips // group
    return pl.pallas_call(
        partial_kernel,
        grid_spec=pltpu.PrefetchScalarGridSpec(
            num_scalar_prefetch=1,
            grid=(steps,),
            in_specs=[
                pl.BlockSpec((rows, depth), lambda q, core: (block, 0)),
                pl.BlockSpec((depth, group * width), lambda q, core: (0, (core[0] ^ other) * steps + q)),
            ],
            out_specs=pl.BlockSpec((group, rows, width), lambda q, core: (q, 0, 0)),
        ),
        out_shape=jax.ShapeDtypeStruct((chips, rows, width), dtype),
        compiler_params=pltpu.CompilerParams(vmem_limit_bytes=VMEM),
        cost_estimate=cost(rows * depth * columns, depth * (2 * rows + columns)),
        name="partial_product",
    )(core, sigma_hist, g_hist)


def own_kernel(count_all, place, memory, w, prev, *refs):
    squares = refs[0] if count_all else None
    coupling, cubic, total = refs[-3:]
    rows = memory.shape[0]
    if count_all:
        before = (prev[...] * scale_of(squares[...], count_all)).astype(BF16)
    else:
        before = prev[...]
    g = jnp.dot(w[0, :, :rows], memory[...], preferred_element_type=F32)
    g += jnp.dot(w[0, :, rows:], before, preferred_element_type=F32)
    c = cubed(g, coupling[...])
    cubic[...] = c
    total[...] = fold_rows(c * c)


def own_columns(place, memory, volterra, block, prev, squares, coupling, count_all):
    rows, width = memory.shape
    full = lambda *shape: pl.BlockSpec(shape, lambda i, place: (0,) * len(shape))
    here = lambda size: pl.BlockSpec((size, width), lambda i, place: (0, place[0]))
    w_spec = pl.BlockSpec((1, rows, 2 * rows), lambda i, place: (block, 0, 0))
    in_specs, operands = [full(rows, width), w_spec], [memory, volterra, prev]
    if squares is None:
        in_specs.append(here(rows))
    else:
        in_specs += [full(rows, width), full(*squares.shape)]
        operands.append(squares)
    return pl.pallas_call(
        functools.partial(own_kernel, None if squares is None else count_all),
        grid_spec=pltpu.PrefetchScalarGridSpec(
            num_scalar_prefetch=1,
            grid=(1,),
            in_specs=in_specs + [here(coupling.shape[0])],
            out_specs=[full(rows, width), full(8, width)],
        ),
        out_shape=[jax.ShapeDtypeStruct((rows, width), F32), jax.ShapeDtypeStruct((8, width), F32)],
        compiler_params=pltpu.CompilerParams(vmem_limit_bytes=VMEM),
        cost_estimate=cost(4 * rows * rows * width, 4 * rows * rows + 8 * rows * width),
        name="own_columns",
    )(place, *operands, coupling)


def finish_kernel(count_all, first, last, core, left, right, w, prev, squares, coupling, *refs):
    refs = list(refs)
    w_next = None if last else refs.pop(0)
    refs = refs if first else refs[2:]
    g_out, s_out = refs[:2]
    rows = left.shape[0]
    memory = jnp.concatenate([left[...], right[...]], axis=1)
    g = jnp.dot(w[0, :, :rows], memory, preferred_element_type=F32)
    if first:
        g += jnp.dot(w[0, :, rows:], prev[...], preferred_element_type=F32)
    else:
        g += prev[...]
    g_out[...] = g.astype(BF16)
    sigma = (cubed(g, coupling[...]) * scale_of(squares[...], count_all)).astype(BF16)
    s_out[...] = sigma
    if not last:
        refs[2][...] = jnp.dot(w_next[0, :, rows:], sigma, preferred_element_type=F32)


def finish(core, memory, volterra, block, prev, squares, coupling, outs, count_all):
    rows, width = memory.shape[1:]
    columns = coupling.shape[1]
    chips = memory.shape[0] // 2
    blocks = volterra.shape[0]
    pair = 2 * width
    first, last = block == 0, block == blocks - 1

    def place(side):
        def at(q, core):
            column = 2 * q + side
            return ((column // chips) ^ core[0]) * chips + column % chips, 0, 0

        return pl.BlockSpec((None, rows, width), at)

    w_spec = lambda k: pl.BlockSpec((1, rows, 2 * rows), lambda q, core: (k, 0, 0))
    straight = lambda size, row=0: pl.BlockSpec((size, pair), lambda q, core: (row, q))
    operands = [memory, memory, volterra, prev, squares, coupling]
    in_specs = [
        place(0),
        place(1),
        w_spec(block),
        straight(rows),
        pl.BlockSpec(squares.shape, lambda q, core: (0, 0, 0)),
        straight(coupling.shape[0]),
    ]
    out_specs = [straight(rows, block)] * 2
    out_shape = [jax.ShapeDtypeStruct((blocks * rows, columns), BF16)] * 2
    aliases = {}
    if not last:
        operands.append(volterra)
        in_specs.append(w_spec(block + 1))
        out_specs.append(straight(rows))
        out_shape.append(jax.ShapeDtypeStruct((rows, columns), F32))
    if not first:
        aliases = {1 + len(operands): 0, 2 + len(operands): 1}
        operands += outs
        in_specs += [pl.BlockSpec(memory_space=pl.ANY)] * 2
    return pl.pallas_call(
        functools.partial(finish_kernel, count_all, first, last),
        grid_spec=pltpu.PrefetchScalarGridSpec(
            num_scalar_prefetch=1, grid=(columns // pair,), in_specs=in_specs, out_specs=out_specs
        ),
        out_shape=out_shape,
        input_output_aliases=aliases,
        compiler_params=pltpu.CompilerParams(vmem_limit_bytes=VMEM),
        cost_estimate=cost(4 * rows * rows * columns, 4 * rows * rows + 6 * rows * columns),
        name="finish_block",
    )(core, *operands)


def per_device(sizes, g_hist, sigma_hist, volterra, sigma_edge, coupling):
    outer, chips, cores, second = (sizes[axis] for axis in (*PAST, "second"))
    blocks, rows = volterra.shape[:2]
    columns = g_hist.shape[1]
    count_all = rows * columns * second * outer
    core_id = lax.axis_index("core").astype(jnp.int32)
    core = core_id.reshape(1)
    place = (core_id * chips + lax.axis_index("chip").astype(jnp.int32)).reshape(1)
    everyone = outer * chips * cores * second

    def swap_cores(x):
        return lax.ppermute(x, "core", [(0, 1), (1, 0)])

    def reduced(block):
        send = partial_product(core, sigma_hist, g_hist, block, rows, chips, 1, BF16)
        arrived = swap_cores(send)
        kept = partial_product(core, sigma_hist, g_hist, block, rows, chips, 0, F32)
        both = (kept + arrived.astype(F32)).astype(BF16)
        parts = lax.all_to_all(both, "chip", 0, 0)
        total = jnp.sum(parts.astype(F32), axis=0)
        if outer > 1:
            total = lax.psum(total, "outer")
        return total.astype(BF16)

    def gathered(piece):
        mine = lax.all_to_all(jnp.broadcast_to(piece, (chips,) + piece.shape), "chip", 0, 0)
        return jnp.concatenate([mine, swap_cores(mine)], axis=0)

    def shared(squares):
        copies = jnp.broadcast_to(squares, (everyone,) + squares.shape)
        return lax.all_to_all(copies, (*PAST, "second"), 0, 0)

    own = [reduced(block) for block in range(blocks)]
    whole, squares = [], []
    cubic, total = sigma_edge, None
    for block in range(blocks):
        cubic, local = own_columns(place, own[block], volterra, block, cubic, total, coupling, count_all)
        whole.append(gathered(own[block]))
        total = shared(local)
        squares.append(total)
    outs, start = None, sigma_edge
    for block in range(blocks):
        results = finish(core, whole[block], volterra, block, start, squares[block], coupling, outs, count_all)
        outs = results[:2]
        start = results[2] if block < blocks - 1 else None
    return tuple(outs)


def solution(mesh):
    past, second = mesh.shape["past"], mesh.shape["second"]
    chips = min(past // 2, 4)
    split = Mesh(mesh.devices.reshape(past // (2 * chips), chips, 2, second), (*PAST, "second"))
    return jax.shard_map(
        functools.partial(per_device, dict(split.shape)),
        mesh=split,
        in_specs=(P(PAST, "second"), P(None, PAST), P(), P(None, "second"), P(None, "second")),
        out_specs=(P(None, "second"), P(None, "second")),
        check_vma=False,
    )
```

time: 140 us -> 94.7 us (0.68)
  blocking collectives: 111 us -> 13.2 us
  waiting for transfers between devices: 0 us -> 21.9 us
  Pallas kernels: 0 us -> 21.3 us
  starting transfers between devices: 0 us -> 20.9 us
  matrix products: 15 us -> 0 us
  local copies, waits for them, and re-layouts: 3.51 us -> 10.2 us
  other arithmetic: 7.42 us -> 5.74 us
    psum x3 -> x0, blocking collectives: 111 us -> none  [the longest x1 89.8 us: per_device(): memory = lax.psum(partial_sum, 'past').astype(jnp.bfloat16)]
    all_to_all x0 -> x5, waiting for transfers between devices: none -> 21.8 us  [the longest x2 12.1 us: gathered(): lax.all_to_all(jnp.broadcast_to(piece, (chips,) + piece.shape), 'chip', 0...]
    pallas_call x0 -> x8, Pallas kernels: none -> 21.3 us  [the longest x4 10.7 us: partial_product(): pl.pallas_call(partial_kernel, grid_spec=pltpu.PrefetchScalarGridSpec(num...]
    all_to_all x0 -> x5, starting transfers between devices: none -> 20.1 us  [the longest x2 9.3 us: reduced(): parts = lax.all_to_all(both, 'chip', 0, 0)]
    dot_general x6 -> x0, matrix products: 15 us -> none  [the longest x2 10.3 us: per_device(): partial_sum = jnp.dot(sig_rows, g_hist, preferred_element_type=jnp.float32)]
    all_to_all x0 -> x1, blocking collectives: none -> 13.2 us  [shared(): return lax.all_to_all(copies, (*PAST, 'second'), 0, 0)]
    unnamed x20 -> x16, local copies, waits for them, and re-layouts: 2.37 us -> 7.77 us
    broadcast_in_dim x0 -> x4, local copies, waits for them, and re-layouts: none -> 2.39 us  [the longest x2 1.72 us: gathered(): jnp.broadcast_to(piece, (chips,) + piece.shape)]
  transfers between devices with their start and end apart: 0 -> 9, of which waited for: 0 -> 4; matrix products, arithmetic and copies ran while one was open for 0% -> 7% of each run, Pallas kernels for 0% -> 17%
where the time goes in v3:
time: 94.7 us; the launch traced here: 93.9 us
  waiting for transfers between devices  21.9 us (23%)
  Pallas kernels  21.3 us (22%)
  starting transfers between devices  20.9 us (22%)
  blocking collectives  13.2 us (14%)
  local copies, waits for them, and re-layouts  10.2 us (11%)
  other arithmetic  5.74 us (6%)
    all_to_all x1, blocking collectives, shared(): return lax.all_to_all(copies, (*PAST, 'second'), 0, 0)  13.2 us
    all_to_all x2, waiting for transfers between devices, gathered(): lax.all_to_all(jnp.broadcast_to(piece, (chips,) + piece.shape), 'chip', 0...  12.1 us
    pallas_call x4, Pallas kernels, partial_product(): pl.pallas_call(partial_kernel, grid_spec=pltpu.PrefetchScalarGridSpec(num...  10.7 us
    all_to_all x2, waiting for transfers between devices, reduced(): parts = lax.all_to_all(both, 'chip', 0, 0)  9.72 us
    all_to_all x2, starting transfers between devices, reduced(): parts = lax.all_to_all(both, 'chip', 0, 0)  9.3 us
    pallas_call x2, Pallas kernels, finish(): pl.pallas_call(functools.partial(finish_kernel, count_all, first, last),...  8.71 us
    all_to_all x2, starting transfers between devices, gathered(): lax.all_to_all(jnp.broadcast_to(piece, (chips,) + piece.shape), 'chip', 0...  8.28 us
    unnamed x16, local copies, waits for them, and re-layouts  7.77 us
  transfers between devices with their start and end apart: 9, of which 4 were waited for; matrix products, arithmetic and copies ran while one was open for 7% of the time, Pallas kernels for 17%

profile of v3, /device:TPU:0, one launch (start us, length us, event | category | flops | bytes accessed | tf_op | source)
XLA Modules:
  0.0 93.9 jit_solution(7938417168522853672)
XLA Ops:
  0.6 2.2 %copy-done = bf16[1024,2048]{1,0:T(8,128)(2,1)S(1)} copy-done((bf16[1024,2048]{1,0:T(8,128)(2,1)S(1)}, bf16[1024,2048]{1,0:T(8,128)(2,1)}, u32[]{:S(2)}) %copy-start) | copy-done | bytes 4194328
  2.8 2.7 %partial_product.7 = bf16[4,512,128]{2,1,0:T(8,128)(2,1)S(1)} custom-call(s32[1]{0:T(128)} %bitcast.core, bf16[1024,2048]{1,0:T(8,128)(2,1)S(1)} %copy-done, bf16[2048,1024]{1,0:T(8,128)(2,1)} %g.7), custom_call_target="tpu_custom_call" | custom-call | flops 1073741824 | bytes 4194304 | tf_op jit(solution)/shard_map/partial_product/pallas_call | solution.py:46
  5.5 0.5 collective-permute-start.2
  6.0 2.7 %partial_product.5 = bf16[4,512,128]{2,1,0:T(8,128)(2,1)S(1)} custom-call(s32[1]{0:T(128)} %bitcast.core, bf16[1024,2048]{1,0:T(8,128)(2,1)S(1)} %copy-done, bf16[2048,1024]{1,0:T(8,128)(2,1)} %g.7), custom_call_target="tpu_custom_call" | custom-call | flops 1073741824 | bytes 4194304 | tf_op jit(solution)/shard_map/partial_product/pallas_call | solution.py:46
  8.9 2.7 %partial_product.6 = f32[4,512,128]{2,1,0:T(8,128)S(1)} custom-call(s32[1]{0:T(128)} %bitcast.core, bf16[1024,2048]{1,0:T(8,128)(2,1)S(1)} %copy-done, bf16[2048,1024]{1,0:T(8,128)(2,1)} %g.7), custom_call_target="tpu_custom_call" | custom-call | flops 1073741824 | bytes 4194304 | tf_op jit(solution)/shard_map/partial_product/pallas_call | solution.py:46
  11.6 0.9 add_convert_fusion
  12.5 5.2 %all-to-all-start.2 = ((bf16[4,512,128]{2,1,0:T(8,128)(2,1)}), bf16[4,512,128]{2,1,0:T(8,128)(2,1)S(1)}, u32[]{:S(2)}, u32[]{:S(2)}) async-start(bf16[4,512,128]{2,1,0:T(8,128)(2,1)} %add_convert_fusion), calls=%async_computation.2 | async-start | bytes 1048576 | tf_op jit(solution)/shard_map/all_to_all | solution.py:193
  17.6 2.2 %copy-done.1 = bf16[1024,2048]{1,0:T(8,128)(2,1)S(1)} copy-done((bf16[1024,2048]{1,0:T(8,128)(2,1)S(1)}, bf16[1024,2048]{1,0:T(8,128)(2,1)}, u32[]{:S(2)}) %copy-start.1) | copy-done | bytes 4194328
  19.8 2.7 %partial_product.4 = f32[4,512,128]{2,1,0:T(8,128)S(1)} custom-call(s32[1]{0:T(128)} %bitcast.core, bf16[1024,2048]{1,0:T(8,128)(2,1)S(1)} %copy-done.1, bf16[2048,1024]{1,0:T(8,128)(2,1)} %g.7), custom_call_target="tpu_custom_call" | custom-call | flops 1073741824 | bytes 4194304 | tf_op jit(solution)/shard_map/partial_product/pallas_call | solution.py:46
  22.5 0.9 add_convert_fusion.1
  23.4 2.4 %all-to-all-done.2 = bf16[4,512,128]{2,1,0:T(8,128)(2,1)S(1)} async-done(((bf16[4,512,128]{2,1,0:T(8,128)(2,1)}), bf16[4,512,128]{2,1,0:T(8,128)(2,1)S(1)}, u32[]{:S(2)}, u32[]{:S(2)}) %all-to-all-start.2) | async-done | bytes 524320 | tf_op jit(solution)/shard_map/all_to_all | solution.py:193
  25.8 4.1 %all-to-all-start = ((bf16[4,512,128]{2,1,0:T(8,128)(2,1)}), bf16[4,512,128]{2,1,0:T(8,128)(2,1)}, u32[]{:S(2)}, u32[]{:S(2)}) async-start(bf16[4,512,128]{2,1,0:T(8,128)(2,1)} %add_convert_fusion.1), calls=%async_computation | async-start | bytes 1048576 | tf_op jit(solution)/shard_map/all_to_all | solution.py:193
  30.1 7.3 %all-to-all-done = bf16[4,512,128]{2,1,0:T(8,128)(2,1)} async-done(((bf16[4,512,128]{2,1,0:T(8,128)(2,1)}), bf16[4,512,128]{2,1,0:T(8,128)(2,1)}, u32[]{:S(2)}, u32[]{:S(2)}) %all-to-all-start) | async-done | bytes 524320 | tf_op jit(solution)/shard_map/all_to_all | solution.py:193
  37.4 0.9 broadcast_in_dim.13
  38.3 4.1 %all-to-all-start.3 = ((bf16[4,512,128]{2,1,0:T(8,128)(2,1)}), bf16[4,512,128]{2,1,0:T(8,128)(2,1)}, u32[]{:S(2)}, u32[]{:S(2)}) async-start(bf16[4,512,128]{2,1,0:T(8,128)(2,1)} %broadcast_in_dim.13), calls=%async_computation.3 | async-start | bytes 1048576 | tf_op jit(solution)/shard_map/all_to_all | solution.py:200
  42.4 1.1 %reduce_sum.24.memory = bf16[512,128]{1,0:T(8,128)(2,1)S(1)} reduce(bf16[4,512,128]{2,1,0:T(8,128)(2,1)} %all-to-all-done, bf16[]{:T(256)} %constant.13.clone.1), dimensions={0}, to_apply=%region_0.0 | reduce | flops 196608 | bytes 655362 | tf_op jit(solution)/shard_map/reduce_sum | solution.py:194
  43.5 5.6 %all-to-all-done.3 = bf16[4,512,128]{2,1,0:T(8,128)(2,1)} async-done(((bf16[4,512,128]{2,1,0:T(8,128)(2,1)}), bf16[4,512,128]{2,1,0:T(8,128)(2,1)}, u32[]{:S(2)}, u32[]{:S(2)}) %all-to-all-start.3) | async-done | bytes 524320 | tf_op jit(solution)/shard_map/all_to_all | solution.py:200
  49.1 0.9 broadcast_in_dim.12
  50.0 4.1 %all-to-all-start.1 = ((bf16[4,512,128]{2,1,0:T(8,128)(2,1)}), bf16[4,512,128]{2,1,0:T(8,128)(2,1)}, u32[]{:S(2)}, u32[]{:S(2)}) async-start(bf16[4,512,128]{2,1,0:T(8,128)(2,1)} %broadcast_in_dim.12), calls=%async_computation.1 | async-start | bytes 1048576 | tf_op jit(solution)/shard_map/all_to_all | solution.py:200
  54.2 6.6 %all-to-all-done.1 = bf16[4,512,128]{2,1,0:T(8,128)(2,1)} async-done(((bf16[4,512,128]{2,1,0:T(8,128)(2,1)}), bf16[4,512,128]{2,1,0:T(8,128)(2,1)}, u32[]{:S(2)}, u32[]{:S(2)}) %all-to-all-start.1) | async-done | bytes 524320 | tf_op jit(solution)/shard_map/all_to_all | solution.py:200
  60.8 0.5 own_columns.2
  61.2 13.2 %all_to_all.30.squares.refs_0_ = f32[32,8,128]{2,1,0:T(8,128)S(1)} all-to-all(f32[32,8,128]{2,1,0:T(8,128)S(1)} %broadcast_in_dim.14), channel_id=1, replica_groups=mesh['outer'=1,'chip'=4,'core'=2,'second'=4] {'outer','chip','core','sec..., dimensions={0} | all-to-all | bytes 262144 | tf_op jit(solution)/shard_map/all_to_all | solution.py:205
  74.5 1.4 %own_columns.3 = (f32[512,128]{1,0:T(8,128)}, f32[8,128]{1,0:T(8,128)S(1)}) custom-call(s32[1]{0:T(128)} %bitcast.1.place, bf16[512,128]{1,0:T(8,128)(2,1)S(1)} %reduce_sum.24.memory, bf16[2,512,1024]{2,1,0:T(8,128)(2,1)S(1)} %copy-done.2, f32[512,128]{1,0:T(8,128)S(1)} %get-tuple-element.10.prev, f32[32,8,128]{2,1,0:T(8,128)S(1)} %all_to_all.30.squares.refs_0_, ...), custom_call_target="tpu_custom_call" | custom-call | flops 134217728 | bytes 1572864 | tf_op jit(solution)/shard_map/own_columns/pallas_call | solution.py:90
  75.8 0.7 broadcast_in_dim.15
  76.5 2.6 %all-to-all-start.5 = ((f32[32,8,128]{2,1,0:T(8,128)}), f32[32,8,128]{2,1,0:T(8,128)S(1)}, u32[]{:S(2)}, u32[]{:S(2)}) async-start(f32[32,8,128]{2,1,0:T(8,128)} %broadcast_in_dim.15), calls=%async_computation.5 | async-start | bytes 262144 | tf_op jit(solution)/shard_map/all_to_all | solution.py:205
  79.1 1.3 %pad_maximum_fusion.1.left.right = bf16[8,512,128]{2,1,0:T(8,128)(2,1)S(1)} fusion(bf16[4,512,128]{2,1,0:T(8,128)(2,1)} %collective-permute-done.3, bf16[4,512,128]{2,1,0:T(8,128)(2,1)} %all-to-all-done.3), kind=kLoop, calls=%fused_computation.1 | loop fusion | flops 524288 | bytes 2097152 | tf_op jit(solution)/shard_map/concatenate | solution.py:201
  80.4 6.0 %finish_block.2 = (bf16[1024,1024]{1,0:T(8,128)(2,1)}, bf16[1024,1024]{1,0:T(8,128)(2,1)}, f32[512,1024]{1,0:T(8,128)S(1)}) custom-call(s32[1]{0:T(128)} %bitcast.core, bf16[8,512,128]{2,1,0:T(8,128)(2,1)S(1)} %pad_maximum_fusion.1.left.right, bf16[8,512,128]{2,1,0:T(8,128)(2,1)S(1)} %pad_maximum_fusion.1.left.right, bf16[2,512,1024]{2,1,0:T(8,128)(2,1)} %w.7, ...), custom_call_target="tpu_custom_call" | custom-call | flops 1073741824 | bytes 4194304 | tf_op jit(solution)/shard_map/finish_block/pallas_call | solution.py:162
  86.3 1.3 %copy-done.6 = f32[512,1024]{1,0:T(8,128)} copy-done((f32[512,1024]{1,0:T(8,128)}, f32[512,1024]{1,0:T(8,128)S(1)}, u32[]{:S(2)}) %copy-start.6) | copy-done | bytes 2097176
  87.7 1.4 %pad_maximum_fusion.left.right = bf16[8,512,128]{2,1,0:T(8,128)(2,1)S(1)} fusion(bf16[4,512,128]{2,1,0:T(8,128)(2,1)} %collective-permute-done.1, bf16[4,512,128]{2,1,0:T(8,128)(2,1)} %all-to-all-done.1), kind=kLoop, calls=%fused_computation | loop fusion | flops 524288 | bytes 2097152 | tf_op jit(solution)/shard_map/concatenate | solution.py:201
  89.1 0.4 copy-done.3
  89.6 1.6 %copy-done.7 = f32[512,1024]{1,0:T(8,128)S(1)} copy-done((f32[512,1024]{1,0:T(8,128)S(1)}, f32[512,1024]{1,0:T(8,128)}, u32[]{:S(2)}) %copy-start.7) | copy-done | bytes 2097176
  91.2 2.8 %finish_block.3 = (bf16[1024,1024]{1,0:T(8,128)(2,1)}, bf16[1024,1024]{1,0:T(8,128)(2,1)}) custom-call(s32[1]{0:T(128)} %bitcast.core, bf16[8,512,128]{2,1,0:T(8,128)(2,1)S(1)} %pad_maximum_fusion.left.right, bf16[8,512,128]{2,1,0:T(8,128)(2,1)S(1)} %pad_maximum_fusion.left.right, ...), custom_call_target="tpu_custom_call", output_to_operand_aliasing={{0}: (7, {}), {1}: (8, {})} | custom-call | flops 1073741824 | bytes 4194304 | tf_op jit(solution)/shard_map/finish_block/pallas_call | solution.py:162
  (21 shorter events, 0.3 us)
Async XLA Ops:
  0.6 2.2 %copy-start = (bf16[1024,2048]{1,0:T(8,128)(2,1)S(1)}, bf16[1024,2048]{1,0:T(8,128)(2,1)}, u32[]{:S(2)}) copy-start(bf16[1024,2048]{1,0:T(8,128)(2,1)} %sigma.7) | copy-start | bytes 12582916
  5.5 6.0 %collective-permute-start.2 = (bf16[4,512,128]{2,1,0:T(8,128)(2,1)S(1)}, bf16[4,512,128]{2,1,0:T(8,128)(2,1)S(1)}, u32[]{:S(2)}, u32[]{:S(2)}) collective-permute-start(bf16[4,512,128]{2,1,0:T(8,128)(2,1)S(1)} %partial_product.7), channel_id=1, source_target_pairs={{0,4},{4,0},{1,5},{5,1},{2,6},{6,2},{3,7},{7,3},{8,12},{12,8},{9,1... | collective-permute-start | bytes 1572872 | tf_op jit(solution)/shard_map/ppermute | solution.py:186
  8.7 13.8 %collective-permute-start = (bf16[4,512,128]{2,1,0:T(8,128)(2,1)S(1)}, bf16[4,512,128]{2,1,0:T(8,128)(2,1)S(1)}, u32[]{:S(2)}, u32[]{:S(2)}) collective-permute-start(bf16[4,512,128]{2,1,0:T(8,128)(2,1)S(1)} %partial_product.5), channel_id=1, source_target_pairs={{0,4},{4,0},{1,5},{5,1},{2,6},{6,2},{3,7},{7,3},{8,12},{12,8},{9,1... | collective-permute-start | bytes 1572872 | tf_op jit(solution)/shard_map/ppermute | solution.py:186
  12.5 13.4 %all-to-all-start.2 = ((bf16[4,512,128]{2,1,0:T(8,128)(2,1)}), bf16[4,512,128]{2,1,0:T(8,128)(2,1)S(1)}, u32[]{:S(2)}, u32[]{:S(2)}) async-start(bf16[4,512,128]{2,1,0:T(8,128)(2,1)} %add_convert_fusion), calls=%async_computation.2 | async-start | bytes 1048576 | tf_op jit(solution)/shard_map/all_to_all | solution.py:193
  17.6 2.2 %copy-start.1 = (bf16[1024,2048]{1,0:T(8,128)(2,1)S(1)}, bf16[1024,2048]{1,0:T(8,128)(2,1)}, u32[]{:S(2)}) copy-start(bf16[1024,2048]{1,0:T(8,128)(2,1)} %sigma.7) | copy-start | bytes 12582916
  25.8 11.6 %all-to-all-start = ((bf16[4,512,128]{2,1,0:T(8,128)(2,1)}), bf16[4,512,128]{2,1,0:T(8,128)(2,1)}, u32[]{:S(2)}, u32[]{:S(2)}) async-start(bf16[4,512,128]{2,1,0:T(8,128)(2,1)} %add_convert_fusion.1), calls=%async_computation | async-start | bytes 1048576 | tf_op jit(solution)/shard_map/all_to_all | solution.py:193
  30.1 30.7 %copy-start.2 = (bf16[2,512,1024]{2,1,0:T(8,128)(2,1)S(1)}, bf16[2,512,1024]{2,1,0:T(8,128)(2,1)}, u32[]{:S(2)}) copy-start(bf16[2,512,1024]{2,1,0:T(8,128)(2,1)} %w.7) | copy-start | bytes 6291460
  30.1 30.7 %copy-start.4 = (bf16[512,1024]{1,0:T(8,128)(2,1)S(1)}, bf16[512,1024]{1,0:T(8,128)(2,1)}, u32[]{:S(2)}) copy-start(bf16[512,1024]{1,0:T(8,128)(2,1)} %prev.3) | copy-start | bytes 3145732
  30.1 30.7 %copy-start.5 = (f32[32,1024]{1,0:T(8,128)S(1)}, f32[32,1024]{1,0:T(8,128)}, u32[]{:S(2)}) copy-start(f32[32,1024]{1,0:T(8,128)} %coupling.3) | copy-start | bytes 393220
  38.3 10.8 %all-to-all-start.3 = ((bf16[4,512,128]{2,1,0:T(8,128)(2,1)}), bf16[4,512,128]{2,1,0:T(8,128)(2,1)}, u32[]{:S(2)}, u32[]{:S(2)}) async-start(bf16[4,512,128]{2,1,0:T(8,128)(2,1)} %broadcast_in_dim.13), calls=%async_computation.3 | async-start | bytes 1048576 | tf_op jit(solution)/shard_map/all_to_all | solution.py:200
  50.0 10.8 %all-to-all-start.1 = ((bf16[4,512,128]{2,1,0:T(8,128)(2,1)}), bf16[4,512,128]{2,1,0:T(8,128)(2,1)}, u32[]{:S(2)}, u32[]{:S(2)}) async-start(bf16[4,512,128]{2,1,0:T(8,128)(2,1)} %broadcast_in_dim.12), calls=%async_computation.1 | async-start | bytes 1048576 | tf_op jit(solution)/shard_map/all_to_all | solution.py:200
  54.1 25.0 %collective-permute-start.3 = (bf16[4,512,128]{2,1,0:T(8,128)(2,1)}, bf16[4,512,128]{2,1,0:T(8,128)(2,1)}, u32[]{:S(2)}, u32[]{:S(2)}) collective-permute-start(bf16[4,512,128]{2,1,0:T(8,128)(2,1)} %all-to-all-done.3), channel_id=1, source_target_pairs={{0,4},{4,0},{1,5},{5,1},{2,6},{6,2},{3,7},{7,3},{8,12},{12,8},{9,1... | collective-permute-start | bytes 1572872 | tf_op jit(solution)/shard_map/ppermute | solution.py:186
  60.7 26.9 %collective-permute-start.1 = (bf16[4,512,128]{2,1,0:T(8,128)(2,1)}, bf16[4,512,128]{2,1,0:T(8,128)(2,1)}, u32[]{:S(2)}, u32[]{:S(2)}) collective-permute-start(bf16[4,512,128]{2,1,0:T(8,128)(2,1)} %all-to-all-done.1), channel_id=1, source_target_pairs={{0,4},{4,0},{1,5},{5,1},{2,6},{6,2},{3,7},{7,3},{8,12},{12,8},{9,1... | collective-permute-start | bytes 1572872 | tf_op jit(solution)/shard_map/ppermute | solution.py:186
  76.5 12.6 %all-to-all-start.5 = ((f32[32,8,128]{2,1,0:T(8,128)}), f32[32,8,128]{2,1,0:T(8,128)S(1)}, u32[]{:S(2)}, u32[]{:S(2)}) async-start(f32[32,8,128]{2,1,0:T(8,128)} %broadcast_in_dim.15), calls=%async_computation.5 | async-start | bytes 262144 | tf_op jit(solution)/shard_map/all_to_all | solution.py:205
  86.3 1.3 %copy-start.6 = (f32[512,1024]{1,0:T(8,128)}, f32[512,1024]{1,0:T(8,128)S(1)}, u32[]{:S(2)}) copy-start(f32[512,1024]{1,0:T(8,128)S(1)} %get-tuple-element.9.prev) | copy-start | bytes 6291460
  87.7 1.9 %copy-start.3 = (bf16[2,512,1024]{2,1,0:T(8,128)(2,1)S(1)}, bf16[2,512,1024]{2,1,0:T(8,128)(2,1)}, u32[]{:S(2)}) copy-start(bf16[2,512,1024]{2,1,0:T(8,128)(2,1)} %w.7) | copy-start | bytes 6291460
  89.6 1.6 %copy-start.7 = (f32[512,1024]{1,0:T(8,128)S(1)}, f32[512,1024]{1,0:T(8,128)}, u32[]{:S(2)}) copy-start(f32[512,1024]{1,0:T(8,128)} %copy-done.6) | copy-start | bytes 6291460

commit v4 on v0

v4 whole, which is shorter than its diff:
```python
import functools

import jax
import jax.numpy as jnp
from jax import lax
from jax.experimental import pallas as pl
from jax.experimental.pallas import tpu as pltpu
from jax.sharding import PartitionSpec as P

VMEM = 20 * 1024 * 1024
F32 = jnp.float32
BF16 = jnp.bfloat16
EPS = 1e-06
BINOMIAL = (1.0, 6.0, 15.0, 20.0, 15.0, 6.0, 1.0)

WHOLE = pl.BlockSpec(memory_space=pltpu.VMEM)
FAR = pl.BlockSpec(memory_space=pl.ANY)
SCALAR = pl.BlockSpec(memory_space=pltpu.SMEM)


def log2(n):
    bits = n.bit_length() - 1
    assert n == 1 << bits
    return bits


def call(kernel, name, flops, size, **kwargs):
    return pl.pallas_call(
        kernel,
        name=name,
        compiler_params=pltpu.CompilerParams(vmem_limit_bytes=VMEM),
        cost_estimate=pl.CostEstimate(flops=flops, bytes_accessed=size, transcendentals=0),
        **kwargs,
    )


class Place:
    def __init__(self, me, bits):
        low, high = (me >> 1) & 1, (me >> (bits - 1)) & 1
        self.core = me & 1
        self.side = jnp.where(self.core == 1, high, low)
        self.other_side = jnp.where(self.core == 1, low, high)

    def quarter(self):
        return self.core * 2 + self.side

    def slot(self, quarter):
        same = (quarter >> 1) == self.core
        return jnp.where(same, (quarter & 1) ^ self.side, 2 + ((quarter & 1) ^ self.other_side))


def product(me, sigma, g, block, rows, half, bits, send, after=None):
    load_sigma, load_g = sigma.shape[0] != rows, g.shape[1] != half
    depth = g.shape[0]
    quarter = half // 2
    dtype = BF16 if send else F32
    pieces = 4 if load_sigma and load_g else 2
    out_shape = [jax.ShapeDtypeStruct((2, rows, quarter), dtype)]
    if load_sigma:
        out_shape.append(jax.ShapeDtypeStruct((rows, depth), BF16))
    if load_g:
        out_shape.append(jax.ShapeDtypeStruct((depth, half), BF16))

    def kernel(me_ref, sigma_ref, g_ref, *refs):
        refs = list(refs)
        if after is not None:
            refs.pop(0)
        out = refs.pop(0)
        sigma_v = refs.pop(0) if load_sigma else sigma_ref
        g_v = refs.pop(0) if load_g else g_ref
        total, sems = refs
        place = Place(me_ref[0], bits)
        first = pl.multiple_of((place.core ^ int(send)) * half, half)
        side = place.other_side if send else place.side

        def put(j, value):
            out[1 ^ j ^ side] = value.astype(dtype)

        if load_sigma and load_g:
            chunk = depth // pieces
            copies = []
            for k in range(pieces):
                at = pl.ds(k * chunk, chunk)
                copies.append(
                    (
                        pltpu.make_async_copy(
                            sigma_ref.at[pl.ds(block * rows, rows), at], sigma_v.at[:, at], sems.at[2 * k]
                        ),
                        pltpu.make_async_copy(g_ref.at[at, pl.ds(first, half)], g_v.at[at, :], sems.at[2 * k + 1]),
                    )
                )
            for pair in copies:
                for copy in pair:
                    copy.start()
            for k in range(pieces):
                for copy in copies[k]:
                    copy.wait()
                at = pl.ds(k * chunk, chunk)
                term = jnp.dot(sigma_v[:, at], g_v[at, :], preferred_element_type=F32)
                if k == 0:
                    total[...] = term
                elif k < pieces - 1:
                    total[...] += term
                else:
                    term += total[...]
                    for j in range(2):
                        put(j, term[:, j * quarter : (j + 1) * quarter])
        elif load_g:
            copies = [
                pltpu.make_async_copy(
                    g_ref.at[:, pl.ds(first + j * quarter, quarter)], g_v.at[:, pl.ds(j * quarter, quarter)], sems.at[j]
                )
                for j in range(2)
            ]
            for copy in copies:
                copy.start()
            for j in range(2):
                copies[j].wait()
                put(j, jnp.dot(sigma_v[...], g_v[:, pl.ds(j * quarter, quarter)], preferred_element_type=F32))
        elif load_sigma:
            tall = rows // 2
            copies = [
                pltpu.make_async_copy(
                    sigma_ref.at[pl.ds(block * rows + i * tall, tall), :], sigma_v.at[pl.ds(i * tall, tall), :], sems.at[i]
                )
                for i in range(2)
            ]
            for copy in copies:
                copy.start()
            for i in range(2):
                copies[i].wait()
                here = pl.ds(i * tall, tall)
                term = jnp.dot(sigma_v[here, :], g_v[...], preferred_element_type=F32).astype(dtype)
                for j in range(2):
                    out[1 ^ j ^ side, here, :] = term[:, j * quarter : (j + 1) * quarter]
        else:
            term = jnp.dot(sigma_v[...], g_v[...], preferred_element_type=F32)
            for j in range(2):
                put(j, term[:, j * quarter : (j + 1) * quarter])

    return call(
        kernel,
        "memory_product",
        2 * rows * depth * half,
        2 * depth * (rows * load_sigma + half * load_g),
        in_specs=[SCALAR, FAR if load_sigma else WHOLE, FAR if load_g else WHOLE] + [FAR] * (after is not None),
        out_specs=[WHOLE] * len(out_shape),
        out_shape=out_shape,
        scratch_shapes=[pltpu.VMEM((rows, half), F32), pltpu.SemaphoreType.DMA((2 * pieces,))],
    )(me, sigma, g, *([] if after is None else [after]))


def cubed(g, coupling):
    orbitals = coupling.shape[0]
    g3 = g.reshape(g.shape[0] // orbitals, orbitals, g.shape[1])
    return (g3 * g3 * g3 * coupling[None]).reshape(g.shape)


def folded(x):
    line = jnp.sum(x, axis=0, keepdims=True)
    parts = [line[:, i : i + 128] for i in range(0, line.shape[1], 128)]
    return functools.reduce(lambda a, b: a + b, parts)


def own_first(me, memory, volterra, edge, coupling, bits):
    rows, quarter = memory.shape

    def kernel(me_ref, memory, w, edge, coupling, response, squares):
        at = pl.ds(pl.multiple_of(Place(me_ref[0], bits).quarter() * quarter, quarter), quarter)
        g = jnp.dot(w[0, :, :rows], memory[...], preferred_element_type=F32)
        g += jnp.dot(w[0, :, rows:], edge[:, at], preferred_element_type=F32)
        cubic = cubed(g, coupling[:, at])
        line = folded(cubic * cubic * (1.0 / (rows * quarter)))
        squares[...] = line
        scale = lax.rsqrt(jnp.sum(line) + EPS)
        response[...] = jnp.dot(w[1, :, rows:], (cubic * scale).astype(BF16), preferred_element_type=F32)

    return call(
        kernel,
        "own_first",
        6 * rows * rows * quarter,
        8 * rows * rows,
        in_specs=[SCALAR] + [WHOLE] * 4,
        out_specs=[WHOLE] * 2,
        out_shape=[jax.ShapeDtypeStruct((rows, quarter), F32), jax.ShapeDtypeStruct((1, 128), F32)],
    )(me, memory, volterra, edge, coupling)


def own_second(me, memory, volterra, response, squares, coupling, bits):
    rows, quarter = memory.shape
    orbitals = coupling.shape[0]

    def kernel(me_ref, memory, w, response, squares, coupling, out):
        at = pl.ds(pl.multiple_of(Place(me_ref[0], bits).quarter() * quarter, quarter), quarter)
        c = coupling[:, at]
        c2 = (c * c * (1.0 / (rows * quarter)))[None]
        a = jnp.dot(w[1, :, :rows], memory[...], preferred_element_type=F32)
        b = response[...]
        a2, b2 = a * a, b * b
        a3, b3, a2b, ab2 = a2 * a, b2 * b, a2 * b, a * b2
        out[0:1, :] = squares[...]
        terms = (a3 * a3, a3 * a2b, a2b * a2b, a3 * b3, ab2 * ab2, ab2 * b3, b3 * b3)
        for k, term in enumerate(terms):
            weighted = (term.reshape(rows // orbitals, orbitals, quarter) * c2).reshape(rows, quarter)
            out[k + 1 : k + 2, :] = folded(weighted)

    return call(
        kernel,
        "own_second",
        2 * rows * rows * quarter,
        4 * rows * rows,
        in_specs=[SCALAR] + [WHOLE] * 5,
        out_specs=WHOLE,
        out_shape=jax.ShapeDtypeStruct((8, 128), F32),
    )(me, memory, volterra, response, squares, coupling)


def finish_first(me, memory, volterra, edge, coupling, bits):
    rows, quarter = memory.shape[1:]
    columns = coupling.shape[1]

    def kernel(me_ref, memory, w, edge, coupling, g_out, cubic):
        q = pl.program_id(0)
        g = jnp.dot(w[0, :, :rows], memory[Place(me_ref[0], bits).slot(q)], preferred_element_type=F32)
        g += jnp.dot(w[0, :, rows:], edge[...], preferred_element_type=F32)
        g_out[...] = g.astype(BF16)
        cubic[q] = cubed(g, coupling[...])

    straight = lambda size: pl.BlockSpec((size, quarter), lambda q: (0, q))
    return call(
        kernel,
        "finish_first",
        4 * rows * rows * columns,
        4 * rows * columns,
        grid=(4,),
        in_specs=[SCALAR, WHOLE, WHOLE, straight(rows), straight(coupling.shape[0])],
        out_specs=[straight(rows), WHOLE],
        out_shape=[
            jax.ShapeDtypeStruct((2 * rows, columns), BF16),
            jax.ShapeDtypeStruct((4, rows, quarter), F32),
        ],
    )(me, memory, volterra, edge, coupling)


def finish_second(me, memory, volterra, cubic, shares, coupling, g_first, bits):
    rows, quarter = memory.shape[1:]
    columns = coupling.shape[1]
    everyone = shares.shape[0]

    def kernel(me_ref, memory, w, cubic, shares, coupling, _, g_out, sigma, scales):
        q = pl.program_id(0)

        @pl.when(q == 0)
        def _():
            sums = jnp.sum(shares[...], axis=2, keepdims=True)
            means = sums[:, 0:1, :]
            mean = jnp.sum(means) / everyone
            ratio = jnp.sqrt((means + EPS) / (mean + EPS))
            power, series = jnp.ones_like(ratio), jnp.zeros_like(ratio)
            for k, weight in enumerate(BINOMIAL):
                series += weight * sums[:, k + 1 : k + 2, :] * power
                power = power * ratio
            scales[0] = 1.0 / jnp.sqrt(mean + EPS)
            scales[1] = 1.0 / jnp.sqrt(jnp.maximum(jnp.sum(series) / everyone, 0.0) + EPS)

        before = (cubic[q] * scales[0]).astype(BF16)
        g = jnp.dot(w[1, :, :rows], memory[Place(me_ref[0], bits).slot(q)], preferred_element_type=F32)
        g += jnp.dot(w[1, :, rows:], before, preferred_element_type=F32)
        g_out[...] = g.astype(BF16)
        sigma[:rows, :] = before
        sigma[rows:, :] = (cubed(g, coupling[...]) * scales[1]).astype(BF16)

    return call(
        kernel,
        "finish_second",
        4 * rows * rows * columns,
        10 * rows * columns,
        grid=(4,),
        in_specs=[
            SCALAR,
            WHOLE,
            WHOLE,
            WHOLE,
            WHOLE,
            pl.BlockSpec((coupling.shape[0], quarter), lambda q: (0, q)),
            FAR,
        ],
        out_specs=[
            pl.BlockSpec((rows, quarter), lambda q: (1, q)),
            pl.BlockSpec((2 * rows, quarter), lambda q: (0, q)),
        ],
        out_shape=[jax.ShapeDtypeStruct((2 * rows, columns), BF16)] * 2,
        scratch_shapes=[pltpu.SMEM((2,), F32)],
        input_output_aliases={6: 0},
    )(me, memory, volterra, cubic, shares, coupling, g_first)


def per_device(past, second, g_hist, sigma_hist, volterra, sigma_edge, coupling):
    blocks, rows = volterra.shape[:2]
    assert blocks == 2 and past >= 4
    bits = log2(past)
    half = g_hist.shape[1] // 2
    me = lax.axis_index("past").astype(jnp.int32).reshape(1)
    even = list(range(bits))
    odd = even[:1] + even[1:][::-1]

    def swap(x, level):
        pairs = [(d, d ^ (1 << (odd if d % 2 else even)[level])) for d in range(past)]
        return lax.ppermute(x, "past", pairs)

    def summed(kept, arrived, sent):
        total = kept[1] + arrived[1].astype(F32) + swap(sent, 1).astype(F32)
        for level in range(2, bits):
            rounded = total.astype(BF16)
            total = rounded.astype(F32) + swap(rounded, level).astype(F32)
        return total.astype(BF16)

    def passed_on(kept, arrived):
        return (kept[0] + arrived[0].astype(F32)).astype(BF16)

    def gathered(own):
        partner = swap(own, 1)
        return jnp.stack([own, partner, swap(own, 0), swap(partner, 0)])

    send, sigma_0, g_send = product(me, sigma_hist, g_hist, 0, rows, half, bits, True)
    arrived_0 = swap(send, 0)
    kept_0, g_keep = product(me, sigma_0, g_hist, 0, rows, half, bits, False)
    sent_0 = passed_on(kept_0, arrived_0)
    send, sigma_1 = product(me, sigma_hist, g_send, 1, rows, half, bits, True, after=sent_0)
    arrived_1 = swap(send, 0)
    (kept_1,) = product(me, sigma_1, g_keep, 1, rows, half, bits, False)
    sent_1 = passed_on(kept_1, arrived_1)

    own_0 = summed(kept_0, arrived_0, sent_0)
    own_1 = summed(kept_1, arrived_1, sent_1)
    response, squares = own_first(me, own_0, volterra, sigma_edge, coupling, bits)
    share = own_second(me, own_1, volterra, response, squares, coupling, bits)
    copies = jnp.broadcast_to(share, (past * second,) + share.shape)
    shares = lax.all_to_all(copies, ("past", "second"), 0, 0)

    g_first, cubic = finish_first(me, gathered(own_0), volterra, sigma_edge, coupling, bits)
    return tuple(finish_second(me, gathered(own_1), volterra, cubic, shares, coupling, g_first, bits))


def solution(mesh):
    return jax.shard_map(
        functools.partial(per_device, mesh.shape["past"], mesh.shape["second"]),
        mesh=mesh,
        in_specs=(P("past", "second"), P(None, "past"), P(), P(None, "second"), P(None, "second")),
        out_specs=(P(None, "second"), P(None, "second")),
        check_vma=False,
    )
```

time: 140 us -> 62.5 us (0.45)
  blocking collectives: 111 us -> 0 us
  Pallas kernels: 0 us -> 18.5 us
  waiting for transfers between devices: 0 us -> 15.6 us
  starting transfers between devices: 0 us -> 15.5 us
  matrix products: 15 us -> 0 us
  local copies, waits for them, and re-layouts: 3.51 us -> 7.98 us
  other arithmetic: 7.42 us -> 3.68 us
    psum x3 -> x0, blocking collectives: 111 us -> none  [the longest x1 89.8 us: per_device(): memory = lax.psum(partial_sum, 'past').astype(jnp.bfloat16)]
    pallas_call x0 -> x8, Pallas kernels: none -> 18.5 us  [the longest x4 7.99 us: product(): call(kernel, 'memory_product', 2 * rows * depth * half, 2 * depth * (rows...]
    dot_general x6 -> x0, matrix products: 15 us -> none  [the longest x2 10.3 us: per_device(): partial_sum = jnp.dot(sig_rows, g_hist, preferred_element_type=jnp.float32)]
    ppermute x0 -> x12, waiting for transfers between devices: none -> 14.1 us  [swap(): return lax.ppermute(x, 'past', pairs)]
    ppermute x0 -> x12, starting transfers between devices: none -> 10.4 us  [swap(): return lax.ppermute(x, 'past', pairs)]
    all_to_all x0 -> x1, starting transfers between devices: none -> 5.1 us  [per_device(): shares = lax.all_to_all(copies, ('past', 'second'), 0, 0)]
    unnamed x20 -> x16, local copies, waits for them, and re-layouts: 2.37 us -> 7.3 us
    concatenate x2 -> x0, other arithmetic: 4.52 us -> none  [the longest x1 3.03 us: per_device(): jnp.concatenate(g_blocks, axis=0)]
  transfers between devices with their start and end apart: 0 -> 13, of which waited for: 0 -> 7; matrix products, arithmetic and copies ran while one was open for 0% -> 7% of each run, Pallas kernels for 0% -> 16%
where the time goes in v4:
time: 62.5 us; the launch traced here: 62.1 us
  Pallas kernels  18.5 us (30%)
  waiting for transfers between devices  15.6 us (25%)
  starting transfers between devices  15.5 us (25%)
  local copies, waits for them, and re-layouts  7.98 us (13%)
  other arithmetic  3.68 us (6%)
  between operations  0.81 us (1%)
    ppermute x12, waiting for transfers between devices, swap(): return lax.ppermute(x, 'past', pairs)  14.1 us
    ppermute x12, starting transfers between devices, swap(): return lax.ppermute(x, 'past', pairs)  10.4 us
    pallas_call x4, Pallas kernels, product(): call(kernel, 'memory_product', 2 * rows * depth * half, 2 * depth * (rows...  7.99 us
    unnamed x16, local copies, waits for them, and re-layouts  7.3 us
    all_to_all x1, starting transfers between devices, per_device(): shares = lax.all_to_all(copies, ('past', 'second'), 0, 0)  5.1 us
    pallas_call x1, Pallas kernels, finish_second(): call(kernel, 'finish_second', 4 * rows * rows * columns, 10 * rows * colu...  4.72 us
    pallas_call x1, Pallas kernels, finish_first(): call(kernel, 'finish_first', 4 * rows * rows * columns, 4 * rows * column...  2.93 us
    another operation x2, other arithmetic, gathered(): return jnp.stack([own, partner, swap(own, 0), swap(partner, 0)])  2.56 us
  transfers between devices with their start and end apart: 13, of which 7 were waited for; matrix products, arithmetic and copies ran while one was open for 7% of the time, Pallas kernels for 16%

profile of v4, /device:TPU:0, one launch (start us, length us, event | category | flops | bytes accessed | tf_op | source)
XLA Modules:
  0.0 62.1 jit_solution(18167509499065013225)
XLA Ops:
  0.6 2.2 %copy-done.1 = bf16[2048,1024]{1,0:T(8,128)(2,1)S(1)} copy-done((bf16[2048,1024]{1,0:T(8,128)(2,1)S(1)}, bf16[2048,1024]{1,0:T(8,128)(2,1)}, u32[]{:S(2)}) %copy-start.1) | copy-done | bytes 4194328
  2.8 2.2 %copy-done.3 = bf16[1024,2048]{1,0:T(8,128)(2,1)S(1)} copy-done((bf16[1024,2048]{1,0:T(8,128)(2,1)S(1)}, bf16[1024,2048]{1,0:T(8,128)(2,1)}, u32[]{:S(2)}) %copy-start.3) | copy-done | bytes 4194328
  5.0 2.3 %memory_product.4 = (bf16[2,512,256]{2,1,0:T(8,128)(2,1)S(1)}, bf16[512,2048]{1,0:T(8,128)(2,1)S(1)}, bf16[2048,512]{1,0:T(8,128)(2,1)S(1)}) custom-call(s32[1]{0:T(128)} %bitcast.me_ref, bf16[1024,2048]{1,0:T(8,128)(2,1)S(1)} %copy-done.3, bf16[2048,1024]{1,0:T(8,128)(2,1)S(1)} %copy-done.1), custom_call_target="tpu_custom_call" | custom-call | flops 1073741824 | bytes 4194304 | tf_op jit(solution)/shard_map/memory_product/pallas_call | solution.py:141
  7.3 0.5 collective-permute-start
  7.8 2.8 %memory_product.5 = (f32[2,512,256]{2,1,0:T(8,128)S(1)}, bf16[2048,512]{1,0:T(8,128)(2,1)S(1)}) custom-call(s32[1]{0:T(128)} %bitcast.me_ref, bf16[512,2048]{1,0:T(8,128)(2,1)S(1)} %get-tuple-element.14.sigma_ref, bf16[2048,1024]{1,0:T(8,128)(2,1)S(1)} %copy-done.2), custom_call_target="tpu_custom_call" | custom-call | flops 1073741824 | bytes 2097152 | tf_op jit(solution)/shard_map/memory_product/pallas_call | solution.py:141
  10.7 1.6 %memory_product.6 = (bf16[2,512,256]{2,1,0:T(8,128)(2,1)S(1)}, bf16[512,2048]{1,0:T(8,128)(2,1)S(1)}) custom-call(s32[1]{0:T(128)} %bitcast.me_ref, bf16[1024,2048]{1,0:T(8,128)(2,1)S(1)} %copy-done.3, bf16[2048,512]{1,0:T(8,128)(2,1)S(1)} %get-tuple-element.13.g_ref, bf16[512,256]{1,0:T(8,128)(2,1)S(1)} %fusion.5.refs_0_), custom_call_target="tpu_custom_call" | custom-call | flops 1073741824 | bytes 2097152 | tf_op jit(solution)/shard_map/memory_product/pallas_call | solution.py:141
  12.4 2.9 %collective-permute-start.7 = (bf16[512,256]{1,0:T(8,128)(2,1)S(1)}, bf16[512,256]{1,0:T(8,128)(2,1)S(1)}, u32[]{:S(2)}, u32[]{:S(2)}) collective-permute-start(bf16[512,256]{1,0:T(8,128)(2,1)S(1)} %fusion.5.refs_0_), channel_id=1, source_target_pairs={{0,8},{4,20},{8,0},{12,28},{16,24},{20,4},{24,16},{28,12},{1,9},{5... | collective-permute-start | bytes 786440 | tf_op jit(solution)/shard_map/ppermute | solution.py:309
  15.4 1.3 %memory_product.7 = f32[2,512,256]{2,1,0:T(8,128)S(1)} custom-call(s32[1]{0:T(128)} %bitcast.me_ref, bf16[512,2048]{1,0:T(8,128)(2,1)S(1)} %get-tuple-element.17.sigma_ref, bf16[2048,512]{1,0:T(8,128)(2,1)S(1)} %get-tuple-element.18.g_ref), custom_call_target="tpu_custom_call" | custom-call | flops 1073741824 | tf_op jit(solution)/shard_map/memory_product/pallas_call | solution.py:141
  16.8 0.3 collective-permute-start.2
  17.1 2.7 %collective-permute-done.7 = bf16[512,256]{1,0:T(8,128)(2,1)S(1)} collective-permute-done((bf16[512,256]{1,0:T(8,128)(2,1)S(1)}, bf16[512,256]{1,0:T(8,128)(2,1)S(1)}, u32[]{:S(2)}, u32[]{:S(2)}) %collective-permute-start.7) | collective-permute-done | bytes 262176 | tf_op jit(solution)/shard_map/ppermute | solution.py:309
  19.8 2.1 %collective-permute-start.8 = (bf16[512,256]{1,0:T(8,128)(2,1)S(1)}, bf16[512,256]{1,0:T(8,128)(2,1)S(1)}, u32[]{:S(2)}, u32[]{:S(2)}) collective-permute-start(bf16[512,256]{1,0:T(8,128)(2,1)S(1)} %fusion.4), channel_id=1, source_target_pairs={{0,16},{4,12},{8,24},{12,4},{16,0},{20,28},{24,8},{28,20},{1,17},{... | collective-permute-start | bytes 786440 | tf_op jit(solution)/shard_map/ppermute | solution.py:309
  21.9 2.5 %collective-permute-done.2 = bf16[512,256]{1,0:T(8,128)(2,1)S(1)} collective-permute-done((bf16[512,256]{1,0:T(8,128)(2,1)S(1)}, bf16[512,256]{1,0:T(8,128)(2,1)S(1)}, u32[]{:S(2)}, u32[]{:S(2)}) %collective-permute-start.2) | collective-permute-done | bytes 262176 | tf_op jit(solution)/shard_map/ppermute | solution.py:309
  24.5 1.4 %collective-permute-start.3 = (bf16[512,256]{1,0:T(8,128)(2,1)S(1)}, bf16[512,256]{1,0:T(8,128)(2,1)S(1)}, u32[]{:S(2)}, u32[]{:S(2)}) collective-permute-start(bf16[512,256]{1,0:T(8,128)(2,1)S(1)} %fusion.3), channel_id=1, source_target_pairs={{0,16},{4,12},{8,24},{12,4},{16,0},{20,28},{24,8},{28,20},{1,17},{... | collective-permute-start | bytes 786440 | tf_op jit(solution)/shard_map/ppermute | solution.py:309
  25.9 0.4 collective-permute-done.8
  26.3 0.8 %add_convert_fusion.memory = bf16[512,256]{1,0:T(8,128)(2,1)} fusion(bf16[512,256]{1,0:T(8,128)(2,1)S(1)} %collective-permute-done.8, bf16[512,256]{1,0:T(8,128)(2,1)S(1)} %fusion.4), kind=kLoop, calls=%fused_computation.10 | loop fusion | flops 524288 | bytes 786432 | tf_op jit(solution)/shard_map/convert_element_type | solution.py:316
  27.0 2.0 %collective-permute-start.9 = (bf16[512,256]{1,0:T(8,128)(2,1)}, bf16[512,256]{1,0:T(8,128)(2,1)}, u32[]{:S(2)}, u32[]{:S(2)}) collective-permute-start(bf16[512,256]{1,0:T(8,128)(2,1)} %add_convert_fusion.memory), channel_id=1, source_target_pairs={{0,8},{4,20},{8,0},{12,28},{16,24},{20,4},{24,16},{28,12},{1,9},{5... | collective-permute-start | bytes 786440 | tf_op jit(solution)/shard_map/ppermute | solution.py:309
  29.0 3.1 %collective-permute-done.3 = bf16[512,256]{1,0:T(8,128)(2,1)S(1)} collective-permute-done((bf16[512,256]{1,0:T(8,128)(2,1)S(1)}, bf16[512,256]{1,0:T(8,128)(2,1)S(1)}, u32[]{:S(2)}, u32[]{:S(2)}) %collective-permute-start.3) | collective-permute-done | bytes 262176 | tf_op jit(solution)/shard_map/ppermute | solution.py:309
  32.2 0.6 collective-permute-start.4
  32.7 1.0 %collective-permute-done.9 = bf16[512,256]{1,0:T(8,128)(2,1)} collective-permute-done((bf16[512,256]{1,0:T(8,128)(2,1)}, bf16[512,256]{1,0:T(8,128)(2,1)}, u32[]{:S(2)}, u32[]{:S(2)}) %collective-permute-start.9) | collective-permute-done | bytes 262176 | tf_op jit(solution)/shard_map/ppermute | solution.py:309
  33.8 0.4 collective-permute-start.5
  34.2 4.5 %collective-permute-done.4 = bf16[512,256]{1,0:T(8,128)(2,1)} collective-permute-done((bf16[512,256]{1,0:T(8,128)(2,1)S(1)}, bf16[512,256]{1,0:T(8,128)(2,1)}, u32[]{:S(2)}, u32[]{:S(2)}) %collective-permute-start.4) | collective-permute-done | bytes 262176 | tf_op jit(solution)/shard_map/ppermute | solution.py:309
  38.7 2.1 %own_first.1 = (f32[512,256]{1,0:T(8,128)S(1)}, f32[1,128]{1,0:T(1,128)S(1)}) custom-call(s32[1]{0:T(128)} %bitcast.me_ref, bf16[512,256]{1,0:T(8,128)(2,1)} %add_convert_fusion.memory, bf16[2,512,1024]{2,1,0:T(8,128)(2,1)S(1)} %copy-done, bf16[512,1024]{1,0:T(8,128)(2,1)S(1)} %copy-done.4, f32[32,1024]{1,0:T(8,128)S(1)} %copy-done.5), custom_call_target="tpu_custom_call" | custom-call | flops 402653184 | bytes 2097152 | tf_op jit(solution)/shard_map/own_first/pallas_call | solution.py:178
  40.8 0.8 %own_second.1 = f32[8,128]{1,0:T(8,128)S(1)} custom-call(s32[1]{0:T(128)} %bitcast.me_ref, bf16[512,256]{1,0:T(8,128)(2,1)S(1)} %add_convert_fusion.1.memory, bf16[2,512,1024]{2,1,0:T(8,128)(2,1)S(1)} %copy-done, f32[512,256]{1,0:T(8,128)S(1)} %get-tuple-element.21.response, f32[1,128]{1,0:T(1,128)S(1)} %get-tuple-element.22.squares, f32[32,1024]{1,0:T(8,128)S(1)} %copy-done.5), custom_call_target="tpu_custom_call" | custom-call | flops 134217728 | bytes 1048576 | tf_op jit(solution)/shard_map/own_second/pallas_call | solution.py:207
  41.6 0.7 %broadcast_in_dim.3 = f32[32,8,128]{2,1,0:T(8,128)} broadcast(f32[8,128]{1,0:T(8,128)S(1)} %own_second.1), dimensions={1,2} | broadcast | bytes 135168 | tf_op jit(solution)/shard_map/broadcast_in_dim | solution.py:338
  42.3 5.1 %all-to-all-start = ((f32[32,8,128]{2,1,0:T(8,128)}), f32[32,8,128]{2,1,0:T(8,128)}, u32[]{:S(2)}, u32[]{:S(2)}) async-start(f32[32,8,128]{2,1,0:T(8,128)} %broadcast_in_dim.3), calls=%async_computation | async-start | bytes 262144 | tf_op jit(solution)/shard_map/all_to_all | solution.py:339
  47.4 1.3 %pad_maximum_fusion.1.memory = bf16[4,512,256]{2,1,0:T(8,128)(2,1)S(1)} fusion(bf16[1,512,256]{2,1,0:T(8,128)(2,1)} %bitcast.12, bf16[1,512,256]{2,1,0:T(8,128)(2,1)} %bitcast.11, bf16[1,512,256]{2,1,0:T(8,128)(2,1)} %bitcast.10, bf16[1,512,256]{2,1,0:T(8,128)(2,1)} %bitcast.9), kind=kLoop, calls=%fused_computation.1 | loop fusion | flops 1572864 | bytes 2097152 | tf_op jit(solution)/shard_map/stack | solution.py:323
  48.8 2.9 %finish_first.1 = (bf16[1024,1024]{1,0:T(8,128)(2,1)}, f32[4,512,256]{2,1,0:T(8,128)S(1)}) custom-call(s32[1]{0:T(128)} %bitcast.me_ref, bf16[4,512,256]{2,1,0:T(8,128)(2,1)S(1)} %pad_maximum_fusion.1.memory, bf16[2,512,1024]{2,1,0:T(8,128)(2,1)S(1)} %copy-done, bf16[512,1024]{1,0:T(8,128)(2,1)S(1)} %copy-done.4, f32[32,1024]{1,0:T(8,128)S(1)} %copy-done.5), custom_call_target="tpu_custom_call" | custom-call | flops 1073741824 | bytes 2097152 | tf_op jit(solution)/shard_map/finish_first/pallas_call | solution.py:230
  51.7 1.3 %copy-done.6 = f32[4,512,256]{2,1,0:T(8,128)} copy-done((f32[4,512,256]{2,1,0:T(8,128)}, f32[4,512,256]{2,1,0:T(8,128)S(1)}, u32[]{:S(2)}) %copy-start.6) | copy-done | bytes 2097176
  53.0 1.2 %pad_maximum_fusion.memory = bf16[4,512,256]{2,1,0:T(8,128)(2,1)S(1)} fusion(bf16[1,512,256]{2,1,0:T(8,128)(2,1)} %bitcast.7, bf16[1,512,256]{2,1,0:T(8,128)(2,1)} %bitcast.6, bf16[1,512,256]{2,1,0:T(8,128)(2,1)} %bitcast.5, bf16[1,512,256]{2,1,0:T(8,128)(2,1)S(1)} %bitcast.23), kind=kLoop, calls=%fused_computation | loop fusion | flops 1572864 | bytes 2097152 | tf_op jit(solution)/shard_map/stack | solution.py:323
  54.3 1.5 %all-to-all-done.shares = f32[32,8,128]{2,1,0:T(8,128)} async-done(((f32[32,8,128]{2,1,0:T(8,128)}), f32[32,8,128]{2,1,0:T(8,128)}, u32[]{:S(2)}, u32[]{:S(2)}) %all-to-all-start) | async-done | bytes 131104 | tf_op jit(solution)/shard_map/all_to_all | solution.py:339
  55.8 1.6 %copy-done.7 = f32[4,512,256]{2,1,0:T(8,128)S(1)} copy-done((f32[4,512,256]{2,1,0:T(8,128)S(1)}, f32[4,512,256]{2,1,0:T(8,128)}, u32[]{:S(2)}) %copy-start.7) | copy-done | bytes 2097176
  57.4 4.7 %finish_second.1 = (bf16[1024,1024]{1,0:T(8,128)(2,1)}, bf16[1024,1024]{1,0:T(8,128)(2,1)}) custom-call(s32[1]{0:T(128)} %bitcast.me_ref, bf16[4,512,256]{2,1,0:T(8,128)(2,1)S(1)} %pad_maximum_fusion.memory, bf16[2,512,1024]{2,1,0:T(8,128)(2,1)S(1)} %copy-done, f32[4,512,256]{2,1,0:T(8,128)S(1)} %copy-done.7, ...), custom_call_target="tpu_custom_call", output_to_operand_aliasing={{0}: (6, {})} | custom-call | flops 1073741824 | bytes 5242880 | tf_op jit(solution)/shard_map/finish_second/pallas_call | solution.py:273
  (27 shorter events, 0.6 us)
Async XLA Ops:
  0.6 2.2 %copy-start.1 = (bf16[2048,1024]{1,0:T(8,128)(2,1)S(1)}, bf16[2048,1024]{1,0:T(8,128)(2,1)}, u32[]{:S(2)}) copy-start(bf16[2048,1024]{1,0:T(8,128)(2,1)} %g_ref.3) | copy-start | bytes 12582916
  2.8 2.2 %copy-start.3 = (bf16[1024,2048]{1,0:T(8,128)(2,1)S(1)}, bf16[1024,2048]{1,0:T(8,128)(2,1)}, u32[]{:S(2)}) copy-start(bf16[1024,2048]{1,0:T(8,128)(2,1)} %sigma_ref.3) | copy-start | bytes 12582916
  5.0 2.8 %copy-start.2 = (bf16[2048,1024]{1,0:T(8,128)(2,1)S(1)}, bf16[2048,1024]{1,0:T(8,128)(2,1)}, u32[]{:S(2)}) copy-start(bf16[2048,1024]{1,0:T(8,128)(2,1)} %g_ref.3) | copy-start | bytes 12582916
  7.3 3.3 %collective-permute-start = (bf16[2,512,256]{2,1,0:T(8,128)(2,1)S(1)}, bf16[2,512,256]{2,1,0:T(8,128)(2,1)S(1)}, u32[]{:S(2)}, u32[]{:S(2)}) collective-permute-start(bf16[2,512,256]{2,1,0:T(8,128)(2,1)S(1)} %get-tuple-element.16), channel_id=1, source_target_pairs={{0,4},{4,0},{8,12},{12,8},{16,20},{20,16},{24,28},{28,24},{1,5},{5... | collective-permute-start | bytes 1572872 | tf_op jit(solution)/shard_map/ppermute | solution.py:309
  12.3 4.4 %collective-permute-start.1 = (bf16[2,512,256]{2,1,0:T(8,128)(2,1)S(1)}, bf16[2,512,256]{2,1,0:T(8,128)(2,1)S(1)}, u32[]{:S(2)}, u32[]{:S(2)}) collective-permute-start(bf16[2,512,256]{2,1,0:T(8,128)(2,1)S(1)} %get-tuple-element.19), channel_id=1, source_target_pairs={{0,4},{4,0},{8,12},{12,8},{16,20},{20,16},{24,28},{28,24},{1,5},{5... | collective-permute-start | bytes 1572872 | tf_op jit(solution)/shard_map/ppermute | solution.py:309
  12.4 7.3 %collective-permute-start.7 = (bf16[512,256]{1,0:T(8,128)(2,1)S(1)}, bf16[512,256]{1,0:T(8,128)(2,1)S(1)}, u32[]{:S(2)}, u32[]{:S(2)}) collective-permute-start(bf16[512,256]{1,0:T(8,128)(2,1)S(1)} %fusion.5.refs_0_), channel_id=1, source_target_pairs={{0,8},{4,20},{8,0},{12,28},{16,24},{20,4},{24,16},{28,12},{1,9},{5... | collective-permute-start | bytes 786440 | tf_op jit(solution)/shard_map/ppermute | solution.py:309
  16.8 21.9 %copy-start = (bf16[2,512,1024]{2,1,0:T(8,128)(2,1)S(1)}, bf16[2,512,1024]{2,1,0:T(8,128)(2,1)}, u32[]{:S(2)}) copy-start(bf16[2,512,1024]{2,1,0:T(8,128)(2,1)} %w.7) | copy-start | bytes 6291460
  16.8 21.9 %copy-start.4 = (bf16[512,1024]{1,0:T(8,128)(2,1)S(1)}, bf16[512,1024]{1,0:T(8,128)(2,1)}, u32[]{:S(2)}) copy-start(bf16[512,1024]{1,0:T(8,128)(2,1)} %edge.3) | copy-start | bytes 3145732
  16.8 21.9 %copy-start.5 = (f32[32,1024]{1,0:T(8,128)S(1)}, f32[32,1024]{1,0:T(8,128)}, u32[]{:S(2)}) copy-start(f32[32,1024]{1,0:T(8,128)} %coupling.7) | copy-start | bytes 393220
  16.8 7.6 %collective-permute-start.2 = (bf16[512,256]{1,0:T(8,128)(2,1)S(1)}, bf16[512,256]{1,0:T(8,128)(2,1)S(1)}, u32[]{:S(2)}, u32[]{:S(2)}) collective-permute-start(bf16[512,256]{1,0:T(8,128)(2,1)S(1)} %fusion.6), channel_id=1, source_target_pairs={{0,8},{4,20},{8,0},{12,28},{16,24},{20,4},{24,16},{28,12},{1,9},{5... | collective-permute-start | bytes 786440 | tf_op jit(solution)/shard_map/ppermute | solution.py:309
  19.8 6.5 %collective-permute-start.8 = (bf16[512,256]{1,0:T(8,128)(2,1)S(1)}, bf16[512,256]{1,0:T(8,128)(2,1)S(1)}, u32[]{:S(2)}, u32[]{:S(2)}) collective-permute-start(bf16[512,256]{1,0:T(8,128)(2,1)S(1)} %fusion.4), channel_id=1, source_target_pairs={{0,16},{4,12},{8,24},{12,4},{16,0},{20,28},{24,8},{28,20},{1,17},{... | collective-permute-start | bytes 786440 | tf_op jit(solution)/shard_map/ppermute | solution.py:309
  24.5 7.6 %collective-permute-start.3 = (bf16[512,256]{1,0:T(8,128)(2,1)S(1)}, bf16[512,256]{1,0:T(8,128)(2,1)S(1)}, u32[]{:S(2)}, u32[]{:S(2)}) collective-permute-start(bf16[512,256]{1,0:T(8,128)(2,1)S(1)} %fusion.3), channel_id=1, source_target_pairs={{0,16},{4,12},{8,24},{12,4},{16,0},{20,28},{24,8},{28,20},{1,17},{... | collective-permute-start | bytes 786440 | tf_op jit(solution)/shard_map/ppermute | solution.py:309
  27.0 6.7 %collective-permute-start.9 = (bf16[512,256]{1,0:T(8,128)(2,1)}, bf16[512,256]{1,0:T(8,128)(2,1)}, u32[]{:S(2)}, u32[]{:S(2)}) collective-permute-start(bf16[512,256]{1,0:T(8,128)(2,1)} %add_convert_fusion.memory), channel_id=1, source_target_pairs={{0,8},{4,20},{8,0},{12,28},{16,24},{20,4},{24,16},{28,12},{1,9},{5... | collective-permute-start | bytes 786440 | tf_op jit(solution)/shard_map/ppermute | solution.py:309
  32.2 6.5 %collective-permute-start.4 = (bf16[512,256]{1,0:T(8,128)(2,1)S(1)}, bf16[512,256]{1,0:T(8,128)(2,1)}, u32[]{:S(2)}, u32[]{:S(2)}) collective-permute-start(bf16[512,256]{1,0:T(8,128)(2,1)S(1)} %add_convert_fusion.1.memory), channel_id=1, source_target_pairs={{0,8},{4,20},{8,0},{12,28},{16,24},{20,4},{24,16},{28,12},{1,9},{5... | collective-permute-start | bytes 786440 | tf_op jit(solution)/shard_map/ppermute | solution.py:309
  32.7 14.7 %collective-permute-start.10 = (bf16[512,256]{1,0:T(8,128)(2,1)}, bf16[512,256]{1,0:T(8,128)(2,1)}, u32[]{:S(2)}, u32[]{:S(2)}) collective-permute-start(bf16[512,256]{1,0:T(8,128)(2,1)} %add_convert_fusion.memory), channel_id=1, source_target_pairs={{0,4},{4,0},{8,12},{12,8},{16,20},{20,16},{24,28},{28,24},{1,5},{5... | collective-permute-start | bytes 786440 | tf_op jit(solution)/shard_map/ppermute | solution.py:309
  33.7 13.7 %collective-permute-start.11 = (bf16[512,256]{1,0:T(8,128)(2,1)}, bf16[512,256]{1,0:T(8,128)(2,1)}, u32[]{:S(2)}, u32[]{:S(2)}) collective-permute-start(bf16[512,256]{1,0:T(8,128)(2,1)} %collective-permute-done.9), channel_id=1, source_target_pairs={{0,4},{4,0},{8,12},{12,8},{16,20},{20,16},{24,28},{28,24},{1,5},{5... | collective-permute-start | bytes 786440 | tf_op jit(solution)/shard_map/ppermute | solution.py:309
  33.8 19.2 %collective-permute-start.5 = (bf16[512,256]{1,0:T(8,128)(2,1)S(1)}, bf16[512,256]{1,0:T(8,128)(2,1)}, u32[]{:S(2)}, u32[]{:S(2)}) collective-permute-start(bf16[512,256]{1,0:T(8,128)(2,1)S(1)} %add_convert_fusion.1.memory), channel_id=1, source_target_pairs={{0,4},{4,0},{8,12},{12,8},{16,20},{20,16},{24,28},{28,24},{1,5},{5... | collective-permute-start | bytes 786440 | tf_op jit(solution)/shard_map/ppermute | solution.py:309
  38.7 14.3 %collective-permute-start.6 = (bf16[512,256]{1,0:T(8,128)(2,1)}, bf16[512,256]{1,0:T(8,128)(2,1)}, u32[]{:S(2)}, u32[]{:S(2)}) collective-permute-start(bf16[512,256]{1,0:T(8,128)(2,1)} %collective-permute-done.4), channel_id=1, source_target_pairs={{0,4},{4,0},{8,12},{12,8},{16,20},{20,16},{24,28},{28,24},{1,5},{5... | collective-permute-start | bytes 786440 | tf_op jit(solution)/shard_map/ppermute | solution.py:309
  42.3 13.5 %all-to-all-start = ((f32[32,8,128]{2,1,0:T(8,128)}), f32[32,8,128]{2,1,0:T(8,128)}, u32[]{:S(2)}, u32[]{:S(2)}) async-start(f32[32,8,128]{2,1,0:T(8,128)} %broadcast_in_dim.3), calls=%async_computation | async-start | bytes 262144 | tf_op jit(solution)/shard_map/all_to_all | solution.py:339
  51.7 1.3 %copy-start.6 = (f32[4,512,256]{2,1,0:T(8,128)}, f32[4,512,256]{2,1,0:T(8,128)S(1)}, u32[]{:S(2)}) copy-start(f32[4,512,256]{2,1,0:T(8,128)S(1)} %get-tuple-element.20.cubic) | copy-start | bytes 6291460
  55.8 1.6 %copy-start.7 = (f32[4,512,256]{2,1,0:T(8,128)S(1)}, f32[4,512,256]{2,1,0:T(8,128)}, u32[]{:S(2)}) copy-start(f32[4,512,256]{2,1,0:T(8,128)} %copy-done.6) | copy-start | bytes 6291460

commit v5 on v4

v5 whole, which is shorter than its diff:
```python
import functools

import jax
import jax.numpy as jnp
from jax import lax
from jax.experimental import pallas as pl
from jax.experimental.pallas import tpu as pltpu
from jax.sharding import PartitionSpec as P

VMEM = 20 * 1024 * 1024
F32 = jnp.float32
BF16 = jnp.bfloat16
EPS = 1e-06
BINOMIAL = (1.0, 6.0, 15.0, 20.0, 15.0, 6.0, 1.0)

WHOLE = pl.BlockSpec(memory_space=pltpu.VMEM)
FAR = pl.BlockSpec(memory_space=pl.ANY)
HBM = pl.BlockSpec(memory_space=pltpu.HBM)
SCALAR = pl.BlockSpec(memory_space=pltpu.SMEM)


def log2(n):
    bits = n.bit_length() - 1
    assert n == 1 << bits
    return bits


def call(kernel, name, **kwargs):
    return pl.pallas_call(
        kernel,
        name=name,
        compiler_params=pltpu.CompilerParams(vmem_limit_bytes=VMEM),
        cost_estimate=pl.CostEstimate(flops=1024, bytes_accessed=1024, transcendentals=0),
        **kwargs,
    )


class Place:
    def __init__(self, me, bits):
        low, high = (me >> 1) & 1, (me >> (bits - 1)) & 1
        self.core = me & 1
        self.side = jnp.where(self.core == 1, high, low)
        self.other_side = jnp.where(self.core == 1, low, high)

    def quarter(self):
        return self.core * 2 + self.side

    def quarter_of(self, slot):
        if slot < 2:
            return self.core * 2 + (self.side ^ slot)
        return (self.core ^ 1) * 2 + (self.other_side ^ (slot - 2))


def product(me, sigma, g, block, rows, half, bits, send, after=None):
    load_sigma, load_g = sigma.shape[0] != rows, g.shape[1] != half
    depth = g.shape[0]
    quarter = half // 2
    dtype = BF16 if send else F32
    pieces = 4 if load_sigma and load_g else 2
    out_shape = [jax.ShapeDtypeStruct((2, rows, quarter), dtype)]
    if load_sigma:
        out_shape.append(jax.ShapeDtypeStruct((rows, depth), BF16))
    if load_g:
        out_shape.append(jax.ShapeDtypeStruct((depth, half), BF16))

    def kernel(me_ref, sigma_ref, g_ref, *refs):
        refs = list(refs)
        if after is not None:
            refs.pop(0)
        out = refs.pop(0)
        sigma_v = refs.pop(0) if load_sigma else sigma_ref
        g_v = refs.pop(0) if load_g else g_ref
        total, sems = refs
        place = Place(me_ref[0], bits)
        first = pl.multiple_of((place.core ^ int(send)) * half, half)
        side = place.other_side if send else place.side

        def put(j, value):
            out[1 ^ j ^ side] = value.astype(dtype)

        if load_sigma and load_g:
            chunk = depth // pieces
            copies = []
            for k in range(pieces):
                at = pl.ds(k * chunk, chunk)
                copies.append(
                    (
                        pltpu.make_async_copy(
                            sigma_ref.at[pl.ds(block * rows, rows), at], sigma_v.at[:, at], sems.at[2 * k]
                        ),
                        pltpu.make_async_copy(g_ref.at[at, pl.ds(first, half)], g_v.at[at, :], sems.at[2 * k + 1]),
                    )
                )
            for pair in copies:
                for copy in pair:
                    copy.start()
            for k in range(pieces):
                for copy in copies[k]:
                    copy.wait()
                at = pl.ds(k * chunk, chunk)
                term = jnp.dot(sigma_v[:, at], g_v[at, :], preferred_element_type=F32)
                if k == 0:
                    total[...] = term
                elif k < pieces - 1:
                    total[...] += term
                else:
                    term += total[...]
                    for j in range(2):
                        put(j, term[:, j * quarter : (j + 1) * quarter])
        elif load_g:
            copies = [
                pltpu.make_async_copy(
                    g_ref.at[:, pl.ds(first + j * quarter, quarter)], g_v.at[:, pl.ds(j * quarter, quarter)], sems.at[j]
                )
                for j in range(2)
            ]
            for copy in copies:
                copy.start()
            for j in range(2):
                copies[j].wait()
                put(j, jnp.dot(sigma_v[...], g_v[:, pl.ds(j * quarter, quarter)], preferred_element_type=F32))
        elif load_sigma:
            tall = rows // 2
            copies = [
                pltpu.make_async_copy(
                    sigma_ref.at[pl.ds(block * rows + i * tall, tall), :], sigma_v.at[pl.ds(i * tall, tall), :], sems.at[i]
                )
                for i in range(2)
            ]
            for copy in copies:
                copy.start()
            for i in range(2):
                copies[i].wait()
                here = pl.ds(i * tall, tall)
                term = jnp.dot(sigma_v[here, :], g_v[...], preferred_element_type=F32).astype(dtype)
                for j in range(2):
                    out[1 ^ j ^ side, here, :] = term[:, j * quarter : (j + 1) * quarter]
        else:
            term = jnp.dot(sigma_v[...], g_v[...], preferred_element_type=F32)
            for j in range(2):
                put(j, term[:, j * quarter : (j + 1) * quarter])

    return call(
        kernel,
        "memory_product",
        in_specs=[SCALAR, HBM if load_sigma else WHOLE, HBM if load_g else WHOLE] + [FAR] * (after is not None),
        out_specs=[WHOLE] * len(out_shape),
        out_shape=out_shape,
        scratch_shapes=[pltpu.VMEM((rows, half), F32), pltpu.SemaphoreType.DMA((2 * pieces,))],
    )(me, sigma, g, *([] if after is None else [after]))


def cubed(g, coupling):
    orbitals = coupling.shape[0]
    g3 = g.reshape(g.shape[0] // orbitals, orbitals, g.shape[1])
    return (g3 * g3 * g3 * coupling[None]).reshape(g.shape)


def folded(x):
    line = jnp.sum(x, axis=0, keepdims=True)
    parts = [line[:, i : i + 128] for i in range(0, line.shape[1], 128)]
    return functools.reduce(lambda a, b: a + b, parts)


def columns_of(quarter, width):
    return pl.ds(pl.multiple_of(quarter * width, width), width)


def own_first(me, mine, theirs, volterra, edge, coupling, bits):
    rows, width = mine.shape

    def kernel(me_ref, mine, theirs, w, edge, coupling, memory, response, squares):
        at = columns_of(Place(me_ref[0], bits).quarter(), width)
        summed = (mine[...].astype(F32) + theirs[...].astype(F32)).astype(BF16)
        memory[...] = summed
        g = jnp.dot(w[0, :, :rows], summed, preferred_element_type=F32)
        g += jnp.dot(w[0, :, rows:], edge[:, at], preferred_element_type=F32)
        cubic = cubed(g, coupling[:, at])
        line = folded(cubic * cubic * (1.0 / (rows * width)))
        squares[...] = line
        scale = lax.rsqrt(jnp.sum(line) + EPS)
        response[...] = jnp.dot(w[1, :, rows:], (cubic * scale).astype(BF16), preferred_element_type=F32)

    return call(
        kernel,
        "own_first",
        in_specs=[SCALAR] + [WHOLE] * 5,
        out_specs=[WHOLE] * 3,
        out_shape=[
            jax.ShapeDtypeStruct((rows, width), BF16),
            jax.ShapeDtypeStruct((rows, width), F32),
            jax.ShapeDtypeStruct((1, 128), F32),
        ],
    )(me, mine, theirs, volterra, edge, coupling)


def own_second(me, mine, theirs, volterra, response, squares, coupling, bits):
    rows, width = mine.shape
    orbitals = coupling.shape[0]

    def kernel(me_ref, mine, theirs, w, response, squares, coupling, memory, out):
        at = columns_of(Place(me_ref[0], bits).quarter(), width)
        summed = (mine[...].astype(F32) + theirs[...].astype(F32)).astype(BF16)
        memory[...] = summed
        c = coupling[:, at]
        c2 = (c * c * (1.0 / (rows * width)))[None]
        a = jnp.dot(w[1, :, :rows], summed, preferred_element_type=F32)
        b = response[...]
        a2, b2 = a * a, b * b
        a3, b3, a2b, ab2 = a2 * a, b2 * b, a2 * b, a * b2
        out[0:1, :] = squares[...]
        terms = (a3 * a3, a3 * a2b, a2b * a2b, a3 * b3, ab2 * ab2, ab2 * b3, b3 * b3)
        for k, term in enumerate(terms):
            weighted = (term.reshape(rows // orbitals, orbitals, width) * c2).reshape(rows, width)
            out[k + 1 : k + 2, :] = folded(weighted)

    return call(
        kernel,
        "own_second",
        in_specs=[SCALAR] + [WHOLE] * 6,
        out_specs=[WHOLE] * 2,
        out_shape=[jax.ShapeDtypeStruct((rows, width), BF16), jax.ShapeDtypeStruct((8, 128), F32)],
    )(me, mine, theirs, volterra, response, squares, coupling)


def finish_first(me, pieces, volterra, edge, coupling, bits):
    rows, width = pieces[0].shape
    columns = coupling.shape[1]

    def kernel(me_ref, *refs):
        pieces, (w, edge, coupling, g_out, cubic, held, sems) = refs[:4], refs[4:]
        place = Place(me_ref[0], bits)
        copies = []
        for slot in range(4):
            at = columns_of(place.quarter_of(slot), width)
            g = jnp.dot(w[0, :, :rows], pieces[slot][...], preferred_element_type=F32)
            g += jnp.dot(w[0, :, rows:], edge[:, at], preferred_element_type=F32)
            held[slot] = g.astype(BF16)
            copies.append(pltpu.make_async_copy(held.at[slot], g_out.at[pl.ds(0, rows), at], sems.at[slot]))
            copies[-1].start()
            cubic[slot] = cubed(g, coupling[:, at])
        for copy in copies:
            copy.wait()

    return call(
        kernel,
        "finish_first",
        in_specs=[SCALAR] + [WHOLE] * 7,
        out_specs=[HBM, WHOLE],
        out_shape=[jax.ShapeDtypeStruct((2 * rows, columns), BF16), jax.ShapeDtypeStruct((4, rows, width), F32)],
        scratch_shapes=[pltpu.VMEM((4, rows, width), BF16), pltpu.SemaphoreType.DMA((4,))],
    )(me, *pieces, volterra, edge, coupling)


def finish_second(me, pieces, volterra, cubic, shares, coupling, g_first, bits):
    rows, width = pieces[0].shape
    columns = coupling.shape[1]
    everyone = shares.shape[0]

    def kernel(me_ref, *refs):
        pieces, (w, cubic, shares, coupling, _, g_out, sigma, g_held, s_held, sems) = refs[:4], refs[4:]
        place = Place(me_ref[0], bits)
        sums = jnp.sum(shares[...], axis=2, keepdims=True)
        means = sums[:, 0:1, :]
        mean = jnp.sum(means) / everyone
        ratio = jnp.sqrt((means + EPS) / (mean + EPS))
        power, series = jnp.ones_like(ratio), jnp.zeros_like(ratio)
        for k, weight in enumerate(BINOMIAL):
            series += weight * sums[:, k + 1 : k + 2, :] * power
            power = power * ratio
        scale_0 = 1.0 / jnp.sqrt(mean + EPS)
        scale_1 = 1.0 / jnp.sqrt(jnp.maximum(jnp.sum(series) / everyone, 0.0) + EPS)

        copies = []

        def write(value, held, slot, out, block, at):
            held[slot] = value
            sem = sems.at[len(copies)]
            copies.append(pltpu.make_async_copy(held.at[slot], out.at[pl.ds(block * rows, rows), at], sem))
            copies[-1].start()

        for slot in range(4):
            at = columns_of(place.quarter_of(slot), width)
            before = (cubic[slot] * scale_0).astype(BF16)
            write(before, s_held, slot, sigma, 0, at)
            g = jnp.dot(w[1, :, :rows], pieces[slot][...], preferred_element_type=F32)
            g += jnp.dot(w[1, :, rows:], before, preferred_element_type=F32)
            write(g.astype(BF16), g_held, slot, g_out, 1, at)
            write((cubed(g, coupling[:, at]) * scale_1).astype(BF16), s_held, 4 + slot, sigma, 1, at)
        for copy in copies:
            copy.wait()

    return call(
        kernel,
        "finish_second",
        in_specs=[SCALAR] + [WHOLE] * 8 + [HBM],
        out_specs=[HBM, HBM],
        out_shape=[jax.ShapeDtypeStruct((2 * rows, columns), BF16)] * 2,
        scratch_shapes=[
            pltpu.VMEM((4, rows, width), BF16),
            pltpu.VMEM((8, rows, width), BF16),
            pltpu.SemaphoreType.DMA((12,)),
        ],
        input_output_aliases={9: 0},
    )(me, *pieces, volterra, cubic, shares, coupling, g_first)


def per_device(past, second, g_hist, sigma_hist, volterra, sigma_edge, coupling):
    blocks, rows = volterra.shape[:2]
    assert blocks == 2 and past >= 8
    bits = log2(past)
    half = g_hist.shape[1] // 2
    me = lax.axis_index("past").astype(jnp.int32).reshape(1)
    even = list(range(bits))
    odd = even[:1] + even[1:][::-1]

    def swap(x, level):
        pairs = [(d, d ^ (1 << (odd if d % 2 else even)[level])) for d in range(past)]
        return lax.ppermute(x, "past", pairs)

    def exchanged(kept, arrived, sent):
        total = kept[1] + arrived[1].astype(F32) + swap(sent, 1).astype(F32)
        for level in range(2, bits):
            mine = total.astype(BF16)
            theirs = swap(mine, level)
            total = mine.astype(F32) + theirs.astype(F32)
        return mine, theirs

    def passed_on(kept, arrived):
        return (kept[0] + arrived[0].astype(F32)).astype(BF16)

    def gathered(own):
        partner = swap(own, 1)
        return [own, partner, swap(own, 0), swap(partner, 0)]

    send, sigma_0, g_send = product(me, sigma_hist, g_hist, 0, rows, half, bits, True)
    arrived_0 = swap(send, 0)
    kept_0, g_keep = product(me, sigma_0, g_hist, 0, rows, half, bits, False)
    sent_0 = passed_on(kept_0, arrived_0)
    send, sigma_1 = product(me, sigma_hist, g_send, 1, rows, half, bits, True, after=sent_0)
    arrived_1 = swap(send, 0)
    (kept_1,) = product(me, sigma_1, g_keep, 1, rows, half, bits, False)
    sent_1 = passed_on(kept_1, arrived_1)

    mine, theirs = exchanged(kept_0, arrived_0, sent_0)
    own_0, response, squares = own_first(me, mine, theirs, volterra, sigma_edge, coupling, bits)
    mine, theirs = exchanged(kept_1, arrived_1, sent_1)
    own_1, share = own_second(me, mine, theirs, volterra, response, squares, coupling, bits)
    copies = jnp.broadcast_to(share, (past * second,) + share.shape)
    shares = lax.all_to_all(copies, ("past", "second"), 0, 0)

    g_first, cubic = finish_first(me, gathered(own_0), volterra, sigma_edge, coupling, bits)
    return tuple(finish_second(me, gathered(own_1), volterra, cubic, shares, coupling, g_first, bits))


def solution(mesh):
    return jax.shard_map(
        functools.partial(per_device, mesh.shape["past"], mesh.shape["second"]),
        mesh=mesh,
        in_specs=(P("past", "second"), P(None, "past"), P(), P(None, "second"), P(None, "second")),
        out_specs=(P(None, "second"), P(None, "second")),
        check_vma=False,
    )
```

time: 62.5 us -> 60 us (0.960)
  other arithmetic: 3.68 us -> 0.29 us
  waiting for transfers between devices: 15.6 us -> 17.1 us
    another operation x2 -> x0, other arithmetic: 2.56 us -> none  [gathered(): return jnp.stack([own, partner, swap(own, 0), swap(partner, 0)])]
    all_to_all x1, waiting for transfers between devices: 1.54 us -> 3.73 us  [per_device(): shares = lax.all_to_all(copies, ('past', 'second'), 0, 0)]
    convert_element_type x4 -> x2, other arithmetic: 1.01 us -> 0.17 us  [exchanged(): mine = total.astype(BF16)]
    ppermute x12, waiting for transfers between devices: 14.1 us -> 13.4 us  [swap(): return lax.ppermute(x, 'past', pairs)]
  transfers between devices with their start and end apart: 13 -> 13, of which waited for: 7 -> 7; matrix products, arithmetic and copies ran while one was open for 7% -> 1% of each run, Pallas kernels for 16% -> 17%
where the time goes in v5:
time: 60 us; the launch traced here: 59.7 us
  Pallas kernels  18.2 us (30%)
  waiting for transfers between devices  17.1 us (29%)
  starting transfers between devices  15.3 us (26%)
  local copies, waits for them, and re-layouts  7.96 us (13%)
  between operations  0.79 us (1%)
    ppermute x12, waiting for transfers between devices, swap(): return lax.ppermute(x, 'past', pairs)  13.4 us
    ppermute x12, starting transfers between devices, swap(): return lax.ppermute(x, 'past', pairs)  10.3 us
    pallas_call x4, Pallas kernels, product(): call(kernel, 'memory_product', in_specs=[SCALAR, HBM if load_sigma else W...  7.99 us
    unnamed x16, local copies, waits for them, and re-layouts  7.3 us
    all_to_all x1, starting transfers between devices, per_device(): shares = lax.all_to_all(copies, ('past', 'second'), 0, 0)  4.96 us
    pallas_call x1, Pallas kernels, finish_second(): call(kernel, 'finish_second', in_specs=[SCALAR] + [WHOLE] * 8 + [HBM], ou...  4.3 us
    all_to_all x1, waiting for transfers between devices, per_device(): shares = lax.all_to_all(copies, ('past', 'second'), 0, 0)  3.73 us
    pallas_call x1, Pallas kernels, finish_first(): call(kernel, 'finish_first', in_specs=[SCALAR] + [WHOLE] * 7, out_specs=[...  3.32 us
  transfers between devices with their start and end apart: 13, of which 7 were waited for; matrix products, arithmetic and copies ran while one was open for 1% of the time, Pallas kernels for 17%

profile of v5, /device:TPU:0, one launch (start us, length us, event | category | flops | bytes accessed | tf_op | source)
XLA Modules:
  0.0 59.7 jit_solution(16733751044546501821)
XLA Ops:
  0.6 2.2 %copy-done.1 = bf16[2048,1024]{1,0:T(8,128)(2,1)S(1)} copy-done((bf16[2048,1024]{1,0:T(8,128)(2,1)S(1)}, bf16[2048,1024]{1,0:T(8,128)(2,1)}, u32[]{:S(2)}) %copy-start.1) | copy-done | bytes 4194328
  2.8 2.2 %copy-done.3 = bf16[1024,2048]{1,0:T(8,128)(2,1)S(1)} copy-done((bf16[1024,2048]{1,0:T(8,128)(2,1)S(1)}, bf16[1024,2048]{1,0:T(8,128)(2,1)}, u32[]{:S(2)}) %copy-start.3) | copy-done | bytes 4194328
  5.0 2.3 %memory_product.4 = (bf16[2,512,256]{2,1,0:T(8,128)(2,1)S(1)}, bf16[512,2048]{1,0:T(8,128)(2,1)S(1)}, bf16[2048,512]{1,0:T(8,128)(2,1)S(1)}) custom-call(s32[1]{0:T(128)} %bitcast.me_ref, bf16[1024,2048]{1,0:T(8,128)(2,1)S(1)} %copy-done.3, bf16[2048,1024]{1,0:T(8,128)(2,1)S(1)} %copy-done.1), custom_call_target="tpu_custom_call" | custom-call | flops 1024 | bytes 1024 | tf_op jit(solution)/shard_map/memory_product/pallas_call | solution.py:143
  7.3 0.5 collective-permute-start
  7.8 2.8 %memory_product.5 = (f32[2,512,256]{2,1,0:T(8,128)S(1)}, bf16[2048,512]{1,0:T(8,128)(2,1)S(1)}) custom-call(s32[1]{0:T(128)} %bitcast.me_ref, bf16[512,2048]{1,0:T(8,128)(2,1)S(1)} %get-tuple-element.17.sigma_ref, bf16[2048,1024]{1,0:T(8,128)(2,1)S(1)} %copy-done.2), custom_call_target="tpu_custom_call" | custom-call | flops 1024 | bytes 1024 | tf_op jit(solution)/shard_map/memory_product/pallas_call | solution.py:143
  10.7 1.6 %memory_product.6 = (bf16[2,512,256]{2,1,0:T(8,128)(2,1)S(1)}, bf16[512,2048]{1,0:T(8,128)(2,1)S(1)}) custom-call(s32[1]{0:T(128)} %bitcast.me_ref, bf16[1024,2048]{1,0:T(8,128)(2,1)S(1)} %copy-done.3, bf16[2048,512]{1,0:T(8,128)(2,1)S(1)} %get-tuple-element.16.g_ref, bf16[512,256]{1,0:T(8,128)(2,1)S(1)} %fusion.5.refs_0_), custom_call_target="tpu_custom_call" | custom-call | flops 1024 | bytes 1024 | tf_op jit(solution)/shard_map/memory_product/pallas_call | solution.py:143
  12.3 0.1 collective-permute-start.1
  12.4 2.9 %collective-permute-start.4 = (bf16[512,256]{1,0:T(8,128)(2,1)S(1)}, bf16[512,256]{1,0:T(8,128)(2,1)S(1)}, u32[]{:S(2)}, u32[]{:S(2)}) collective-permute-start(bf16[512,256]{1,0:T(8,128)(2,1)S(1)} %fusion.5.refs_0_), channel_id=1, source_target_pairs={{0,8},{4,20},{8,0},{12,28},{16,24},{20,4},{24,16},{28,12},{1,9},{5... | collective-permute-start | bytes 786440 | tf_op jit(solution)/shard_map/ppermute | solution.py:319
  15.4 1.3 %memory_product.7 = f32[2,512,256]{2,1,0:T(8,128)S(1)} custom-call(s32[1]{0:T(128)} %bitcast.me_ref, bf16[512,2048]{1,0:T(8,128)(2,1)S(1)} %get-tuple-element.20.sigma_ref, bf16[2048,512]{1,0:T(8,128)(2,1)S(1)} %get-tuple-element.21.g_ref), custom_call_target="tpu_custom_call" | custom-call | flops 1024 | bytes 1024 | tf_op jit(solution)/shard_map/memory_product/pallas_call | solution.py:143
  16.8 0.2 collective-permute-start.2
  17.0 2.7 %collective-permute-done.4 = bf16[512,256]{1,0:T(8,128)(2,1)S(1)} collective-permute-done((bf16[512,256]{1,0:T(8,128)(2,1)S(1)}, bf16[512,256]{1,0:T(8,128)(2,1)S(1)}, u32[]{:S(2)}, u32[]{:S(2)}) %collective-permute-start.4) | collective-permute-done | bytes 262176 | tf_op jit(solution)/shard_map/ppermute | solution.py:319
  19.7 0.1 fusion.4.mine
  19.8 2.1 %collective-permute-start.5 = (bf16[512,256]{1,0:T(8,128)(2,1)S(1)}, bf16[512,256]{1,0:T(8,128)(2,1)S(1)}, u32[]{:S(2)}, u32[]{:S(2)}) collective-permute-start(bf16[512,256]{1,0:T(8,128)(2,1)S(1)} %fusion.4.mine), channel_id=1, source_target_pairs={{0,16},{4,12},{8,24},{12,4},{16,0},{20,28},{24,8},{28,20},{1,17},{... | collective-permute-start | bytes 786440 | tf_op jit(solution)/shard_map/ppermute | solution.py:319
  21.9 2.5 %collective-permute-done.2 = bf16[512,256]{1,0:T(8,128)(2,1)S(1)} collective-permute-done((bf16[512,256]{1,0:T(8,128)(2,1)S(1)}, bf16[512,256]{1,0:T(8,128)(2,1)S(1)}, u32[]{:S(2)}, u32[]{:S(2)}) %collective-permute-start.2) | collective-permute-done | bytes 262176 | tf_op jit(solution)/shard_map/ppermute | solution.py:319
  24.4 0.1 fusion.3.mine
  24.5 1.4 %collective-permute-start.3 = (bf16[512,256]{1,0:T(8,128)(2,1)S(1)}, bf16[512,256]{1,0:T(8,128)(2,1)S(1)}, u32[]{:S(2)}, u32[]{:S(2)}) collective-permute-start(bf16[512,256]{1,0:T(8,128)(2,1)S(1)} %fusion.3.mine), channel_id=1, source_target_pairs={{0,16},{4,12},{8,24},{12,4},{16,0},{20,28},{24,8},{28,20},{1,17},{... | collective-permute-start | bytes 786440 | tf_op jit(solution)/shard_map/ppermute | solution.py:319
  25.9 0.4 collective-permute-done.5.theirs
  26.3 1.2 %own_first.1 = (bf16[512,256]{1,0:T(8,128)(2,1)}, f32[512,256]{1,0:T(8,128)S(1)}, f32[1,128]{1,0:T(1,128)S(1)}) custom-call(s32[1]{0:T(128)} %bitcast.me_ref, bf16[512,256]{1,0:T(8,128)(2,1)S(1)} %fusion.4.mine, bf16[512,256]{1,0:T(8,128)(2,1)S(1)} %collective-permute-done.5.theirs, bf16[2,512,1024]{2,1,0:T(8,128)(2,1)S(1)} %copy-done, ...), custom_call_target="tpu_custom_call" | custom-call | flops 1024 | bytes 1024 | tf_op jit(solution)/shard_map/own_first/pallas_call | solution.py:184
  27.5 2.1 %collective-permute-start.9 = (bf16[512,256]{1,0:T(8,128)(2,1)}, bf16[512,256]{1,0:T(8,128)(2,1)}, u32[]{:S(2)}, u32[]{:S(2)}) collective-permute-start(bf16[512,256]{1,0:T(8,128)(2,1)} %get-tuple-element.26.refs_0_), channel_id=1, source_target_pairs={{0,8},{4,20},{8,0},{12,28},{16,24},{20,4},{24,16},{28,12},{1,9},{5... | collective-permute-start | bytes 786440 | tf_op jit(solution)/shard_map/ppermute | solution.py:319
  29.5 2.1 %collective-permute-done.3.theirs = bf16[512,256]{1,0:T(8,128)(2,1)S(1)} collective-permute-done((bf16[512,256]{1,0:T(8,128)(2,1)S(1)}, bf16[512,256]{1,0:T(8,128)(2,1)S(1)}, u32[]{:S(2)}, u32[]{:S(2)}) %collective-permute-start.3) | collective-permute-done | bytes 262176 | tf_op jit(solution)/shard_map/ppermute | solution.py:319
  31.6 1.4 %own_second.1 = (bf16[512,256]{1,0:T(8,128)(2,1)}, f32[8,128]{1,0:T(8,128)S(1)}) custom-call(s32[1]{0:T(128)} %bitcast.me_ref, bf16[512,256]{1,0:T(8,128)(2,1)S(1)} %fusion.3.mine, bf16[512,256]{1,0:T(8,128)(2,1)S(1)} %collective-permute-done.3.theirs, bf16[2,512,1024]{2,1,0:T(8,128)(2,1)S(1)} %copy-done, f32[512,256]{1,0:T(8,128)S(1)} %get-tuple-element.23.response, ...), custom_call_target="tpu_custom_call" | custom-call | flops 1024 | bytes 1024 | tf_op jit(solution)/shard_map/own_second/pallas_call | solution.py:217
  33.1 0.5 collective-permute-start.6
  33.5 0.7 %collective-permute-done.9.refs_1_ = bf16[512,256]{1,0:T(8,128)(2,1)} collective-permute-done((bf16[512,256]{1,0:T(8,128)(2,1)}, bf16[512,256]{1,0:T(8,128)(2,1)}, u32[]{:S(2)}, u32[]{:S(2)}) %collective-permute-start.9) | collective-permute-done | bytes 262176 | tf_op jit(solution)/shard_map/ppermute | solution.py:319
  34.2 0.5 collective-permute-start.7
  34.7 5.0 %collective-permute-done.6.refs_1_ = bf16[512,256]{1,0:T(8,128)(2,1)} collective-permute-done((bf16[512,256]{1,0:T(8,128)(2,1)}, bf16[512,256]{1,0:T(8,128)(2,1)}, u32[]{:S(2)}, u32[]{:S(2)}) %collective-permute-start.6) | collective-permute-done | bytes 262176 | tf_op jit(solution)/shard_map/ppermute | solution.py:319
  39.7 0.7 %broadcast_in_dim.3 = f32[32,8,128]{2,1,0:T(8,128)} broadcast(f32[8,128]{1,0:T(8,128)S(1)} %get-tuple-element.28), dimensions={1,2} | broadcast | bytes 135168 | tf_op jit(solution)/shard_map/broadcast_in_dim | solution.py:349
  40.4 5.0 %all-to-all-start = ((f32[32,8,128]{2,1,0:T(8,128)}), f32[32,8,128]{2,1,0:T(8,128)S(1)}, u32[]{:S(2)}, u32[]{:S(2)}) async-start(f32[32,8,128]{2,1,0:T(8,128)} %broadcast_in_dim.3), calls=%async_computation | async-start | bytes 262144 | tf_op jit(solution)/shard_map/all_to_all | solution.py:350
  45.4 3.3 %finish_first.1 = (bf16[1024,1024]{1,0:T(8,128)(2,1)}, f32[4,512,256]{2,1,0:T(8,128)S(1)}) custom-call(s32[1]{0:T(128)} %bitcast.me_ref, bf16[512,256]{1,0:T(8,128)(2,1)} %get-tuple-element.26.refs_0_, bf16[512,256]{1,0:T(8,128)(2,1)} %collective-permute-done.9.refs_1_, bf16[512,256]{1,0:T(8,128)(2,1)} %collective-permute-done.10.refs_2_, ...), custom_call_target="tpu_custom_call" | custom-call | flops 1024 | bytes 1024 | tf_op jit(solution)/shard_map/finish_first/pallas_call | solution.py:245
  48.7 1.3 %copy-done.6 = f32[4,512,256]{2,1,0:T(8,128)} copy-done((f32[4,512,256]{2,1,0:T(8,128)}, f32[4,512,256]{2,1,0:T(8,128)S(1)}, u32[]{:S(2)}) %copy-start.6) | copy-done | bytes 2097176
  50.0 3.7 %all-to-all-done.refs_6_ = f32[32,8,128]{2,1,0:T(8,128)S(1)} async-done(((f32[32,8,128]{2,1,0:T(8,128)}), f32[32,8,128]{2,1,0:T(8,128)S(1)}, u32[]{:S(2)}, u32[]{:S(2)}) %all-to-all-start) | async-done | bytes 131104 | tf_op jit(solution)/shard_map/all_to_all | solution.py:350
  53.8 1.6 %copy-done.7 = f32[4,512,256]{2,1,0:T(8,128)S(1)} copy-done((f32[4,512,256]{2,1,0:T(8,128)S(1)}, f32[4,512,256]{2,1,0:T(8,128)}, u32[]{:S(2)}) %copy-start.7) | copy-done | bytes 2097176
  55.4 4.3 %finish_second.1 = (bf16[1024,1024]{1,0:T(8,128)(2,1)}, bf16[1024,1024]{1,0:T(8,128)(2,1)}) custom-call(s32[1]{0:T(128)} %bitcast.me_ref, bf16[512,256]{1,0:T(8,128)(2,1)} %get-tuple-element.25.refs_0_, bf16[512,256]{1,0:T(8,128)(2,1)} %collective-permute-done.6.refs_1_, ...), custom_call_target="tpu_custom_call", output_to_operand_aliasing={{0}: (9, {})} | custom-call | flops 1024 | bytes 1024 | tf_op jit(solution)/shard_map/finish_second/pallas_call | solution.py:293
  (23 shorter events, 0.2 us)
Async XLA Ops:
  0.6 2.2 %copy-start.1 = (bf16[2048,1024]{1,0:T(8,128)(2,1)S(1)}, bf16[2048,1024]{1,0:T(8,128)(2,1)}, u32[]{:S(2)}) copy-start(bf16[2048,1024]{1,0:T(8,128)(2,1)} %g_ref.3) | copy-start | bytes 12582916
  2.8 2.2 %copy-start.3 = (bf16[1024,2048]{1,0:T(8,128)(2,1)S(1)}, bf16[1024,2048]{1,0:T(8,128)(2,1)}, u32[]{:S(2)}) copy-start(bf16[1024,2048]{1,0:T(8,128)(2,1)} %sigma_ref.3) | copy-start | bytes 12582916
  5.0 2.8 %copy-start.2 = (bf16[2048,1024]{1,0:T(8,128)(2,1)S(1)}, bf16[2048,1024]{1,0:T(8,128)(2,1)}, u32[]{:S(2)}) copy-start(bf16[2048,1024]{1,0:T(8,128)(2,1)} %g_ref.3) | copy-start | bytes 12582916
  7.3 3.3 %collective-permute-start = (bf16[2,512,256]{2,1,0:T(8,128)(2,1)S(1)}, bf16[2,512,256]{2,1,0:T(8,128)(2,1)S(1)}, u32[]{:S(2)}, u32[]{:S(2)}) collective-permute-start(bf16[2,512,256]{2,1,0:T(8,128)(2,1)S(1)} %get-tuple-element.19), channel_id=1, source_target_pairs={{0,4},{4,0},{8,12},{12,8},{16,20},{20,16},{24,28},{28,24},{1,5},{5... | collective-permute-start | bytes 1572872 | tf_op jit(solution)/shard_map/ppermute | solution.py:319
  12.3 4.4 %collective-permute-start.1 = (bf16[2,512,256]{2,1,0:T(8,128)(2,1)S(1)}, bf16[2,512,256]{2,1,0:T(8,128)(2,1)S(1)}, u32[]{:S(2)}, u32[]{:S(2)}) collective-permute-start(bf16[2,512,256]{2,1,0:T(8,128)(2,1)S(1)} %get-tuple-element.22), channel_id=1, source_target_pairs={{0,4},{4,0},{8,12},{12,8},{16,20},{20,16},{24,28},{28,24},{1,5},{5... | collective-permute-start | bytes 1572872 | tf_op jit(solution)/shard_map/ppermute | solution.py:319
  12.4 7.3 %collective-permute-start.4 = (bf16[512,256]{1,0:T(8,128)(2,1)S(1)}, bf16[512,256]{1,0:T(8,128)(2,1)S(1)}, u32[]{:S(2)}, u32[]{:S(2)}) collective-permute-start(bf16[512,256]{1,0:T(8,128)(2,1)S(1)} %fusion.5.refs_0_), channel_id=1, source_target_pairs={{0,8},{4,20},{8,0},{12,28},{16,24},{20,4},{24,16},{28,12},{1,9},{5... | collective-permute-start | bytes 786440 | tf_op jit(solution)/shard_map/ppermute | solution.py:319
  16.7 9.6 %copy-start = (bf16[2,512,1024]{2,1,0:T(8,128)(2,1)S(1)}, bf16[2,512,1024]{2,1,0:T(8,128)(2,1)}, u32[]{:S(2)}) copy-start(bf16[2,512,1024]{2,1,0:T(8,128)(2,1)} %refs_4_.3) | copy-start | bytes 6291460
  16.7 9.6 %copy-start.4 = (bf16[512,1024]{1,0:T(8,128)(2,1)S(1)}, bf16[512,1024]{1,0:T(8,128)(2,1)}, u32[]{:S(2)}) copy-start(bf16[512,1024]{1,0:T(8,128)(2,1)} %refs_5_.1) | copy-start | bytes 3145732
  16.7 9.6 %copy-start.5 = (f32[32,1024]{1,0:T(8,128)S(1)}, f32[32,1024]{1,0:T(8,128)}, u32[]{:S(2)}) copy-start(f32[32,1024]{1,0:T(8,128)} %refs_7_.1) | copy-start | bytes 393220
  16.8 7.6 %collective-permute-start.2 = (bf16[512,256]{1,0:T(8,128)(2,1)S(1)}, bf16[512,256]{1,0:T(8,128)(2,1)S(1)}, u32[]{:S(2)}, u32[]{:S(2)}) collective-permute-start(bf16[512,256]{1,0:T(8,128)(2,1)S(1)} %fusion.6), channel_id=1, source_target_pairs={{0,8},{4,20},{8,0},{12,28},{16,24},{20,4},{24,16},{28,12},{1,9},{5... | collective-permute-start | bytes 786440 | tf_op jit(solution)/shard_map/ppermute | solution.py:319
  19.8 6.5 %collective-permute-start.5 = (bf16[512,256]{1,0:T(8,128)(2,1)S(1)}, bf16[512,256]{1,0:T(8,128)(2,1)S(1)}, u32[]{:S(2)}, u32[]{:S(2)}) collective-permute-start(bf16[512,256]{1,0:T(8,128)(2,1)S(1)} %fusion.4.mine), channel_id=1, source_target_pairs={{0,16},{4,12},{8,24},{12,4},{16,0},{20,28},{24,8},{28,20},{1,17},{... | collective-permute-start | bytes 786440 | tf_op jit(solution)/shard_map/ppermute | solution.py:319
  24.5 7.1 %collective-permute-start.3 = (bf16[512,256]{1,0:T(8,128)(2,1)S(1)}, bf16[512,256]{1,0:T(8,128)(2,1)S(1)}, u32[]{:S(2)}, u32[]{:S(2)}) collective-permute-start(bf16[512,256]{1,0:T(8,128)(2,1)S(1)} %fusion.3.mine), channel_id=1, source_target_pairs={{0,16},{4,12},{8,24},{12,4},{16,0},{20,28},{24,8},{28,20},{1,17},{... | collective-permute-start | bytes 786440 | tf_op jit(solution)/shard_map/ppermute | solution.py:319
  27.5 6.8 %collective-permute-start.9 = (bf16[512,256]{1,0:T(8,128)(2,1)}, bf16[512,256]{1,0:T(8,128)(2,1)}, u32[]{:S(2)}, u32[]{:S(2)}) collective-permute-start(bf16[512,256]{1,0:T(8,128)(2,1)} %get-tuple-element.26.refs_0_), channel_id=1, source_target_pairs={{0,8},{4,20},{8,0},{12,28},{16,24},{20,4},{24,16},{28,12},{1,9},{5... | collective-permute-start | bytes 786440 | tf_op jit(solution)/shard_map/ppermute | solution.py:319
  33.1 6.7 %collective-permute-start.6 = (bf16[512,256]{1,0:T(8,128)(2,1)}, bf16[512,256]{1,0:T(8,128)(2,1)}, u32[]{:S(2)}, u32[]{:S(2)}) collective-permute-start(bf16[512,256]{1,0:T(8,128)(2,1)} %get-tuple-element.25.refs_0_), channel_id=1, source_target_pairs={{0,8},{4,20},{8,0},{12,28},{16,24},{20,4},{24,16},{28,12},{1,9},{5... | collective-permute-start | bytes 786440 | tf_op jit(solution)/shard_map/ppermute | solution.py:319
  33.5 11.8 %collective-permute-start.10 = (bf16[512,256]{1,0:T(8,128)(2,1)}, bf16[512,256]{1,0:T(8,128)(2,1)}, u32[]{:S(2)}, u32[]{:S(2)}) collective-permute-start(bf16[512,256]{1,0:T(8,128)(2,1)} %get-tuple-element.26.refs_0_), channel_id=1, source_target_pairs={{0,4},{4,0},{8,12},{12,8},{16,20},{20,16},{24,28},{28,24},{1,5},{5... | collective-permute-start | bytes 786440 | tf_op jit(solution)/shard_map/ppermute | solution.py:319
  34.2 11.2 %collective-permute-start.11 = (bf16[512,256]{1,0:T(8,128)(2,1)}, bf16[512,256]{1,0:T(8,128)(2,1)}, u32[]{:S(2)}, u32[]{:S(2)}) collective-permute-start(bf16[512,256]{1,0:T(8,128)(2,1)} %collective-permute-done.9.refs_1_), channel_id=1, source_target_pairs={{0,4},{4,0},{8,12},{12,8},{16,20},{20,16},{24,28},{28,24},{1,5},{5... | collective-permute-start | bytes 786440 | tf_op jit(solution)/shard_map/ppermute | solution.py:319
  34.2 19.6 %collective-permute-start.7 = (bf16[512,256]{1,0:T(8,128)(2,1)}, bf16[512,256]{1,0:T(8,128)(2,1)}, u32[]{:S(2)}, u32[]{:S(2)}) collective-permute-start(bf16[512,256]{1,0:T(8,128)(2,1)} %get-tuple-element.25.refs_0_), channel_id=1, source_target_pairs={{0,4},{4,0},{8,12},{12,8},{16,20},{20,16},{24,28},{28,24},{1,5},{5... | collective-permute-start | bytes 786440 | tf_op jit(solution)/shard_map/ppermute | solution.py:319
  39.7 14.0 %collective-permute-start.8 = (bf16[512,256]{1,0:T(8,128)(2,1)}, bf16[512,256]{1,0:T(8,128)(2,1)}, u32[]{:S(2)}, u32[]{:S(2)}) collective-permute-start(bf16[512,256]{1,0:T(8,128)(2,1)} %collective-permute-done.6.refs_1_), channel_id=1, source_target_pairs={{0,4},{4,0},{8,12},{12,8},{16,20},{20,16},{24,28},{28,24},{1,5},{5... | collective-permute-start | bytes 786440 | tf_op jit(solution)/shard_map/ppermute | solution.py:319
  40.4 13.4 %all-to-all-start = ((f32[32,8,128]{2,1,0:T(8,128)}), f32[32,8,128]{2,1,0:T(8,128)S(1)}, u32[]{:S(2)}, u32[]{:S(2)}) async-start(f32[32,8,128]{2,1,0:T(8,128)} %broadcast_in_dim.3), calls=%async_computation | async-start | bytes 262144 | tf_op jit(solution)/shard_map/all_to_all | solution.py:350
  48.7 1.3 %copy-start.6 = (f32[4,512,256]{2,1,0:T(8,128)}, f32[4,512,256]{2,1,0:T(8,128)S(1)}, u32[]{:S(2)}) copy-start(f32[4,512,256]{2,1,0:T(8,128)S(1)} %get-tuple-element.27.refs_5_) | copy-start | bytes 6291460
  53.8 1.6 %copy-start.7 = (f32[4,512,256]{2,1,0:T(8,128)S(1)}, f32[4,512,256]{2,1,0:T(8,128)}, u32[]{:S(2)}) copy-start(f32[4,512,256]{2,1,0:T(8,128)} %copy-done.6) | copy-start | bytes 6291460

commit v6 on v5

--- a/solution.py
+++ b/solution.py
@@ -25,6 +25,14 @@
     return bits
 
 
+def near(shape, dtype):
+    return pltpu.VMEM(shape, dtype)
+
+
+def far(x):
+    return pltpu.with_memory_space_constraint(x, pltpu.HBM)
+
+
 def call(kernel, name, **kwargs):
     return pl.pallas_call(
         kernel,
@@ -57,11 +65,11 @@
     quarter = half // 2
     dtype = BF16 if send else F32
     pieces = 4 if load_sigma and load_g else 2
-    out_shape = [jax.ShapeDtypeStruct((2, rows, quarter), dtype)]
+    out_shape = [near((2, rows, quarter), dtype)]
     if load_sigma:
-        out_shape.append(jax.ShapeDtypeStruct((rows, depth), BF16))
+        out_shape.append(near((rows, depth), BF16))
     if load_g:
-        out_shape.append(jax.ShapeDtypeStruct((depth, half), BF16))
+        out_shape.append(near((depth, half), BF16))
 
     def kernel(me_ref, sigma_ref, g_ref, *refs):
         refs = list(refs)
@@ -147,7 +155,20 @@
         out_specs=[WHOLE] * len(out_shape),
         out_shape=out_shape,
         scratch_shapes=[pltpu.VMEM((rows, half), F32), pltpu.SemaphoreType.DMA((2 * pieces,))],
-    )(me, sigma, g, *([] if after is None else [after]))
+    )(me, far(sigma) if load_sigma else sigma, far(g) if load_g else g, *([] if after is None else [after]))
+
+
+def combined(kept, arrived, more, after):
+    rows, width = more.shape
+    if after is None:
+        return (kept[1] + arrived[1].astype(F32) + more.astype(F32)).astype(BF16)
+
+    def kernel(kept, arrived, more, _, out):
+        out[...] = (kept[1] + arrived[1].astype(F32) + more[...].astype(F32)).astype(BF16)
+
+    return call(
+        kernel, "combined", in_specs=[WHOLE] * 3 + [FAR], out_specs=WHOLE, out_shape=near((rows, width), BF16)
+    )(kept, arrived, more, after)
 
 
 def cubed(g, coupling):
@@ -166,10 +187,17 @@
     return pl.ds(pl.multiple_of(quarter * width, width), width)
 
 
-def own_first(me, mine, theirs, volterra, edge, coupling, bits):
+def over_halves(x):
+    while x.shape[0] > 1:
+        half = x.shape[0] // 2
+        x = x[:half] + x[half:]
+    return x
+
+
+def own_first(me, mine, theirs, volterra, edge, coupling, bits, after):
     rows, width = mine.shape
 
-    def kernel(me_ref, mine, theirs, w, edge, coupling, memory, response, squares):
+    def kernel(me_ref, mine, theirs, w, edge, coupling, _, memory, response, squares):
         at = columns_of(Place(me_ref[0], bits).quarter(), width)
         summed = (mine[...].astype(F32) + theirs[...].astype(F32)).astype(BF16)
         memory[...] = summed
@@ -184,14 +212,14 @@
     return call(
         kernel,
         "own_first",
-        in_specs=[SCALAR] + [WHOLE] * 5,
+        in_specs=[SCALAR] + [WHOLE] * 5 + [FAR],
         out_specs=[WHOLE] * 3,
         out_shape=[
-            jax.ShapeDtypeStruct((rows, width), BF16),
-            jax.ShapeDtypeStruct((rows, width), F32),
-            jax.ShapeDtypeStruct((1, 128), F32),
+            near((rows, width), BF16),
+            near((rows, width), F32),
+            near((1, 128), F32),
         ],
-    )(me, mine, theirs, volterra, edge, coupling)
+    )(me, mine, theirs, volterra, edge, coupling, after)
 
 
 def own_second(me, mine, theirs, volterra, response, squares, coupling, bits):
@@ -208,18 +236,19 @@
         b = response[...]
         a2, b2 = a * a, b * b
         a3, b3, a2b, ab2 = a2 * a, b2 * b, a2 * b, a * b2
-        out[0:1, :] = squares[...]
+        lines = [squares[...]]
         terms = (a3 * a3, a3 * a2b, a2b * a2b, a3 * b3, ab2 * ab2, ab2 * b3, b3 * b3)
-        for k, term in enumerate(terms):
+        for term in terms:
             weighted = (term.reshape(rows // orbitals, orbitals, width) * c2).reshape(rows, width)
-            out[k + 1 : k + 2, :] = folded(weighted)
+            lines.append(folded(weighted))
+        out[0] = jnp.concatenate(lines, axis=0)
 
     return call(
         kernel,
         "own_second",
         in_specs=[SCALAR] + [WHOLE] * 6,
         out_specs=[WHOLE] * 2,
-        out_shape=[jax.ShapeDtypeStruct((rows, width), BF16), jax.ShapeDtypeStruct((8, 128), F32)],
+        out_shape=[near((rows, width), BF16), near((1, 8, 128), F32)],
     )(me, mine, theirs, volterra, response, squares, coupling)
 
 
@@ -247,7 +276,10 @@
         "finish_first",
         in_specs=[SCALAR] + [WHOLE] * 7,
         out_specs=[HBM, WHOLE],
-        out_shape=[jax.ShapeDtypeStruct((2 * rows, columns), BF16), jax.ShapeDtypeStruct((4, rows, width), F32)],
+        out_shape=[
+            jax.ShapeDtypeStruct((2 * rows, columns), BF16),
+            near((4, rows, width), F32),
+        ],
         scratch_shapes=[pltpu.VMEM((4, rows, width), BF16), pltpu.SemaphoreType.DMA((4,))],
     )(me, *pieces, volterra, edge, coupling)
 
@@ -262,14 +294,14 @@
         place = Place(me_ref[0], bits)
         sums = jnp.sum(shares[...], axis=2, keepdims=True)
         means = sums[:, 0:1, :]
-        mean = jnp.sum(means) / everyone
+        mean = jnp.sum(over_halves(means)) / everyone
         ratio = jnp.sqrt((means + EPS) / (mean + EPS))
         power, series = jnp.ones_like(ratio), jnp.zeros_like(ratio)
         for k, weight in enumerate(BINOMIAL):
             series += weight * sums[:, k + 1 : k + 2, :] * power
             power = power * ratio
         scale_0 = 1.0 / jnp.sqrt(mean + EPS)
-        scale_1 = 1.0 / jnp.sqrt(jnp.maximum(jnp.sum(series) / everyone, 0.0) + EPS)
+        scale_1 = 1.0 / jnp.sqrt(jnp.maximum(jnp.sum(over_halves(series)) / everyone, 0.0) + EPS)
 
         copies = []
 
@@ -318,12 +350,12 @@
         pairs = [(d, d ^ (1 << (odd if d % 2 else even)[level])) for d in range(past)]
         return lax.ppermute(x, "past", pairs)
 
-    def exchanged(kept, arrived, sent):
-        total = kept[1] + arrived[1].astype(F32) + swap(sent, 1).astype(F32)
-        for level in range(2, bits):
-            mine = total.astype(BF16)
+    def exchanged(kept, arrived, sent, after=None):
+        mine = combined(kept, arrived, swap(sent, 1), after)
+        theirs = swap(mine, 2)
+        for level in range(3, bits):
+            mine = (mine.astype(F32) + theirs.astype(F32)).astype(BF16)
             theirs = swap(mine, level)
-            total = mine.astype(F32) + theirs.astype(F32)
         return mine, theirs
 
     def passed_on(kept, arrived):
@@ -332,6 +364,14 @@
     def gathered(own):
         partner = swap(own, 1)
         return [own, partner, swap(own, 0), swap(partner, 0)]
+
+    def shared(share):
+        for level in range(log2(second)):
+            pairs = [(z, z ^ (1 << level)) for z in range(second)]
+            share = jnp.concatenate([share, lax.ppermute(share, "second", pairs)], axis=0)
+        for level in (1, 0):
+            share = jnp.concatenate([share, swap(share, level)], axis=0)
+        return share
 
     send, sigma_0, g_send = product(me, sigma_hist, g_hist, 0, rows, half, bits, True)
     arrived_0 = swap(send, 0)
@@ -342,15 +382,15 @@
     (kept_1,) = product(me, sigma_1, g_keep, 1, rows, half, bits, False)
     sent_1 = passed_on(kept_1, arrived_1)
 
-    mine, theirs = exchanged(kept_0, arrived_0, sent_0)
-    own_0, response, squares = own_first(me, mine, theirs, volterra, sigma_edge, coupling, bits)
-    mine, theirs = exchanged(kept_1, arrived_1, sent_1)
-    own_1, share = own_second(me, mine, theirs, volterra, response, squares, coupling, bits)
-    copies = jnp.broadcast_to(share, (past * second,) + share.shape)
-    shares = lax.all_to_all(copies, ("past", "second"), 0, 0)
+    mine, theirs = exchanged(kept_0, arrived_0, sent_0, after=sent_1)
+    mine_1, theirs_1 = exchanged(kept_1, arrived_1, sent_1)
+    own_0, response, squares = own_first(me, mine, theirs, volterra, sigma_edge, coupling, bits, after=mine_1)
+    own_1, share = own_second(me, mine_1, theirs_1, volterra, response, squares, coupling, bits)
+    shares = shared(share)
 
     g_first, cubic = finish_first(me, gathered(own_0), volterra, sigma_edge, coupling, bits)
-    return tuple(finish_second(me, gathered(own_1), volterra, cubic, shares, coupling, g_first, bits))
+    pieces = gathered(own_1)
+    return tuple(finish_second(me, pieces, volterra, cubic, shares, coupling, g_first, bits))
 
 
 def solution(mesh):

time: 60 us -> 49.2 us (0.82)
  local copies, waits for them, and re-layouts: 7.96 us -> 0.03 us
  waiting for transfers between devices: 17.1 us -> 15.4 us
    unnamed x16 -> x10, local copies, waits for them, and re-layouts: 7.3 us -> 0.03 us
    all_to_all x1 -> x0, starting transfers between devices: 4.96 us -> none  [per_device(): shares = lax.all_to_all(copies, ('past', 'second'), 0, 0)]
    all_to_all x1 -> x0, waiting for transfers between devices: 3.73 us -> none  [per_device(): shares = lax.all_to_all(copies, ('past', 'second'), 0, 0)]
    ppermute x0 -> x2, starting transfers between devices: none -> 3.35 us  [shared(): lax.ppermute(share, 'second', pairs)]
    ppermute x0 -> x2, waiting for transfers between devices: none -> 3.11 us  [shared(): lax.ppermute(share, 'second', pairs)]
    pallas_call x4, Pallas kernels: 7.99 us -> 10.5 us  [product(): call(kernel, 'memory_product', in_specs=[SCALAR, HBM if load_sigma else W...]
    pallas_call x1, Pallas kernels: 4.3 us -> 2.88 us  [finish_second(): call(kernel, 'finish_second', in_specs=[SCALAR] + [WHOLE] * 8 + [HBM], ou...]
    ppermute x12 -> x14, starting transfers between devices: 10.3 us -> 11.6 us  [swap(): return lax.ppermute(x, 'past', pairs)]
  transfers between devices with their start and end apart: 13 -> 16, of which waited for: 7 -> 8; matrix products, arithmetic and copies ran while one was open for 1% -> 0% of each run, Pallas kernels for 17% -> 19%
where the time goes in v6:
time: 49.2 us; the launch traced here: 49 us
  Pallas kernels  17.6 us (36%)
  waiting for transfers between devices  15.4 us (31%)
  starting transfers between devices  15 us (30%)
  between operations  0.79 us (2%)
    ppermute x14, waiting for transfers between devices, swap(): return lax.ppermute(x, 'past', pairs)  12.3 us
    ppermute x14, starting transfers between devices, swap(): return lax.ppermute(x, 'past', pairs)  11.6 us
    pallas_call x4, Pallas kernels, product(): call(kernel, 'memory_product', in_specs=[SCALAR, HBM if load_sigma else W...  10.5 us
    ppermute x2, starting transfers between devices, shared(): lax.ppermute(share, 'second', pairs)  3.35 us
    ppermute x2, waiting for transfers between devices, shared(): lax.ppermute(share, 'second', pairs)  3.11 us
    pallas_call x1, Pallas kernels, finish_second(): call(kernel, 'finish_second', in_specs=[SCALAR] + [WHOLE] * 8 + [HBM], ou...  2.88 us
    pallas_call x1, Pallas kernels, finish_first(): call(kernel, 'finish_first', in_specs=[SCALAR] + [WHOLE] * 7, out_specs=[...  2.14 us
    pallas_call x1, Pallas kernels, own_first(): call(kernel, 'own_first', in_specs=[SCALAR] + [WHOLE] * 5 + [FAR], out_sp...  1.16 us
  transfers between devices with their start and end apart: 16, of which 8 were waited for; matrix products, arithmetic and copies ran while one was open for 0% of the time, Pallas kernels for 19%

profile of v6, /device:TPU:0, one launch (start us, length us, event | category | flops | bytes accessed | tf_op | source)
XLA Modules:
  0.0 49.0 jit_solution(16366994756576542854)
XLA Ops:
  0.6 2.8 %memory_product.4 = (bf16[2,512,256]{2,1,0:T(8,128)(2,1)S(1)}, bf16[512,2048]{1,0:T(8,128)(2,1)S(1)}, bf16[2048,512]{1,0:T(8,128)(2,1)S(1)}) custom-call(s32[1]{0:T(128)} %bitcast.me_ref, bf16[1024,2048]{1,0:T(8,128)(2,1)} %sigma_ref.3, bf16[2048,1024]{1,0:T(8,128)(2,1)} %g_ref.3), custom_call_target="tpu_custom_call" | custom-call | flops 1024 | bytes 1024 | tf_op jit(solution)/shard_map/memory_product/pallas_call | solution.py:151
  3.4 0.5 collective-permute-start
  3.9 3.7 %memory_product.5 = (f32[2,512,256]{2,1,0:T(8,128)S(1)}, bf16[2048,512]{1,0:T(8,128)(2,1)S(1)}) custom-call(s32[1]{0:T(128)} %bitcast.me_ref, bf16[512,2048]{1,0:T(8,128)(2,1)S(1)} %get-tuple-element.17.sigma_ref, bf16[2048,1024]{1,0:T(8,128)(2,1)} %g_ref.3), custom_call_target="tpu_custom_call" | custom-call | flops 1024 | bytes 1024 | tf_op jit(solution)/shard_map/memory_product/pallas_call | solution.py:151
  7.6 0.1 fusion.4.refs_0_
  7.7 2.7 %memory_product.6 = (bf16[2,512,256]{2,1,0:T(8,128)(2,1)S(1)}, bf16[512,2048]{1,0:T(8,128)(2,1)S(1)}) custom-call(s32[1]{0:T(128)} %bitcast.me_ref, bf16[1024,2048]{1,0:T(8,128)(2,1)} %sigma_ref.3, bf16[2048,512]{1,0:T(8,128)(2,1)S(1)} %get-tuple-element.16.g_ref, bf16[512,256]{1,0:T(8,128)(2,1)S(1)} %fusion.4.refs_0_), custom_call_target="tpu_custom_call" | custom-call | flops 1024 | bytes 1024 | tf_op jit(solution)/shard_map/memory_product/pallas_call | solution.py:151
  10.4 0.2 collective-permute-start.1
  10.5 2.9 %collective-permute-start.4 = (bf16[512,256]{1,0:T(8,128)(2,1)S(1)}, bf16[512,256]{1,0:T(8,128)(2,1)S(1)}, u32[]{:S(2)}, u32[]{:S(2)}) collective-permute-start(bf16[512,256]{1,0:T(8,128)(2,1)S(1)} %fusion.4.refs_0_), channel_id=1, source_target_pairs={{0,8},{4,20},{8,0},{12,28},{16,24},{20,4},{24,16},{28,12},{1,9},{5... | collective-permute-start | bytes 786440 | tf_op jit(solution)/shard_map/ppermute | solution.py:351
  13.5 1.3 %memory_product.7 = f32[2,512,256]{2,1,0:T(8,128)S(1)} custom-call(s32[1]{0:T(128)} %bitcast.me_ref, bf16[512,2048]{1,0:T(8,128)(2,1)S(1)} %get-tuple-element.20.sigma_ref, bf16[2048,512]{1,0:T(8,128)(2,1)S(1)} %get-tuple-element.21.g_ref), custom_call_target="tpu_custom_call" | custom-call | flops 1024 | bytes 1024 | tf_op jit(solution)/shard_map/memory_product/pallas_call | solution.py:151
  14.8 0.1 fusion.5._
  14.9 0.3 collective-permute-start.2
  15.2 2.6 %collective-permute-done.4.more = bf16[512,256]{1,0:T(8,128)(2,1)S(1)} collective-permute-done((bf16[512,256]{1,0:T(8,128)(2,1)S(1)}, bf16[512,256]{1,0:T(8,128)(2,1)S(1)}, u32[]{:S(2)}, u32[]{:S(2)}) %collective-permute-start.4) | collective-permute-done | bytes 262176 | tf_op jit(solution)/shard_map/ppermute | solution.py:351
  17.8 0.1 combined.1.mine
  17.9 2.1 %collective-permute-start.5 = (bf16[512,256]{1,0:T(8,128)(2,1)S(1)}, bf16[512,256]{1,0:T(8,128)(2,1)S(1)}, u32[]{:S(2)}, u32[]{:S(2)}) collective-permute-start(bf16[512,256]{1,0:T(8,128)(2,1)S(1)} %combined.1.mine), channel_id=1, source_target_pairs={{0,16},{4,12},{8,24},{12,4},{16,0},{20,28},{24,8},{28,20},{1,17},{... | collective-permute-start | bytes 786440 | tf_op jit(solution)/shard_map/ppermute | solution.py:351
  20.0 2.5 %collective-permute-done.2 = bf16[512,256]{1,0:T(8,128)(2,1)S(1)} collective-permute-done((bf16[512,256]{1,0:T(8,128)(2,1)S(1)}, bf16[512,256]{1,0:T(8,128)(2,1)S(1)}, u32[]{:S(2)}, u32[]{:S(2)}) %collective-permute-start.2) | collective-permute-done | bytes 262176 | tf_op jit(solution)/shard_map/ppermute | solution.py:351
  22.5 0.1 fusion.3._.mine
  22.6 1.4 %collective-permute-start.3 = (bf16[512,256]{1,0:T(8,128)(2,1)S(1)}, bf16[512,256]{1,0:T(8,128)(2,1)S(1)}, u32[]{:S(2)}, u32[]{:S(2)}) collective-permute-start(bf16[512,256]{1,0:T(8,128)(2,1)S(1)} %fusion.3._.mine), channel_id=1, source_target_pairs={{0,16},{4,12},{8,24},{12,4},{16,0},{20,28},{24,8},{28,20},{1,17},{... | collective-permute-start | bytes 786440 | tf_op jit(solution)/shard_map/ppermute | solution.py:351
  24.0 0.4 collective-permute-done.5.theirs
  24.4 1.2 %own_first.1 = (bf16[512,256]{1,0:T(8,128)(2,1)S(1)}, f32[512,256]{1,0:T(8,128)S(1)}, f32[1,128]{1,0:T(1,128)S(1)}) custom-call(s32[1]{0:T(128)} %bitcast.me_ref, bf16[512,256]{1,0:T(8,128)(2,1)S(1)} %combined.1.mine, bf16[512,256]{1,0:T(8,128)(2,1)S(1)} %collective-permute-done.5.theirs, bf16[2,512,1024]{2,1,0:T(8,128)(2,1)S(1)} %copy-done, ...), custom_call_target="tpu_custom_call" | custom-call | flops 1024 | bytes 1024 | tf_op jit(solution)/shard_map/own_first/pallas_call | solution.py:212
  25.6 2.1 %collective-permute-start.9 = (bf16[512,256]{1,0:T(8,128)(2,1)S(1)}, bf16[512,256]{1,0:T(8,128)(2,1)S(1)}, u32[]{:S(2)}, u32[]{:S(2)}) collective-permute-start(bf16[512,256]{1,0:T(8,128)(2,1)S(1)} %get-tuple-element.26.refs_0_), channel_id=1, source_target_pairs={{0,8},{4,20},{8,0},{12,28},{16,24},{20,4},{24,16},{28,12},{1,9},{5... | collective-permute-start | bytes 786440 | tf_op jit(solution)/shard_map/ppermute | solution.py:351
  27.6 2.3 %collective-permute-done.3.theirs = bf16[512,256]{1,0:T(8,128)(2,1)S(1)} collective-permute-done((bf16[512,256]{1,0:T(8,128)(2,1)S(1)}, bf16[512,256]{1,0:T(8,128)(2,1)S(1)}, u32[]{:S(2)}, u32[]{:S(2)}) %collective-permute-start.3) | collective-permute-done | bytes 262176 | tf_op jit(solution)/shard_map/ppermute | solution.py:351
  29.9 0.8 %own_second.1 = (bf16[512,256]{1,0:T(8,128)(2,1)S(1)}, f32[1,8,128]{2,1,0:T(8,128)S(1)}) custom-call(s32[1]{0:T(128)} %bitcast.me_ref, bf16[512,256]{1,0:T(8,128)(2,1)S(1)} %fusion.3._.mine, bf16[512,256]{1,0:T(8,128)(2,1)S(1)} %collective-permute-done.3.theirs, bf16[2,512,1024]{2,1,0:T(8,128)(2,1)S(1)} %copy-done, ...), custom_call_target="tpu_custom_call" | custom-call | flops 1024 | bytes 1024 | tf_op jit(solution)/shard_map/own_second/pallas_call | solution.py:246
  30.8 1.2 %collective-permute-start.12 = (f32[1,8,128]{2,1,0:T(8,128)S(1)}, f32[1,8,128]{2,1,0:T(8,128)S(1)}, u32[]{:S(2)}, u32[]{:S(2)}) collective-permute-start(f32[1,8,128]{2,1,0:T(8,128)S(1)} %get-tuple-element.28), channel_id=1, source_target_pairs={{0,1},{1,0},{2,3},{3,2},{4,5},{5,4},{6,7},{7,6},{8,9},{9,8},{10,11... | collective-permute-start | bytes 12296 | tf_op jit(solution)/shard_map/ppermute | solution.py:371
  32.0 0.9 %collective-permute-start.6 = (bf16[512,256]{1,0:T(8,128)(2,1)S(1)}, bf16[512,256]{1,0:T(8,128)(2,1)S(1)}, u32[]{:S(2)}, u32[]{:S(2)}) collective-permute-start(bf16[512,256]{1,0:T(8,128)(2,1)S(1)} %get-tuple-element.25.refs_0_), channel_id=1, source_target_pairs={{0,8},{4,20},{8,0},{12,28},{16,24},{20,4},{24,16},{28,12},{1,9},{5... | collective-permute-start | bytes 786440 | tf_op jit(solution)/shard_map/ppermute | solution.py:351
  32.9 0.8 %collective-permute-start.11 = (bf16[512,256]{1,0:T(8,128)(2,1)S(1)}, bf16[512,256]{1,0:T(8,128)(2,1)S(1)}, u32[]{:S(2)}, u32[]{:S(2)}) collective-permute-start(bf16[512,256]{1,0:T(8,128)(2,1)S(1)} %collective-permute-done.9.refs_1_), channel_id=1, source_target_pairs={{0,4},{4,0},{8,12},{12,8},{16,20},{20,16},{24,28},{28,24},{1,5},{5... | collective-permute-start | bytes 786440 | tf_op jit(solution)/shard_map/ppermute | solution.py:351
  33.7 0.7 %collective-permute-done.12 = f32[1,8,128]{2,1,0:T(8,128)S(1)} collective-permute-done((f32[1,8,128]{2,1,0:T(8,128)S(1)}, f32[1,8,128]{2,1,0:T(8,128)S(1)}, u32[]{:S(2)}, u32[]{:S(2)}) %collective-permute-start.12) | collective-permute-done | bytes 4128 | tf_op jit(solution)/shard_map/ppermute | solution.py:371
  34.4 2.2 %collective-permute-start.13 = (f32[2,8,128]{2,1,0:T(8,128)S(1)}, f32[2,8,128]{2,1,0:T(8,128)S(1)}, u32[]{:S(2)}, u32[]{:S(2)}) collective-permute-start(f32[2,8,128]{2,1,0:T(8,128)S(1)} %pad_maximum_fusion.2), channel_id=1, source_target_pairs={{0,2},{1,3},{2,0},{3,1},{4,6},{5,7},{6,4},{7,5},{8,10},{9,11},{10,... | collective-permute-start | bytes 24584 | tf_op jit(solution)/shard_map/ppermute | solution.py:371
  36.6 2.4 %collective-permute-done.13 = f32[2,8,128]{2,1,0:T(8,128)S(1)} collective-permute-done((f32[2,8,128]{2,1,0:T(8,128)S(1)}, f32[2,8,128]{2,1,0:T(8,128)S(1)}, u32[]{:S(2)}, u32[]{:S(2)}) %collective-permute-start.13) | collective-permute-done | bytes 8224 | tf_op jit(solution)/shard_map/ppermute | solution.py:371
  39.0 0.5 %collective-permute-start.14 = (f32[4,8,128]{2,1,0:T(8,128)S(1)}, f32[4,8,128]{2,1,0:T(8,128)S(1)}, u32[]{:S(2)}, u32[]{:S(2)}) collective-permute-start(f32[4,8,128]{2,1,0:T(8,128)S(1)} %pad_maximum_fusion.1), channel_id=1, source_target_pairs={{0,8},{4,20},{8,0},{12,28},{16,24},{20,4},{24,16},{28,12},{1,9},{5... | collective-permute-start | bytes 49160 | tf_op jit(solution)/shard_map/ppermute | solution.py:351
  39.5 3.2 %collective-permute-done.14 = f32[4,8,128]{2,1,0:T(8,128)S(1)} collective-permute-done((f32[4,8,128]{2,1,0:T(8,128)S(1)}, f32[4,8,128]{2,1,0:T(8,128)S(1)}, u32[]{:S(2)}, u32[]{:S(2)}) %collective-permute-start.14) | collective-permute-done | bytes 16416 | tf_op jit(solution)/shard_map/ppermute | solution.py:351
  42.7 1.2 %collective-permute-done.15 = f32[8,8,128]{2,1,0:T(8,128)S(1)} collective-permute-done((f32[8,8,128]{2,1,0:T(8,128)S(1)}, f32[8,8,128]{2,1,0:T(8,128)S(1)}, u32[]{:S(2)}, u32[]{:S(2)}) %collective-permute-start.15) | collective-permute-done | bytes 32800 | tf_op jit(solution)/shard_map/ppermute | solution.py:351
  44.0 2.1 %finish_first.1 = (bf16[1024,1024]{1,0:T(8,128)(2,1)}, f32[4,512,256]{2,1,0:T(8,128)S(1)}) custom-call(s32[1]{0:T(128)} %bitcast.me_ref, bf16[512,256]{1,0:T(8,128)(2,1)S(1)} %get-tuple-element.26.refs_0_, bf16[512,256]{1,0:T(8,128)(2,1)S(1)} %collective-permute-done.9.refs_1_, bf16[512,256]{1,0:T(8,128)(2,1)S(1)} %collective-permute-done.10.refs_2_, ...), custom_call_target="tpu_custom_call" | custom-call | flops 1024 | bytes 1024 | tf_op jit(solution)/shard_map/finish_first/pallas_call | solution.py:274
  46.1 2.9 %finish_second.1 = (bf16[1024,1024]{1,0:T(8,128)(2,1)}, bf16[1024,1024]{1,0:T(8,128)(2,1)}) custom-call(s32[1]{0:T(128)} %bitcast.me_ref, bf16[512,256]{1,0:T(8,128)(2,1)S(1)} %get-tuple-element.25.refs_0_, bf16[512,256]{1,0:T(8,128)(2,1)S(1)} %collective-permute-done.6.refs_1_, ...), custom_call_target="tpu_custom_call", output_to_operand_aliasing={{0}: (9, {})} | custom-call | flops 1024 | bytes 1024 | tf_op jit(solution)/shard_map/finish_second/pallas_call | solution.py:325
  (26 shorter events, 0.1 us)
Async XLA Ops:
  3.4 4.2 %collective-permute-start = (bf16[2,512,256]{2,1,0:T(8,128)(2,1)S(1)}, bf16[2,512,256]{2,1,0:T(8,128)(2,1)S(1)}, u32[]{:S(2)}, u32[]{:S(2)}) collective-permute-start(bf16[2,512,256]{2,1,0:T(8,128)(2,1)S(1)} %get-tuple-element.19), channel_id=1, source_target_pairs={{0,4},{4,0},{8,12},{12,8},{16,20},{20,16},{24,28},{28,24},{1,5},{5... | collective-permute-start | bytes 1572872 | tf_op jit(solution)/shard_map/ppermute | solution.py:351
  10.4 4.4 %collective-permute-start.1 = (bf16[2,512,256]{2,1,0:T(8,128)(2,1)S(1)}, bf16[2,512,256]{2,1,0:T(8,128)(2,1)S(1)}, u32[]{:S(2)}, u32[]{:S(2)}) collective-permute-start(bf16[2,512,256]{2,1,0:T(8,128)(2,1)S(1)} %get-tuple-element.22), channel_id=1, source_target_pairs={{0,4},{4,0},{8,12},{12,8},{16,20},{20,16},{24,28},{28,24},{1,5},{5... | collective-permute-start | bytes 1572872 | tf_op jit(solution)/shard_map/ppermute | solution.py:351
  10.5 7.3 %collective-permute-start.4 = (bf16[512,256]{1,0:T(8,128)(2,1)S(1)}, bf16[512,256]{1,0:T(8,128)(2,1)S(1)}, u32[]{:S(2)}, u32[]{:S(2)}) collective-permute-start(bf16[512,256]{1,0:T(8,128)(2,1)S(1)} %fusion.4.refs_0_), channel_id=1, source_target_pairs={{0,8},{4,20},{8,0},{12,28},{16,24},{20,4},{24,16},{28,12},{1,9},{5... | collective-permute-start | bytes 786440 | tf_op jit(solution)/shard_map/ppermute | solution.py:351
  14.9 9.5 %copy-start = (bf16[2,512,1024]{2,1,0:T(8,128)(2,1)S(1)}, bf16[2,512,1024]{2,1,0:T(8,128)(2,1)}, u32[]{:S(2)}) copy-start(bf16[2,512,1024]{2,1,0:T(8,128)(2,1)} %refs_4_.3) | copy-start | bytes 6291460
  14.9 9.5 %copy-start.1 = (bf16[512,1024]{1,0:T(8,128)(2,1)S(1)}, bf16[512,1024]{1,0:T(8,128)(2,1)}, u32[]{:S(2)}) copy-start(bf16[512,1024]{1,0:T(8,128)(2,1)} %refs_5_.1) | copy-start | bytes 3145732
  14.9 9.5 %copy-start.2 = (f32[32,1024]{1,0:T(8,128)S(1)}, f32[32,1024]{1,0:T(8,128)}, u32[]{:S(2)}) copy-start(f32[32,1024]{1,0:T(8,128)} %refs_7_.1) | copy-start | bytes 393220
  14.9 7.6 %collective-permute-start.2 = (bf16[512,256]{1,0:T(8,128)(2,1)S(1)}, bf16[512,256]{1,0:T(8,128)(2,1)S(1)}, u32[]{:S(2)}, u32[]{:S(2)}) collective-permute-start(bf16[512,256]{1,0:T(8,128)(2,1)S(1)} %fusion.5._), channel_id=1, source_target_pairs={{0,8},{4,20},{8,0},{12,28},{16,24},{20,4},{24,16},{28,12},{1,9},{5... | collective-permute-start | bytes 786440 | tf_op jit(solution)/shard_map/ppermute | solution.py:351
  17.9 6.5 %collective-permute-start.5 = (bf16[512,256]{1,0:T(8,128)(2,1)S(1)}, bf16[512,256]{1,0:T(8,128)(2,1)S(1)}, u32[]{:S(2)}, u32[]{:S(2)}) collective-permute-start(bf16[512,256]{1,0:T(8,128)(2,1)S(1)} %combined.1.mine), channel_id=1, source_target_pairs={{0,16},{4,12},{8,24},{12,4},{16,0},{20,28},{24,8},{28,20},{1,17},{... | collective-permute-start | bytes 786440 | tf_op jit(solution)/shard_map/ppermute | solution.py:351
  22.6 7.3 %collective-permute-start.3 = (bf16[512,256]{1,0:T(8,128)(2,1)S(1)}, bf16[512,256]{1,0:T(8,128)(2,1)S(1)}, u32[]{:S(2)}, u32[]{:S(2)}) collective-permute-start(bf16[512,256]{1,0:T(8,128)(2,1)S(1)} %fusion.3._.mine), channel_id=1, source_target_pairs={{0,16},{4,12},{8,24},{12,4},{16,0},{20,28},{24,8},{28,20},{1,17},{... | collective-permute-start | bytes 786440 | tf_op jit(solution)/shard_map/ppermute | solution.py:351
  25.6 7.4 %collective-permute-start.9 = (bf16[512,256]{1,0:T(8,128)(2,1)S(1)}, bf16[512,256]{1,0:T(8,128)(2,1)S(1)}, u32[]{:S(2)}, u32[]{:S(2)}) collective-permute-start(bf16[512,256]{1,0:T(8,128)(2,1)S(1)} %get-tuple-element.26.refs_0_), channel_id=1, source_target_pairs={{0,8},{4,20},{8,0},{12,28},{16,24},{20,4},{24,16},{28,12},{1,9},{5... | collective-permute-start | bytes 786440 | tf_op jit(solution)/shard_map/ppermute | solution.py:351
  27.6 16.3 %collective-permute-start.10 = (bf16[512,256]{1,0:T(8,128)(2,1)S(1)}, bf16[512,256]{1,0:T(8,128)(2,1)S(1)}, u32[]{:S(2)}, u32[]{:S(2)}) collective-permute-start(bf16[512,256]{1,0:T(8,128)(2,1)S(1)} %get-tuple-element.26.refs_0_), channel_id=1, source_target_pairs={{0,4},{4,0},{8,12},{12,8},{16,20},{20,16},{24,28},{28,24},{1,5},{5... | collective-permute-start | bytes 786440 | tf_op jit(solution)/shard_map/ppermute | solution.py:351
  30.8 3.7 %collective-permute-start.12 = (f32[1,8,128]{2,1,0:T(8,128)S(1)}, f32[1,8,128]{2,1,0:T(8,128)S(1)}, u32[]{:S(2)}, u32[]{:S(2)}) collective-permute-start(f32[1,8,128]{2,1,0:T(8,128)S(1)} %get-tuple-element.28), channel_id=1, source_target_pairs={{0,1},{1,0},{2,3},{3,2},{4,5},{5,4},{6,7},{7,6},{8,9},{9,8},{10,11... | collective-permute-start | bytes 12296 | tf_op jit(solution)/shard_map/ppermute | solution.py:371
  32.0 14.1 %collective-permute-start.7 = (bf16[512,256]{1,0:T(8,128)(2,1)S(1)}, bf16[512,256]{1,0:T(8,128)(2,1)S(1)}, u32[]{:S(2)}, u32[]{:S(2)}) collective-permute-start(bf16[512,256]{1,0:T(8,128)(2,1)S(1)} %get-tuple-element.25.refs_0_), channel_id=1, source_target_pairs={{0,4},{4,0},{8,12},{12,8},{16,20},{20,16},{24,28},{28,24},{1,5},{5... | collective-permute-start | bytes 786440 | tf_op jit(solution)/shard_map/ppermute | solution.py:351
  32.0 7.5 %collective-permute-start.6 = (bf16[512,256]{1,0:T(8,128)(2,1)S(1)}, bf16[512,256]{1,0:T(8,128)(2,1)S(1)}, u32[]{:S(2)}, u32[]{:S(2)}) collective-permute-start(bf16[512,256]{1,0:T(8,128)(2,1)S(1)} %get-tuple-element.25.refs_0_), channel_id=1, source_target_pairs={{0,8},{4,20},{8,0},{12,28},{16,24},{20,4},{24,16},{28,12},{1,9},{5... | collective-permute-start | bytes 786440 | tf_op jit(solution)/shard_map/ppermute | solution.py:351
  32.9 11.0 %collective-permute-start.11 = (bf16[512,256]{1,0:T(8,128)(2,1)S(1)}, bf16[512,256]{1,0:T(8,128)(2,1)S(1)}, u32[]{:S(2)}, u32[]{:S(2)}) collective-permute-start(bf16[512,256]{1,0:T(8,128)(2,1)S(1)} %collective-permute-done.9.refs_1_), channel_id=1, source_target_pairs={{0,4},{4,0},{8,12},{12,8},{16,20},{20,16},{24,28},{28,24},{1,5},{5... | collective-permute-start | bytes 786440 | tf_op jit(solution)/shard_map/ppermute | solution.py:351
  34.4 4.5 %collective-permute-start.13 = (f32[2,8,128]{2,1,0:T(8,128)S(1)}, f32[2,8,128]{2,1,0:T(8,128)S(1)}, u32[]{:S(2)}, u32[]{:S(2)}) collective-permute-start(f32[2,8,128]{2,1,0:T(8,128)S(1)} %pad_maximum_fusion.2), channel_id=1, source_target_pairs={{0,2},{1,3},{2,0},{3,1},{4,6},{5,7},{6,4},{7,5},{8,10},{9,11},{10,... | collective-permute-start | bytes 24584 | tf_op jit(solution)/shard_map/ppermute | solution.py:371
  39.0 3.7 %collective-permute-start.14 = (f32[4,8,128]{2,1,0:T(8,128)S(1)}, f32[4,8,128]{2,1,0:T(8,128)S(1)}, u32[]{:S(2)}, u32[]{:S(2)}) collective-permute-start(f32[4,8,128]{2,1,0:T(8,128)S(1)} %pad_maximum_fusion.1), channel_id=1, source_target_pairs={{0,8},{4,20},{8,0},{12,28},{16,24},{20,4},{24,16},{28,12},{1,9},{5... | collective-permute-start | bytes 49160 | tf_op jit(solution)/shard_map/ppermute | solution.py:351
  39.5 6.6 %collective-permute-start.8 = (bf16[512,256]{1,0:T(8,128)(2,1)S(1)}, bf16[512,256]{1,0:T(8,128)(2,1)S(1)}, u32[]{:S(2)}, u32[]{:S(2)}) collective-permute-start(bf16[512,256]{1,0:T(8,128)(2,1)S(1)} %collective-permute-done.6.refs_1_), channel_id=1, source_target_pairs={{0,4},{4,0},{8,12},{12,8},{16,20},{20,16},{24,28},{28,24},{1,5},{5... | collective-permute-start | bytes 786440 | tf_op jit(solution)/shard_map/ppermute | solution.py:351
  42.7 1.2 %collective-permute-start.15 = (f32[8,8,128]{2,1,0:T(8,128)S(1)}, f32[8,8,128]{2,1,0:T(8,128)S(1)}, u32[]{:S(2)}, u32[]{:S(2)}) collective-permute-start(f32[8,8,128]{2,1,0:T(8,128)S(1)} %pad_maximum_fusion), channel_id=1, source_target_pairs={{0,4},{4,0},{8,12},{12,8},{16,20},{20,16},{24,28},{28,24},{1,5},{5... | collective-permute-start | bytes 98312 | tf_op jit(solution)/shard_map/ppermute | solution.py:351

commit v7 on v6

--- a/solution.py
+++ b/solution.py
@@ -64,7 +64,6 @@
     depth = g.shape[0]
     quarter = half // 2
     dtype = BF16 if send else F32
-    pieces = 4 if load_sigma and load_g else 2
     out_shape = [near((2, rows, quarter), dtype)]
     if load_sigma:
         out_shape.append(near((rows, depth), BF16))
@@ -86,59 +85,56 @@
         def put(j, value):
             out[1 ^ j ^ side] = value.astype(dtype)
 
-        if load_sigma and load_g:
-            chunk = depth // pieces
+        started = []
+
+        def load(source, target, row, column, at, where):
+            part = at[0].size // 4
             copies = []
-            for k in range(pieces):
-                at = pl.ds(k * chunk, chunk)
+            for i in range(4):
+                into = pl.ds(at[0].start + i * part, part)
+                from_rows = pl.ds(row + at[0].start + i * part, part)
+                from_columns = pl.ds(column + at[1].start, at[1].size) if where is None else where
                 copies.append(
-                    (
-                        pltpu.make_async_copy(
-                            sigma_ref.at[pl.ds(block * rows, rows), at], sigma_v.at[:, at], sems.at[2 * k]
-                        ),
-                        pltpu.make_async_copy(g_ref.at[at, pl.ds(first, half)], g_v.at[at, :], sems.at[2 * k + 1]),
+                    pltpu.make_async_copy(
+                        source.at[from_rows, from_columns], target.at[into, at[1]], sems.at[len(started)]
                     )
                 )
-            for pair in copies:
-                for copy in pair:
-                    copy.start()
-            for k in range(pieces):
-                for copy in copies[k]:
+                copies[-1].start()
+                started.append(copies[-1])
+            return copies
+
+        chunk = depth // 4
+        if load_g:
+            pieces = []
+            for k in range(4):
+                deep = pl.ds(k * chunk, chunk)
+                piece = []
+                if load_sigma:
+                    piece += load(sigma_ref, sigma_v, block * rows, 0, (pl.ds(0, rows), deep), None)
+                piece += load(g_ref, g_v, 0, 0, (deep, pl.ds(0, half)), pl.ds(first, half))
+                pieces.append(piece)
+            for k, piece in enumerate(pieces):
+                for copy in piece:
                     copy.wait()
-                at = pl.ds(k * chunk, chunk)
-                term = jnp.dot(sigma_v[:, at], g_v[at, :], preferred_element_type=F32)
+                deep = pl.ds(k * chunk, chunk)
+                term = jnp.dot(sigma_v[:, deep], g_v[deep, :], preferred_element_type=F32)
                 if k == 0:
                     total[...] = term
-                elif k < pieces - 1:
+                elif k < 3:
                     total[...] += term
                 else:
                     term += total[...]
                     for j in range(2):
                         put(j, term[:, j * quarter : (j + 1) * quarter])
-        elif load_g:
-            copies = [
-                pltpu.make_async_copy(
-                    g_ref.at[:, pl.ds(first + j * quarter, quarter)], g_v.at[:, pl.ds(j * quarter, quarter)], sems.at[j]
-                )
-                for j in range(2)
-            ]
-            for copy in copies:
-                copy.start()
-            for j in range(2):
-                copies[j].wait()
-                put(j, jnp.dot(sigma_v[...], g_v[:, pl.ds(j * quarter, quarter)], preferred_element_type=F32))
         elif load_sigma:
             tall = rows // 2
-            copies = [
-                pltpu.make_async_copy(
-                    sigma_ref.at[pl.ds(block * rows + i * tall, tall), :], sigma_v.at[pl.ds(i * tall, tall), :], sems.at[i]
-                )
+            pieces = [
+                load(sigma_ref, sigma_v, block * rows, 0, (pl.ds(i * tall, tall), pl.ds(0, depth)), None)
                 for i in range(2)
             ]
-            for copy in copies:
-                copy.start()
-            for i in range(2):
-                copies[i].wait()
+            for i, piece in enumerate(pieces):
+                for copy in piece:
+                    copy.wait()
                 here = pl.ds(i * tall, tall)
                 term = jnp.dot(sigma_v[here, :], g_v[...], preferred_element_type=F32).astype(dtype)
                 for j in range(2):
@@ -154,7 +150,7 @@
         in_specs=[SCALAR, HBM if load_sigma else WHOLE, HBM if load_g else WHOLE] + [FAR] * (after is not None),
         out_specs=[WHOLE] * len(out_shape),
         out_shape=out_shape,
-        scratch_shapes=[pltpu.VMEM((rows, half), F32), pltpu.SemaphoreType.DMA((2 * pieces,))],
+        scratch_shapes=[pltpu.VMEM((rows, half), F32), pltpu.SemaphoreType.DMA((32,))],
     )(me, far(sigma) if load_sigma else sigma, far(g) if load_g else g, *([] if after is None else [after]))
 
 
@@ -284,14 +280,52 @@
     )(me, *pieces, volterra, edge, coupling)
 
 
-def finish_second(me, pieces, volterra, cubic, shares, coupling, g_first, bits):
+def memory_terms(pieces, volterra):
     rows, width = pieces[0].shape
+    count = len(pieces)
+
+    def kernel(*refs):
+        pieces, (w, out) = refs[:count], refs[count:]
+        for slot in range(count):
+            out[slot] = jnp.dot(w[1, :, :rows], pieces[slot][...], preferred_element_type=F32)
+
+    return call(
+        kernel,
+        "memory_terms",
+        in_specs=[WHOLE] * (count + 1),
+        out_specs=WHOLE,
+        out_shape=near((count, rows, width), F32),
+    )(*pieces, volterra)
+
+
+def joined(a, b, *after):
+    size = a.shape[0]
+
+    def kernel(a, b, *refs):
+        out = refs[-1]
+        out[:size] = a[...]
+        out[size:] = b[...]
+
+    shape = (2 * size,) + a.shape[1:]
+    in_specs = [WHOLE] * 2 + [FAR] * len(after)
+    return call(kernel, "joined", in_specs=in_specs, out_specs=WHOLE, out_shape=near(shape, F32))(a, b, *after)
+
+
+def ordered(x, after):
+    def kernel(x, _, out):
+        out[...] = x[...]
+
+    return call(kernel, "ordered", in_specs=[WHOLE, FAR], out_specs=WHOLE, out_shape=near(x.shape, x.dtype))(x, after)
+
+
+def finish_second(me, last, terms, volterra, cubic, shares, coupling, g_first, bits):
+    rows, width = last.shape
     columns = coupling.shape[1]
     everyone = shares.shape[0]
 
-    def kernel(me_ref, *refs):
-        pieces, (w, cubic, shares, coupling, _, g_out, sigma, g_held, s_held, sems) = refs[:4], refs[4:]
+    def kernel(me_ref, last, terms, w, cubic, shares, coupling, _, g_out, sigma, g_held, s_held, sems):
         place = Place(me_ref[0], bits)
+        last_term = jnp.dot(w[1, :, :rows], last[...], preferred_element_type=F32)
         sums = jnp.sum(shares[...], axis=2, keepdims=True)
         means = sums[:, 0:1, :]
         mean = jnp.sum(over_halves(means)) / everyone
@@ -311,11 +345,11 @@
             copies.append(pltpu.make_async_copy(held.at[slot], out.at[pl.ds(block * rows, rows), at], sem))
             copies[-1].start()
 
-        for slot in range(4):
+        for slot in (3, 0, 1, 2):
             at = columns_of(place.quarter_of(slot), width)
             before = (cubic[slot] * scale_0).astype(BF16)
             write(before, s_held, slot, sigma, 0, at)
-            g = jnp.dot(w[1, :, :rows], pieces[slot][...], preferred_element_type=F32)
+            g = last_term if slot == 3 else terms[slot]
             g += jnp.dot(w[1, :, rows:], before, preferred_element_type=F32)
             write(g.astype(BF16), g_held, slot, g_out, 1, at)
             write((cubed(g, coupling[:, at]) * scale_1).astype(BF16), s_held, 4 + slot, sigma, 1, at)
@@ -325,7 +359,7 @@
     return call(
         kernel,
         "finish_second",
-        in_specs=[SCALAR] + [WHOLE] * 8 + [HBM],
+        in_specs=[SCALAR] + [WHOLE] * 6 + [HBM],
         out_specs=[HBM, HBM],
         out_shape=[jax.ShapeDtypeStruct((2 * rows, columns), BF16)] * 2,
         scratch_shapes=[
@@ -333,8 +367,8 @@
             pltpu.VMEM((8, rows, width), BF16),
             pltpu.SemaphoreType.DMA((12,)),
         ],
-        input_output_aliases={9: 0},
-    )(me, *pieces, volterra, cubic, shares, coupling, g_first)
+        input_output_aliases={7: 0},
+    )(me, last, terms, volterra, cubic, shares, coupling, g_first)
 
 
 def per_device(past, second, g_hist, sigma_hist, volterra, sigma_edge, coupling):
@@ -361,17 +395,8 @@
     def passed_on(kept, arrived):
         return (kept[0] + arrived[0].astype(F32)).astype(BF16)
 
-    def gathered(own):
-        partner = swap(own, 1)
-        return [own, partner, swap(own, 0), swap(partner, 0)]
-
-    def shared(share):
-        for level in range(log2(second)):
-            pairs = [(z, z ^ (1 << level)) for z in range(second)]
-            share = jnp.concatenate([share, lax.ppermute(share, "second", pairs)], axis=0)
-        for level in (1, 0):
-            share = jnp.concatenate([share, swap(share, level)], axis=0)
-        return share
+    def widened(share, level):
+        return lax.ppermute(share, "second", [(z, z ^ (1 << level)) for z in range(second)])
 
     send, sigma_0, g_send = product(me, sigma_hist, g_hist, 0, rows, half, bits, True)
     arrived_0 = swap(send, 0)
@@ -386,11 +411,19 @@
     mine_1, theirs_1 = exchanged(kept_1, arrived_1, sent_1)
     own_0, response, squares = own_first(me, mine, theirs, volterra, sigma_edge, coupling, bits, after=mine_1)
     own_1, share = own_second(me, mine_1, theirs_1, volterra, response, squares, coupling, bits)
-    shares = shared(share)
-
-    g_first, cubic = finish_first(me, gathered(own_0), volterra, sigma_edge, coupling, bits)
-    pieces = gathered(own_1)
-    return tuple(finish_second(me, pieces, volterra, cubic, shares, coupling, g_first, bits))
+    rounds = log2(second)
+    share = jnp.concatenate([share, widened(share, 0)])
+    partner = ordered(swap(own_0, 1), share)
+    pieces = [own_0, partner, swap(own_0, 0), swap(partner, 0)]
+    g_first, cubic = finish_first(me, pieces, volterra, sigma_edge, coupling, bits)
+    for level in range(1, rounds):
+        share = jnp.concatenate([share, widened(share, level)])
+    partner = ordered(swap(own_1, 1), share)
+    terms = memory_terms([own_1, partner, swap(own_1, 0)], volterra)
+    last = swap(partner, 0)
+    share = joined(share, swap(share, 1), cubic, terms)
+    shares = jnp.concatenate([share, swap(share, 0)])
+    return tuple(finish_second(me, last, terms, volterra, cubic, shares, coupling, g_first, bits))
 
 
 def solution(mesh):

time: 49.2 us -> 47.6 us (0.967)
  starting transfers between devices: 15 us -> 12.9 us
    ppermute x14, starting transfers between devices: 11.6 us -> 9.68 us  [swap(): return lax.ppermute(x, 'past', pairs)]
    ppermute x2, waiting for transfers between devices: 3.11 us -> 4.88 us  [widened(): lax.ppermute(share, 'second', [(z, z ^ 1 << level) for z in range(second)])]
    ppermute x14, waiting for transfers between devices: 12.3 us -> 10.7 us  [swap(): return lax.ppermute(x, 'past', pairs)]
    pallas_call x1 -> x5, Pallas kernels: 2.88 us -> 3.27 us  [the longest x1 2.65 us: finish_second(): call(kernel, 'finish_second', in_specs=[SCALAR] + [WHOLE] * 6 + [HBM], ou...]
  transfers between devices with their start and end apart: 16 -> 16, of which waited for: 8 -> 7; matrix products, arithmetic and copies ran while one was open for 0% -> 0% of each run, Pallas kernels for 19% -> 19%
where the time goes in v7:
time: 47.6 us; the launch traced here: 47.5 us
  Pallas kernels  17.8 us (37%)
  waiting for transfers between devices  15.6 us (33%)
  starting transfers between devices  12.9 us (27%)
  between operations  0.84 us (2%)
    ppermute x14, waiting for transfers between devices, swap(): return lax.ppermute(x, 'past', pairs)  10.7 us
    pallas_call x4, Pallas kernels, product(): call(kernel, 'memory_product', in_specs=[SCALAR, HBM if load_sigma else W...  10.3 us
    ppermute x14, starting transfers between devices, swap(): return lax.ppermute(x, 'past', pairs)  9.68 us
    ppermute x2, waiting for transfers between devices, widened(): lax.ppermute(share, 'second', [(z, z ^ 1 << level) for z in range(second)])  4.88 us
    ppermute x2, starting transfers between devices, widened(): lax.ppermute(share, 'second', [(z, z ^ 1 << level) for z in range(second)])  3.27 us
    pallas_call x1, Pallas kernels, finish_second(): call(kernel, 'finish_second', in_specs=[SCALAR] + [WHOLE] * 6 + [HBM], ou...  2.65 us
    pallas_call x1, Pallas kernels, finish_first(): call(kernel, 'finish_first', in_specs=[SCALAR] + [WHOLE] * 7, out_specs=[...  2.15 us
    pallas_call x1, Pallas kernels, own_first(): call(kernel, 'own_first', in_specs=[SCALAR] + [WHOLE] * 5 + [FAR], out_sp...  1.16 us
  transfers between devices with their start and end apart: 16, of which 7 were waited for; matrix products, arithmetic and copies ran while one was open for 0% of the time, Pallas kernels for 19%

profile of v7, /device:TPU:0, one launch (start us, length us, event | category | flops | bytes accessed | tf_op | source)
XLA Modules:
  0.0 47.5 jit_solution(16230722357742152284)
XLA Ops:
  0.6 3.0 %memory_product.4 = (bf16[2,512,256]{2,1,0:T(8,128)(2,1)S(1)}, bf16[512,2048]{1,0:T(8,128)(2,1)S(1)}, bf16[2048,512]{1,0:T(8,128)(2,1)S(1)}) custom-call(s32[1]{0:T(128)} %bitcast.me_ref, bf16[1024,2048]{1,0:T(8,128)(2,1)} %sigma_ref.3, bf16[2048,1024]{1,0:T(8,128)(2,1)} %g_ref.3), custom_call_target="tpu_custom_call" | custom-call | flops 1024 | bytes 1024 | tf_op jit(solution)/shard_map/memory_product/pallas_call | solution.py:147
  3.7 0.5 %collective-permute-start = (bf16[2,512,256]{2,1,0:T(8,128)(2,1)S(1)}, bf16[2,512,256]{2,1,0:T(8,128)(2,1)S(1)}, u32[]{:S(2)}, u32[]{:S(2)}) collective-permute-start(bf16[2,512,256]{2,1,0:T(8,128)(2,1)S(1)} %get-tuple-element.19), channel_id=1, source_target_pairs={{0,4},{4,0},{8,12},{12,8},{16,20},{20,16},{24,28},{28,24},{1,5},{5... | collective-permute-start | bytes 1572872 | tf_op jit(solution)/shard_map/ppermute | solution.py:385
  4.2 2.8 %memory_product.5 = (f32[2,512,256]{2,1,0:T(8,128)S(1)}, bf16[2048,512]{1,0:T(8,128)(2,1)S(1)}) custom-call(s32[1]{0:T(128)} %bitcast.me_ref, bf16[512,2048]{1,0:T(8,128)(2,1)S(1)} %get-tuple-element.17.sigma_ref, bf16[2048,1024]{1,0:T(8,128)(2,1)} %g_ref.3), custom_call_target="tpu_custom_call" | custom-call | flops 1024 | bytes 1024 | tf_op jit(solution)/shard_map/memory_product/pallas_call | solution.py:147
  7.1 2.9 %memory_product.6 = (bf16[2,512,256]{2,1,0:T(8,128)(2,1)S(1)}, bf16[512,2048]{1,0:T(8,128)(2,1)S(1)}) custom-call(s32[1]{0:T(128)} %bitcast.me_ref, bf16[1024,2048]{1,0:T(8,128)(2,1)} %sigma_ref.3, bf16[2048,512]{1,0:T(8,128)(2,1)S(1)} %get-tuple-element.16.g_ref, bf16[512,256]{1,0:T(8,128)(2,1)S(1)} %fusion.4.refs_0_), custom_call_target="tpu_custom_call" | custom-call | flops 1024 | bytes 1024 | tf_op jit(solution)/shard_map/memory_product/pallas_call | solution.py:147
  10.0 0.1 collective-permute-start.1
  10.2 2.9 %collective-permute-start.4 = (bf16[512,256]{1,0:T(8,128)(2,1)S(1)}, bf16[512,256]{1,0:T(8,128)(2,1)S(1)}, u32[]{:S(2)}, u32[]{:S(2)}) collective-permute-start(bf16[512,256]{1,0:T(8,128)(2,1)S(1)} %fusion.4.refs_0_), channel_id=1, source_target_pairs={{0,8},{4,20},{8,0},{12,28},{16,24},{20,4},{24,16},{28,12},{1,9},{5... | collective-permute-start | bytes 786440 | tf_op jit(solution)/shard_map/ppermute | solution.py:385
  13.1 1.6 %memory_product.7 = f32[2,512,256]{2,1,0:T(8,128)S(1)} custom-call(s32[1]{0:T(128)} %bitcast.me_ref, bf16[512,2048]{1,0:T(8,128)(2,1)S(1)} %get-tuple-element.20.sigma_ref, bf16[2048,512]{1,0:T(8,128)(2,1)S(1)} %get-tuple-element.21.g_ref), custom_call_target="tpu_custom_call" | custom-call | flops 1024 | bytes 1024 | tf_op jit(solution)/shard_map/memory_product/pallas_call | solution.py:147
  14.8 0.1 collective-permute-start.2
  14.9 2.6 %collective-permute-done.4.more = bf16[512,256]{1,0:T(8,128)(2,1)S(1)} collective-permute-done((bf16[512,256]{1,0:T(8,128)(2,1)S(1)}, bf16[512,256]{1,0:T(8,128)(2,1)S(1)}, u32[]{:S(2)}, u32[]{:S(2)}) %collective-permute-start.4) | collective-permute-done | bytes 262176 | tf_op jit(solution)/shard_map/ppermute | solution.py:385
  17.4 0.1 combined.1.mine
  17.5 2.1 %collective-permute-start.5 = (bf16[512,256]{1,0:T(8,128)(2,1)S(1)}, bf16[512,256]{1,0:T(8,128)(2,1)S(1)}, u32[]{:S(2)}, u32[]{:S(2)}) collective-permute-start(bf16[512,256]{1,0:T(8,128)(2,1)S(1)} %combined.1.mine), channel_id=1, source_target_pairs={{0,16},{4,12},{8,24},{12,4},{16,0},{20,28},{24,8},{28,20},{1,17},{... | collective-permute-start | bytes 786440 | tf_op jit(solution)/shard_map/ppermute | solution.py:385
  19.6 3.0 %collective-permute-done.2 = bf16[512,256]{1,0:T(8,128)(2,1)S(1)} collective-permute-done((bf16[512,256]{1,0:T(8,128)(2,1)S(1)}, bf16[512,256]{1,0:T(8,128)(2,1)S(1)}, u32[]{:S(2)}, u32[]{:S(2)}) %collective-permute-start.2) | collective-permute-done | bytes 262176 | tf_op jit(solution)/shard_map/ppermute | solution.py:385
  22.7 0.1 fusion.3._.mine
  22.8 1.3 %collective-permute-start.3 = (bf16[512,256]{1,0:T(8,128)(2,1)S(1)}, bf16[512,256]{1,0:T(8,128)(2,1)S(1)}, u32[]{:S(2)}, u32[]{:S(2)}) collective-permute-start(bf16[512,256]{1,0:T(8,128)(2,1)S(1)} %fusion.3._.mine), channel_id=1, source_target_pairs={{0,16},{4,12},{8,24},{12,4},{16,0},{20,28},{24,8},{28,20},{1,17},{... | collective-permute-start | bytes 786440 | tf_op jit(solution)/shard_map/ppermute | solution.py:385
  24.1 1.2 %own_first.1 = (bf16[512,256]{1,0:T(8,128)(2,1)S(1)}, f32[512,256]{1,0:T(8,128)S(1)}, f32[1,128]{1,0:T(1,128)S(1)}) custom-call(s32[1]{0:T(128)} %bitcast.me_ref, bf16[512,256]{1,0:T(8,128)(2,1)S(1)} %combined.1.mine, bf16[512,256]{1,0:T(8,128)(2,1)S(1)} %collective-permute-done.5.theirs, bf16[2,512,1024]{2,1,0:T(8,128)(2,1)S(1)} %copy-done, ...), custom_call_target="tpu_custom_call" | custom-call | flops 1024 | bytes 1024 | tf_op jit(solution)/shard_map/own_first/pallas_call | solution.py:208
  25.3 1.9 %collective-permute-start.11 = (bf16[512,256]{1,0:T(8,128)(2,1)S(1)}, bf16[512,256]{1,0:T(8,128)(2,1)S(1)}, u32[]{:S(2)}, u32[]{:S(2)}) collective-permute-start(bf16[512,256]{1,0:T(8,128)(2,1)S(1)} %get-tuple-element.27.refs_0_), channel_id=1, source_target_pairs={{0,8},{4,20},{8,0},{12,28},{16,24},{20,4},{24,16},{28,12},{1,9},{5... | collective-permute-start | bytes 786440 | tf_op jit(solution)/shard_map/ppermute | solution.py:385
  27.2 3.1 %collective-permute-done.3.theirs = bf16[512,256]{1,0:T(8,128)(2,1)S(1)} collective-permute-done((bf16[512,256]{1,0:T(8,128)(2,1)S(1)}, bf16[512,256]{1,0:T(8,128)(2,1)S(1)}, u32[]{:S(2)}, u32[]{:S(2)}) %collective-permute-start.3) | collective-permute-done | bytes 262176 | tf_op jit(solution)/shard_map/ppermute | solution.py:385
  30.4 0.8 %own_second.1 = (bf16[512,256]{1,0:T(8,128)(2,1)S(1)}, f32[1,8,128]{2,1,0:T(8,128)S(1)}) custom-call(s32[1]{0:T(128)} %bitcast.me_ref, bf16[512,256]{1,0:T(8,128)(2,1)S(1)} %fusion.3._.mine, bf16[512,256]{1,0:T(8,128)(2,1)S(1)} %collective-permute-done.3.theirs, bf16[2,512,1024]{2,1,0:T(8,128)(2,1)S(1)} %copy-done, ...), custom_call_target="tpu_custom_call" | custom-call | flops 1024 | bytes 1024 | tf_op jit(solution)/shard_map/own_second/pallas_call | solution.py:242
  31.2 1.1 %collective-permute-start.7 = (f32[1,8,128]{2,1,0:T(8,128)S(1)}, f32[1,8,128]{2,1,0:T(8,128)S(1)}, u32[]{:S(2)}, u32[]{:S(2)}) collective-permute-start(f32[1,8,128]{2,1,0:T(8,128)S(1)} %get-tuple-element.26), channel_id=1, source_target_pairs={{0,1},{1,0},{2,3},{3,2},{4,5},{5,4},{6,7},{7,6},{8,9},{9,8},{10,11... | collective-permute-start | bytes 12296 | tf_op jit(solution)/shard_map/ppermute | solution.py:399
  32.3 0.2 collective-permute-start.6
  32.5 2.3 %collective-permute-done.7 = f32[1,8,128]{2,1,0:T(8,128)S(1)} collective-permute-done((f32[1,8,128]{2,1,0:T(8,128)S(1)}, f32[1,8,128]{2,1,0:T(8,128)S(1)}, u32[]{:S(2)}, u32[]{:S(2)}) %collective-permute-start.7) | collective-permute-done | bytes 4128 | tf_op jit(solution)/shard_map/ppermute | solution.py:399
  34.9 0.1 collective-permute-start.13
  35.0 2.1 %collective-permute-start.8 = (f32[2,8,128]{2,1,0:T(8,128)S(1)}, f32[2,8,128]{2,1,0:T(8,128)S(1)}, u32[]{:S(2)}, u32[]{:S(2)}) collective-permute-start(f32[2,8,128]{2,1,0:T(8,128)S(1)} %get-tuple-element.30._), channel_id=1, source_target_pairs={{0,2},{1,3},{2,0},{3,1},{4,6},{5,7},{6,4},{7,5},{8,10},{9,11},{10,... | collective-permute-start | bytes 24584 | tf_op jit(solution)/shard_map/ppermute | solution.py:399
  37.1 2.5 %collective-permute-done.8 = f32[2,8,128]{2,1,0:T(8,128)S(1)} collective-permute-done((f32[2,8,128]{2,1,0:T(8,128)S(1)}, f32[2,8,128]{2,1,0:T(8,128)S(1)}, u32[]{:S(2)}, u32[]{:S(2)}) %collective-permute-start.8) | collective-permute-done | bytes 8224 | tf_op jit(solution)/shard_map/ppermute | solution.py:399
  39.7 0.1 collective-permute-start.9
  39.8 0.1 collective-permute-start.14
  39.9 0.6 %memory_terms.1.refs_1_.terms = f32[3,512,256]{2,1,0:T(8,128)S(1)} custom-call(bf16[512,256]{1,0:T(8,128)(2,1)S(1)} %get-tuple-element.25.refs_0_, bf16[512,256]{1,0:T(8,128)(2,1)S(1)} %ordered.2.refs_1_, bf16[512,256]{1,0:T(8,128)(2,1)S(1)} %collective-permute-done.10.refs_2_, bf16[2,512,1024]{2,1,0:T(8,128)(2,1)S(1)} %copy-done), custom_call_target="tpu_custom_call" | custom-call | flops 1024 | bytes 1024 | tf_op jit(solution)/shard_map/memory_terms/pallas_call | solution.py:292
  40.5 2.1 %finish_first.1 = (bf16[1024,1024]{1,0:T(8,128)(2,1)}, f32[4,512,256]{2,1,0:T(8,128)S(1)}) custom-call(s32[1]{0:T(128)} %bitcast.me_ref, bf16[512,256]{1,0:T(8,128)(2,1)S(1)} %get-tuple-element.27.refs_0_, bf16[512,256]{1,0:T(8,128)(2,1)S(1)} %ordered.3.refs_1_, bf16[512,256]{1,0:T(8,128)(2,1)S(1)} %collective-permute-done.12.refs_2_, ...), custom_call_target="tpu_custom_call" | custom-call | flops 1024 | bytes 1024 | tf_op jit(solution)/shard_map/finish_first/pallas_call | solution.py:270
  42.6 1.0 %collective-permute-done.14.b = f32[4,8,128]{2,1,0:T(8,128)S(1)} collective-permute-done((f32[4,8,128]{2,1,0:T(8,128)S(1)}, f32[4,8,128]{2,1,0:T(8,128)S(1)}, u32[]{:S(2)}, u32[]{:S(2)}) %collective-permute-start.14) | collective-permute-done | bytes 16416 | tf_op jit(solution)/shard_map/ppermute | solution.py:385
  43.6 0.2 collective-permute-start.15
  43.8 1.0 %collective-permute-done.15 = f32[8,8,128]{2,1,0:T(8,128)S(1)} collective-permute-done((f32[8,8,128]{2,1,0:T(8,128)S(1)}, f32[8,8,128]{2,1,0:T(8,128)S(1)}, u32[]{:S(2)}, u32[]{:S(2)}) %collective-permute-start.15) | collective-permute-done | bytes 32800 | tf_op jit(solution)/shard_map/ppermute | solution.py:385
  44.8 2.7 %finish_second.1 = (bf16[1024,1024]{1,0:T(8,128)(2,1)}, bf16[1024,1024]{1,0:T(8,128)(2,1)}) custom-call(s32[1]{0:T(128)} %bitcast.me_ref, bf16[512,256]{1,0:T(8,128)(2,1)S(1)} %collective-permute-done.9.last, f32[3,512,256]{2,1,0:T(8,128)S(1)} %memory_terms.1.refs_1_.terms, bf16[2,512,1024]{2,1,0:T(8,128)(2,1)S(1)} %copy-done, ...), custom_call_target="tpu_custom_call", output_to_operand_aliasing={{0}: (7, {})} | custom-call | flops 1024 | bytes 1024 | tf_op jit(solution)/shard_map/finish_second/pallas_call | solution.py:359
  (26 shorter events, 0.2 us)
Async XLA Ops:
  3.7 3.4 %collective-permute-start = (bf16[2,512,256]{2,1,0:T(8,128)(2,1)S(1)}, bf16[2,512,256]{2,1,0:T(8,128)(2,1)S(1)}, u32[]{:S(2)}, u32[]{:S(2)}) collective-permute-start(bf16[2,512,256]{2,1,0:T(8,128)(2,1)S(1)} %get-tuple-element.19), channel_id=1, source_target_pairs={{0,4},{4,0},{8,12},{12,8},{16,20},{20,16},{24,28},{28,24},{1,5},{5... | collective-permute-start | bytes 1572872 | tf_op jit(solution)/shard_map/ppermute | solution.py:385
  10.0 4.6 %collective-permute-start.1 = (bf16[2,512,256]{2,1,0:T(8,128)(2,1)S(1)}, bf16[2,512,256]{2,1,0:T(8,128)(2,1)S(1)}, u32[]{:S(2)}, u32[]{:S(2)}) collective-permute-start(bf16[2,512,256]{2,1,0:T(8,128)(2,1)S(1)} %get-tuple-element.22), channel_id=1, source_target_pairs={{0,4},{4,0},{8,12},{12,8},{16,20},{20,16},{24,28},{28,24},{1,5},{5... | collective-permute-start | bytes 1572872 | tf_op jit(solution)/shard_map/ppermute | solution.py:385
  10.2 7.3 %collective-permute-start.4 = (bf16[512,256]{1,0:T(8,128)(2,1)S(1)}, bf16[512,256]{1,0:T(8,128)(2,1)S(1)}, u32[]{:S(2)}, u32[]{:S(2)}) collective-permute-start(bf16[512,256]{1,0:T(8,128)(2,1)S(1)} %fusion.4.refs_0_), channel_id=1, source_target_pairs={{0,8},{4,20},{8,0},{12,28},{16,24},{20,4},{24,16},{28,12},{1,9},{5... | collective-permute-start | bytes 786440 | tf_op jit(solution)/shard_map/ppermute | solution.py:385
  14.7 9.4 %copy-start = (bf16[2,512,1024]{2,1,0:T(8,128)(2,1)S(1)}, bf16[2,512,1024]{2,1,0:T(8,128)(2,1)}, u32[]{:S(2)}) copy-start(bf16[2,512,1024]{2,1,0:T(8,128)(2,1)} %w.5) | copy-start | bytes 6291460
  14.8 9.3 %copy-start.1 = (bf16[512,1024]{1,0:T(8,128)(2,1)S(1)}, bf16[512,1024]{1,0:T(8,128)(2,1)}, u32[]{:S(2)}) copy-start(bf16[512,1024]{1,0:T(8,128)(2,1)} %refs_5_.1) | copy-start | bytes 3145732
  14.8 9.3 %copy-start.2 = (f32[32,1024]{1,0:T(8,128)S(1)}, f32[32,1024]{1,0:T(8,128)}, u32[]{:S(2)}) copy-start(f32[32,1024]{1,0:T(8,128)} %coupling.5) | copy-start | bytes 393220
  14.8 7.9 %collective-permute-start.2 = (bf16[512,256]{1,0:T(8,128)(2,1)S(1)}, bf16[512,256]{1,0:T(8,128)(2,1)S(1)}, u32[]{:S(2)}, u32[]{:S(2)}) collective-permute-start(bf16[512,256]{1,0:T(8,128)(2,1)S(1)} %fusion.5._), channel_id=1, source_target_pairs={{0,8},{4,20},{8,0},{12,28},{16,24},{20,4},{24,16},{28,12},{1,9},{5... | collective-permute-start | bytes 786440 | tf_op jit(solution)/shard_map/ppermute | solution.py:385
  17.5 6.6 %collective-permute-start.5 = (bf16[512,256]{1,0:T(8,128)(2,1)S(1)}, bf16[512,256]{1,0:T(8,128)(2,1)S(1)}, u32[]{:S(2)}, u32[]{:S(2)}) collective-permute-start(bf16[512,256]{1,0:T(8,128)(2,1)S(1)} %combined.1.mine), channel_id=1, source_target_pairs={{0,16},{4,12},{8,24},{12,4},{16,0},{20,28},{24,8},{28,20},{1,17},{... | collective-permute-start | bytes 786440 | tf_op jit(solution)/shard_map/ppermute | solution.py:385
  22.8 7.6 %collective-permute-start.3 = (bf16[512,256]{1,0:T(8,128)(2,1)S(1)}, bf16[512,256]{1,0:T(8,128)(2,1)S(1)}, u32[]{:S(2)}, u32[]{:S(2)}) collective-permute-start(bf16[512,256]{1,0:T(8,128)(2,1)S(1)} %fusion.3._.mine), channel_id=1, source_target_pairs={{0,16},{4,12},{8,24},{12,4},{16,0},{20,28},{24,8},{28,20},{1,17},{... | collective-permute-start | bytes 786440 | tf_op jit(solution)/shard_map/ppermute | solution.py:385
  25.3 9.6 %collective-permute-start.11 = (bf16[512,256]{1,0:T(8,128)(2,1)S(1)}, bf16[512,256]{1,0:T(8,128)(2,1)S(1)}, u32[]{:S(2)}, u32[]{:S(2)}) collective-permute-start(bf16[512,256]{1,0:T(8,128)(2,1)S(1)} %get-tuple-element.27.refs_0_), channel_id=1, source_target_pairs={{0,8},{4,20},{8,0},{12,28},{16,24},{20,4},{24,16},{28,12},{1,9},{5... | collective-permute-start | bytes 786440 | tf_op jit(solution)/shard_map/ppermute | solution.py:385
  27.2 13.2 %collective-permute-start.12 = (bf16[512,256]{1,0:T(8,128)(2,1)S(1)}, bf16[512,256]{1,0:T(8,128)(2,1)S(1)}, u32[]{:S(2)}, u32[]{:S(2)}) collective-permute-start(bf16[512,256]{1,0:T(8,128)(2,1)S(1)} %get-tuple-element.27.refs_0_), channel_id=1, source_target_pairs={{0,4},{4,0},{8,12},{12,8},{16,20},{20,16},{24,28},{28,24},{1,5},{5... | collective-permute-start | bytes 786440 | tf_op jit(solution)/shard_map/ppermute | solution.py:385
  31.2 3.7 %collective-permute-start.7 = (f32[1,8,128]{2,1,0:T(8,128)S(1)}, f32[1,8,128]{2,1,0:T(8,128)S(1)}, u32[]{:S(2)}, u32[]{:S(2)}) collective-permute-start(f32[1,8,128]{2,1,0:T(8,128)S(1)} %get-tuple-element.26), channel_id=1, source_target_pairs={{0,1},{1,0},{2,3},{3,2},{4,5},{5,4},{6,7},{7,6},{8,9},{9,8},{10,11... | collective-permute-start | bytes 12296 | tf_op jit(solution)/shard_map/ppermute | solution.py:399
  32.3 7.3 %collective-permute-start.6 = (bf16[512,256]{1,0:T(8,128)(2,1)S(1)}, bf16[512,256]{1,0:T(8,128)(2,1)S(1)}, u32[]{:S(2)}, u32[]{:S(2)}) collective-permute-start(bf16[512,256]{1,0:T(8,128)(2,1)S(1)} %get-tuple-element.25.refs_0_), channel_id=1, source_target_pairs={{0,8},{4,20},{8,0},{12,28},{16,24},{20,4},{24,16},{28,12},{1,9},{5... | collective-permute-start | bytes 786440 | tf_op jit(solution)/shard_map/ppermute | solution.py:385
  32.5 7.3 %collective-permute-start.10 = (bf16[512,256]{1,0:T(8,128)(2,1)S(1)}, bf16[512,256]{1,0:T(8,128)(2,1)S(1)}, u32[]{:S(2)}, u32[]{:S(2)}) collective-permute-start(bf16[512,256]{1,0:T(8,128)(2,1)S(1)} %get-tuple-element.25.refs_0_), channel_id=1, source_target_pairs={{0,4},{4,0},{8,12},{12,8},{16,20},{20,16},{24,28},{28,24},{1,5},{5... | collective-permute-start | bytes 786440 | tf_op jit(solution)/shard_map/ppermute | solution.py:385
  34.9 5.6 %collective-permute-start.13 = (bf16[512,256]{1,0:T(8,128)(2,1)S(1)}, bf16[512,256]{1,0:T(8,128)(2,1)S(1)}, u32[]{:S(2)}, u32[]{:S(2)}) collective-permute-start(bf16[512,256]{1,0:T(8,128)(2,1)S(1)} %ordered.3.refs_1_), channel_id=1, source_target_pairs={{0,4},{4,0},{8,12},{12,8},{16,20},{20,16},{24,28},{28,24},{1,5},{5... | collective-permute-start | bytes 786440 | tf_op jit(solution)/shard_map/ppermute | solution.py:385
  35.0 4.7 %collective-permute-start.8 = (f32[2,8,128]{2,1,0:T(8,128)S(1)}, f32[2,8,128]{2,1,0:T(8,128)S(1)}, u32[]{:S(2)}, u32[]{:S(2)}) collective-permute-start(f32[2,8,128]{2,1,0:T(8,128)S(1)} %get-tuple-element.30._), channel_id=1, source_target_pairs={{0,2},{1,3},{2,0},{3,1},{4,6},{5,7},{6,4},{7,5},{8,10},{9,11},{10,... | collective-permute-start | bytes 24584 | tf_op jit(solution)/shard_map/ppermute | solution.py:399
  39.7 5.1 %collective-permute-start.9 = (bf16[512,256]{1,0:T(8,128)(2,1)S(1)}, bf16[512,256]{1,0:T(8,128)(2,1)S(1)}, u32[]{:S(2)}, u32[]{:S(2)}) collective-permute-start(bf16[512,256]{1,0:T(8,128)(2,1)S(1)} %ordered.2.refs_1_), channel_id=1, source_target_pairs={{0,4},{4,0},{8,12},{12,8},{16,20},{20,16},{24,28},{28,24},{1,5},{5... | collective-permute-start | bytes 786440 | tf_op jit(solution)/shard_map/ppermute | solution.py:385
  39.8 3.8 %collective-permute-start.14 = (f32[4,8,128]{2,1,0:T(8,128)S(1)}, f32[4,8,128]{2,1,0:T(8,128)S(1)}, u32[]{:S(2)}, u32[]{:S(2)}) collective-permute-start(f32[4,8,128]{2,1,0:T(8,128)S(1)} %constant_dynamic-update-slice_fusion.2._.a), channel_id=1, source_target_pairs={{0,8},{4,20},{8,0},{12,28},{16,24},{20,4},{24,16},{28,12},{1,9},{5... | collective-permute-start | bytes 49160 | tf_op jit(solution)/shard_map/ppermute | solution.py:385
  43.6 1.2 %collective-permute-start.15 = (f32[8,8,128]{2,1,0:T(8,128)S(1)}, f32[8,8,128]{2,1,0:T(8,128)S(1)}, u32[]{:S(2)}, u32[]{:S(2)}) collective-permute-start(f32[8,8,128]{2,1,0:T(8,128)S(1)} %joined.1), channel_id=1, source_target_pairs={{0,4},{4,0},{8,12},{12,8},{16,20},{20,16},{24,28},{28,24},{1,5},{5... | collective-permute-start | bytes 98312 | tf_op jit(solution)/shard_map/ppermute | solution.py:385

commit v8 on v7

--- a/solution.py
+++ b/solution.py
@@ -59,99 +59,104 @@
         return (self.core ^ 1) * 2 + (self.other_side ^ (slot - 2))
 
 
-def product(me, sigma, g, block, rows, half, bits, send, after=None):
-    load_sigma, load_g = sigma.shape[0] != rows, g.shape[1] != half
-    depth = g.shape[0]
+def first_product(me, sigma_hist, g_hist, rows, half, bits):
+    depth = g_hist.shape[0]
+    quarter = half // 2
+    chunks, parts = 4, 4
+    chunk = depth // chunks
+
+    def kernel(me_ref, sigma_ref, g_ref, out, sigma, g_sent, g_kept, total, sems):
+        place = Place(me_ref[0], bits)
+        sent_at = pl.ds(pl.multiple_of((place.core ^ 1) * half, half), half)
+        kept_at = pl.ds(pl.multiple_of(place.core * half, half), half)
+        started = []
+
+        def load(source, target):
+            started.append(pltpu.make_async_copy(source, target, sems.at[len(started)]))
+            started[-1].start()
+            return started[-1]
+
+        pieces = []
+        for k in range(chunks):
+            deep = pl.ds(k * chunk, chunk)
+            piece = []
+            for i in range(parts):
+                here = pl.ds(i * (rows // parts), rows // parts)
+                piece.append(load(sigma_ref.at[here, deep], sigma.at[here, deep]))
+                here = pl.ds(k * chunk + i * (chunk // parts), chunk // parts)
+                piece.append(load(g_ref.at[here, sent_at], g_sent.at[here, :]))
+            pieces.append(piece)
+        ahead = []
+        for i in range(8):
+            here = pl.ds(i * (depth // 8), depth // 8)
+            ahead.append(load(g_ref.at[here, kept_at], g_kept.at[here, :]))
+        for k in range(chunks):
+            for copy in pieces[k]:
+                copy.wait()
+            deep = pl.ds(k * chunk, chunk)
+            term = jnp.dot(sigma[:, deep], g_sent[deep, :], preferred_element_type=F32)
+            if k == 0:
+                total[...] = term
+            elif k < chunks - 1:
+                total[...] += term
+            else:
+                term += total[...]
+                for j in range(2):
+                    out[1 ^ j ^ place.other_side] = term[:, j * quarter : (j + 1) * quarter].astype(BF16)
+        for copy in ahead:
+            copy.wait()
+
+    return call(
+        kernel,
+        "first_product",
+        in_specs=[SCALAR, HBM, HBM],
+        out_specs=[WHOLE] * 4,
+        out_shape=[
+            near((2, rows, quarter), BF16),
+            near((rows, depth), BF16),
+            near((depth, half), BF16),
+            near((depth, half), BF16),
+        ],
+        scratch_shapes=[pltpu.VMEM((rows, half), F32), pltpu.SemaphoreType.DMA((2 * chunks * parts + 8,))],
+    )(me, far(sigma_hist), far(g_hist))
+
+
+def product(me, sigma, g, bits, send, after=None, sigma_hist=None):
+    rows, depth = sigma.shape
+    half = g.shape[1]
     quarter = half // 2
     dtype = BF16 if send else F32
-    out_shape = [near((2, rows, quarter), dtype)]
-    if load_sigma:
-        out_shape.append(near((rows, depth), BF16))
-    if load_g:
-        out_shape.append(near((depth, half), BF16))
-
-    def kernel(me_ref, sigma_ref, g_ref, *refs):
-        refs = list(refs)
-        if after is not None:
-            refs.pop(0)
-        out = refs.pop(0)
-        sigma_v = refs.pop(0) if load_sigma else sigma_ref
-        g_v = refs.pop(0) if load_g else g_ref
-        total, sems = refs
+    parts = 8
+
+    def kernel(me_ref, sigma, g, *refs):
+        refs = refs[after is not None :]
+        copies = []
+        if sigma_hist is not None:
+            source, out, target, sems = refs
+            for i in range(parts):
+                here = pl.ds(i * (rows // parts), rows // parts)
+                there = pl.ds(rows + i * (rows // parts), rows // parts)
+                copies.append(pltpu.make_async_copy(source.at[there, :], target.at[here, :], sems.at[i]))
+                copies[-1].start()
+        else:
+            (out,) = refs
         place = Place(me_ref[0], bits)
-        first = pl.multiple_of((place.core ^ int(send)) * half, half)
         side = place.other_side if send else place.side
-
-        def put(j, value):
-            out[1 ^ j ^ side] = value.astype(dtype)
-
-        started = []
-
-        def load(source, target, row, column, at, where):
-            part = at[0].size // 4
-            copies = []
-            for i in range(4):
-                into = pl.ds(at[0].start + i * part, part)
-                from_rows = pl.ds(row + at[0].start + i * part, part)
-                from_columns = pl.ds(column + at[1].start, at[1].size) if where is None else where
-                copies.append(
-                    pltpu.make_async_copy(
-                        source.at[from_rows, from_columns], target.at[into, at[1]], sems.at[len(started)]
-                    )
-                )
-                copies[-1].start()
-                started.append(copies[-1])
-            return copies
-
-        chunk = depth // 4
-        if load_g:
-            pieces = []
-            for k in range(4):
-                deep = pl.ds(k * chunk, chunk)
-                piece = []
-                if load_sigma:
-                    piece += load(sigma_ref, sigma_v, block * rows, 0, (pl.ds(0, rows), deep), None)
-                piece += load(g_ref, g_v, 0, 0, (deep, pl.ds(0, half)), pl.ds(first, half))
-                pieces.append(piece)
-            for k, piece in enumerate(pieces):
-                for copy in piece:
-                    copy.wait()
-                deep = pl.ds(k * chunk, chunk)
-                term = jnp.dot(sigma_v[:, deep], g_v[deep, :], preferred_element_type=F32)
-                if k == 0:
-                    total[...] = term
-                elif k < 3:
-                    total[...] += term
-                else:
-                    term += total[...]
-                    for j in range(2):
-                        put(j, term[:, j * quarter : (j + 1) * quarter])
-        elif load_sigma:
-            tall = rows // 2
-            pieces = [
-                load(sigma_ref, sigma_v, block * rows, 0, (pl.ds(i * tall, tall), pl.ds(0, depth)), None)
-                for i in range(2)
-            ]
-            for i, piece in enumerate(pieces):
-                for copy in piece:
-                    copy.wait()
-                here = pl.ds(i * tall, tall)
-                term = jnp.dot(sigma_v[here, :], g_v[...], preferred_element_type=F32).astype(dtype)
-                for j in range(2):
-                    out[1 ^ j ^ side, here, :] = term[:, j * quarter : (j + 1) * quarter]
-        else:
-            term = jnp.dot(sigma_v[...], g_v[...], preferred_element_type=F32)
-            for j in range(2):
-                put(j, term[:, j * quarter : (j + 1) * quarter])
-
+        term = jnp.dot(sigma[...], g[...], preferred_element_type=F32)
+        for j in range(2):
+            out[1 ^ j ^ side] = term[:, j * quarter : (j + 1) * quarter].astype(dtype)
+        for copy in copies:
+            copy.wait()
+
+    loads = sigma_hist is not None
     return call(
         kernel,
         "memory_product",
-        in_specs=[SCALAR, HBM if load_sigma else WHOLE, HBM if load_g else WHOLE] + [FAR] * (after is not None),
-        out_specs=[WHOLE] * len(out_shape),
-        out_shape=out_shape,
-        scratch_shapes=[pltpu.VMEM((rows, half), F32), pltpu.SemaphoreType.DMA((32,))],
-    )(me, far(sigma) if load_sigma else sigma, far(g) if load_g else g, *([] if after is None else [after]))
+        in_specs=[SCALAR, WHOLE, WHOLE] + [FAR] * (after is not None) + [HBM] * loads,
+        out_specs=[WHOLE] * (1 + loads),
+        out_shape=[near((2, rows, quarter), dtype)] + [near((rows, depth), BF16)] * loads,
+        scratch_shapes=[pltpu.SemaphoreType.DMA((parts,))] * loads,
+    )(me, sigma, g, *([] if after is None else [after]), *([far(sigma_hist)] if loads else []))
 
 
 def combined(kept, arrived, more, after):
@@ -398,19 +403,20 @@
     def widened(share, level):
         return lax.ppermute(share, "second", [(z, z ^ (1 << level)) for z in range(second)])
 
-    send, sigma_0, g_send = product(me, sigma_hist, g_hist, 0, rows, half, bits, True)
+    send, sigma_0, g_sent, g_kept = first_product(me, sigma_hist, g_hist, rows, half, bits)
     arrived_0 = swap(send, 0)
-    kept_0, g_keep = product(me, sigma_0, g_hist, 0, rows, half, bits, False)
+    kept_0, sigma_1 = product(me, sigma_0, g_kept, bits, False, sigma_hist=sigma_hist)
     sent_0 = passed_on(kept_0, arrived_0)
-    send, sigma_1 = product(me, sigma_hist, g_send, 1, rows, half, bits, True, after=sent_0)
+    (send,) = product(me, sigma_1, g_sent, bits, True, after=sent_0)
     arrived_1 = swap(send, 0)
-    (kept_1,) = product(me, sigma_1, g_keep, 1, rows, half, bits, False)
+    (kept_1,) = product(me, sigma_1, g_kept, bits, False, after=arrived_1)
     sent_1 = passed_on(kept_1, arrived_1)
 
     mine, theirs = exchanged(kept_0, arrived_0, sent_0, after=sent_1)
     mine_1, theirs_1 = exchanged(kept_1, arrived_1, sent_1)
     own_0, response, squares = own_first(me, mine, theirs, volterra, sigma_edge, coupling, bits, after=mine_1)
     own_1, share = own_second(me, mine_1, theirs_1, volterra, response, squares, coupling, bits)
+
     rounds = log2(second)
     share = jnp.concatenate([share, widened(share, 0)])
     partner = ordered(swap(own_0, 1), share)

time: 47.6 us -> 44.9 us (0.943)
  waiting for transfers between devices: 15.6 us -> 10.5 us
  starting transfers between devices: 12.9 us -> 17.6 us
  Pallas kernels: 17.8 us -> 15.7 us
    ppermute x14, starting transfers between devices: 9.68 us -> 13.9 us  [swap(): return lax.ppermute(x, 'past', pairs)]
    ppermute x14, waiting for transfers between devices: 10.7 us -> 7.36 us  [swap(): return lax.ppermute(x, 'past', pairs)]
    pallas_call x4, Pallas kernels: 10.3 us -> 8.15 us  [the longest x3 4.92 us: product(): call(kernel, 'memory_product', in_specs=[SCALAR, WHOLE, WHOLE] + [FAR] *...]
    ppermute x2, waiting for transfers between devices: 4.88 us -> 3.11 us  [widened(): lax.ppermute(share, 'second', [(z, z ^ 1 << level) for z in range(second)])]
where the time goes in v8:
time: 44.9 us; the launch traced here: 44.8 us
  starting transfers between devices  17.6 us (39%)
  Pallas kernels  15.7 us (35%)
  waiting for transfers between devices  10.5 us (23%)
  between operations  0.82 us (2%)
    ppermute x14, starting transfers between devices, swap(): return lax.ppermute(x, 'past', pairs)  13.9 us
    ppermute x14, waiting for transfers between devices, swap(): return lax.ppermute(x, 'past', pairs)  7.36 us
    pallas_call x3, Pallas kernels, product(): call(kernel, 'memory_product', in_specs=[SCALAR, WHOLE, WHOLE] + [FAR] *...  4.92 us
    ppermute x2, starting transfers between devices, widened(): lax.ppermute(share, 'second', [(z, z ^ 1 << level) for z in range(second)])  3.68 us
    pallas_call x1, Pallas kernels, first_product(): call(kernel, 'first_product', in_specs=[SCALAR, HBM, HBM], out_specs=[WHO...  3.23 us
    ppermute x2, waiting for transfers between devices, widened(): lax.ppermute(share, 'second', [(z, z ^ 1 << level) for z in range(second)])  3.11 us
    pallas_call x1, Pallas kernels, finish_second(): call(kernel, 'finish_second', in_specs=[SCALAR] + [WHOLE] * 6 + [HBM], ou...  2.65 us
    pallas_call x1, Pallas kernels, finish_first(): call(kernel, 'finish_first', in_specs=[SCALAR] + [WHOLE] * 7, out_specs=[...  2.15 us
  transfers between devices with their start and end apart: 16, of which 7 were waited for; matrix products, arithmetic and copies ran while one was open for 0% of the time, Pallas kernels for 19%

profile of v8, /device:TPU:0, one launch (start us, length us, event | category | flops | bytes accessed | tf_op | source)
XLA Modules:
  0.0 44.8 jit_solution(10629673971645859824)
XLA Ops:
  0.6 3.2 %first_product.1 = (bf16[2,512,256]{2,1,0:T(8,128)(2,1)S(1)}, bf16[512,2048]{1,0:T(8,128)(2,1)S(1)}, bf16[2048,512]{1,0:T(8,128)(2,1)S(1)}, bf16[2048,512]{1,0:T(8,128)(2,1)S(1)}) custom-call(s32[1]{0:T(128)} %bitcast.me_ref, bf16[1024,2048]{1,0:T(8,128)(2,1)} %refs_0_.1, bf16[2048,1024]{1,0:T(8,128)(2,1)} %g_ref.1), custom_call_target="tpu_custom_call" | custom-call | flops 1024 | bytes 1024 | tf_op jit(solution)/shard_map/first_product/pallas_call | solution.py:109
  3.9 0.5 %collective-permute-start = (bf16[2,512,256]{2,1,0:T(8,128)(2,1)S(1)}, bf16[2,512,256]{2,1,0:T(8,128)(2,1)S(1)}, u32[]{:S(2)}, u32[]{:S(2)}) collective-permute-start(bf16[2,512,256]{2,1,0:T(8,128)(2,1)S(1)} %get-tuple-element.20), channel_id=1, source_target_pairs={{0,4},{4,0},{8,12},{12,8},{16,20},{20,16},{24,28},{28,24},{1,5},{5... | collective-permute-start | bytes 1572872 | tf_op jit(solution)/shard_map/ppermute | solution.py:390
  4.4 2.4 %memory_product.3 = (f32[2,512,256]{2,1,0:T(8,128)S(1)}, bf16[512,2048]{1,0:T(8,128)(2,1)S(1)}) custom-call(s32[1]{0:T(128)} %bitcast.me_ref, bf16[512,2048]{1,0:T(8,128)(2,1)S(1)} %get-tuple-element.15.sigma, bf16[2048,512]{1,0:T(8,128)(2,1)S(1)} %get-tuple-element.16.g, bf16[1024,2048]{1,0:T(8,128)(2,1)} %refs_0_.1), custom_call_target="tpu_custom_call" | custom-call | flops 1024 | bytes 1024 | tf_op jit(solution)/shard_map/memory_product/pallas_call | solution.py:152
  6.9 1.3 %memory_product.4 = bf16[2,512,256]{2,1,0:T(8,128)(2,1)S(1)} custom-call(s32[1]{0:T(128)} %bitcast.me_ref, bf16[512,2048]{1,0:T(8,128)(2,1)S(1)} %get-tuple-element.17.sigma, bf16[2048,512]{1,0:T(8,128)(2,1)S(1)} %get-tuple-element.18.g, bf16[512,256]{1,0:T(8,128)(2,1)S(1)} %fusion.4.refs_0_), custom_call_target="tpu_custom_call" | custom-call | flops 1024 | bytes 1024 | tf_op jit(solution)/shard_map/memory_product/pallas_call | solution.py:152
  8.1 0.1 collective-permute-start.1
  8.2 2.9 %collective-permute-start.4 = (bf16[512,256]{1,0:T(8,128)(2,1)S(1)}, bf16[512,256]{1,0:T(8,128)(2,1)S(1)}, u32[]{:S(2)}, u32[]{:S(2)}) collective-permute-start(bf16[512,256]{1,0:T(8,128)(2,1)S(1)} %fusion.4.refs_0_), channel_id=1, source_target_pairs={{0,8},{4,20},{8,0},{12,28},{16,24},{20,4},{24,16},{28,12},{1,9},{5... | collective-permute-start | bytes 786440 | tf_op jit(solution)/shard_map/ppermute | solution.py:390
  11.2 1.3 %memory_product.5 = f32[2,512,256]{2,1,0:T(8,128)S(1)} custom-call(s32[1]{0:T(128)} %bitcast.me_ref, bf16[512,2048]{1,0:T(8,128)(2,1)S(1)} %get-tuple-element.17.sigma, bf16[2048,512]{1,0:T(8,128)(2,1)S(1)} %get-tuple-element.16.g, bf16[2,512,256]{2,1,0:T(8,128)(2,1)S(1)} %collective-permute-done.1.refs_0_), custom_call_target="tpu_custom_call" | custom-call | flops 1024 | bytes 1024 | tf_op jit(solution)/shard_map/memory_product/pallas_call | solution.py:152
  12.6 1.6 %collective-permute-start.2 = (bf16[512,256]{1,0:T(8,128)(2,1)S(1)}, bf16[512,256]{1,0:T(8,128)(2,1)S(1)}, u32[]{:S(2)}, u32[]{:S(2)}) collective-permute-start(bf16[512,256]{1,0:T(8,128)(2,1)S(1)} %fusion.5._), channel_id=1, source_target_pairs={{0,8},{4,20},{8,0},{12,28},{16,24},{20,4},{24,16},{28,12},{1,9},{5... | collective-permute-start | bytes 786440 | tf_op jit(solution)/shard_map/ppermute | solution.py:390
  14.2 1.4 %collective-permute-done.4.more = bf16[512,256]{1,0:T(8,128)(2,1)S(1)} collective-permute-done((bf16[512,256]{1,0:T(8,128)(2,1)S(1)}, bf16[512,256]{1,0:T(8,128)(2,1)S(1)}, u32[]{:S(2)}, u32[]{:S(2)}) %collective-permute-start.4) | collective-permute-done | bytes 262176 | tf_op jit(solution)/shard_map/ppermute | solution.py:390
  15.5 0.1 combined.1.mine
  15.6 2.1 %collective-permute-start.5 = (bf16[512,256]{1,0:T(8,128)(2,1)S(1)}, bf16[512,256]{1,0:T(8,128)(2,1)S(1)}, u32[]{:S(2)}, u32[]{:S(2)}) collective-permute-start(bf16[512,256]{1,0:T(8,128)(2,1)S(1)} %combined.1.mine), channel_id=1, source_target_pairs={{0,16},{4,12},{8,24},{12,4},{16,0},{20,28},{24,8},{28,20},{1,17},{... | collective-permute-start | bytes 786440 | tf_op jit(solution)/shard_map/ppermute | solution.py:390
  17.7 2.4 %collective-permute-done.2 = bf16[512,256]{1,0:T(8,128)(2,1)S(1)} collective-permute-done((bf16[512,256]{1,0:T(8,128)(2,1)S(1)}, bf16[512,256]{1,0:T(8,128)(2,1)S(1)}, u32[]{:S(2)}, u32[]{:S(2)}) %collective-permute-start.2) | collective-permute-done | bytes 262176 | tf_op jit(solution)/shard_map/ppermute | solution.py:390
  20.1 0.1 fusion.3._.mine
  20.2 1.5 %collective-permute-start.3 = (bf16[512,256]{1,0:T(8,128)(2,1)S(1)}, bf16[512,256]{1,0:T(8,128)(2,1)S(1)}, u32[]{:S(2)}, u32[]{:S(2)}) collective-permute-start(bf16[512,256]{1,0:T(8,128)(2,1)S(1)} %fusion.3._.mine), channel_id=1, source_target_pairs={{0,16},{4,12},{8,24},{12,4},{16,0},{20,28},{24,8},{28,20},{1,17},{... | collective-permute-start | bytes 786440 | tf_op jit(solution)/shard_map/ppermute | solution.py:390
  21.7 0.4 collective-permute-done.5.theirs
  22.1 1.2 %own_first.1 = (bf16[512,256]{1,0:T(8,128)(2,1)S(1)}, f32[512,256]{1,0:T(8,128)S(1)}, f32[1,128]{1,0:T(1,128)S(1)}) custom-call(s32[1]{0:T(128)} %bitcast.me_ref, bf16[512,256]{1,0:T(8,128)(2,1)S(1)} %combined.1.mine, bf16[512,256]{1,0:T(8,128)(2,1)S(1)} %collective-permute-done.5.theirs, bf16[2,512,1024]{2,1,0:T(8,128)(2,1)S(1)} %copy-done, ...), custom_call_target="tpu_custom_call" | custom-call | flops 1024 | bytes 1024 | tf_op jit(solution)/shard_map/own_first/pallas_call | solution.py:213
  23.3 2.1 %collective-permute-start.11 = (bf16[512,256]{1,0:T(8,128)(2,1)S(1)}, bf16[512,256]{1,0:T(8,128)(2,1)S(1)}, u32[]{:S(2)}, u32[]{:S(2)}) collective-permute-start(bf16[512,256]{1,0:T(8,128)(2,1)S(1)} %get-tuple-element.25.refs_0_), channel_id=1, source_target_pairs={{0,8},{4,20},{8,0},{12,28},{16,24},{20,4},{24,16},{28,12},{1,9},{5... | collective-permute-start | bytes 786440 | tf_op jit(solution)/shard_map/ppermute | solution.py:390
  25.3 2.1 %collective-permute-done.3.theirs = bf16[512,256]{1,0:T(8,128)(2,1)S(1)} collective-permute-done((bf16[512,256]{1,0:T(8,128)(2,1)S(1)}, bf16[512,256]{1,0:T(8,128)(2,1)S(1)}, u32[]{:S(2)}, u32[]{:S(2)}) %collective-permute-start.3) | collective-permute-done | bytes 262176 | tf_op jit(solution)/shard_map/ppermute | solution.py:390
  27.5 0.8 %own_second.1 = (bf16[512,256]{1,0:T(8,128)(2,1)S(1)}, f32[1,8,128]{2,1,0:T(8,128)S(1)}) custom-call(s32[1]{0:T(128)} %bitcast.me_ref, bf16[512,256]{1,0:T(8,128)(2,1)S(1)} %fusion.3._.mine, bf16[512,256]{1,0:T(8,128)(2,1)S(1)} %collective-permute-done.3.theirs, bf16[2,512,1024]{2,1,0:T(8,128)(2,1)S(1)} %copy-done, ...), custom_call_target="tpu_custom_call" | custom-call | flops 1024 | bytes 1024 | tf_op jit(solution)/shard_map/own_second/pallas_call | solution.py:247
  28.3 1.3 %collective-permute-start.7 = (f32[1,8,128]{2,1,0:T(8,128)S(1)}, f32[1,8,128]{2,1,0:T(8,128)S(1)}, u32[]{:S(2)}, u32[]{:S(2)}) collective-permute-start(f32[1,8,128]{2,1,0:T(8,128)S(1)} %get-tuple-element.24), channel_id=1, source_target_pairs={{0,1},{1,0},{2,3},{3,2},{4,5},{5,4},{6,7},{7,6},{8,9},{9,8},{10,11... | collective-permute-start | bytes 12296 | tf_op jit(solution)/shard_map/ppermute | solution.py:404
  29.6 1.5 %collective-permute-start.6 = (bf16[512,256]{1,0:T(8,128)(2,1)S(1)}, bf16[512,256]{1,0:T(8,128)(2,1)S(1)}, u32[]{:S(2)}, u32[]{:S(2)}) collective-permute-start(bf16[512,256]{1,0:T(8,128)(2,1)S(1)} %get-tuple-element.23.refs_0_), channel_id=1, source_target_pairs={{0,8},{4,20},{8,0},{12,28},{16,24},{20,4},{24,16},{28,12},{1,9},{5... | collective-permute-start | bytes 786440 | tf_op jit(solution)/shard_map/ppermute | solution.py:390
  31.1 0.8 %collective-permute-done.7 = f32[1,8,128]{2,1,0:T(8,128)S(1)} collective-permute-done((f32[1,8,128]{2,1,0:T(8,128)S(1)}, f32[1,8,128]{2,1,0:T(8,128)S(1)}, u32[]{:S(2)}, u32[]{:S(2)}) %collective-permute-start.7) | collective-permute-done | bytes 4128 | tf_op jit(solution)/shard_map/ppermute | solution.py:404
  32.0 0.1 collective-permute-start.13
  32.1 2.3 %collective-permute-start.8 = (f32[2,8,128]{2,1,0:T(8,128)S(1)}, f32[2,8,128]{2,1,0:T(8,128)S(1)}, u32[]{:S(2)}, u32[]{:S(2)}) collective-permute-start(f32[2,8,128]{2,1,0:T(8,128)S(1)} %get-tuple-element.28._), channel_id=1, source_target_pairs={{0,2},{1,3},{2,0},{3,1},{4,6},{5,7},{6,4},{7,5},{8,10},{9,11},{10,... | collective-permute-start | bytes 24584 | tf_op jit(solution)/shard_map/ppermute | solution.py:404
  34.4 2.3 %collective-permute-done.8 = f32[2,8,128]{2,1,0:T(8,128)S(1)} collective-permute-done((f32[2,8,128]{2,1,0:T(8,128)S(1)}, f32[2,8,128]{2,1,0:T(8,128)S(1)}, u32[]{:S(2)}, u32[]{:S(2)}) %collective-permute-start.8) | collective-permute-done | bytes 8224 | tf_op jit(solution)/shard_map/ppermute | solution.py:404
  36.7 0.1 collective-permute-start.9
  36.8 1.2 %collective-permute-start.14 = (f32[4,8,128]{2,1,0:T(8,128)S(1)}, f32[4,8,128]{2,1,0:T(8,128)S(1)}, u32[]{:S(2)}, u32[]{:S(2)}) collective-permute-start(f32[4,8,128]{2,1,0:T(8,128)S(1)} %constant_dynamic-update-slice_fusion.2._.a), channel_id=1, source_target_pairs={{0,8},{4,20},{8,0},{12,28},{16,24},{20,4},{24,16},{28,12},{1,9},{5... | collective-permute-start | bytes 49160 | tf_op jit(solution)/shard_map/ppermute | solution.py:390
  38.1 0.6 %memory_terms.1.refs_1_.terms = f32[3,512,256]{2,1,0:T(8,128)S(1)} custom-call(bf16[512,256]{1,0:T(8,128)(2,1)S(1)} %get-tuple-element.23.refs_0_, bf16[512,256]{1,0:T(8,128)(2,1)S(1)} %ordered.2.refs_1_, bf16[512,256]{1,0:T(8,128)(2,1)S(1)} %collective-permute-done.10.refs_2_, bf16[2,512,1024]{2,1,0:T(8,128)(2,1)S(1)} %copy-done), custom_call_target="tpu_custom_call" | custom-call | flops 1024 | bytes 1024 | tf_op jit(solution)/shard_map/memory_terms/pallas_call | solution.py:297
  38.7 2.1 %finish_first.1 = (bf16[1024,1024]{1,0:T(8,128)(2,1)}, f32[4,512,256]{2,1,0:T(8,128)S(1)}) custom-call(s32[1]{0:T(128)} %bitcast.me_ref, bf16[512,256]{1,0:T(8,128)(2,1)S(1)} %get-tuple-element.25.refs_0_, bf16[512,256]{1,0:T(8,128)(2,1)S(1)} %ordered.3.refs_1_, bf16[512,256]{1,0:T(8,128)(2,1)S(1)} %collective-permute-done.12.refs_2_, ...), custom_call_target="tpu_custom_call" | custom-call | flops 1024 | bytes 1024 | tf_op jit(solution)/shard_map/finish_first/pallas_call | solution.py:275
  40.8 0.2 collective-permute-start.15
  41.1 1.0 %collective-permute-done.15 = f32[8,8,128]{2,1,0:T(8,128)S(1)} collective-permute-done((f32[8,8,128]{2,1,0:T(8,128)S(1)}, f32[8,8,128]{2,1,0:T(8,128)S(1)}, u32[]{:S(2)}, u32[]{:S(2)}) %collective-permute-start.15) | collective-permute-done | bytes 32800 | tf_op jit(solution)/shard_map/ppermute | solution.py:390
  42.1 2.7 %finish_second.1 = (bf16[1024,1024]{1,0:T(8,128)(2,1)}, bf16[1024,1024]{1,0:T(8,128)(2,1)}) custom-call(s32[1]{0:T(128)} %bitcast.me_ref, bf16[512,256]{1,0:T(8,128)(2,1)S(1)} %collective-permute-done.9.last, f32[3,512,256]{2,1,0:T(8,128)S(1)} %memory_terms.1.refs_1_.terms, bf16[2,512,1024]{2,1,0:T(8,128)(2,1)S(1)} %copy-done, ...), custom_call_target="tpu_custom_call", output_to_operand_aliasing={{0}: (7, {})} | custom-call | flops 1024 | bytes 1024 | tf_op jit(solution)/shard_map/finish_second/pallas_call | solution.py:364
  (26 shorter events, 0.2 us)
Async XLA Ops:
  3.9 2.9 %collective-permute-start = (bf16[2,512,256]{2,1,0:T(8,128)(2,1)S(1)}, bf16[2,512,256]{2,1,0:T(8,128)(2,1)S(1)}, u32[]{:S(2)}, u32[]{:S(2)}) collective-permute-start(bf16[2,512,256]{2,1,0:T(8,128)(2,1)S(1)} %get-tuple-element.20), channel_id=1, source_target_pairs={{0,4},{4,0},{8,12},{12,8},{16,20},{20,16},{24,28},{28,24},{1,5},{5... | collective-permute-start | bytes 1572872 | tf_op jit(solution)/shard_map/ppermute | solution.py:390
  8.1 3.1 %collective-permute-start.1 = (bf16[2,512,256]{2,1,0:T(8,128)(2,1)S(1)}, bf16[2,512,256]{2,1,0:T(8,128)(2,1)S(1)}, u32[]{:S(2)}, u32[]{:S(2)}) collective-permute-start(bf16[2,512,256]{2,1,0:T(8,128)(2,1)S(1)} %memory_product.4), channel_id=1, source_target_pairs={{0,4},{4,0},{8,12},{12,8},{16,20},{20,16},{24,28},{28,24},{1,5},{5... | collective-permute-start | bytes 1572872 | tf_op jit(solution)/shard_map/ppermute | solution.py:390
  8.2 7.3 %collective-permute-start.4 = (bf16[512,256]{1,0:T(8,128)(2,1)S(1)}, bf16[512,256]{1,0:T(8,128)(2,1)S(1)}, u32[]{:S(2)}, u32[]{:S(2)}) collective-permute-start(bf16[512,256]{1,0:T(8,128)(2,1)S(1)} %fusion.4.refs_0_), channel_id=1, source_target_pairs={{0,8},{4,20},{8,0},{12,28},{16,24},{20,4},{24,16},{28,12},{1,9},{5... | collective-permute-start | bytes 786440 | tf_op jit(solution)/shard_map/ppermute | solution.py:390
  12.5 9.6 %copy-start = (bf16[2,512,1024]{2,1,0:T(8,128)(2,1)S(1)}, bf16[2,512,1024]{2,1,0:T(8,128)(2,1)}, u32[]{:S(2)}) copy-start(bf16[2,512,1024]{2,1,0:T(8,128)(2,1)} %w.5) | copy-start | bytes 6291460
  12.5 9.6 %copy-start.1 = (bf16[512,1024]{1,0:T(8,128)(2,1)S(1)}, bf16[512,1024]{1,0:T(8,128)(2,1)}, u32[]{:S(2)}) copy-start(bf16[512,1024]{1,0:T(8,128)(2,1)} %refs_5_.1) | copy-start | bytes 3145732
  12.6 9.5 %copy-start.2 = (f32[32,1024]{1,0:T(8,128)S(1)}, f32[32,1024]{1,0:T(8,128)}, u32[]{:S(2)}) copy-start(f32[32,1024]{1,0:T(8,128)} %coupling.5) | copy-start | bytes 393220
  12.6 7.6 %collective-permute-start.2 = (bf16[512,256]{1,0:T(8,128)(2,1)S(1)}, bf16[512,256]{1,0:T(8,128)(2,1)S(1)}, u32[]{:S(2)}, u32[]{:S(2)}) collective-permute-start(bf16[512,256]{1,0:T(8,128)(2,1)S(1)} %fusion.5._), channel_id=1, source_target_pairs={{0,8},{4,20},{8,0},{12,28},{16,24},{20,4},{24,16},{28,12},{1,9},{5... | collective-permute-start | bytes 786440 | tf_op jit(solution)/shard_map/ppermute | solution.py:390
  15.6 6.5 %collective-permute-start.5 = (bf16[512,256]{1,0:T(8,128)(2,1)S(1)}, bf16[512,256]{1,0:T(8,128)(2,1)S(1)}, u32[]{:S(2)}, u32[]{:S(2)}) collective-permute-start(bf16[512,256]{1,0:T(8,128)(2,1)S(1)} %combined.1.mine), channel_id=1, source_target_pairs={{0,16},{4,12},{8,24},{12,4},{16,0},{20,28},{24,8},{28,20},{1,17},{... | collective-permute-start | bytes 786440 | tf_op jit(solution)/shard_map/ppermute | solution.py:390
  20.2 7.2 %collective-permute-start.3 = (bf16[512,256]{1,0:T(8,128)(2,1)S(1)}, bf16[512,256]{1,0:T(8,128)(2,1)S(1)}, u32[]{:S(2)}, u32[]{:S(2)}) collective-permute-start(bf16[512,256]{1,0:T(8,128)(2,1)S(1)} %fusion.3._.mine), channel_id=1, source_target_pairs={{0,16},{4,12},{8,24},{12,4},{16,0},{20,28},{24,8},{28,20},{1,17},{... | collective-permute-start | bytes 786440 | tf_op jit(solution)/shard_map/ppermute | solution.py:390
  23.3 8.7 %collective-permute-start.11 = (bf16[512,256]{1,0:T(8,128)(2,1)S(1)}, bf16[512,256]{1,0:T(8,128)(2,1)S(1)}, u32[]{:S(2)}, u32[]{:S(2)}) collective-permute-start(bf16[512,256]{1,0:T(8,128)(2,1)S(1)} %get-tuple-element.25.refs_0_), channel_id=1, source_target_pairs={{0,8},{4,20},{8,0},{12,28},{16,24},{20,4},{24,16},{28,12},{1,9},{5... | collective-permute-start | bytes 786440 | tf_op jit(solution)/shard_map/ppermute | solution.py:390
  25.3 13.3 %collective-permute-start.12 = (bf16[512,256]{1,0:T(8,128)(2,1)S(1)}, bf16[512,256]{1,0:T(8,128)(2,1)S(1)}, u32[]{:S(2)}, u32[]{:S(2)}) collective-permute-start(bf16[512,256]{1,0:T(8,128)(2,1)S(1)} %get-tuple-element.25.refs_0_), channel_id=1, source_target_pairs={{0,4},{4,0},{8,12},{12,8},{16,20},{20,16},{24,28},{28,24},{1,5},{5... | collective-permute-start | bytes 786440 | tf_op jit(solution)/shard_map/ppermute | solution.py:390
  28.3 3.7 %collective-permute-start.7 = (f32[1,8,128]{2,1,0:T(8,128)S(1)}, f32[1,8,128]{2,1,0:T(8,128)S(1)}, u32[]{:S(2)}, u32[]{:S(2)}) collective-permute-start(f32[1,8,128]{2,1,0:T(8,128)S(1)} %get-tuple-element.24), channel_id=1, source_target_pairs={{0,1},{1,0},{2,3},{3,2},{4,5},{5,4},{6,7},{7,6},{8,9},{9,8},{10,11... | collective-permute-start | bytes 12296 | tf_op jit(solution)/shard_map/ppermute | solution.py:404
  29.6 7.1 %collective-permute-start.6 = (bf16[512,256]{1,0:T(8,128)(2,1)S(1)}, bf16[512,256]{1,0:T(8,128)(2,1)S(1)}, u32[]{:S(2)}, u32[]{:S(2)}) collective-permute-start(bf16[512,256]{1,0:T(8,128)(2,1)S(1)} %get-tuple-element.23.refs_0_), channel_id=1, source_target_pairs={{0,8},{4,20},{8,0},{12,28},{16,24},{20,4},{24,16},{28,12},{1,9},{5... | collective-permute-start | bytes 786440 | tf_op jit(solution)/shard_map/ppermute | solution.py:390
  31.1 6.9 %collective-permute-start.10 = (bf16[512,256]{1,0:T(8,128)(2,1)S(1)}, bf16[512,256]{1,0:T(8,128)(2,1)S(1)}, u32[]{:S(2)}, u32[]{:S(2)}) collective-permute-start(bf16[512,256]{1,0:T(8,128)(2,1)S(1)} %get-tuple-element.23.refs_0_), channel_id=1, source_target_pairs={{0,4},{4,0},{8,12},{12,8},{16,20},{20,16},{24,28},{28,24},{1,5},{5... | collective-permute-start | bytes 786440 | tf_op jit(solution)/shard_map/ppermute | solution.py:390
  32.0 6.6 %collective-permute-start.13 = (bf16[512,256]{1,0:T(8,128)(2,1)S(1)}, bf16[512,256]{1,0:T(8,128)(2,1)S(1)}, u32[]{:S(2)}, u32[]{:S(2)}) collective-permute-start(bf16[512,256]{1,0:T(8,128)(2,1)S(1)} %ordered.3.refs_1_), channel_id=1, source_target_pairs={{0,4},{4,0},{8,12},{12,8},{16,20},{20,16},{24,28},{28,24},{1,5},{5... | collective-permute-start | bytes 786440 | tf_op jit(solution)/shard_map/ppermute | solution.py:390
  32.1 4.6 %collective-permute-start.8 = (f32[2,8,128]{2,1,0:T(8,128)S(1)}, f32[2,8,128]{2,1,0:T(8,128)S(1)}, u32[]{:S(2)}, u32[]{:S(2)}) collective-permute-start(f32[2,8,128]{2,1,0:T(8,128)S(1)} %get-tuple-element.28._), channel_id=1, source_target_pairs={{0,2},{1,3},{2,0},{3,1},{4,6},{5,7},{6,4},{7,5},{8,10},{9,11},{10,... | collective-permute-start | bytes 24584 | tf_op jit(solution)/shard_map/ppermute | solution.py:404
  36.7 5.4 %collective-permute-start.9 = (bf16[512,256]{1,0:T(8,128)(2,1)S(1)}, bf16[512,256]{1,0:T(8,128)(2,1)S(1)}, u32[]{:S(2)}, u32[]{:S(2)}) collective-permute-start(bf16[512,256]{1,0:T(8,128)(2,1)S(1)} %ordered.2.refs_1_), channel_id=1, source_target_pairs={{0,4},{4,0},{8,12},{12,8},{16,20},{20,16},{24,28},{28,24},{1,5},{5... | collective-permute-start | bytes 786440 | tf_op jit(solution)/shard_map/ppermute | solution.py:390
  36.8 4.0 %collective-permute-start.14 = (f32[4,8,128]{2,1,0:T(8,128)S(1)}, f32[4,8,128]{2,1,0:T(8,128)S(1)}, u32[]{:S(2)}, u32[]{:S(2)}) collective-permute-start(f32[4,8,128]{2,1,0:T(8,128)S(1)} %constant_dynamic-update-slice_fusion.2._.a), channel_id=1, source_target_pairs={{0,8},{4,20},{8,0},{12,28},{16,24},{20,4},{24,16},{28,12},{1,9},{5... | collective-permute-start | bytes 49160 | tf_op jit(solution)/shard_map/ppermute | solution.py:390
  40.8 1.3 %collective-permute-start.15 = (f32[8,8,128]{2,1,0:T(8,128)S(1)}, f32[8,8,128]{2,1,0:T(8,128)S(1)}, u32[]{:S(2)}, u32[]{:S(2)}) collective-permute-start(f32[8,8,128]{2,1,0:T(8,128)S(1)} %joined.1), channel_id=1, source_target_pairs={{0,4},{4,0},{8,12},{12,8},{16,20},{20,16},{24,28},{28,24},{1,5},{5... | collective-permute-start | bytes 98312 | tf_op jit(solution)/shard_map/ppermute | solution.py:390

commit v9 on v8

--- a/solution.py
+++ b/solution.py
@@ -223,14 +223,15 @@
     )(me, mine, theirs, volterra, edge, coupling, after)
 
 
-def own_second(me, mine, theirs, volterra, response, squares, coupling, bits):
+def own_second(me, mine, theirs, first, volterra, response, squares, coupling, bits):
     rows, width = mine.shape
     orbitals = coupling.shape[0]
 
-    def kernel(me_ref, mine, theirs, w, response, squares, coupling, memory, out):
+    def kernel(me_ref, mine, theirs, first, w, response, squares, coupling, passed, memory, out):
         at = columns_of(Place(me_ref[0], bits).quarter(), width)
         summed = (mine[...].astype(F32) + theirs[...].astype(F32)).astype(BF16)
         memory[...] = summed
+        passed[...] = first[...]
         c = coupling[:, at]
         c2 = (c * c * (1.0 / (rows * width)))[None]
         a = jnp.dot(w[1, :, :rows], summed, preferred_element_type=F32)
@@ -247,10 +248,10 @@
     return call(
         kernel,
         "own_second",
-        in_specs=[SCALAR] + [WHOLE] * 6,
-        out_specs=[WHOLE] * 2,
-        out_shape=[near((rows, width), BF16), near((1, 8, 128), F32)],
-    )(me, mine, theirs, volterra, response, squares, coupling)
+        in_specs=[SCALAR] + [WHOLE] * 7,
+        out_specs=[WHOLE] * 3,
+        out_shape=[near((rows, width), BF16)] * 2 + [near((1, 8, 128), F32)],
+    )(me, mine, theirs, first, volterra, response, squares, coupling)
 
 
 def finish_first(me, pieces, volterra, edge, coupling, bits):
@@ -316,6 +317,19 @@
     return call(kernel, "joined", in_specs=in_specs, out_specs=WHOLE, out_shape=near(shape, F32))(a, b, *after)
 
 
+def chosen(me, even, odd, after):
+    def kernel(me_ref, even, odd, _, out):
+        out[...] = jnp.where(me_ref[0] % 2 == 1, odd[...], even[...])
+
+    return call(
+        kernel,
+        "chosen",
+        in_specs=[SCALAR, WHOLE, WHOLE, FAR],
+        out_specs=WHOLE,
+        out_shape=near(even.shape, even.dtype),
+    )(me, even, odd, after)
+
+
 def ordered(x, after):
     def kernel(x, _, out):
         out[...] = x[...]
@@ -333,14 +347,14 @@
         last_term = jnp.dot(w[1, :, :rows], last[...], preferred_element_type=F32)
         sums = jnp.sum(shares[...], axis=2, keepdims=True)
         means = sums[:, 0:1, :]
-        mean = jnp.sum(over_halves(means)) / everyone
+        mean = over_halves(means) * (1.0 / everyone)
         ratio = jnp.sqrt((means + EPS) / (mean + EPS))
         power, series = jnp.ones_like(ratio), jnp.zeros_like(ratio)
         for k, weight in enumerate(BINOMIAL):
             series += weight * sums[:, k + 1 : k + 2, :] * power
             power = power * ratio
-        scale_0 = 1.0 / jnp.sqrt(mean + EPS)
-        scale_1 = 1.0 / jnp.sqrt(jnp.maximum(jnp.sum(over_halves(series)) / everyone, 0.0) + EPS)
+        scale_0 = (1.0 / jnp.sqrt(mean + EPS))[0]
+        scale_1 = (1.0 / jnp.sqrt(jnp.maximum(over_halves(series) * (1.0 / everyone), 0.0) + EPS))[0]
 
         copies = []
 
@@ -385,8 +399,8 @@
     even = list(range(bits))
     odd = even[:1] + even[1:][::-1]
 
-    def swap(x, level):
-        pairs = [(d, d ^ (1 << (odd if d % 2 else even)[level])) for d in range(past)]
+    def swap(x, level, devices=range(past)):
+        pairs = [(d, d ^ (1 << (odd if d % 2 else even)[level])) for d in devices]
         return lax.ppermute(x, "past", pairs)
 
     def exchanged(kept, arrived, sent, after=None):
@@ -415,15 +429,15 @@
     mine, theirs = exchanged(kept_0, arrived_0, sent_0, after=sent_1)
     mine_1, theirs_1 = exchanged(kept_1, arrived_1, sent_1)
     own_0, response, squares = own_first(me, mine, theirs, volterra, sigma_edge, coupling, bits, after=mine_1)
-    own_1, share = own_second(me, mine_1, theirs_1, volterra, response, squares, coupling, bits)
+    own_0_late, own_1, share = own_second(me, mine_1, theirs_1, own_0, volterra, response, squares, coupling, bits)
 
     rounds = log2(second)
     share = jnp.concatenate([share, widened(share, 0)])
-    partner = ordered(swap(own_0, 1), share)
+    for level in range(1, rounds):
+        share = jnp.concatenate([share, widened(share, level)])
+    partner = chosen(me, swap(own_0, 1, range(0, past, 2)), swap(own_0_late, 1, range(1, past, 2)), share)
     pieces = [own_0, partner, swap(own_0, 0), swap(partner, 0)]
     g_first, cubic = finish_first(me, pieces, volterra, sigma_edge, coupling, bits)
-    for level in range(1, rounds):
-        share = jnp.concatenate([share, widened(share, level)])
     partner = ordered(swap(own_1, 1), share)
     terms = memory_terms([own_1, partner, swap(own_1, 0)], volterra)
     last = swap(partner, 0)

time: 44.9 us -> 45.6 us (1.016)
  starting transfers between devices: 17.6 us -> 20.9 us
  waiting for transfers between devices: 10.5 us -> 7.84 us
    ppermute x14 -> x15, starting transfers between devices: 13.9 us -> 16.6 us  [swap(): return lax.ppermute(x, 'past', pairs)]
    ppermute x14 -> x15, waiting for transfers between devices: 7.36 us -> 5.34 us  [swap(): return lax.ppermute(x, 'past', pairs)]
    ppermute x2, waiting for transfers between devices: 3.11 us -> 2.51 us  [widened(): lax.ppermute(share, 'second', [(z, z ^ 1 << level) for z in range(second)])]
    ppermute x2, starting transfers between devices: 3.68 us -> 4.23 us  [widened(): lax.ppermute(share, 'second', [(z, z ^ 1 << level) for z in range(second)])]
  transfers between devices with their start and end apart: 16 -> 17, of which waited for: 7 -> 6; matrix products, arithmetic and copies ran while one was open for 0% -> 0% of each run, Pallas kernels for 19% -> 19%
where the time goes in v9:
time: 45.6 us; the launch traced here: 45.4 us
  starting transfers between devices  20.9 us (46%)
  Pallas kernels  15.6 us (34%)
  waiting for transfers between devices  7.84 us (17%)
  between operations  0.85 us (2%)
    ppermute x15, starting transfers between devices, swap(): return lax.ppermute(x, 'past', pairs)  16.6 us
    ppermute x15, waiting for transfers between devices, swap(): return lax.ppermute(x, 'past', pairs)  5.34 us
    pallas_call x3, Pallas kernels, product(): call(kernel, 'memory_product', in_specs=[SCALAR, WHOLE, WHOLE] + [FAR] *...  4.92 us
    ppermute x2, starting transfers between devices, widened(): lax.ppermute(share, 'second', [(z, z ^ 1 << level) for z in range(second)])  4.23 us
    pallas_call x1, Pallas kernels, first_product(): call(kernel, 'first_product', in_specs=[SCALAR, HBM, HBM], out_specs=[WHO...  3.23 us
    pallas_call x1, Pallas kernels, finish_second(): call(kernel, 'finish_second', in_specs=[SCALAR] + [WHOLE] * 6 + [HBM], ou...  2.6 us
    ppermute x2, waiting for transfers between devices, widened(): lax.ppermute(share, 'second', [(z, z ^ 1 << level) for z in range(second)])  2.51 us
    pallas_call x1, Pallas kernels, finish_first(): call(kernel, 'finish_first', in_specs=[SCALAR] + [WHOLE] * 7, out_specs=[...  2.16 us
  transfers between devices with their start and end apart: 17, of which 6 were waited for; matrix products, arithmetic and copies ran while one was open for 0% of the time, Pallas kernels for 19%

profile of v9, /device:TPU:0, one launch (start us, length us, event | category | flops | bytes accessed | tf_op | source)
XLA Modules:
  0.0 45.4 jit_solution(11679988522422155552)
XLA Ops:
  0.6 3.2 %first_product.1 = (bf16[2,512,256]{2,1,0:T(8,128)(2,1)S(1)}, bf16[512,2048]{1,0:T(8,128)(2,1)S(1)}, bf16[2048,512]{1,0:T(8,128)(2,1)S(1)}, bf16[2048,512]{1,0:T(8,128)(2,1)S(1)}) custom-call(s32[1]{0:T(128)} %bitcast.me_ref, bf16[1024,2048]{1,0:T(8,128)(2,1)} %refs_0_.1, bf16[2048,1024]{1,0:T(8,128)(2,1)} %g_ref.1), custom_call_target="tpu_custom_call" | custom-call | flops 1024 | bytes 1024 | tf_op jit(solution)/shard_map/first_product/pallas_call | solution.py:109
  3.9 0.5 %collective-permute-start = (bf16[2,512,256]{2,1,0:T(8,128)(2,1)S(1)}, bf16[2,512,256]{2,1,0:T(8,128)(2,1)S(1)}, u32[]{:S(2)}, u32[]{:S(2)}) collective-permute-start(bf16[2,512,256]{2,1,0:T(8,128)(2,1)S(1)} %get-tuple-element.21), channel_id=1, source_target_pairs={{0,4},{4,0},{8,12},{12,8},{16,20},{20,16},{24,28},{28,24},{1,5},{5... | collective-permute-start | bytes 1572872 | tf_op jit(solution)/shard_map/ppermute | solution.py:404
  4.4 2.4 %memory_product.3 = (f32[2,512,256]{2,1,0:T(8,128)S(1)}, bf16[512,2048]{1,0:T(8,128)(2,1)S(1)}) custom-call(s32[1]{0:T(128)} %bitcast.me_ref, bf16[512,2048]{1,0:T(8,128)(2,1)S(1)} %get-tuple-element.16.sigma, bf16[2048,512]{1,0:T(8,128)(2,1)S(1)} %get-tuple-element.17.g, bf16[1024,2048]{1,0:T(8,128)(2,1)} %refs_0_.1), custom_call_target="tpu_custom_call" | custom-call | flops 1024 | bytes 1024 | tf_op jit(solution)/shard_map/memory_product/pallas_call | solution.py:152
  6.9 1.3 %memory_product.4 = bf16[2,512,256]{2,1,0:T(8,128)(2,1)S(1)} custom-call(s32[1]{0:T(128)} %bitcast.me_ref, bf16[512,2048]{1,0:T(8,128)(2,1)S(1)} %get-tuple-element.18.sigma, bf16[2048,512]{1,0:T(8,128)(2,1)S(1)} %get-tuple-element.19.g, bf16[512,256]{1,0:T(8,128)(2,1)S(1)} %fusion.4.refs_0_), custom_call_target="tpu_custom_call" | custom-call | flops 1024 | bytes 1024 | tf_op jit(solution)/shard_map/memory_product/pallas_call | solution.py:152
  8.1 0.1 collective-permute-start.1
  8.2 2.9 %collective-permute-start.4 = (bf16[512,256]{1,0:T(8,128)(2,1)S(1)}, bf16[512,256]{1,0:T(8,128)(2,1)S(1)}, u32[]{:S(2)}, u32[]{:S(2)}) collective-permute-start(bf16[512,256]{1,0:T(8,128)(2,1)S(1)} %fusion.4.refs_0_), channel_id=1, source_target_pairs={{0,8},{4,20},{8,0},{12,28},{16,24},{20,4},{24,16},{28,12},{1,9},{5... | collective-permute-start | bytes 786440 | tf_op jit(solution)/shard_map/ppermute | solution.py:404
  11.2 1.3 %memory_product.5 = f32[2,512,256]{2,1,0:T(8,128)S(1)} custom-call(s32[1]{0:T(128)} %bitcast.me_ref, bf16[512,2048]{1,0:T(8,128)(2,1)S(1)} %get-tuple-element.18.sigma, bf16[2048,512]{1,0:T(8,128)(2,1)S(1)} %get-tuple-element.17.g, bf16[2,512,256]{2,1,0:T(8,128)(2,1)S(1)} %collective-permute-done.1.refs_0_), custom_call_target="tpu_custom_call" | custom-call | flops 1024 | bytes 1024 | tf_op jit(solution)/shard_map/memory_product/pallas_call | solution.py:152
  12.6 1.6 %collective-permute-start.2 = (bf16[512,256]{1,0:T(8,128)(2,1)S(1)}, bf16[512,256]{1,0:T(8,128)(2,1)S(1)}, u32[]{:S(2)}, u32[]{:S(2)}) collective-permute-start(bf16[512,256]{1,0:T(8,128)(2,1)S(1)} %fusion.5._), channel_id=1, source_target_pairs={{0,8},{4,20},{8,0},{12,28},{16,24},{20,4},{24,16},{28,12},{1,9},{5... | collective-permute-start | bytes 786440 | tf_op jit(solution)/shard_map/ppermute | solution.py:404
  14.2 1.4 %collective-permute-done.4.more = bf16[512,256]{1,0:T(8,128)(2,1)S(1)} collective-permute-done((bf16[512,256]{1,0:T(8,128)(2,1)S(1)}, bf16[512,256]{1,0:T(8,128)(2,1)S(1)}, u32[]{:S(2)}, u32[]{:S(2)}) %collective-permute-start.4) | collective-permute-done | bytes 262176 | tf_op jit(solution)/shard_map/ppermute | solution.py:404
  15.5 0.1 combined.1.mine
  15.6 2.1 %collective-permute-start.5 = (bf16[512,256]{1,0:T(8,128)(2,1)S(1)}, bf16[512,256]{1,0:T(8,128)(2,1)S(1)}, u32[]{:S(2)}, u32[]{:S(2)}) collective-permute-start(bf16[512,256]{1,0:T(8,128)(2,1)S(1)} %combined.1.mine), channel_id=1, source_target_pairs={{0,16},{4,12},{8,24},{12,4},{16,0},{20,28},{24,8},{28,20},{1,17},{... | collective-permute-start | bytes 786440 | tf_op jit(solution)/shard_map/ppermute | solution.py:404
  17.7 2.4 %collective-permute-done.2 = bf16[512,256]{1,0:T(8,128)(2,1)S(1)} collective-permute-done((bf16[512,256]{1,0:T(8,128)(2,1)S(1)}, bf16[512,256]{1,0:T(8,128)(2,1)S(1)}, u32[]{:S(2)}, u32[]{:S(2)}) %collective-permute-start.2) | collective-permute-done | bytes 262176 | tf_op jit(solution)/shard_map/ppermute | solution.py:404
  20.1 0.1 fusion.3._.mine
  20.2 1.5 %collective-permute-start.3 = (bf16[512,256]{1,0:T(8,128)(2,1)S(1)}, bf16[512,256]{1,0:T(8,128)(2,1)S(1)}, u32[]{:S(2)}, u32[]{:S(2)}) collective-permute-start(bf16[512,256]{1,0:T(8,128)(2,1)S(1)} %fusion.3._.mine), channel_id=1, source_target_pairs={{0,16},{4,12},{8,24},{12,4},{16,0},{20,28},{24,8},{28,20},{1,17},{... | collective-permute-start | bytes 786440 | tf_op jit(solution)/shard_map/ppermute | solution.py:404
  21.7 0.4 collective-permute-done.5.theirs
  22.1 1.2 %own_first.1 = (bf16[512,256]{1,0:T(8,128)(2,1)S(1)}, f32[512,256]{1,0:T(8,128)S(1)}, f32[1,128]{1,0:T(1,128)S(1)}) custom-call(s32[1]{0:T(128)} %bitcast.me_ref, bf16[512,256]{1,0:T(8,128)(2,1)S(1)} %combined.1.mine, bf16[512,256]{1,0:T(8,128)(2,1)S(1)} %collective-permute-done.5.theirs, bf16[2,512,1024]{2,1,0:T(8,128)(2,1)S(1)} %copy-done, ...), custom_call_target="tpu_custom_call" | custom-call | flops 1024 | bytes 1024 | tf_op jit(solution)/shard_map/own_first/pallas_call | solution.py:213
  23.4 3.9 %collective-permute-start.11 = (bf16[512,256]{1,0:T(8,128)(2,1)S(1)}, bf16[512,256]{1,0:T(8,128)(2,1)S(1)}, u32[]{:S(2)}, u32[]{:S(2)}) collective-permute-start(bf16[512,256]{1,0:T(8,128)(2,1)S(1)} %get-tuple-element.22.first.refs_0_), channel_id=1, source_target_pairs={{0,8},{8,0},{16,24},{24,16},{1,9},{9,1},{17,25},{25,17},{2,10},{10... | collective-permute-start | bytes 786440 | tf_op jit(solution)/shard_map/ppermute | solution.py:404
  27.3 0.8 %own_second.1 = (bf16[512,256]{1,0:T(8,128)(2,1)S(1)}, bf16[512,256]{1,0:T(8,128)(2,1)S(1)}, f32[1,8,128]{2,1,0:T(8,128)S(1)}) custom-call(s32[1]{0:T(128)} %bitcast.me_ref, bf16[512,256]{1,0:T(8,128)(2,1)S(1)} %fusion.3._.mine, bf16[512,256]{1,0:T(8,128)(2,1)S(1)} %collective-permute-done.3.theirs, bf16[512,256]{1,0:T(8,128)(2,1)S(1)} %get-tuple-element.22.first.refs_0_, ...), custom_call_target="tpu_custom_call" | custom-call | flops 1024 | bytes 1024 | tf_op jit(solution)/shard_map/own_second/pallas_call | solution.py:248
  28.1 1.6 %collective-permute-start.7 = (f32[1,8,128]{2,1,0:T(8,128)S(1)}, f32[1,8,128]{2,1,0:T(8,128)S(1)}, u32[]{:S(2)}, u32[]{:S(2)}) collective-permute-start(f32[1,8,128]{2,1,0:T(8,128)S(1)} %get-tuple-element.26), channel_id=1, source_target_pairs={{0,1},{1,0},{2,3},{3,2},{4,5},{5,4},{6,7},{7,6},{8,9},{9,8},{10,11... | collective-permute-start | bytes 12296 | tf_op jit(solution)/shard_map/ppermute | solution.py:418
  29.8 0.7 %collective-permute-start.12 = (bf16[512,256]{1,0:T(8,128)(2,1)S(1)}, bf16[512,256]{1,0:T(8,128)(2,1)S(1)}, u32[]{:S(2)}, u32[]{:S(2)}) collective-permute-start(bf16[512,256]{1,0:T(8,128)(2,1)S(1)} %get-tuple-element.27), channel_id=1, source_target_pairs={{4,20},{12,28},{20,4},{28,12},{5,21},{13,29},{21,5},{29,13},{6,22}... | collective-permute-start | bytes 786440 | tf_op jit(solution)/shard_map/ppermute | solution.py:404
  30.4 0.8 %collective-permute-start.6 = (bf16[512,256]{1,0:T(8,128)(2,1)S(1)}, bf16[512,256]{1,0:T(8,128)(2,1)S(1)}, u32[]{:S(2)}, u32[]{:S(2)}) collective-permute-start(bf16[512,256]{1,0:T(8,128)(2,1)S(1)} %get-tuple-element.25.refs_0_), channel_id=1, source_target_pairs={{0,8},{4,20},{8,0},{12,28},{16,24},{20,4},{24,16},{28,12},{1,9},{5... | collective-permute-start | bytes 786440 | tf_op jit(solution)/shard_map/ppermute | solution.py:404
  31.2 0.5 %collective-permute-done.7 = f32[1,8,128]{2,1,0:T(8,128)S(1)} collective-permute-done((f32[1,8,128]{2,1,0:T(8,128)S(1)}, f32[1,8,128]{2,1,0:T(8,128)S(1)}, u32[]{:S(2)}, u32[]{:S(2)}) %collective-permute-start.7) | collective-permute-done | bytes 4128 | tf_op jit(solution)/shard_map/ppermute | solution.py:418
  31.8 2.6 %collective-permute-start.8 = (f32[2,8,128]{2,1,0:T(8,128)S(1)}, f32[2,8,128]{2,1,0:T(8,128)S(1)}, u32[]{:S(2)}, u32[]{:S(2)}) collective-permute-start(f32[2,8,128]{2,1,0:T(8,128)S(1)} %pad_maximum_fusion.1), channel_id=1, source_target_pairs={{0,2},{1,3},{2,0},{3,1},{4,6},{5,7},{6,4},{7,5},{8,10},{9,11},{10,... | collective-permute-start | bytes 24584 | tf_op jit(solution)/shard_map/ppermute | solution.py:418
  34.4 2.0 %collective-permute-done.8 = f32[2,8,128]{2,1,0:T(8,128)S(1)} collective-permute-done((f32[2,8,128]{2,1,0:T(8,128)S(1)}, f32[2,8,128]{2,1,0:T(8,128)S(1)}, u32[]{:S(2)}, u32[]{:S(2)}) %collective-permute-start.8) | collective-permute-done | bytes 8224 | tf_op jit(solution)/shard_map/ppermute | solution.py:418
  36.4 0.6 %collective-permute-start.14 = (bf16[512,256]{1,0:T(8,128)(2,1)S(1)}, bf16[512,256]{1,0:T(8,128)(2,1)S(1)}, u32[]{:S(2)}, u32[]{:S(2)}) collective-permute-start(bf16[512,256]{1,0:T(8,128)(2,1)S(1)} %chosen.1.refs_1_), channel_id=1, source_target_pairs={{0,4},{4,0},{8,12},{12,8},{16,20},{20,16},{24,28},{28,24},{1,5},{5... | collective-permute-start | bytes 786440 | tf_op jit(solution)/shard_map/ppermute | solution.py:404
  37.0 0.3 collective-permute-start.9
  37.3 1.5 %collective-permute-start.15 = (f32[4,8,128]{2,1,0:T(8,128)S(1)}, f32[4,8,128]{2,1,0:T(8,128)S(1)}, u32[]{:S(2)}, u32[]{:S(2)}) collective-permute-start(f32[4,8,128]{2,1,0:T(8,128)S(1)} %constant_dynamic-update-slice_fusion._.a), channel_id=1, source_target_pairs={{0,8},{4,20},{8,0},{12,28},{16,24},{20,4},{24,16},{28,12},{1,9},{5... | collective-permute-start | bytes 49160 | tf_op jit(solution)/shard_map/ppermute | solution.py:404
  38.7 0.6 %memory_terms.1.refs_1_.terms = f32[3,512,256]{2,1,0:T(8,128)S(1)} custom-call(bf16[512,256]{1,0:T(8,128)(2,1)S(1)} %get-tuple-element.25.refs_0_, bf16[512,256]{1,0:T(8,128)(2,1)S(1)} %ordered.1.refs_1_, bf16[512,256]{1,0:T(8,128)(2,1)S(1)} %collective-permute-done.10.refs_2_, bf16[2,512,1024]{2,1,0:T(8,128)(2,1)S(1)} %copy-done), custom_call_target="tpu_custom_call" | custom-call | flops 1024 | bytes 1024 | tf_op jit(solution)/shard_map/memory_terms/pallas_call | solution.py:298
  39.3 2.2 %finish_first.1 = (bf16[1024,1024]{1,0:T(8,128)(2,1)}, f32[4,512,256]{2,1,0:T(8,128)S(1)}) custom-call(s32[1]{0:T(128)} %bitcast.me_ref, bf16[512,256]{1,0:T(8,128)(2,1)S(1)} %get-tuple-element.22.first.refs_0_, bf16[512,256]{1,0:T(8,128)(2,1)S(1)} %chosen.1.refs_1_, bf16[512,256]{1,0:T(8,128)(2,1)S(1)} %collective-permute-done.13.refs_2_, ...), custom_call_target="tpu_custom_call" | custom-call | flops 1024 | bytes 1024 | tf_op jit(solution)/shard_map/finish_first/pallas_call | solution.py:276
  41.5 0.1 collective-permute-start.16
  41.7 1.1 %collective-permute-done.16 = f32[8,8,128]{2,1,0:T(8,128)S(1)} collective-permute-done((f32[8,8,128]{2,1,0:T(8,128)S(1)}, f32[8,8,128]{2,1,0:T(8,128)S(1)}, u32[]{:S(2)}, u32[]{:S(2)}) %collective-permute-start.16) | collective-permute-done | bytes 32800 | tf_op jit(solution)/shard_map/ppermute | solution.py:404
  42.8 2.6 %finish_second.1 = (bf16[1024,1024]{1,0:T(8,128)(2,1)}, bf16[1024,1024]{1,0:T(8,128)(2,1)}) custom-call(s32[1]{0:T(128)} %bitcast.me_ref, bf16[512,256]{1,0:T(8,128)(2,1)S(1)} %collective-permute-done.9.last, f32[3,512,256]{2,1,0:T(8,128)S(1)} %memory_terms.1.refs_1_.terms, bf16[2,512,1024]{2,1,0:T(8,128)(2,1)S(1)} %copy-done, ...), custom_call_target="tpu_custom_call", output_to_operand_aliasing={{0}: (7, {})} | custom-call | flops 1024 | bytes 1024 | tf_op jit(solution)/shard_map/finish_second/pallas_call | solution.py:378
  (29 shorter events, 0.3 us)
Async XLA Ops:
  3.9 2.9 %collective-permute-start = (bf16[2,512,256]{2,1,0:T(8,128)(2,1)S(1)}, bf16[2,512,256]{2,1,0:T(8,128)(2,1)S(1)}, u32[]{:S(2)}, u32[]{:S(2)}) collective-permute-start(bf16[2,512,256]{2,1,0:T(8,128)(2,1)S(1)} %get-tuple-element.21), channel_id=1, source_target_pairs={{0,4},{4,0},{8,12},{12,8},{16,20},{20,16},{24,28},{28,24},{1,5},{5... | collective-permute-start | bytes 1572872 | tf_op jit(solution)/shard_map/ppermute | solution.py:404
  8.1 3.1 %collective-permute-start.1 = (bf16[2,512,256]{2,1,0:T(8,128)(2,1)S(1)}, bf16[2,512,256]{2,1,0:T(8,128)(2,1)S(1)}, u32[]{:S(2)}, u32[]{:S(2)}) collective-permute-start(bf16[2,512,256]{2,1,0:T(8,128)(2,1)S(1)} %memory_product.4), channel_id=1, source_target_pairs={{0,4},{4,0},{8,12},{12,8},{16,20},{20,16},{24,28},{28,24},{1,5},{5... | collective-permute-start | bytes 1572872 | tf_op jit(solution)/shard_map/ppermute | solution.py:404
  8.2 7.3 %collective-permute-start.4 = (bf16[512,256]{1,0:T(8,128)(2,1)S(1)}, bf16[512,256]{1,0:T(8,128)(2,1)S(1)}, u32[]{:S(2)}, u32[]{:S(2)}) collective-permute-start(bf16[512,256]{1,0:T(8,128)(2,1)S(1)} %fusion.4.refs_0_), channel_id=1, source_target_pairs={{0,8},{4,20},{8,0},{12,28},{16,24},{20,4},{24,16},{28,12},{1,9},{5... | collective-permute-start | bytes 786440 | tf_op jit(solution)/shard_map/ppermute | solution.py:404
  12.5 9.6 %copy-start = (bf16[2,512,1024]{2,1,0:T(8,128)(2,1)S(1)}, bf16[2,512,1024]{2,1,0:T(8,128)(2,1)}, u32[]{:S(2)}) copy-start(bf16[2,512,1024]{2,1,0:T(8,128)(2,1)} %w.5) | copy-start | bytes 6291460
  12.5 9.6 %copy-start.1 = (bf16[512,1024]{1,0:T(8,128)(2,1)S(1)}, bf16[512,1024]{1,0:T(8,128)(2,1)}, u32[]{:S(2)}) copy-start(bf16[512,1024]{1,0:T(8,128)(2,1)} %refs_5_.1) | copy-start | bytes 3145732
  12.6 9.5 %copy-start.2 = (f32[32,1024]{1,0:T(8,128)S(1)}, f32[32,1024]{1,0:T(8,128)}, u32[]{:S(2)}) copy-start(f32[32,1024]{1,0:T(8,128)} %coupling.5) | copy-start | bytes 393220
  12.6 7.6 %collective-permute-start.2 = (bf16[512,256]{1,0:T(8,128)(2,1)S(1)}, bf16[512,256]{1,0:T(8,128)(2,1)S(1)}, u32[]{:S(2)}, u32[]{:S(2)}) collective-permute-start(bf16[512,256]{1,0:T(8,128)(2,1)S(1)} %fusion.5._), channel_id=1, source_target_pairs={{0,8},{4,20},{8,0},{12,28},{16,24},{20,4},{24,16},{28,12},{1,9},{5... | collective-permute-start | bytes 786440 | tf_op jit(solution)/shard_map/ppermute | solution.py:404
  15.6 6.5 %collective-permute-start.5 = (bf16[512,256]{1,0:T(8,128)(2,1)S(1)}, bf16[512,256]{1,0:T(8,128)(2,1)S(1)}, u32[]{:S(2)}, u32[]{:S(2)}) collective-permute-start(bf16[512,256]{1,0:T(8,128)(2,1)S(1)} %combined.1.mine), channel_id=1, source_target_pairs={{0,16},{4,12},{8,24},{12,4},{16,0},{20,28},{24,8},{28,20},{1,17},{... | collective-permute-start | bytes 786440 | tf_op jit(solution)/shard_map/ppermute | solution.py:404
  20.2 7.0 %collective-permute-start.3 = (bf16[512,256]{1,0:T(8,128)(2,1)S(1)}, bf16[512,256]{1,0:T(8,128)(2,1)S(1)}, u32[]{:S(2)}, u32[]{:S(2)}) collective-permute-start(bf16[512,256]{1,0:T(8,128)(2,1)S(1)} %fusion.3._.mine), channel_id=1, source_target_pairs={{0,16},{4,12},{8,24},{12,4},{16,0},{20,28},{24,8},{28,20},{1,17},{... | collective-permute-start | bytes 786440 | tf_op jit(solution)/shard_map/ppermute | solution.py:404
  23.3 16.1 %collective-permute-start.13 = (bf16[512,256]{1,0:T(8,128)(2,1)S(1)}, bf16[512,256]{1,0:T(8,128)(2,1)S(1)}, u32[]{:S(2)}, u32[]{:S(2)}) collective-permute-start(bf16[512,256]{1,0:T(8,128)(2,1)S(1)} %get-tuple-element.22.first.refs_0_), channel_id=1, source_target_pairs={{0,4},{4,0},{8,12},{12,8},{16,20},{20,16},{24,28},{28,24},{1,5},{5... | collective-permute-start | bytes 786440 | tf_op jit(solution)/shard_map/ppermute | solution.py:404
  23.4 13.0 %collective-permute-start.11 = (bf16[512,256]{1,0:T(8,128)(2,1)S(1)}, bf16[512,256]{1,0:T(8,128)(2,1)S(1)}, u32[]{:S(2)}, u32[]{:S(2)}) collective-permute-start(bf16[512,256]{1,0:T(8,128)(2,1)S(1)} %get-tuple-element.22.first.refs_0_), channel_id=1, source_target_pairs={{0,8},{8,0},{16,24},{24,16},{1,9},{9,1},{17,25},{25,17},{2,10},{10... | collective-permute-start | bytes 786440 | tf_op jit(solution)/shard_map/ppermute | solution.py:404
  28.1 3.7 %collective-permute-start.7 = (f32[1,8,128]{2,1,0:T(8,128)S(1)}, f32[1,8,128]{2,1,0:T(8,128)S(1)}, u32[]{:S(2)}, u32[]{:S(2)}) collective-permute-start(f32[1,8,128]{2,1,0:T(8,128)S(1)} %get-tuple-element.26), channel_id=1, source_target_pairs={{0,1},{1,0},{2,3},{3,2},{4,5},{5,4},{6,7},{7,6},{8,9},{9,8},{10,11... | collective-permute-start | bytes 12296 | tf_op jit(solution)/shard_map/ppermute | solution.py:418
  29.8 6.6 %collective-permute-start.12 = (bf16[512,256]{1,0:T(8,128)(2,1)S(1)}, bf16[512,256]{1,0:T(8,128)(2,1)S(1)}, u32[]{:S(2)}, u32[]{:S(2)}) collective-permute-start(bf16[512,256]{1,0:T(8,128)(2,1)S(1)} %get-tuple-element.27), channel_id=1, source_target_pairs={{4,20},{12,28},{20,4},{28,12},{5,21},{13,29},{21,5},{29,13},{6,22}... | collective-permute-start | bytes 786440 | tf_op jit(solution)/shard_map/ppermute | solution.py:404
  30.4 6.5 %collective-permute-start.6 = (bf16[512,256]{1,0:T(8,128)(2,1)S(1)}, bf16[512,256]{1,0:T(8,128)(2,1)S(1)}, u32[]{:S(2)}, u32[]{:S(2)}) collective-permute-start(bf16[512,256]{1,0:T(8,128)(2,1)S(1)} %get-tuple-element.25.refs_0_), channel_id=1, source_target_pairs={{0,8},{4,20},{8,0},{12,28},{16,24},{20,4},{24,16},{28,12},{1,9},{5... | collective-permute-start | bytes 786440 | tf_op jit(solution)/shard_map/ppermute | solution.py:404
  31.8 4.5 %collective-permute-start.8 = (f32[2,8,128]{2,1,0:T(8,128)S(1)}, f32[2,8,128]{2,1,0:T(8,128)S(1)}, u32[]{:S(2)}, u32[]{:S(2)}) collective-permute-start(f32[2,8,128]{2,1,0:T(8,128)S(1)} %pad_maximum_fusion.1), channel_id=1, source_target_pairs={{0,2},{1,3},{2,0},{3,1},{4,6},{5,7},{6,4},{7,5},{8,10},{9,11},{10,... | collective-permute-start | bytes 24584 | tf_op jit(solution)/shard_map/ppermute | solution.py:418
  36.3 2.4 %collective-permute-start.10 = (bf16[512,256]{1,0:T(8,128)(2,1)S(1)}, bf16[512,256]{1,0:T(8,128)(2,1)S(1)}, u32[]{:S(2)}, u32[]{:S(2)}) collective-permute-start(bf16[512,256]{1,0:T(8,128)(2,1)S(1)} %get-tuple-element.25.refs_0_), channel_id=1, source_target_pairs={{0,4},{4,0},{8,12},{12,8},{16,20},{20,16},{24,28},{28,24},{1,5},{5... | collective-permute-start | bytes 786440 | tf_op jit(solution)/shard_map/ppermute | solution.py:404
  36.4 2.9 %collective-permute-start.14 = (bf16[512,256]{1,0:T(8,128)(2,1)S(1)}, bf16[512,256]{1,0:T(8,128)(2,1)S(1)}, u32[]{:S(2)}, u32[]{:S(2)}) collective-permute-start(bf16[512,256]{1,0:T(8,128)(2,1)S(1)} %chosen.1.refs_1_), channel_id=1, source_target_pairs={{0,4},{4,0},{8,12},{12,8},{16,20},{20,16},{24,28},{28,24},{1,5},{5... | collective-permute-start | bytes 786440 | tf_op jit(solution)/shard_map/ppermute | solution.py:404
  37.0 5.8 %collective-permute-start.9 = (bf16[512,256]{1,0:T(8,128)(2,1)S(1)}, bf16[512,256]{1,0:T(8,128)(2,1)S(1)}, u32[]{:S(2)}, u32[]{:S(2)}) collective-permute-start(bf16[512,256]{1,0:T(8,128)(2,1)S(1)} %ordered.1.refs_1_), channel_id=1, source_target_pairs={{0,4},{4,0},{8,12},{12,8},{16,20},{20,16},{24,28},{28,24},{1,5},{5... | collective-permute-start | bytes 786440 | tf_op jit(solution)/shard_map/ppermute | solution.py:404
  37.3 4.3 %collective-permute-start.15 = (f32[4,8,128]{2,1,0:T(8,128)S(1)}, f32[4,8,128]{2,1,0:T(8,128)S(1)}, u32[]{:S(2)}, u32[]{:S(2)}) collective-permute-start(f32[4,8,128]{2,1,0:T(8,128)S(1)} %constant_dynamic-update-slice_fusion._.a), channel_id=1, source_target_pairs={{0,8},{4,20},{8,0},{12,28},{16,24},{20,4},{24,16},{28,12},{1,9},{5... | collective-permute-start | bytes 49160 | tf_op jit(solution)/shard_map/ppermute | solution.py:404
  41.5 1.3 %collective-permute-start.16 = (f32[8,8,128]{2,1,0:T(8,128)S(1)}, f32[8,8,128]{2,1,0:T(8,128)S(1)}, u32[]{:S(2)}, u32[]{:S(2)}) collective-permute-start(f32[8,8,128]{2,1,0:T(8,128)S(1)} %joined.1), channel_id=1, source_target_pairs={{0,4},{4,0},{8,12},{12,8},{16,20},{20,16},{24,28},{28,24},{1,5},{5... | collective-permute-start | bytes 98312 | tf_op jit(solution)/shard_map/ppermute | solution.py:404

commit v10 on v8

--- a/solution.py
+++ b/solution.py
@@ -101,8 +101,7 @@
                 total[...] += term
             else:
                 term += total[...]
-                for j in range(2):
-                    out[1 ^ j ^ place.other_side] = term[:, j * quarter : (j + 1) * quarter].astype(BF16)
+                halves_to(out, term, place.other_side)
         for copy in ahead:
             copy.wait()
 
@@ -121,42 +120,56 @@
     )(me, far(sigma_hist), far(g_hist))
 
 
-def product(me, sigma, g, bits, send, after=None, sigma_hist=None):
+def halves_to(out, value, side, here=slice(None)):
+    quarter = out.shape[2]
+    for j in range(2):
+        out[1 ^ j ^ side, here, :] = value[:, j * quarter : (j + 1) * quarter].astype(out.dtype)
+
+
+def middle_products(me, sigma, g_kept, g_sent, sigma_hist, bits):
     rows, depth = sigma.shape
-    half = g.shape[1]
-    quarter = half // 2
-    dtype = BF16 if send else F32
-    parts = 8
-
-    def kernel(me_ref, sigma, g, *refs):
-        refs = refs[after is not None :]
+    half = g_kept.shape[1]
+    parts, chunks = 8, 2
+
+    def kernel(me_ref, sigma, g_kept, g_sent, source, kept, sent, target, sems):
         copies = []
-        if sigma_hist is not None:
-            source, out, target, sems = refs
-            for i in range(parts):
-                here = pl.ds(i * (rows // parts), rows // parts)
-                there = pl.ds(rows + i * (rows // parts), rows // parts)
-                copies.append(pltpu.make_async_copy(source.at[there, :], target.at[here, :], sems.at[i]))
-                copies[-1].start()
-        else:
-            (out,) = refs
+        for i in range(parts):
+            here = pl.ds(i * (rows // parts), rows // parts)
+            there = pl.ds(rows + i * (rows // parts), rows // parts)
+            copies.append(pltpu.make_async_copy(source.at[there, :], target.at[here, :], sems.at[i]))
+            copies[-1].start()
         place = Place(me_ref[0], bits)
-        side = place.other_side if send else place.side
-        term = jnp.dot(sigma[...], g[...], preferred_element_type=F32)
-        for j in range(2):
-            out[1 ^ j ^ side] = term[:, j * quarter : (j + 1) * quarter].astype(dtype)
-        for copy in copies:
-            copy.wait()
-
-    loads = sigma_hist is not None
-    return call(
-        kernel,
-        "memory_product",
-        in_specs=[SCALAR, WHOLE, WHOLE] + [FAR] * (after is not None) + [HBM] * loads,
-        out_specs=[WHOLE] * (1 + loads),
-        out_shape=[near((2, rows, quarter), dtype)] + [near((rows, depth), BF16)] * loads,
-        scratch_shapes=[pltpu.SemaphoreType.DMA((parts,))] * loads,
-    )(me, sigma, g, *([] if after is None else [after]), *([far(sigma_hist)] if loads else []))
+        halves_to(kept, jnp.dot(sigma[...], g_kept[...], preferred_element_type=F32), place.side)
+        for k in range(chunks):
+            for copy in copies[k * (parts // chunks) : (k + 1) * (parts // chunks)]:
+                copy.wait()
+            here = pl.ds(k * (rows // chunks), rows // chunks)
+            term = jnp.dot(target[here, :], g_sent[...], preferred_element_type=F32)
+            halves_to(sent, term, place.other_side, here)
+
+    return call(
+        kernel,
+        "middle_products",
+        in_specs=[SCALAR] + [WHOLE] * 3 + [HBM],
+        out_specs=[WHOLE] * 3,
+        out_shape=[near((2, rows, half // 2), F32), near((2, rows, half // 2), BF16), near((rows, depth), BF16)],
+        scratch_shapes=[pltpu.SemaphoreType.DMA((parts,))],
+    )(me, sigma, g_kept, g_sent, far(sigma_hist))
+
+
+def last_product(me, sigma, g_kept, bits, after):
+    rows, half = sigma.shape[0], g_kept.shape[1]
+
+    def kernel(me_ref, sigma, g_kept, _, kept):
+        halves_to(kept, jnp.dot(sigma[...], g_kept[...], preferred_element_type=F32), Place(me_ref[0], bits).side)
+
+    return call(
+        kernel,
+        "last_product",
+        in_specs=[SCALAR, WHOLE, WHOLE, FAR],
+        out_specs=WHOLE,
+        out_shape=near((2, rows, half // 2), F32),
+    )(me, sigma, g_kept, after)
 
 
 def combined(kept, arrived, more, after):
@@ -198,13 +211,15 @@
 def own_first(me, mine, theirs, volterra, edge, coupling, bits, after):
     rows, width = mine.shape
 
-    def kernel(me_ref, mine, theirs, w, edge, coupling, _, memory, response, squares):
+    def kernel(me_ref, mine, theirs, w, edge, coupling, _, memory, response, squares, g_own, cubic_own):
         at = columns_of(Place(me_ref[0], bits).quarter(), width)
         summed = (mine[...].astype(F32) + theirs[...].astype(F32)).astype(BF16)
         memory[...] = summed
         g = jnp.dot(w[0, :, :rows], summed, preferred_element_type=F32)
         g += jnp.dot(w[0, :, rows:], edge[:, at], preferred_element_type=F32)
+        g_own[...] = g.astype(BF16)
         cubic = cubed(g, coupling[:, at])
+        cubic_own[...] = cubic
         line = folded(cubic * cubic * (1.0 / (rows * width)))
         squares[...] = line
         scale = lax.rsqrt(jnp.sum(line) + EPS)
@@ -214,11 +229,13 @@
         kernel,
         "own_first",
         in_specs=[SCALAR] + [WHOLE] * 5 + [FAR],
-        out_specs=[WHOLE] * 3,
+        out_specs=[WHOLE] * 5,
         out_shape=[
             near((rows, width), BF16),
             near((rows, width), F32),
             near((1, 128), F32),
+            near((rows, width), BF16),
+            near((rows, width), F32),
         ],
     )(me, mine, theirs, volterra, edge, coupling, after)
 
@@ -227,13 +244,14 @@
     rows, width = mine.shape
     orbitals = coupling.shape[0]
 
-    def kernel(me_ref, mine, theirs, w, response, squares, coupling, memory, out):
+    def kernel(me_ref, mine, theirs, w, response, squares, coupling, memory, out, term_own):
         at = columns_of(Place(me_ref[0], bits).quarter(), width)
         summed = (mine[...].astype(F32) + theirs[...].astype(F32)).astype(BF16)
         memory[...] = summed
         c = coupling[:, at]
         c2 = (c * c * (1.0 / (rows * width)))[None]
         a = jnp.dot(w[1, :, :rows], summed, preferred_element_type=F32)
+        term_own[...] = a
         b = response[...]
         a2, b2 = a * a, b * b
         a3, b3, a2b, ab2 = a2 * a, b2 * b, a2 * b, a * b2
@@ -248,27 +266,33 @@
         kernel,
         "own_second",
         in_specs=[SCALAR] + [WHOLE] * 6,
-        out_specs=[WHOLE] * 2,
-        out_shape=[near((rows, width), BF16), near((1, 8, 128), F32)],
+        out_specs=[WHOLE] * 3,
+        out_shape=[near((rows, width), BF16), near((1, 8, 128), F32), near((rows, width), F32)],
     )(me, mine, theirs, volterra, response, squares, coupling)
 
 
-def finish_first(me, pieces, volterra, edge, coupling, bits):
+def finish_first(me, pieces, g_own, volterra, edge, coupling, bits):
     rows, width = pieces[0].shape
     columns = coupling.shape[1]
 
     def kernel(me_ref, *refs):
-        pieces, (w, edge, coupling, g_out, cubic, held, sems) = refs[:4], refs[4:]
+        pieces, (g_own, w, edge, coupling, g_out, cubic, held, sems) = refs[:3], refs[3:]
         place = Place(me_ref[0], bits)
+
+        def write(source, slot):
+            at = columns_of(place.quarter_of(slot), width)
+            copies.append(pltpu.make_async_copy(source, g_out.at[pl.ds(0, rows), at], sems.at[slot]))
+            copies[-1].start()
+
         copies = []
-        for slot in range(4):
-            at = columns_of(place.quarter_of(slot), width)
-            g = jnp.dot(w[0, :, :rows], pieces[slot][...], preferred_element_type=F32)
+        write(g_own, 0)
+        for i in range(3):
+            at = columns_of(place.quarter_of(i + 1), width)
+            g = jnp.dot(w[0, :, :rows], pieces[i][...], preferred_element_type=F32)
             g += jnp.dot(w[0, :, rows:], edge[:, at], preferred_element_type=F32)
-            held[slot] = g.astype(BF16)
-            copies.append(pltpu.make_async_copy(held.at[slot], g_out.at[pl.ds(0, rows), at], sems.at[slot]))
-            copies[-1].start()
-            cubic[slot] = cubed(g, coupling[:, at])
+            held[i] = g.astype(BF16)
+            write(held.at[i], i + 1)
+            cubic[i] = cubed(g, coupling[:, at])
         for copy in copies:
             copy.wait()
 
@@ -277,12 +301,9 @@
         "finish_first",
         in_specs=[SCALAR] + [WHOLE] * 7,
         out_specs=[HBM, WHOLE],
-        out_shape=[
-            jax.ShapeDtypeStruct((2 * rows, columns), BF16),
-            near((4, rows, width), F32),
-        ],
-        scratch_shapes=[pltpu.VMEM((4, rows, width), BF16), pltpu.SemaphoreType.DMA((4,))],
-    )(me, *pieces, volterra, edge, coupling)
+        out_shape=[jax.ShapeDtypeStruct((2 * rows, columns), BF16), near((3, rows, width), F32)],
+        scratch_shapes=[pltpu.VMEM((3, rows, width), BF16), pltpu.SemaphoreType.DMA((4,))],
+    )(me, *pieces, g_own, volterra, edge, coupling)
 
 
 def memory_terms(pieces, volterra):
@@ -323,24 +344,24 @@
     return call(kernel, "ordered", in_specs=[WHOLE, FAR], out_specs=WHOLE, out_shape=near(x.shape, x.dtype))(x, after)
 
 
-def finish_second(me, last, terms, volterra, cubic, shares, coupling, g_first, bits):
+def finish_second(me, last, term_own, terms, volterra, cubic_own, cubic, shares, coupling, g_first, bits):
     rows, width = last.shape
     columns = coupling.shape[1]
     everyone = shares.shape[0]
 
-    def kernel(me_ref, last, terms, w, cubic, shares, coupling, _, g_out, sigma, g_held, s_held, sems):
+    def kernel(me_ref, last, term_own, terms, w, cubic_own, cubic, shares, coupling, _, g_out, sigma, g_held, s_held, sems):
         place = Place(me_ref[0], bits)
         last_term = jnp.dot(w[1, :, :rows], last[...], preferred_element_type=F32)
         sums = jnp.sum(shares[...], axis=2, keepdims=True)
         means = sums[:, 0:1, :]
-        mean = jnp.sum(over_halves(means)) / everyone
+        mean = over_halves(means) * (1.0 / everyone)
         ratio = jnp.sqrt((means + EPS) / (mean + EPS))
         power, series = jnp.ones_like(ratio), jnp.zeros_like(ratio)
         for k, weight in enumerate(BINOMIAL):
             series += weight * sums[:, k + 1 : k + 2, :] * power
             power = power * ratio
-        scale_0 = 1.0 / jnp.sqrt(mean + EPS)
-        scale_1 = 1.0 / jnp.sqrt(jnp.maximum(jnp.sum(over_halves(series)) / everyone, 0.0) + EPS)
+        scale_0 = (1.0 / jnp.sqrt(mean + EPS))[0]
+        scale_1 = (1.0 / jnp.sqrt(jnp.maximum(over_halves(series) * (1.0 / everyone), 0.0) + EPS))[0]
 
         copies = []
 
@@ -352,9 +373,9 @@
 
         for slot in (3, 0, 1, 2):
             at = columns_of(place.quarter_of(slot), width)
-            before = (cubic[slot] * scale_0).astype(BF16)
+            before = ((cubic[slot - 1] if slot else cubic_own[...]) * scale_0).astype(BF16)
             write(before, s_held, slot, sigma, 0, at)
-            g = last_term if slot == 3 else terms[slot]
+            g = last_term if slot == 3 else terms[slot - 1] if slot else term_own[...]
             g += jnp.dot(w[1, :, rows:], before, preferred_element_type=F32)
             write(g.astype(BF16), g_held, slot, g_out, 1, at)
             write((cubed(g, coupling[:, at]) * scale_1).astype(BF16), s_held, 4 + slot, sigma, 1, at)
@@ -364,7 +385,7 @@
     return call(
         kernel,
         "finish_second",
-        in_specs=[SCALAR] + [WHOLE] * 6 + [HBM],
+        in_specs=[SCALAR] + [WHOLE] * 8 + [HBM],
         out_specs=[HBM, HBM],
         out_shape=[jax.ShapeDtypeStruct((2 * rows, columns), BF16)] * 2,
         scratch_shapes=[
@@ -372,8 +393,8 @@
             pltpu.VMEM((8, rows, width), BF16),
             pltpu.SemaphoreType.DMA((12,)),
         ],
-        input_output_aliases={7: 0},
-    )(me, last, terms, volterra, cubic, shares, coupling, g_first)
+        input_output_aliases={9: 0},
+    )(me, last, term_own, terms, volterra, cubic_own, cubic, shares, coupling, g_first)
 
 
 def per_device(past, second, g_hist, sigma_hist, volterra, sigma_edge, coupling):
@@ -405,31 +426,35 @@
 
     send, sigma_0, g_sent, g_kept = first_product(me, sigma_hist, g_hist, rows, half, bits)
     arrived_0 = swap(send, 0)
-    kept_0, sigma_1 = product(me, sigma_0, g_kept, bits, False, sigma_hist=sigma_hist)
+    kept_0, send, sigma_1 = middle_products(me, sigma_0, g_kept, g_sent, sigma_hist, bits)
     sent_0 = passed_on(kept_0, arrived_0)
-    (send,) = product(me, sigma_1, g_sent, bits, True, after=sent_0)
     arrived_1 = swap(send, 0)
-    (kept_1,) = product(me, sigma_1, g_kept, bits, False, after=arrived_1)
+    kept_1 = last_product(me, sigma_1, g_kept, bits, after=arrived_1)
     sent_1 = passed_on(kept_1, arrived_1)
 
     mine, theirs = exchanged(kept_0, arrived_0, sent_0, after=sent_1)
     mine_1, theirs_1 = exchanged(kept_1, arrived_1, sent_1)
-    own_0, response, squares = own_first(me, mine, theirs, volterra, sigma_edge, coupling, bits, after=mine_1)
-    own_1, share = own_second(me, mine_1, theirs_1, volterra, response, squares, coupling, bits)
+    own_0, response, squares, g_own, cubic_own = own_first(
+        me, mine, theirs, volterra, sigma_edge, coupling, bits, after=mine_1
+    )
+    own_1, share, term_own = own_second(me, mine_1, theirs_1, volterra, response, squares, coupling, bits)
 
     rounds = log2(second)
     share = jnp.concatenate([share, widened(share, 0)])
     partner = ordered(swap(own_0, 1), share)
-    pieces = [own_0, partner, swap(own_0, 0), swap(partner, 0)]
-    g_first, cubic = finish_first(me, pieces, volterra, sigma_edge, coupling, bits)
+    pieces = [partner, swap(own_0, 0), swap(partner, 0)]
+    g_first, cubic = finish_first(me, pieces, g_own, volterra, sigma_edge, coupling, bits)
     for level in range(1, rounds):
         share = jnp.concatenate([share, widened(share, level)])
     partner = ordered(swap(own_1, 1), share)
-    terms = memory_terms([own_1, partner, swap(own_1, 0)], volterra)
+    terms = memory_terms([partner, swap(own_1, 0)], volterra)
     last = swap(partner, 0)
     share = joined(share, swap(share, 1), cubic, terms)
     shares = jnp.concatenate([share, swap(share, 0)])
-    return tuple(finish_second(me, last, terms, volterra, cubic, shares, coupling, g_first, bits))
+    results = finish_second(
+        me, last, term_own, terms, volterra, cubic_own, cubic, shares, coupling, g_first, bits
+    )
+    return tuple(results)
 
 
 def solution(mesh):

time: 44.9 us -> 44.5 us (level)
  waiting for transfers between devices: 10.5 us -> 11.6 us
  starting transfers between devices: 17.6 us -> 16.8 us
  Pallas kernels: 15.7 us -> 14.9 us
    ppermute x14, waiting for transfers between devices: 7.36 us -> 8.51 us  [swap(): return lax.ppermute(x, 'past', pairs)]
    ppermute x14, starting transfers between devices: 13.9 us -> 13.4 us  [swap(): return lax.ppermute(x, 'past', pairs)]
    pallas_call x4 -> x3, Pallas kernels: 7.57 us -> 7.28 us  [the longest x1 3.4 us: middle_products(): call(kernel, 'middle_products', in_specs=[SCALAR] + [WHOLE] * 3 + [HBM],...]
  transfers between devices with their start and end apart: 16 -> 16, of which waited for: 7 -> 8; matrix products, arithmetic and copies ran while one was open for 0% -> 0% of each run, Pallas kernels for 19% -> 20%
where the time goes in v10:
time: 44.5 us; the launch traced here: 44.4 us
  starting transfers between devices  16.8 us (38%)
  Pallas kernels  14.9 us (33%)
  waiting for transfers between devices  11.6 us (26%)
  between operations  0.78 us (2%)
    ppermute x14, starting transfers between devices, swap(): return lax.ppermute(x, 'past', pairs)  13.4 us
    ppermute x14, waiting for transfers between devices, swap(): return lax.ppermute(x, 'past', pairs)  8.51 us
    ppermute x2, starting transfers between devices, widened(): lax.ppermute(share, 'second', [(z, z ^ 1 << level) for z in range(second)])  3.42 us
    pallas_call x1, Pallas kernels, middle_products(): call(kernel, 'middle_products', in_specs=[SCALAR] + [WHOLE] * 3 + [HBM],...  3.4 us
    pallas_call x1, Pallas kernels, first_product(): call(kernel, 'first_product', in_specs=[SCALAR, HBM, HBM], out_specs=[WHO...  3.23 us
    ppermute x2, waiting for transfers between devices, widened(): lax.ppermute(share, 'second', [(z, z ^ 1 << level) for z in range(second)])  3.13 us
    pallas_call x1, Pallas kernels, finish_second(): call(kernel, 'finish_second', in_specs=[SCALAR] + [WHOLE] * 8 + [HBM], ou...  2.61 us
    pallas_call x1, Pallas kernels, finish_first(): call(kernel, 'finish_first', in_specs=[SCALAR] + [WHOLE] * 7, out_specs=[...  1.84 us
  transfers between devices with their start and end apart: 16, of which 8 were waited for; matrix products, arithmetic and copies ran while one was open for 0% of the time, Pallas kernels for 20%

profile of v10, /device:TPU:0, one launch (start us, length us, event | category | flops | bytes accessed | tf_op | source)
XLA Modules:
  0.0 44.4 jit_solution(2431080740368852333)
XLA Ops:
  0.6 3.2 %first_product.1 = (bf16[2,512,256]{2,1,0:T(8,128)(2,1)S(1)}, bf16[512,2048]{1,0:T(8,128)(2,1)S(1)}, bf16[2048,512]{1,0:T(8,128)(2,1)S(1)}, bf16[2048,512]{1,0:T(8,128)(2,1)S(1)}) custom-call(s32[1]{0:T(128)} %bitcast.me_ref, bf16[1024,2048]{1,0:T(8,128)(2,1)} %source.1, bf16[2048,1024]{1,0:T(8,128)(2,1)} %g_ref.1), custom_call_target="tpu_custom_call" | custom-call | flops 1024 | bytes 1024 | tf_op jit(solution)/shard_map/first_product/pallas_call | solution.py:108
  3.9 0.5 %collective-permute-start.3 = (bf16[2,512,256]{2,1,0:T(8,128)(2,1)S(1)}, bf16[2,512,256]{2,1,0:T(8,128)(2,1)S(1)}, u32[]{:S(2)}, u32[]{:S(2)}) collective-permute-start(bf16[2,512,256]{2,1,0:T(8,128)(2,1)S(1)} %get-tuple-element.25), channel_id=1, source_target_pairs={{0,4},{4,0},{8,12},{12,8},{16,20},{20,16},{24,28},{28,24},{1,5},{5... | collective-permute-start | bytes 1572872 | tf_op jit(solution)/shard_map/ppermute | solution.py:411
  4.4 3.4 %middle_products.1 = (f32[2,512,256]{2,1,0:T(8,128)S(1)}, bf16[2,512,256]{2,1,0:T(8,128)(2,1)S(1)}, bf16[512,2048]{1,0:T(8,128)(2,1)S(1)}) custom-call(s32[1]{0:T(128)} %bitcast.me_ref, bf16[512,2048]{1,0:T(8,128)(2,1)S(1)} %get-tuple-element.19.sigma, bf16[2048,512]{1,0:T(8,128)(2,1)S(1)} %get-tuple-element.20.g_kept, ...), custom_call_target="tpu_custom_call" | custom-call | flops 1024 | bytes 1024 | tf_op jit(solution)/shard_map/middle_products/pallas_call | solution.py:150
  7.8 0.1 collective-permute-start
  8.0 3.0 %collective-permute-start.4 = (bf16[512,256]{1,0:T(8,128)(2,1)S(1)}, bf16[512,256]{1,0:T(8,128)(2,1)S(1)}, u32[]{:S(2)}, u32[]{:S(2)}) collective-permute-start(bf16[512,256]{1,0:T(8,128)(2,1)S(1)} %fusion.4), channel_id=1, source_target_pairs={{0,8},{4,20},{8,0},{12,28},{16,24},{20,4},{24,16},{28,12},{1,9},{5... | collective-permute-start | bytes 786440 | tf_op jit(solution)/shard_map/ppermute | solution.py:411
  11.0 1.3 %last_product.1 = f32[2,512,256]{2,1,0:T(8,128)S(1)} custom-call(s32[1]{0:T(128)} %bitcast.me_ref, bf16[512,2048]{1,0:T(8,128)(2,1)S(1)} %get-tuple-element.22.sigma, bf16[2048,512]{1,0:T(8,128)(2,1)S(1)} %get-tuple-element.20.g_kept, bf16[2,512,256]{2,1,0:T(8,128)(2,1)S(1)} %collective-permute-done._), custom_call_target="tpu_custom_call" | custom-call | flops 1024 | bytes 1024 | tf_op jit(solution)/shard_map/last_product/pallas_call | solution.py:166
  12.4 1.5 %collective-permute-start.1 = (bf16[512,256]{1,0:T(8,128)(2,1)S(1)}, bf16[512,256]{1,0:T(8,128)(2,1)S(1)}, u32[]{:S(2)}, u32[]{:S(2)}) collective-permute-start(bf16[512,256]{1,0:T(8,128)(2,1)S(1)} %fusion.5._), channel_id=1, source_target_pairs={{0,8},{4,20},{8,0},{12,28},{16,24},{20,4},{24,16},{28,12},{1,9},{5... | collective-permute-start | bytes 786440 | tf_op jit(solution)/shard_map/ppermute | solution.py:411
  13.8 1.5 %collective-permute-done.4.more = bf16[512,256]{1,0:T(8,128)(2,1)S(1)} collective-permute-done((bf16[512,256]{1,0:T(8,128)(2,1)S(1)}, bf16[512,256]{1,0:T(8,128)(2,1)S(1)}, u32[]{:S(2)}, u32[]{:S(2)}) %collective-permute-start.4) | collective-permute-done | bytes 262176 | tf_op jit(solution)/shard_map/ppermute | solution.py:411
  15.3 0.1 combined.1.mine
  15.4 2.1 %collective-permute-start.5 = (bf16[512,256]{1,0:T(8,128)(2,1)S(1)}, bf16[512,256]{1,0:T(8,128)(2,1)S(1)}, u32[]{:S(2)}, u32[]{:S(2)}) collective-permute-start(bf16[512,256]{1,0:T(8,128)(2,1)S(1)} %combined.1.mine), channel_id=1, source_target_pairs={{0,16},{4,12},{8,24},{12,4},{16,0},{20,28},{24,8},{28,20},{1,17},{... | collective-permute-start | bytes 786440 | tf_op jit(solution)/shard_map/ppermute | solution.py:411
  17.5 2.4 %collective-permute-done.1 = bf16[512,256]{1,0:T(8,128)(2,1)S(1)} collective-permute-done((bf16[512,256]{1,0:T(8,128)(2,1)S(1)}, bf16[512,256]{1,0:T(8,128)(2,1)S(1)}, u32[]{:S(2)}, u32[]{:S(2)}) %collective-permute-start.1) | collective-permute-done | bytes 262176 | tf_op jit(solution)/shard_map/ppermute | solution.py:411
  20.0 0.1 fusion.3._.mine
  20.1 1.4 %collective-permute-start.2 = (bf16[512,256]{1,0:T(8,128)(2,1)S(1)}, bf16[512,256]{1,0:T(8,128)(2,1)S(1)}, u32[]{:S(2)}, u32[]{:S(2)}) collective-permute-start(bf16[512,256]{1,0:T(8,128)(2,1)S(1)} %fusion.3._.mine), channel_id=1, source_target_pairs={{0,16},{4,12},{8,24},{12,4},{16,0},{20,28},{24,8},{28,20},{1,17},{... | collective-permute-start | bytes 786440 | tf_op jit(solution)/shard_map/ppermute | solution.py:411
  21.4 0.5 %collective-permute-done.5.theirs = bf16[512,256]{1,0:T(8,128)(2,1)S(1)} collective-permute-done((bf16[512,256]{1,0:T(8,128)(2,1)S(1)}, bf16[512,256]{1,0:T(8,128)(2,1)S(1)}, u32[]{:S(2)}, u32[]{:S(2)}) %collective-permute-start.5) | collective-permute-done | bytes 262176 | tf_op jit(solution)/shard_map/ppermute | solution.py:411
  21.9 1.2 %own_first.1 = (bf16[512,256]{1,0:T(8,128)(2,1)S(1)}, f32[512,256]{1,0:T(8,128)S(1)}, f32[1,128]{1,0:T(1,128)S(1)}, bf16[512,256]{1,0:T(8,128)(2,1)S(1)}, f32[512,256]{1,0:T(8,128)S(1)}) custom-call(s32[1]{0:T(128)} %bitcast.me_ref, bf16[512,256]{1,0:T(8,128)(2,1)S(1)} %combined.1.mine, bf16[512,256]{1,0:T(8,128)(2,1)S(1)} %collective-permute-done.5.theirs, ...), custom_call_target="tpu_custom_call" | custom-call | flops 1024 | bytes 1024 | tf_op jit(solution)/shard_map/own_first/pallas_call | solution.py:228
  23.1 2.1 %collective-permute-start.11 = (bf16[512,256]{1,0:T(8,128)(2,1)S(1)}, bf16[512,256]{1,0:T(8,128)(2,1)S(1)}, u32[]{:S(2)}, u32[]{:S(2)}) collective-permute-start(bf16[512,256]{1,0:T(8,128)(2,1)S(1)} %get-tuple-element.32), channel_id=1, source_target_pairs={{0,8},{4,20},{8,0},{12,28},{16,24},{20,4},{24,16},{28,12},{1,9},{5... | collective-permute-start | bytes 786440 | tf_op jit(solution)/shard_map/ppermute | solution.py:411
  25.1 2.3 %collective-permute-done.2.theirs = bf16[512,256]{1,0:T(8,128)(2,1)S(1)} collective-permute-done((bf16[512,256]{1,0:T(8,128)(2,1)S(1)}, bf16[512,256]{1,0:T(8,128)(2,1)S(1)}, u32[]{:S(2)}, u32[]{:S(2)}) %collective-permute-start.2) | collective-permute-done | bytes 262176 | tf_op jit(solution)/shard_map/ppermute | solution.py:411
  27.4 0.8 %own_second.1 = (bf16[512,256]{1,0:T(8,128)(2,1)S(1)}, f32[1,8,128]{2,1,0:T(8,128)S(1)}, f32[512,256]{1,0:T(8,128)S(1)}) custom-call(s32[1]{0:T(128)} %bitcast.me_ref, bf16[512,256]{1,0:T(8,128)(2,1)S(1)} %fusion.3._.mine, bf16[512,256]{1,0:T(8,128)(2,1)S(1)} %collective-permute-done.2.theirs, bf16[2,512,1024]{2,1,0:T(8,128)(2,1)S(1)} %copy-done, ...), custom_call_target="tpu_custom_call" | custom-call | flops 1024 | bytes 1024 | tf_op jit(solution)/shard_map/own_second/pallas_call | solution.py:265
  28.2 1.2 %collective-permute-start.7 = (f32[1,8,128]{2,1,0:T(8,128)S(1)}, f32[1,8,128]{2,1,0:T(8,128)S(1)}, u32[]{:S(2)}, u32[]{:S(2)}) collective-permute-start(f32[1,8,128]{2,1,0:T(8,128)S(1)} %get-tuple-element.29), channel_id=1, source_target_pairs={{0,1},{1,0},{2,3},{3,2},{4,5},{5,4},{6,7},{7,6},{8,9},{9,8},{10,11... | collective-permute-start | bytes 12296 | tf_op jit(solution)/shard_map/ppermute | solution.py:425
  29.4 1.2 %collective-permute-start.6 = (bf16[512,256]{1,0:T(8,128)(2,1)S(1)}, bf16[512,256]{1,0:T(8,128)(2,1)S(1)}, u32[]{:S(2)}, u32[]{:S(2)}) collective-permute-start(bf16[512,256]{1,0:T(8,128)(2,1)S(1)} %get-tuple-element.28), channel_id=1, source_target_pairs={{0,8},{4,20},{8,0},{12,28},{16,24},{20,4},{24,16},{28,12},{1,9},{5... | collective-permute-start | bytes 786440 | tf_op jit(solution)/shard_map/ppermute | solution.py:411
  30.7 0.5 %collective-permute-start.12 = (bf16[512,256]{1,0:T(8,128)(2,1)S(1)}, bf16[512,256]{1,0:T(8,128)(2,1)S(1)}, u32[]{:S(2)}, u32[]{:S(2)}) collective-permute-start(bf16[512,256]{1,0:T(8,128)(2,1)S(1)} %get-tuple-element.32), channel_id=1, source_target_pairs={{0,4},{4,0},{8,12},{12,8},{16,20},{20,16},{24,28},{28,24},{1,5},{5... | collective-permute-start | bytes 786440 | tf_op jit(solution)/shard_map/ppermute | solution.py:411
  31.2 0.7 %collective-permute-done.7 = f32[1,8,128]{2,1,0:T(8,128)S(1)} collective-permute-done((f32[1,8,128]{2,1,0:T(8,128)S(1)}, f32[1,8,128]{2,1,0:T(8,128)S(1)}, u32[]{:S(2)}, u32[]{:S(2)}) %collective-permute-start.7) | collective-permute-done | bytes 4128 | tf_op jit(solution)/shard_map/ppermute | solution.py:425
  31.9 0.1 collective-permute-start.13
  32.0 2.2 %collective-permute-start.8 = (f32[2,8,128]{2,1,0:T(8,128)S(1)}, f32[2,8,128]{2,1,0:T(8,128)S(1)}, u32[]{:S(2)}, u32[]{:S(2)}) collective-permute-start(f32[2,8,128]{2,1,0:T(8,128)S(1)} %get-tuple-element.36._), channel_id=1, source_target_pairs={{0,2},{1,3},{2,0},{3,1},{4,6},{5,7},{6,4},{7,5},{8,10},{9,11},{10,... | collective-permute-start | bytes 24584 | tf_op jit(solution)/shard_map/ppermute | solution.py:425
  34.2 2.4 %collective-permute-done.8 = f32[2,8,128]{2,1,0:T(8,128)S(1)} collective-permute-done((f32[2,8,128]{2,1,0:T(8,128)S(1)}, f32[2,8,128]{2,1,0:T(8,128)S(1)}, u32[]{:S(2)}, u32[]{:S(2)}) %collective-permute-start.8) | collective-permute-done | bytes 8224 | tf_op jit(solution)/shard_map/ppermute | solution.py:425
  36.7 0.1 collective-permute-start.9
  36.7 0.8 %collective-permute-start.14 = (f32[4,8,128]{2,1,0:T(8,128)S(1)}, f32[4,8,128]{2,1,0:T(8,128)S(1)}, u32[]{:S(2)}, u32[]{:S(2)}) collective-permute-start(f32[4,8,128]{2,1,0:T(8,128)S(1)} %constant_dynamic-update-slice_fusion.2._.a), channel_id=1, source_target_pairs={{0,8},{4,20},{8,0},{12,28},{16,24},{20,4},{24,16},{28,12},{1,9},{5... | collective-permute-start | bytes 49160 | tf_op jit(solution)/shard_map/ppermute | solution.py:411
  37.6 0.4 memory_terms.1.refs_1_.terms
  38.1 1.8 %finish_first.1 = (bf16[1024,1024]{1,0:T(8,128)(2,1)}, f32[3,512,256]{2,1,0:T(8,128)S(1)}) custom-call(s32[1]{0:T(128)} %bitcast.me_ref, bf16[512,256]{1,0:T(8,128)(2,1)S(1)} %ordered.3.refs_0_, bf16[512,256]{1,0:T(8,128)(2,1)S(1)} %collective-permute-done.12.refs_1_, bf16[512,256]{1,0:T(8,128)(2,1)S(1)} %collective-permute-done.13.refs_2_, ...), custom_call_target="tpu_custom_call" | custom-call | flops 1024 | bytes 1024 | tf_op jit(solution)/shard_map/finish_first/pallas_call | solution.py:299
  39.9 0.6 %collective-permute-done.14.b = f32[4,8,128]{2,1,0:T(8,128)S(1)} collective-permute-done((f32[4,8,128]{2,1,0:T(8,128)S(1)}, f32[4,8,128]{2,1,0:T(8,128)S(1)}, u32[]{:S(2)}, u32[]{:S(2)}) %collective-permute-start.14) | collective-permute-done | bytes 16416 | tf_op jit(solution)/shard_map/ppermute | solution.py:411
  40.6 1.2 %collective-permute-done.15 = f32[8,8,128]{2,1,0:T(8,128)S(1)} collective-permute-done((f32[8,8,128]{2,1,0:T(8,128)S(1)}, f32[8,8,128]{2,1,0:T(8,128)S(1)}, u32[]{:S(2)}, u32[]{:S(2)}) %collective-permute-start.15) | collective-permute-done | bytes 32800 | tf_op jit(solution)/shard_map/ppermute | solution.py:411
  41.8 2.6 %finish_second.1 = (bf16[1024,1024]{1,0:T(8,128)(2,1)}, bf16[1024,1024]{1,0:T(8,128)(2,1)}) custom-call(s32[1]{0:T(128)} %bitcast.me_ref, bf16[512,256]{1,0:T(8,128)(2,1)S(1)} %collective-permute-done.9.last, f32[512,256]{1,0:T(8,128)S(1)} %get-tuple-element.30.term_own, ...), custom_call_target="tpu_custom_call", output_to_operand_aliasing={{0}: (9, {})} | custom-call | flops 1024 | bytes 1024 | tf_op jit(solution)/shard_map/finish_second/pallas_call | solution.py:385
  (25 shorter events, 0.2 us)
Async XLA Ops:
  3.9 4.0 %collective-permute-start.3 = (bf16[2,512,256]{2,1,0:T(8,128)(2,1)S(1)}, bf16[2,512,256]{2,1,0:T(8,128)(2,1)S(1)}, u32[]{:S(2)}, u32[]{:S(2)}) collective-permute-start(bf16[2,512,256]{2,1,0:T(8,128)(2,1)S(1)} %get-tuple-element.25), channel_id=1, source_target_pairs={{0,4},{4,0},{8,12},{12,8},{16,20},{20,16},{24,28},{28,24},{1,5},{5... | collective-permute-start | bytes 1572872 | tf_op jit(solution)/shard_map/ppermute | solution.py:411
  7.8 3.2 %collective-permute-start = (bf16[2,512,256]{2,1,0:T(8,128)(2,1)S(1)}, bf16[2,512,256]{2,1,0:T(8,128)(2,1)S(1)}, u32[]{:S(2)}, u32[]{:S(2)}) collective-permute-start(bf16[2,512,256]{2,1,0:T(8,128)(2,1)S(1)} %get-tuple-element.23), channel_id=1, source_target_pairs={{0,4},{4,0},{8,12},{12,8},{16,20},{20,16},{24,28},{28,24},{1,5},{5... | collective-permute-start | bytes 1572872 | tf_op jit(solution)/shard_map/ppermute | solution.py:411
  8.0 7.4 %collective-permute-start.4 = (bf16[512,256]{1,0:T(8,128)(2,1)S(1)}, bf16[512,256]{1,0:T(8,128)(2,1)S(1)}, u32[]{:S(2)}, u32[]{:S(2)}) collective-permute-start(bf16[512,256]{1,0:T(8,128)(2,1)S(1)} %fusion.4), channel_id=1, source_target_pairs={{0,8},{4,20},{8,0},{12,28},{16,24},{20,4},{24,16},{28,12},{1,9},{5... | collective-permute-start | bytes 786440 | tf_op jit(solution)/shard_map/ppermute | solution.py:411
  12.3 9.6 %copy-start = (bf16[2,512,1024]{2,1,0:T(8,128)(2,1)S(1)}, bf16[2,512,1024]{2,1,0:T(8,128)(2,1)}, u32[]{:S(2)}) copy-start(bf16[2,512,1024]{2,1,0:T(8,128)(2,1)} %w.5) | copy-start | bytes 6291460
  12.4 9.6 %copy-start.1 = (bf16[512,1024]{1,0:T(8,128)(2,1)S(1)}, bf16[512,1024]{1,0:T(8,128)(2,1)}, u32[]{:S(2)}) copy-start(bf16[512,1024]{1,0:T(8,128)(2,1)} %refs_5_.1) | copy-start | bytes 3145732
  12.4 9.5 %copy-start.2 = (f32[32,1024]{1,0:T(8,128)S(1)}, f32[32,1024]{1,0:T(8,128)}, u32[]{:S(2)}) copy-start(f32[32,1024]{1,0:T(8,128)} %coupling.5) | copy-start | bytes 393220
  12.4 7.6 %collective-permute-start.1 = (bf16[512,256]{1,0:T(8,128)(2,1)S(1)}, bf16[512,256]{1,0:T(8,128)(2,1)S(1)}, u32[]{:S(2)}, u32[]{:S(2)}) collective-permute-start(bf16[512,256]{1,0:T(8,128)(2,1)S(1)} %fusion.5._), channel_id=1, source_target_pairs={{0,8},{4,20},{8,0},{12,28},{16,24},{20,4},{24,16},{28,12},{1,9},{5... | collective-permute-start | bytes 786440 | tf_op jit(solution)/shard_map/ppermute | solution.py:411
  15.4 6.5 %collective-permute-start.5 = (bf16[512,256]{1,0:T(8,128)(2,1)S(1)}, bf16[512,256]{1,0:T(8,128)(2,1)S(1)}, u32[]{:S(2)}, u32[]{:S(2)}) collective-permute-start(bf16[512,256]{1,0:T(8,128)(2,1)S(1)} %combined.1.mine), channel_id=1, source_target_pairs={{0,16},{4,12},{8,24},{12,4},{16,0},{20,28},{24,8},{28,20},{1,17},{... | collective-permute-start | bytes 786440 | tf_op jit(solution)/shard_map/ppermute | solution.py:411
  20.1 7.3 %collective-permute-start.2 = (bf16[512,256]{1,0:T(8,128)(2,1)S(1)}, bf16[512,256]{1,0:T(8,128)(2,1)S(1)}, u32[]{:S(2)}, u32[]{:S(2)}) collective-permute-start(bf16[512,256]{1,0:T(8,128)(2,1)S(1)} %fusion.3._.mine), channel_id=1, source_target_pairs={{0,16},{4,12},{8,24},{12,4},{16,0},{20,28},{24,8},{28,20},{1,17},{... | collective-permute-start | bytes 786440 | tf_op jit(solution)/shard_map/ppermute | solution.py:411
  23.1 8.8 %collective-permute-start.11 = (bf16[512,256]{1,0:T(8,128)(2,1)S(1)}, bf16[512,256]{1,0:T(8,128)(2,1)S(1)}, u32[]{:S(2)}, u32[]{:S(2)}) collective-permute-start(bf16[512,256]{1,0:T(8,128)(2,1)S(1)} %get-tuple-element.32), channel_id=1, source_target_pairs={{0,8},{4,20},{8,0},{12,28},{16,24},{20,4},{24,16},{28,12},{1,9},{5... | collective-permute-start | bytes 786440 | tf_op jit(solution)/shard_map/ppermute | solution.py:411
  28.2 3.7 %collective-permute-start.7 = (f32[1,8,128]{2,1,0:T(8,128)S(1)}, f32[1,8,128]{2,1,0:T(8,128)S(1)}, u32[]{:S(2)}, u32[]{:S(2)}) collective-permute-start(f32[1,8,128]{2,1,0:T(8,128)S(1)} %get-tuple-element.29), channel_id=1, source_target_pairs={{0,1},{1,0},{2,3},{3,2},{4,5},{5,4},{6,7},{7,6},{8,9},{9,8},{10,11... | collective-permute-start | bytes 12296 | tf_op jit(solution)/shard_map/ppermute | solution.py:425
  29.4 7.2 %collective-permute-start.6 = (bf16[512,256]{1,0:T(8,128)(2,1)S(1)}, bf16[512,256]{1,0:T(8,128)(2,1)S(1)}, u32[]{:S(2)}, u32[]{:S(2)}) collective-permute-start(bf16[512,256]{1,0:T(8,128)(2,1)S(1)} %get-tuple-element.28), channel_id=1, source_target_pairs={{0,8},{4,20},{8,0},{12,28},{16,24},{20,4},{24,16},{28,12},{1,9},{5... | collective-permute-start | bytes 786440 | tf_op jit(solution)/shard_map/ppermute | solution.py:411
  30.7 6.9 %collective-permute-start.10 = (bf16[512,256]{1,0:T(8,128)(2,1)S(1)}, bf16[512,256]{1,0:T(8,128)(2,1)S(1)}, u32[]{:S(2)}, u32[]{:S(2)}) collective-permute-start(bf16[512,256]{1,0:T(8,128)(2,1)S(1)} %get-tuple-element.28), channel_id=1, source_target_pairs={{0,4},{4,0},{8,12},{12,8},{16,20},{20,16},{24,28},{28,24},{1,5},{5... | collective-permute-start | bytes 786440 | tf_op jit(solution)/shard_map/ppermute | solution.py:411
  30.7 7.4 %collective-permute-start.12 = (bf16[512,256]{1,0:T(8,128)(2,1)S(1)}, bf16[512,256]{1,0:T(8,128)(2,1)S(1)}, u32[]{:S(2)}, u32[]{:S(2)}) collective-permute-start(bf16[512,256]{1,0:T(8,128)(2,1)S(1)} %get-tuple-element.32), channel_id=1, source_target_pairs={{0,4},{4,0},{8,12},{12,8},{16,20},{20,16},{24,28},{28,24},{1,5},{5... | collective-permute-start | bytes 786440 | tf_op jit(solution)/shard_map/ppermute | solution.py:411
  31.9 6.1 %collective-permute-start.13 = (bf16[512,256]{1,0:T(8,128)(2,1)S(1)}, bf16[512,256]{1,0:T(8,128)(2,1)S(1)}, u32[]{:S(2)}, u32[]{:S(2)}) collective-permute-start(bf16[512,256]{1,0:T(8,128)(2,1)S(1)} %ordered.3.refs_0_), channel_id=1, source_target_pairs={{0,4},{4,0},{8,12},{12,8},{16,20},{20,16},{24,28},{28,24},{1,5},{5... | collective-permute-start | bytes 786440 | tf_op jit(solution)/shard_map/ppermute | solution.py:411
  32.0 4.6 %collective-permute-start.8 = (f32[2,8,128]{2,1,0:T(8,128)S(1)}, f32[2,8,128]{2,1,0:T(8,128)S(1)}, u32[]{:S(2)}, u32[]{:S(2)}) collective-permute-start(f32[2,8,128]{2,1,0:T(8,128)S(1)} %get-tuple-element.36._), channel_id=1, source_target_pairs={{0,2},{1,3},{2,0},{3,1},{4,6},{5,7},{6,4},{7,5},{8,10},{9,11},{10,... | collective-permute-start | bytes 24584 | tf_op jit(solution)/shard_map/ppermute | solution.py:425
  36.7 5.1 %collective-permute-start.9 = (bf16[512,256]{1,0:T(8,128)(2,1)S(1)}, bf16[512,256]{1,0:T(8,128)(2,1)S(1)}, u32[]{:S(2)}, u32[]{:S(2)}) collective-permute-start(bf16[512,256]{1,0:T(8,128)(2,1)S(1)} %ordered.2.refs_0_), channel_id=1, source_target_pairs={{0,4},{4,0},{8,12},{12,8},{16,20},{20,16},{24,28},{28,24},{1,5},{5... | collective-permute-start | bytes 786440 | tf_op jit(solution)/shard_map/ppermute | solution.py:411
  36.7 3.8 %collective-permute-start.14 = (f32[4,8,128]{2,1,0:T(8,128)S(1)}, f32[4,8,128]{2,1,0:T(8,128)S(1)}, u32[]{:S(2)}, u32[]{:S(2)}) collective-permute-start(f32[4,8,128]{2,1,0:T(8,128)S(1)} %constant_dynamic-update-slice_fusion.2._.a), channel_id=1, source_target_pairs={{0,8},{4,20},{8,0},{12,28},{16,24},{20,4},{24,16},{28,12},{1,9},{5... | collective-permute-start | bytes 49160 | tf_op jit(solution)/shard_map/ppermute | solution.py:411
  40.5 1.2 %collective-permute-start.15 = (f32[8,8,128]{2,1,0:T(8,128)S(1)}, f32[8,8,128]{2,1,0:T(8,128)S(1)}, u32[]{:S(2)}, u32[]{:S(2)}) collective-permute-start(f32[8,8,128]{2,1,0:T(8,128)S(1)} %joined.1), channel_id=1, source_target_pairs={{0,4},{4,0},{8,12},{12,8},{16,20},{20,16},{24,28},{28,24},{1,5},{5... | collective-permute-start | bytes 98312 | tf_op jit(solution)/shard_map/ppermute | solution.py:411

commit v11 on v10

--- a/solution.py
+++ b/solution.py
@@ -59,16 +59,20 @@
         return (self.core ^ 1) * 2 + (self.other_side ^ (slot - 2))
 
 
-def first_product(me, sigma_hist, g_hist, rows, half, bits):
-    depth = g_hist.shape[0]
-    quarter = half // 2
-    chunks, parts = 4, 4
-    chunk = depth // chunks
-
-    def kernel(me_ref, sigma_ref, g_ref, out, sigma, g_sent, g_kept, total, sems):
-        place = Place(me_ref[0], bits)
-        sent_at = pl.ds(pl.multiple_of((place.core ^ 1) * half, half), half)
-        kept_at = pl.ds(pl.multiple_of(place.core * half, half), half)
+def halves_to(out, value, side):
+    quarter = out.shape[2]
+    for j in range(2):
+        out[1 ^ j ^ side] = value[:, j * quarter : (j + 1) * quarter].astype(out.dtype)
+
+
+def first_products(me, sigma_hist, g_hist, rows, bits):
+    depth, columns = g_hist.shape
+    half = columns // 2
+    parts = 4
+    eighth = depth // 8
+    chunks = [(0, 2 * eighth), (2 * eighth, 3 * eighth), (5 * eighth, 3 * eighth)]
+
+    def kernel(me_ref, sigma_ref, g_ref, sent, kept, sigma_next, g, sigma, total, sems):
         started = []
 
         def load(source, target):
@@ -77,99 +81,75 @@
             return started[-1]
 
         pieces = []
-        for k in range(chunks):
-            deep = pl.ds(k * chunk, chunk)
+        for start, size in chunks:
             piece = []
             for i in range(parts):
                 here = pl.ds(i * (rows // parts), rows // parts)
+                deep = pl.ds(start, size)
                 piece.append(load(sigma_ref.at[here, deep], sigma.at[here, deep]))
-                here = pl.ds(k * chunk + i * (chunk // parts), chunk // parts)
-                piece.append(load(g_ref.at[here, sent_at], g_sent.at[here, :]))
+                here = pl.ds(start + i * (size // parts), size // parts)
+                piece.append(load(g_ref.at[here, :], g.at[here, :]))
             pieces.append(piece)
         ahead = []
-        for i in range(8):
-            here = pl.ds(i * (depth // 8), depth // 8)
-            ahead.append(load(g_ref.at[here, kept_at], g_kept.at[here, :]))
-        for k in range(chunks):
+        for i in range(2 * parts):
+            here = pl.ds(i * (rows // (2 * parts)), rows // (2 * parts))
+            there = pl.ds(rows + i * (rows // (2 * parts)), rows // (2 * parts))
+            ahead.append(load(sigma_ref.at[there, :], sigma_next.at[here, :]))
+        for k, (start, size) in enumerate(chunks):
             for copy in pieces[k]:
                 copy.wait()
-            deep = pl.ds(k * chunk, chunk)
-            term = jnp.dot(sigma[:, deep], g_sent[deep, :], preferred_element_type=F32)
+            deep = pl.ds(start, size)
+            term = jnp.dot(sigma[:, deep], g[deep, :], preferred_element_type=F32)
             if k == 0:
                 total[...] = term
-            elif k < chunks - 1:
+            else:
                 total[...] += term
-            else:
-                term += total[...]
-                halves_to(out, term, place.other_side)
+        place = Place(me_ref[0], bits)
+        halves_to(sent, total[:, half_of(place.core ^ 1, half)], place.other_side)
+        halves_to(kept, total[:, half_of(place.core, half)], place.side)
         for copy in ahead:
             copy.wait()
 
     return call(
         kernel,
-        "first_product",
+        "first_products",
         in_specs=[SCALAR, HBM, HBM],
         out_specs=[WHOLE] * 4,
         out_shape=[
-            near((2, rows, quarter), BF16),
+            near((2, rows, half // 2), BF16),
+            near((2, rows, half // 2), F32),
             near((rows, depth), BF16),
-            near((depth, half), BF16),
-            near((depth, half), BF16),
+            near((depth, columns), BF16),
         ],
-        scratch_shapes=[pltpu.VMEM((rows, half), F32), pltpu.SemaphoreType.DMA((2 * chunks * parts + 8,))],
+        scratch_shapes=[
+            pltpu.VMEM((rows, depth), BF16),
+            pltpu.VMEM((rows, columns), F32),
+            pltpu.SemaphoreType.DMA((2 * parts * (len(chunks) + 1),)),
+        ],
     )(me, far(sigma_hist), far(g_hist))
 
 
-def halves_to(out, value, side, here=slice(None)):
-    quarter = out.shape[2]
-    for j in range(2):
-        out[1 ^ j ^ side, here, :] = value[:, j * quarter : (j + 1) * quarter].astype(out.dtype)
-
-
-def middle_products(me, sigma, g_kept, g_sent, sigma_hist, bits):
-    rows, depth = sigma.shape
-    half = g_kept.shape[1]
-    parts, chunks = 8, 2
-
-    def kernel(me_ref, sigma, g_kept, g_sent, source, kept, sent, target, sems):
-        copies = []
-        for i in range(parts):
-            here = pl.ds(i * (rows // parts), rows // parts)
-            there = pl.ds(rows + i * (rows // parts), rows // parts)
-            copies.append(pltpu.make_async_copy(source.at[there, :], target.at[here, :], sems.at[i]))
-            copies[-1].start()
+def half_of(core, half):
+    return pl.ds(pl.multiple_of(core * half, half), half)
+
+
+def product(me, sigma, g, bits, send, after=None):
+    rows, half = sigma.shape[0], g.shape[1] // 2
+
+    def kernel(me_ref, sigma, g, *refs):
         place = Place(me_ref[0], bits)
-        halves_to(kept, jnp.dot(sigma[...], g_kept[...], preferred_element_type=F32), place.side)
-        for k in range(chunks):
-            for copy in copies[k * (parts // chunks) : (k + 1) * (parts // chunks)]:
-                copy.wait()
-            here = pl.ds(k * (rows // chunks), rows // chunks)
-            term = jnp.dot(target[here, :], g_sent[...], preferred_element_type=F32)
-            halves_to(sent, term, place.other_side, here)
-
-    return call(
-        kernel,
-        "middle_products",
-        in_specs=[SCALAR] + [WHOLE] * 3 + [HBM],
-        out_specs=[WHOLE] * 3,
-        out_shape=[near((2, rows, half // 2), F32), near((2, rows, half // 2), BF16), near((rows, depth), BF16)],
-        scratch_shapes=[pltpu.SemaphoreType.DMA((parts,))],
-    )(me, sigma, g_kept, g_sent, far(sigma_hist))
-
-
-def last_product(me, sigma, g_kept, bits, after):
-    rows, half = sigma.shape[0], g_kept.shape[1]
-
-    def kernel(me_ref, sigma, g_kept, _, kept):
-        halves_to(kept, jnp.dot(sigma[...], g_kept[...], preferred_element_type=F32), Place(me_ref[0], bits).side)
-
-    return call(
-        kernel,
-        "last_product",
-        in_specs=[SCALAR, WHOLE, WHOLE, FAR],
+        columns = half_of(place.core ^ int(send), half)
+        term = jnp.dot(sigma[...], g[:, columns], preferred_element_type=F32)
+        halves_to(refs[-1], term, place.other_side if send else place.side)
+
+    extra = [] if after is None else [after]
+    return call(
+        kernel,
+        "memory_product",
+        in_specs=[SCALAR, WHOLE, WHOLE] + [FAR] * len(extra),
         out_specs=WHOLE,
-        out_shape=near((2, rows, half // 2), F32),
-    )(me, sigma, g_kept, after)
+        out_shape=near((2, rows, half // 2), BF16 if send else F32),
+    )(me, sigma, g, *extra)
 
 
 def combined(kept, arrived, more, after):
@@ -401,7 +381,6 @@
     blocks, rows = volterra.shape[:2]
     assert blocks == 2 and past >= 8
     bits = log2(past)
-    half = g_hist.shape[1] // 2
     me = lax.axis_index("past").astype(jnp.int32).reshape(1)
     even = list(range(bits))
     odd = even[:1] + even[1:][::-1]
@@ -424,12 +403,11 @@
     def widened(share, level):
         return lax.ppermute(share, "second", [(z, z ^ (1 << level)) for z in range(second)])
 
-    send, sigma_0, g_sent, g_kept = first_product(me, sigma_hist, g_hist, rows, half, bits)
+    send, kept_0, sigma_1, g_near = first_products(me, sigma_hist, g_hist, rows, bits)
     arrived_0 = swap(send, 0)
-    kept_0, send, sigma_1 = middle_products(me, sigma_0, g_kept, g_sent, sigma_hist, bits)
+    arrived_1 = swap(product(me, sigma_1, g_near, bits, True), 0)
     sent_0 = passed_on(kept_0, arrived_0)
-    arrived_1 = swap(send, 0)
-    kept_1 = last_product(me, sigma_1, g_kept, bits, after=arrived_1)
+    kept_1 = product(me, sigma_1, g_near, bits, False, after=arrived_1)
     sent_1 = passed_on(kept_1, arrived_1)
 
     mine, theirs = exchanged(kept_0, arrived_0, sent_0, after=sent_1)

time: 44.5 us -> 43.5 us (0.978)
  Pallas kernels: 14.9 us -> 14.1 us
  starting transfers between devices: 16.8 us -> 16.3 us
    pallas_call x3, Pallas kernels: 7.91 us -> 7.06 us  [the longest x1 4.5 us: first_products(): call(kernel, 'first_products', in_specs=[SCALAR, HBM, HBM], out_specs=[WH...]
    ppermute x14, starting transfers between devices: 13.4 us -> 12.9 us  [swap(): return lax.ppermute(x, 'past', pairs)]
  transfers between devices with their start and end apart: 16 -> 16, of which waited for: 8 -> 9; matrix products, arithmetic and copies ran while one was open for 0% -> 0% of each run, Pallas kernels for 20% -> 16%
where the time goes in v11:
time: 43.5 us; the launch traced here: 43.4 us
  starting transfers between devices  16.3 us (37%)
  Pallas kernels  14.1 us (32%)
  waiting for transfers between devices  12 us (28%)
  between operations  0.79 us (2%)
    ppermute x14, starting transfers between devices, swap(): return lax.ppermute(x, 'past', pairs)  12.9 us
    ppermute x14, waiting for transfers between devices, swap(): return lax.ppermute(x, 'past', pairs)  8.69 us
    pallas_call x1, Pallas kernels, first_products(): call(kernel, 'first_products', in_specs=[SCALAR, HBM, HBM], out_specs=[WH...  4.5 us
    ppermute x2, starting transfers between devices, widened(): lax.ppermute(share, 'second', [(z, z ^ 1 << level) for z in range(second)])  3.39 us
    ppermute x2, waiting for transfers between devices, widened(): lax.ppermute(share, 'second', [(z, z ^ 1 << level) for z in range(second)])  3.3 us
    pallas_call x1, Pallas kernels, finish_second(): call(kernel, 'finish_second', in_specs=[SCALAR] + [WHOLE] * 8 + [HBM], ou...  2.6 us
    pallas_call x2, Pallas kernels, product(): call(kernel, 'memory_product', in_specs=[SCALAR, WHOLE, WHOLE] + [FAR] *...  2.56 us
    pallas_call x1, Pallas kernels, finish_first(): call(kernel, 'finish_first', in_specs=[SCALAR] + [WHOLE] * 7, out_specs=[...  1.84 us
  transfers between devices with their start and end apart: 16, of which 9 were waited for; matrix products, arithmetic and copies ran while one was open for 0% of the time, Pallas kernels for 16%

profile of v11, /device:TPU:0, one launch (start us, length us, event | category | flops | bytes accessed | tf_op | source)
XLA Modules:
  0.0 43.4 jit_solution(16331102075028416365)
XLA Ops:
  0.6 4.5 %first_products.1 = (bf16[2,512,256]{2,1,0:T(8,128)(2,1)S(1)}, f32[2,512,256]{2,1,0:T(8,128)S(1)}, bf16[512,2048]{1,0:T(8,128)(2,1)S(1)}, bf16[2048,1024]{1,0:T(8,128)(2,1)S(1)}) custom-call(s32[1]{0:T(128)} %bitcast.me_ref, bf16[1024,2048]{1,0:T(8,128)(2,1)} %sigma_ref.1, bf16[2048,1024]{1,0:T(8,128)(2,1)} %g_ref.1), custom_call_target="tpu_custom_call" | custom-call | flops 1024 | bytes 1024 | tf_op jit(solution)/shard_map/first_products/pallas_call | solution.py:113
  5.1 0.6 %collective-permute-start.3 = (bf16[2,512,256]{2,1,0:T(8,128)(2,1)S(1)}, bf16[2,512,256]{2,1,0:T(8,128)(2,1)S(1)}, u32[]{:S(2)}, u32[]{:S(2)}) collective-permute-start(bf16[2,512,256]{2,1,0:T(8,128)(2,1)S(1)} %get-tuple-element.19), channel_id=1, source_target_pairs={{0,4},{4,0},{8,12},{12,8},{16,20},{20,16},{24,28},{28,24},{1,5},{5... | collective-permute-start | bytes 1572872 | tf_op jit(solution)/shard_map/ppermute | solution.py:390
  5.7 1.3 %memory_product.2 = bf16[2,512,256]{2,1,0:T(8,128)(2,1)S(1)} custom-call(s32[1]{0:T(128)} %bitcast.me_ref, bf16[512,2048]{1,0:T(8,128)(2,1)S(1)} %get-tuple-element.16.sigma, bf16[2048,1024]{1,0:T(8,128)(2,1)S(1)} %get-tuple-element.17.g), custom_call_target="tpu_custom_call" | custom-call | flops 1024 | bytes 1024 | tf_op jit(solution)/shard_map/memory_product/pallas_call | solution.py:146
  7.0 0.1 collective-permute-start
  7.1 0.2 collective-permute-done.3.arrived
  7.3 2.8 %collective-permute-start.4 = (bf16[512,256]{1,0:T(8,128)(2,1)S(1)}, bf16[512,256]{1,0:T(8,128)(2,1)S(1)}, u32[]{:S(2)}, u32[]{:S(2)}) collective-permute-start(bf16[512,256]{1,0:T(8,128)(2,1)S(1)} %fusion.4), channel_id=1, source_target_pairs={{0,8},{4,20},{8,0},{12,28},{16,24},{20,4},{24,16},{28,12},{1,9},{5... | collective-permute-start | bytes 786440 | tf_op jit(solution)/shard_map/ppermute | solution.py:390
  10.2 1.3 %memory_product.3 = f32[2,512,256]{2,1,0:T(8,128)S(1)} custom-call(s32[1]{0:T(128)} %bitcast.me_ref, bf16[512,2048]{1,0:T(8,128)(2,1)S(1)} %get-tuple-element.16.sigma, bf16[2048,1024]{1,0:T(8,128)(2,1)S(1)} %get-tuple-element.17.g, bf16[2,512,256]{2,1,0:T(8,128)(2,1)S(1)} %collective-permute-done.refs_0_), custom_call_target="tpu_custom_call" | custom-call | flops 1024 | bytes 1024 | tf_op jit(solution)/shard_map/memory_product/pallas_call | solution.py:146
  11.6 1.4 %collective-permute-start.1 = (bf16[512,256]{1,0:T(8,128)(2,1)S(1)}, bf16[512,256]{1,0:T(8,128)(2,1)S(1)}, u32[]{:S(2)}, u32[]{:S(2)}) collective-permute-start(bf16[512,256]{1,0:T(8,128)(2,1)S(1)} %fusion.5._), channel_id=1, source_target_pairs={{0,8},{4,20},{8,0},{12,28},{16,24},{20,4},{24,16},{28,12},{1,9},{5... | collective-permute-start | bytes 786440 | tf_op jit(solution)/shard_map/ppermute | solution.py:390
  13.0 1.5 %collective-permute-done.4.more = bf16[512,256]{1,0:T(8,128)(2,1)S(1)} collective-permute-done((bf16[512,256]{1,0:T(8,128)(2,1)S(1)}, bf16[512,256]{1,0:T(8,128)(2,1)S(1)}, u32[]{:S(2)}, u32[]{:S(2)}) %collective-permute-start.4) | collective-permute-done | bytes 262176 | tf_op jit(solution)/shard_map/ppermute | solution.py:390
  14.5 0.1 combined.1.mine
  14.6 2.1 %collective-permute-start.5 = (bf16[512,256]{1,0:T(8,128)(2,1)S(1)}, bf16[512,256]{1,0:T(8,128)(2,1)S(1)}, u32[]{:S(2)}, u32[]{:S(2)}) collective-permute-start(bf16[512,256]{1,0:T(8,128)(2,1)S(1)} %combined.1.mine), channel_id=1, source_target_pairs={{0,16},{4,12},{8,24},{12,4},{16,0},{20,28},{24,8},{28,20},{1,17},{... | collective-permute-start | bytes 786440 | tf_op jit(solution)/shard_map/ppermute | solution.py:390
  16.7 2.3 %collective-permute-done.1 = bf16[512,256]{1,0:T(8,128)(2,1)S(1)} collective-permute-done((bf16[512,256]{1,0:T(8,128)(2,1)S(1)}, bf16[512,256]{1,0:T(8,128)(2,1)S(1)}, u32[]{:S(2)}, u32[]{:S(2)}) %collective-permute-start.1) | collective-permute-done | bytes 262176 | tf_op jit(solution)/shard_map/ppermute | solution.py:390
  19.1 0.1 fusion.3._.mine
  19.2 1.4 %collective-permute-start.2 = (bf16[512,256]{1,0:T(8,128)(2,1)S(1)}, bf16[512,256]{1,0:T(8,128)(2,1)S(1)}, u32[]{:S(2)}, u32[]{:S(2)}) collective-permute-start(bf16[512,256]{1,0:T(8,128)(2,1)S(1)} %fusion.3._.mine), channel_id=1, source_target_pairs={{0,16},{4,12},{8,24},{12,4},{16,0},{20,28},{24,8},{28,20},{1,17},{... | collective-permute-start | bytes 786440 | tf_op jit(solution)/shard_map/ppermute | solution.py:390
  20.5 0.6 %collective-permute-done.5.theirs = bf16[512,256]{1,0:T(8,128)(2,1)S(1)} collective-permute-done((bf16[512,256]{1,0:T(8,128)(2,1)S(1)}, bf16[512,256]{1,0:T(8,128)(2,1)S(1)}, u32[]{:S(2)}, u32[]{:S(2)}) %collective-permute-start.5) | collective-permute-done | bytes 262176 | tf_op jit(solution)/shard_map/ppermute | solution.py:390
  21.1 1.2 %own_first.1 = (bf16[512,256]{1,0:T(8,128)(2,1)S(1)}, f32[512,256]{1,0:T(8,128)S(1)}, f32[1,128]{1,0:T(1,128)S(1)}, bf16[512,256]{1,0:T(8,128)(2,1)S(1)}, f32[512,256]{1,0:T(8,128)S(1)}) custom-call(s32[1]{0:T(128)} %bitcast.me_ref, bf16[512,256]{1,0:T(8,128)(2,1)S(1)} %combined.1.mine, bf16[512,256]{1,0:T(8,128)(2,1)S(1)} %collective-permute-done.5.theirs, ...), custom_call_target="tpu_custom_call" | custom-call | flops 1024 | bytes 1024 | tf_op jit(solution)/shard_map/own_first/pallas_call | solution.py:208
  22.3 2.1 %collective-permute-start.11 = (bf16[512,256]{1,0:T(8,128)(2,1)S(1)}, bf16[512,256]{1,0:T(8,128)(2,1)S(1)}, u32[]{:S(2)}, u32[]{:S(2)}) collective-permute-start(bf16[512,256]{1,0:T(8,128)(2,1)S(1)} %get-tuple-element.26), channel_id=1, source_target_pairs={{0,8},{4,20},{8,0},{12,28},{16,24},{20,4},{24,16},{28,12},{1,9},{5... | collective-permute-start | bytes 786440 | tf_op jit(solution)/shard_map/ppermute | solution.py:390
  24.3 2.0 %collective-permute-done.2.theirs = bf16[512,256]{1,0:T(8,128)(2,1)S(1)} collective-permute-done((bf16[512,256]{1,0:T(8,128)(2,1)S(1)}, bf16[512,256]{1,0:T(8,128)(2,1)S(1)}, u32[]{:S(2)}, u32[]{:S(2)}) %collective-permute-start.2) | collective-permute-done | bytes 262176 | tf_op jit(solution)/shard_map/ppermute | solution.py:390
  26.4 0.8 %own_second.1 = (bf16[512,256]{1,0:T(8,128)(2,1)S(1)}, f32[1,8,128]{2,1,0:T(8,128)S(1)}, f32[512,256]{1,0:T(8,128)S(1)}) custom-call(s32[1]{0:T(128)} %bitcast.me_ref, bf16[512,256]{1,0:T(8,128)(2,1)S(1)} %fusion.3._.mine, bf16[512,256]{1,0:T(8,128)(2,1)S(1)} %collective-permute-done.2.theirs, bf16[2,512,1024]{2,1,0:T(8,128)(2,1)S(1)} %copy-done, ...), custom_call_target="tpu_custom_call" | custom-call | flops 1024 | bytes 1024 | tf_op jit(solution)/shard_map/own_second/pallas_call | solution.py:245
  27.2 1.2 %collective-permute-start.7 = (f32[1,8,128]{2,1,0:T(8,128)S(1)}, f32[1,8,128]{2,1,0:T(8,128)S(1)}, u32[]{:S(2)}, u32[]{:S(2)}) collective-permute-start(f32[1,8,128]{2,1,0:T(8,128)S(1)} %get-tuple-element.23), channel_id=1, source_target_pairs={{0,1},{1,0},{2,3},{3,2},{4,5},{5,4},{6,7},{7,6},{8,9},{9,8},{10,11... | collective-permute-start | bytes 12296 | tf_op jit(solution)/shard_map/ppermute | solution.py:404
  28.4 1.1 %collective-permute-start.6 = (bf16[512,256]{1,0:T(8,128)(2,1)S(1)}, bf16[512,256]{1,0:T(8,128)(2,1)S(1)}, u32[]{:S(2)}, u32[]{:S(2)}) collective-permute-start(bf16[512,256]{1,0:T(8,128)(2,1)S(1)} %get-tuple-element.22), channel_id=1, source_target_pairs={{0,8},{4,20},{8,0},{12,28},{16,24},{20,4},{24,16},{28,12},{1,9},{5... | collective-permute-start | bytes 786440 | tf_op jit(solution)/shard_map/ppermute | solution.py:390
  29.5 0.5 %collective-permute-start.12 = (bf16[512,256]{1,0:T(8,128)(2,1)S(1)}, bf16[512,256]{1,0:T(8,128)(2,1)S(1)}, u32[]{:S(2)}, u32[]{:S(2)}) collective-permute-start(bf16[512,256]{1,0:T(8,128)(2,1)S(1)} %get-tuple-element.26), channel_id=1, source_target_pairs={{0,4},{4,0},{8,12},{12,8},{16,20},{20,16},{24,28},{28,24},{1,5},{5... | collective-permute-start | bytes 786440 | tf_op jit(solution)/shard_map/ppermute | solution.py:390
  30.0 0.9 %collective-permute-done.7 = f32[1,8,128]{2,1,0:T(8,128)S(1)} collective-permute-done((f32[1,8,128]{2,1,0:T(8,128)S(1)}, f32[1,8,128]{2,1,0:T(8,128)S(1)}, u32[]{:S(2)}, u32[]{:S(2)}) %collective-permute-start.7) | collective-permute-done | bytes 4128 | tf_op jit(solution)/shard_map/ppermute | solution.py:404
  31.0 2.2 %collective-permute-start.8 = (f32[2,8,128]{2,1,0:T(8,128)S(1)}, f32[2,8,128]{2,1,0:T(8,128)S(1)}, u32[]{:S(2)}, u32[]{:S(2)}) collective-permute-start(f32[2,8,128]{2,1,0:T(8,128)S(1)} %get-tuple-element.30._), channel_id=1, source_target_pairs={{0,2},{1,3},{2,0},{3,1},{4,6},{5,7},{6,4},{7,5},{8,10},{9,11},{10,... | collective-permute-start | bytes 24584 | tf_op jit(solution)/shard_map/ppermute | solution.py:404
  33.2 2.4 %collective-permute-done.8 = f32[2,8,128]{2,1,0:T(8,128)S(1)} collective-permute-done((f32[2,8,128]{2,1,0:T(8,128)S(1)}, f32[2,8,128]{2,1,0:T(8,128)S(1)}, u32[]{:S(2)}, u32[]{:S(2)}) %collective-permute-start.8) | collective-permute-done | bytes 8224 | tf_op jit(solution)/shard_map/ppermute | solution.py:404
  35.7 0.1 collective-permute-start.9
  35.7 0.7 %collective-permute-start.14 = (f32[4,8,128]{2,1,0:T(8,128)S(1)}, f32[4,8,128]{2,1,0:T(8,128)S(1)}, u32[]{:S(2)}, u32[]{:S(2)}) collective-permute-start(f32[4,8,128]{2,1,0:T(8,128)S(1)} %constant_dynamic-update-slice_fusion.2._.a), channel_id=1, source_target_pairs={{0,8},{4,20},{8,0},{12,28},{16,24},{20,4},{24,16},{28,12},{1,9},{5... | collective-permute-start | bytes 49160 | tf_op jit(solution)/shard_map/ppermute | solution.py:390
  36.4 0.4 %memory_terms.1.refs_1_.terms = f32[2,512,256]{2,1,0:T(8,128)S(1)} custom-call(bf16[512,256]{1,0:T(8,128)(2,1)S(1)} %ordered.2.refs_0_, bf16[512,256]{1,0:T(8,128)(2,1)S(1)} %collective-permute-done.10.refs_1_, bf16[2,512,1024]{2,1,0:T(8,128)(2,1)S(1)} %copy-done), custom_call_target="tpu_custom_call" | custom-call | flops 1024 | bytes 1024 | tf_op jit(solution)/shard_map/memory_terms/pallas_call | solution.py:298
  36.9 1.8 %finish_first.1 = (bf16[1024,1024]{1,0:T(8,128)(2,1)}, f32[3,512,256]{2,1,0:T(8,128)S(1)}) custom-call(s32[1]{0:T(128)} %bitcast.me_ref, bf16[512,256]{1,0:T(8,128)(2,1)S(1)} %ordered.3.refs_0_, bf16[512,256]{1,0:T(8,128)(2,1)S(1)} %collective-permute-done.12.refs_1_, bf16[512,256]{1,0:T(8,128)(2,1)S(1)} %collective-permute-done.13.refs_2_, ...), custom_call_target="tpu_custom_call" | custom-call | flops 1024 | bytes 1024 | tf_op jit(solution)/shard_map/finish_first/pallas_call | solution.py:279
  38.7 0.8 %collective-permute-done.14.b = f32[4,8,128]{2,1,0:T(8,128)S(1)} collective-permute-done((f32[4,8,128]{2,1,0:T(8,128)S(1)}, f32[4,8,128]{2,1,0:T(8,128)S(1)}, u32[]{:S(2)}, u32[]{:S(2)}) %collective-permute-start.14) | collective-permute-done | bytes 16416 | tf_op jit(solution)/shard_map/ppermute | solution.py:390
  39.6 1.2 %collective-permute-done.15 = f32[8,8,128]{2,1,0:T(8,128)S(1)} collective-permute-done((f32[8,8,128]{2,1,0:T(8,128)S(1)}, f32[8,8,128]{2,1,0:T(8,128)S(1)}, u32[]{:S(2)}, u32[]{:S(2)}) %collective-permute-start.15) | collective-permute-done | bytes 32800 | tf_op jit(solution)/shard_map/ppermute | solution.py:390
  40.8 2.6 %finish_second.1 = (bf16[1024,1024]{1,0:T(8,128)(2,1)}, bf16[1024,1024]{1,0:T(8,128)(2,1)}) custom-call(s32[1]{0:T(128)} %bitcast.me_ref, bf16[512,256]{1,0:T(8,128)(2,1)S(1)} %collective-permute-done.9.last, f32[512,256]{1,0:T(8,128)S(1)} %get-tuple-element.24.term_own, ...), custom_call_target="tpu_custom_call", output_to_operand_aliasing={{0}: (9, {})} | custom-call | flops 1024 | bytes 1024 | tf_op jit(solution)/shard_map/finish_second/pallas_call | solution.py:365
  (25 shorter events, 0.3 us)
Async XLA Ops:
  5.1 2.1 %collective-permute-start.3 = (bf16[2,512,256]{2,1,0:T(8,128)(2,1)S(1)}, bf16[2,512,256]{2,1,0:T(8,128)(2,1)S(1)}, u32[]{:S(2)}, u32[]{:S(2)}) collective-permute-start(bf16[2,512,256]{2,1,0:T(8,128)(2,1)S(1)} %get-tuple-element.19), channel_id=1, source_target_pairs={{0,4},{4,0},{8,12},{12,8},{16,20},{20,16},{24,28},{28,24},{1,5},{5... | collective-permute-start | bytes 1572872 | tf_op jit(solution)/shard_map/ppermute | solution.py:390
  7.0 3.2 %collective-permute-start = (bf16[2,512,256]{2,1,0:T(8,128)(2,1)S(1)}, bf16[2,512,256]{2,1,0:T(8,128)(2,1)S(1)}, u32[]{:S(2)}, u32[]{:S(2)}) collective-permute-start(bf16[2,512,256]{2,1,0:T(8,128)(2,1)S(1)} %memory_product.2), channel_id=1, source_target_pairs={{0,4},{4,0},{8,12},{12,8},{16,20},{20,16},{24,28},{28,24},{1,5},{5... | collective-permute-start | bytes 1572872 | tf_op jit(solution)/shard_map/ppermute | solution.py:390
  7.3 7.2 %collective-permute-start.4 = (bf16[512,256]{1,0:T(8,128)(2,1)S(1)}, bf16[512,256]{1,0:T(8,128)(2,1)S(1)}, u32[]{:S(2)}, u32[]{:S(2)}) collective-permute-start(bf16[512,256]{1,0:T(8,128)(2,1)S(1)} %fusion.4), channel_id=1, source_target_pairs={{0,8},{4,20},{8,0},{12,28},{16,24},{20,4},{24,16},{28,12},{1,9},{5... | collective-permute-start | bytes 786440 | tf_op jit(solution)/shard_map/ppermute | solution.py:390
  11.5 9.6 %copy-start = (bf16[2,512,1024]{2,1,0:T(8,128)(2,1)S(1)}, bf16[2,512,1024]{2,1,0:T(8,128)(2,1)}, u32[]{:S(2)}) copy-start(bf16[2,512,1024]{2,1,0:T(8,128)(2,1)} %w.5) | copy-start | bytes 6291460
  11.5 9.6 %copy-start.1 = (bf16[512,1024]{1,0:T(8,128)(2,1)S(1)}, bf16[512,1024]{1,0:T(8,128)(2,1)}, u32[]{:S(2)}) copy-start(bf16[512,1024]{1,0:T(8,128)(2,1)} %refs_5_.1) | copy-start | bytes 3145732
  11.5 9.6 %copy-start.2 = (f32[32,1024]{1,0:T(8,128)S(1)}, f32[32,1024]{1,0:T(8,128)}, u32[]{:S(2)}) copy-start(f32[32,1024]{1,0:T(8,128)} %coupling.5) | copy-start | bytes 393220
  11.6 7.5 %collective-permute-start.1 = (bf16[512,256]{1,0:T(8,128)(2,1)S(1)}, bf16[512,256]{1,0:T(8,128)(2,1)S(1)}, u32[]{:S(2)}, u32[]{:S(2)}) collective-permute-start(bf16[512,256]{1,0:T(8,128)(2,1)S(1)} %fusion.5._), channel_id=1, source_target_pairs={{0,8},{4,20},{8,0},{12,28},{16,24},{20,4},{24,16},{28,12},{1,9},{5... | collective-permute-start | bytes 786440 | tf_op jit(solution)/shard_map/ppermute | solution.py:390
  14.6 6.5 %collective-permute-start.5 = (bf16[512,256]{1,0:T(8,128)(2,1)S(1)}, bf16[512,256]{1,0:T(8,128)(2,1)S(1)}, u32[]{:S(2)}, u32[]{:S(2)}) collective-permute-start(bf16[512,256]{1,0:T(8,128)(2,1)S(1)} %combined.1.mine), channel_id=1, source_target_pairs={{0,16},{4,12},{8,24},{12,4},{16,0},{20,28},{24,8},{28,20},{1,17},{... | collective-permute-start | bytes 786440 | tf_op jit(solution)/shard_map/ppermute | solution.py:390
  19.2 7.2 %collective-permute-start.2 = (bf16[512,256]{1,0:T(8,128)(2,1)S(1)}, bf16[512,256]{1,0:T(8,128)(2,1)S(1)}, u32[]{:S(2)}, u32[]{:S(2)}) collective-permute-start(bf16[512,256]{1,0:T(8,128)(2,1)S(1)} %fusion.3._.mine), channel_id=1, source_target_pairs={{0,16},{4,12},{8,24},{12,4},{16,0},{20,28},{24,8},{28,20},{1,17},{... | collective-permute-start | bytes 786440 | tf_op jit(solution)/shard_map/ppermute | solution.py:390
  22.3 8.6 %collective-permute-start.11 = (bf16[512,256]{1,0:T(8,128)(2,1)S(1)}, bf16[512,256]{1,0:T(8,128)(2,1)S(1)}, u32[]{:S(2)}, u32[]{:S(2)}) collective-permute-start(bf16[512,256]{1,0:T(8,128)(2,1)S(1)} %get-tuple-element.26), channel_id=1, source_target_pairs={{0,8},{4,20},{8,0},{12,28},{16,24},{20,4},{24,16},{28,12},{1,9},{5... | collective-permute-start | bytes 786440 | tf_op jit(solution)/shard_map/ppermute | solution.py:390
  27.2 3.7 %collective-permute-start.7 = (f32[1,8,128]{2,1,0:T(8,128)S(1)}, f32[1,8,128]{2,1,0:T(8,128)S(1)}, u32[]{:S(2)}, u32[]{:S(2)}) collective-permute-start(f32[1,8,128]{2,1,0:T(8,128)S(1)} %get-tuple-element.23), channel_id=1, source_target_pairs={{0,1},{1,0},{2,3},{3,2},{4,5},{5,4},{6,7},{7,6},{8,9},{9,8},{10,11... | collective-permute-start | bytes 12296 | tf_op jit(solution)/shard_map/ppermute | solution.py:404
  28.4 7.2 %collective-permute-start.6 = (bf16[512,256]{1,0:T(8,128)(2,1)S(1)}, bf16[512,256]{1,0:T(8,128)(2,1)S(1)}, u32[]{:S(2)}, u32[]{:S(2)}) collective-permute-start(bf16[512,256]{1,0:T(8,128)(2,1)S(1)} %get-tuple-element.22), channel_id=1, source_target_pairs={{0,8},{4,20},{8,0},{12,28},{16,24},{20,4},{24,16},{28,12},{1,9},{5... | collective-permute-start | bytes 786440 | tf_op jit(solution)/shard_map/ppermute | solution.py:390
  29.5 6.9 %collective-permute-start.10 = (bf16[512,256]{1,0:T(8,128)(2,1)S(1)}, bf16[512,256]{1,0:T(8,128)(2,1)S(1)}, u32[]{:S(2)}, u32[]{:S(2)}) collective-permute-start(bf16[512,256]{1,0:T(8,128)(2,1)S(1)} %get-tuple-element.22), channel_id=1, source_target_pairs={{0,4},{4,0},{8,12},{12,8},{16,20},{20,16},{24,28},{28,24},{1,5},{5... | collective-permute-start | bytes 786440 | tf_op jit(solution)/shard_map/ppermute | solution.py:390
  29.5 7.4 %collective-permute-start.12 = (bf16[512,256]{1,0:T(8,128)(2,1)S(1)}, bf16[512,256]{1,0:T(8,128)(2,1)S(1)}, u32[]{:S(2)}, u32[]{:S(2)}) collective-permute-start(bf16[512,256]{1,0:T(8,128)(2,1)S(1)} %get-tuple-element.26), channel_id=1, source_target_pairs={{0,4},{4,0},{8,12},{12,8},{16,20},{20,16},{24,28},{28,24},{1,5},{5... | collective-permute-start | bytes 786440 | tf_op jit(solution)/shard_map/ppermute | solution.py:390
  30.9 5.9 %collective-permute-start.13 = (bf16[512,256]{1,0:T(8,128)(2,1)S(1)}, bf16[512,256]{1,0:T(8,128)(2,1)S(1)}, u32[]{:S(2)}, u32[]{:S(2)}) collective-permute-start(bf16[512,256]{1,0:T(8,128)(2,1)S(1)} %ordered.3.refs_0_), channel_id=1, source_target_pairs={{0,4},{4,0},{8,12},{12,8},{16,20},{20,16},{24,28},{28,24},{1,5},{5... | collective-permute-start | bytes 786440 | tf_op jit(solution)/shard_map/ppermute | solution.py:390
  31.0 4.6 %collective-permute-start.8 = (f32[2,8,128]{2,1,0:T(8,128)S(1)}, f32[2,8,128]{2,1,0:T(8,128)S(1)}, u32[]{:S(2)}, u32[]{:S(2)}) collective-permute-start(f32[2,8,128]{2,1,0:T(8,128)S(1)} %get-tuple-element.30._), channel_id=1, source_target_pairs={{0,2},{1,3},{2,0},{3,1},{4,6},{5,7},{6,4},{7,5},{8,10},{9,11},{10,... | collective-permute-start | bytes 24584 | tf_op jit(solution)/shard_map/ppermute | solution.py:404
  35.7 5.1 %collective-permute-start.9 = (bf16[512,256]{1,0:T(8,128)(2,1)S(1)}, bf16[512,256]{1,0:T(8,128)(2,1)S(1)}, u32[]{:S(2)}, u32[]{:S(2)}) collective-permute-start(bf16[512,256]{1,0:T(8,128)(2,1)S(1)} %ordered.2.refs_0_), channel_id=1, source_target_pairs={{0,4},{4,0},{8,12},{12,8},{16,20},{20,16},{24,28},{28,24},{1,5},{5... | collective-permute-start | bytes 786440 | tf_op jit(solution)/shard_map/ppermute | solution.py:390
  35.7 3.8 %collective-permute-start.14 = (f32[4,8,128]{2,1,0:T(8,128)S(1)}, f32[4,8,128]{2,1,0:T(8,128)S(1)}, u32[]{:S(2)}, u32[]{:S(2)}) collective-permute-start(f32[4,8,128]{2,1,0:T(8,128)S(1)} %constant_dynamic-update-slice_fusion.2._.a), channel_id=1, source_target_pairs={{0,8},{4,20},{8,0},{12,28},{16,24},{20,4},{24,16},{28,12},{1,9},{5... | collective-permute-start | bytes 49160 | tf_op jit(solution)/shard_map/ppermute | solution.py:390
  39.6 1.2 %collective-permute-start.15 = (f32[8,8,128]{2,1,0:T(8,128)S(1)}, f32[8,8,128]{2,1,0:T(8,128)S(1)}, u32[]{:S(2)}, u32[]{:S(2)}) collective-permute-start(f32[8,8,128]{2,1,0:T(8,128)S(1)} %joined.1), channel_id=1, source_target_pairs={{0,4},{4,0},{8,12},{12,8},{16,20},{20,16},{24,28},{28,24},{1,5},{5... | collective-permute-start | bytes 98312 | tf_op jit(solution)/shard_map/ppermute | solution.py:390

commit v12 on v11

--- a/solution.py
+++ b/solution.py
@@ -70,7 +70,7 @@
     half = columns // 2
     parts = 4
     eighth = depth // 8
-    chunks = [(0, 2 * eighth), (2 * eighth, 3 * eighth), (5 * eighth, 3 * eighth)]
+    chunks = [(0, eighth), (eighth, 3 * eighth), (4 * eighth, 4 * eighth)]
 
     def kernel(me_ref, sigma_ref, g_ref, sent, kept, sigma_next, g, sigma, total, sems):
         started = []
@@ -228,18 +228,19 @@
         at = columns_of(Place(me_ref[0], bits).quarter(), width)
         summed = (mine[...].astype(F32) + theirs[...].astype(F32)).astype(BF16)
         memory[...] = summed
-        c = coupling[:, at]
-        c2 = (c * c * (1.0 / (rows * width)))[None]
+        c = coupling[:, at] * (rows * width) ** -0.5
         a = jnp.dot(w[1, :, :rows], summed, preferred_element_type=F32)
         term_own[...] = a
         b = response[...]
-        a2, b2 = a * a, b * b
-        a3, b3, a2b, ab2 = a2 * a, b2 * b, a2 * b, a * b2
+
+        def weighted(square):
+            return (square.reshape(rows // orbitals, orbitals, width) * c[None]).reshape(rows, width)
+
+        ca2, cb2 = weighted(a * a), weighted(b * b)
+        ca3, ca2b, cab2, cb3 = ca2 * a, ca2 * b, cb2 * a, cb2 * b
         lines = [squares[...]]
-        terms = (a3 * a3, a3 * a2b, a2b * a2b, a3 * b3, ab2 * ab2, ab2 * b3, b3 * b3)
-        for term in terms:
-            weighted = (term.reshape(rows // orbitals, orbitals, width) * c2).reshape(rows, width)
-            lines.append(folded(weighted))
+        for x, y in ((ca3, ca3), (ca3, ca2b), (ca2b, ca2b), (ca3, cb3), (cab2, cab2), (cab2, cb3), (cb3, cb3)):
+            lines.append(folded(x * y))
         out[0] = jnp.concatenate(lines, axis=0)
 
     return call(
@@ -358,7 +359,7 @@
             g = last_term if slot == 3 else terms[slot - 1] if slot else term_own[...]
             g += jnp.dot(w[1, :, rows:], before, preferred_element_type=F32)
             write(g.astype(BF16), g_held, slot, g_out, 1, at)
-            write((cubed(g, coupling[:, at]) * scale_1).astype(BF16), s_held, 4 + slot, sigma, 1, at)
+            write(cubed(g, coupling[:, at] * scale_1).astype(BF16), s_held, 4 + slot, sigma, 1, at)
         for copy in copies:
             copy.wait()
 
@@ -418,11 +419,11 @@
     own_1, share, term_own = own_second(me, mine_1, theirs_1, volterra, response, squares, coupling, bits)
 
     rounds = log2(second)
-    share = jnp.concatenate([share, widened(share, 0)])
+    share = jnp.concatenate([share, widened(share, rounds - 1)])
     partner = ordered(swap(own_0, 1), share)
     pieces = [partner, swap(own_0, 0), swap(partner, 0)]
     g_first, cubic = finish_first(me, pieces, g_own, volterra, sigma_edge, coupling, bits)
-    for level in range(1, rounds):
+    for level in reversed(range(rounds - 1)):
         share = jnp.concatenate([share, widened(share, level)])
     partner = ordered(swap(own_1, 1), share)
     terms = memory_terms([partner, swap(own_1, 0)], volterra)

time: 43.5 us -> 43.6 us (level)
  starting transfers between devices: 16.3 us -> 17 us
  waiting for transfers between devices: 12 us -> 11.4 us
    ppermute x14, starting transfers between devices: 12.9 us -> 13.6 us  [swap(): return lax.ppermute(x, 'past', pairs)]
    ppermute x14, waiting for transfers between devices: 8.69 us -> 8.14 us  [swap(): return lax.ppermute(x, 'past', pairs)]
  transfers between devices with their start and end apart: 16 -> 16, of which waited for: 9 -> 10; matrix products, arithmetic and copies ran while one was open for 0% -> 0% of each run, Pallas kernels for 16% -> 16%
where the time goes in v12:
time: 43.6 us; the launch traced here: 43.5 us
  starting transfers between devices  17 us (39%)
  Pallas kernels  14 us (32%)
  waiting for transfers between devices  11.4 us (26%)
  between operations  0.79 us (2%)
    ppermute x14, starting transfers between devices, swap(): return lax.ppermute(x, 'past', pairs)  13.6 us
    ppermute x14, waiting for transfers between devices, swap(): return lax.ppermute(x, 'past', pairs)  8.14 us
    pallas_call x1, Pallas kernels, first_products(): call(kernel, 'first_products', in_specs=[SCALAR, HBM, HBM], out_specs=[WH...  4.65 us
    ppermute x2, starting transfers between devices, widened(): lax.ppermute(share, 'second', [(z, z ^ 1 << level) for z in range(second)])  3.43 us
    ppermute x2, waiting for transfers between devices, widened(): lax.ppermute(share, 'second', [(z, z ^ 1 << level) for z in range(second)])  3.29 us
    pallas_call x1, Pallas kernels, finish_second(): call(kernel, 'finish_second', in_specs=[SCALAR] + [WHOLE] * 8 + [HBM], ou...  2.56 us
    pallas_call x2, Pallas kernels, product(): call(kernel, 'memory_product', in_specs=[SCALAR, WHOLE, WHOLE] + [FAR] *...  2.56 us
    pallas_call x1, Pallas kernels, finish_first(): call(kernel, 'finish_first', in_specs=[SCALAR] + [WHOLE] * 7, out_specs=[...  1.84 us
  transfers between devices with their start and end apart: 16, of which 10 were waited for; matrix products, arithmetic and copies ran while one was open for 0% of the time, Pallas kernels for 16%

profile of v12, /device:TPU:0, one launch (start us, length us, event | category | flops | bytes accessed | tf_op | source)
XLA Modules:
  0.0 43.5 jit_solution(7492681632067794928)
XLA Ops:
  0.6 4.7 %first_products.1 = (bf16[2,512,256]{2,1,0:T(8,128)(2,1)S(1)}, f32[2,512,256]{2,1,0:T(8,128)S(1)}, bf16[512,2048]{1,0:T(8,128)(2,1)S(1)}, bf16[2048,1024]{1,0:T(8,128)(2,1)S(1)}) custom-call(s32[1]{0:T(128)} %bitcast.me_ref, bf16[1024,2048]{1,0:T(8,128)(2,1)} %sigma_ref.1, bf16[2048,1024]{1,0:T(8,128)(2,1)} %g_ref.1), custom_call_target="tpu_custom_call" | custom-call | flops 1024 | bytes 1024 | tf_op jit(solution)/shard_map/first_products/pallas_call | solution.py:113
  5.3 0.6 %collective-permute-start.3 = (bf16[2,512,256]{2,1,0:T(8,128)(2,1)S(1)}, bf16[2,512,256]{2,1,0:T(8,128)(2,1)S(1)}, u32[]{:S(2)}, u32[]{:S(2)}) collective-permute-start(bf16[2,512,256]{2,1,0:T(8,128)(2,1)S(1)} %get-tuple-element.19), channel_id=1, source_target_pairs={{0,4},{4,0},{8,12},{12,8},{16,20},{20,16},{24,28},{28,24},{1,5},{5... | collective-permute-start | bytes 1572872 | tf_op jit(solution)/shard_map/ppermute | solution.py:391
  5.9 1.3 %memory_product.2 = bf16[2,512,256]{2,1,0:T(8,128)(2,1)S(1)} custom-call(s32[1]{0:T(128)} %bitcast.me_ref, bf16[512,2048]{1,0:T(8,128)(2,1)S(1)} %get-tuple-element.16.sigma, bf16[2048,1024]{1,0:T(8,128)(2,1)S(1)} %get-tuple-element.17.g), custom_call_target="tpu_custom_call" | custom-call | flops 1024 | bytes 1024 | tf_op jit(solution)/shard_map/memory_product/pallas_call | solution.py:146
  7.3 0.2 collective-permute-done.3.arrived
  7.5 2.8 %collective-permute-start.4 = (bf16[512,256]{1,0:T(8,128)(2,1)S(1)}, bf16[512,256]{1,0:T(8,128)(2,1)S(1)}, u32[]{:S(2)}, u32[]{:S(2)}) collective-permute-start(bf16[512,256]{1,0:T(8,128)(2,1)S(1)} %fusion.4), channel_id=1, source_target_pairs={{0,8},{4,20},{8,0},{12,28},{16,24},{20,4},{24,16},{28,12},{1,9},{5... | collective-permute-start | bytes 786440 | tf_op jit(solution)/shard_map/ppermute | solution.py:391
  10.3 1.3 %memory_product.3 = f32[2,512,256]{2,1,0:T(8,128)S(1)} custom-call(s32[1]{0:T(128)} %bitcast.me_ref, bf16[512,2048]{1,0:T(8,128)(2,1)S(1)} %get-tuple-element.16.sigma, bf16[2048,1024]{1,0:T(8,128)(2,1)S(1)} %get-tuple-element.17.g, bf16[2,512,256]{2,1,0:T(8,128)(2,1)S(1)} %collective-permute-done.refs_0_), custom_call_target="tpu_custom_call" | custom-call | flops 1024 | bytes 1024 | tf_op jit(solution)/shard_map/memory_product/pallas_call | solution.py:146
  11.7 1.4 %collective-permute-start.1 = (bf16[512,256]{1,0:T(8,128)(2,1)S(1)}, bf16[512,256]{1,0:T(8,128)(2,1)S(1)}, u32[]{:S(2)}, u32[]{:S(2)}) collective-permute-start(bf16[512,256]{1,0:T(8,128)(2,1)S(1)} %fusion.5._), channel_id=1, source_target_pairs={{0,8},{4,20},{8,0},{12,28},{16,24},{20,4},{24,16},{28,12},{1,9},{5... | collective-permute-start | bytes 786440 | tf_op jit(solution)/shard_map/ppermute | solution.py:391
  13.1 1.5 %collective-permute-done.4.more = bf16[512,256]{1,0:T(8,128)(2,1)S(1)} collective-permute-done((bf16[512,256]{1,0:T(8,128)(2,1)S(1)}, bf16[512,256]{1,0:T(8,128)(2,1)S(1)}, u32[]{:S(2)}, u32[]{:S(2)}) %collective-permute-start.4) | collective-permute-done | bytes 262176 | tf_op jit(solution)/shard_map/ppermute | solution.py:391
  14.7 0.1 combined.1.mine
  14.8 2.1 %collective-permute-start.5 = (bf16[512,256]{1,0:T(8,128)(2,1)S(1)}, bf16[512,256]{1,0:T(8,128)(2,1)S(1)}, u32[]{:S(2)}, u32[]{:S(2)}) collective-permute-start(bf16[512,256]{1,0:T(8,128)(2,1)S(1)} %combined.1.mine), channel_id=1, source_target_pairs={{0,16},{4,12},{8,24},{12,4},{16,0},{20,28},{24,8},{28,20},{1,17},{... | collective-permute-start | bytes 786440 | tf_op jit(solution)/shard_map/ppermute | solution.py:391
  16.9 2.3 %collective-permute-done.1 = bf16[512,256]{1,0:T(8,128)(2,1)S(1)} collective-permute-done((bf16[512,256]{1,0:T(8,128)(2,1)S(1)}, bf16[512,256]{1,0:T(8,128)(2,1)S(1)}, u32[]{:S(2)}, u32[]{:S(2)}) %collective-permute-start.1) | collective-permute-done | bytes 262176 | tf_op jit(solution)/shard_map/ppermute | solution.py:391
  19.2 0.1 fusion.3._.mine
  19.3 1.4 %collective-permute-start.2 = (bf16[512,256]{1,0:T(8,128)(2,1)S(1)}, bf16[512,256]{1,0:T(8,128)(2,1)S(1)}, u32[]{:S(2)}, u32[]{:S(2)}) collective-permute-start(bf16[512,256]{1,0:T(8,128)(2,1)S(1)} %fusion.3._.mine), channel_id=1, source_target_pairs={{0,16},{4,12},{8,24},{12,4},{16,0},{20,28},{24,8},{28,20},{1,17},{... | collective-permute-start | bytes 786440 | tf_op jit(solution)/shard_map/ppermute | solution.py:391
  20.7 0.6 %collective-permute-done.5.theirs = bf16[512,256]{1,0:T(8,128)(2,1)S(1)} collective-permute-done((bf16[512,256]{1,0:T(8,128)(2,1)S(1)}, bf16[512,256]{1,0:T(8,128)(2,1)S(1)}, u32[]{:S(2)}, u32[]{:S(2)}) %collective-permute-start.5) | collective-permute-done | bytes 262176 | tf_op jit(solution)/shard_map/ppermute | solution.py:391
  21.3 1.2 %own_first.1 = (bf16[512,256]{1,0:T(8,128)(2,1)S(1)}, f32[512,256]{1,0:T(8,128)S(1)}, f32[1,128]{1,0:T(1,128)S(1)}, bf16[512,256]{1,0:T(8,128)(2,1)S(1)}, f32[512,256]{1,0:T(8,128)S(1)}) custom-call(s32[1]{0:T(128)} %bitcast.me_ref, bf16[512,256]{1,0:T(8,128)(2,1)S(1)} %combined.1.mine, bf16[512,256]{1,0:T(8,128)(2,1)S(1)} %collective-permute-done.5.theirs, ...), custom_call_target="tpu_custom_call" | custom-call | flops 1024 | bytes 1024 | tf_op jit(solution)/shard_map/own_first/pallas_call | solution.py:208
  22.4 2.1 %collective-permute-start.11 = (bf16[512,256]{1,0:T(8,128)(2,1)S(1)}, bf16[512,256]{1,0:T(8,128)(2,1)S(1)}, u32[]{:S(2)}, u32[]{:S(2)}) collective-permute-start(bf16[512,256]{1,0:T(8,128)(2,1)S(1)} %get-tuple-element.26), channel_id=1, source_target_pairs={{0,8},{4,20},{8,0},{12,28},{16,24},{20,4},{24,16},{28,12},{1,9},{5... | collective-permute-start | bytes 786440 | tf_op jit(solution)/shard_map/ppermute | solution.py:391
  24.5 2.0 %collective-permute-done.2.theirs = bf16[512,256]{1,0:T(8,128)(2,1)S(1)} collective-permute-done((bf16[512,256]{1,0:T(8,128)(2,1)S(1)}, bf16[512,256]{1,0:T(8,128)(2,1)S(1)}, u32[]{:S(2)}, u32[]{:S(2)}) %collective-permute-start.2) | collective-permute-done | bytes 262176 | tf_op jit(solution)/shard_map/ppermute | solution.py:391
  26.5 0.6 %own_second.1 = (bf16[512,256]{1,0:T(8,128)(2,1)S(1)}, f32[1,8,128]{2,1,0:T(8,128)S(1)}, f32[512,256]{1,0:T(8,128)S(1)}) custom-call(s32[1]{0:T(128)} %bitcast.me_ref, bf16[512,256]{1,0:T(8,128)(2,1)S(1)} %fusion.3._.mine, bf16[512,256]{1,0:T(8,128)(2,1)S(1)} %collective-permute-done.2.theirs, bf16[2,512,1024]{2,1,0:T(8,128)(2,1)S(1)} %copy-done, ...), custom_call_target="tpu_custom_call" | custom-call | flops 1024 | bytes 1024 | tf_op jit(solution)/shard_map/own_second/pallas_call | solution.py:246
  27.2 2.2 %collective-permute-start.7 = (f32[1,8,128]{2,1,0:T(8,128)S(1)}, f32[1,8,128]{2,1,0:T(8,128)S(1)}, u32[]{:S(2)}, u32[]{:S(2)}) collective-permute-start(f32[1,8,128]{2,1,0:T(8,128)S(1)} %get-tuple-element.23), channel_id=1, source_target_pairs={{0,2},{1,3},{2,0},{3,1},{4,6},{5,7},{6,4},{7,5},{8,10},{9,11},{10,... | collective-permute-start | bytes 12296 | tf_op jit(solution)/shard_map/ppermute | solution.py:405
  29.4 1.1 %collective-permute-start.6 = (bf16[512,256]{1,0:T(8,128)(2,1)S(1)}, bf16[512,256]{1,0:T(8,128)(2,1)S(1)}, u32[]{:S(2)}, u32[]{:S(2)}) collective-permute-start(bf16[512,256]{1,0:T(8,128)(2,1)S(1)} %get-tuple-element.22), channel_id=1, source_target_pairs={{0,8},{4,20},{8,0},{12,28},{16,24},{20,4},{24,16},{28,12},{1,9},{5... | collective-permute-start | bytes 786440 | tf_op jit(solution)/shard_map/ppermute | solution.py:391
  30.4 0.5 %collective-permute-start.12 = (bf16[512,256]{1,0:T(8,128)(2,1)S(1)}, bf16[512,256]{1,0:T(8,128)(2,1)S(1)}, u32[]{:S(2)}, u32[]{:S(2)}) collective-permute-start(bf16[512,256]{1,0:T(8,128)(2,1)S(1)} %get-tuple-element.26), channel_id=1, source_target_pairs={{0,4},{4,0},{8,12},{12,8},{16,20},{20,16},{24,28},{28,24},{1,5},{5... | collective-permute-start | bytes 786440 | tf_op jit(solution)/shard_map/ppermute | solution.py:391
  31.0 0.8 %collective-permute-done.7 = f32[1,8,128]{2,1,0:T(8,128)S(1)} collective-permute-done((f32[1,8,128]{2,1,0:T(8,128)S(1)}, f32[1,8,128]{2,1,0:T(8,128)S(1)}, u32[]{:S(2)}, u32[]{:S(2)}) %collective-permute-start.7) | collective-permute-done | bytes 4128 | tf_op jit(solution)/shard_map/ppermute | solution.py:405
  31.8 1.2 %collective-permute-start.8 = (f32[2,8,128]{2,1,0:T(8,128)S(1)}, f32[2,8,128]{2,1,0:T(8,128)S(1)}, u32[]{:S(2)}, u32[]{:S(2)}) collective-permute-start(f32[2,8,128]{2,1,0:T(8,128)S(1)} %get-tuple-element.30._), channel_id=1, source_target_pairs={{0,1},{1,0},{2,3},{3,2},{4,5},{5,4},{6,7},{7,6},{8,9},{9,8},{10,11... | collective-permute-start | bytes 24584 | tf_op jit(solution)/shard_map/ppermute | solution.py:405
  33.0 2.5 %collective-permute-done.8 = f32[2,8,128]{2,1,0:T(8,128)S(1)} collective-permute-done((f32[2,8,128]{2,1,0:T(8,128)S(1)}, f32[2,8,128]{2,1,0:T(8,128)S(1)}, u32[]{:S(2)}, u32[]{:S(2)}) %collective-permute-start.8) | collective-permute-done | bytes 8224 | tf_op jit(solution)/shard_map/ppermute | solution.py:405
  35.6 0.2 collective-permute-done.6.x
  35.9 1.1 %collective-permute-start.14 = (f32[4,8,128]{2,1,0:T(8,128)S(1)}, f32[4,8,128]{2,1,0:T(8,128)S(1)}, u32[]{:S(2)}, u32[]{:S(2)}) collective-permute-start(f32[4,8,128]{2,1,0:T(8,128)S(1)} %constant_dynamic-update-slice_fusion.2._.a), channel_id=1, source_target_pairs={{0,8},{4,20},{8,0},{12,28},{16,24},{20,4},{24,16},{28,12},{1,9},{5... | collective-permute-start | bytes 49160 | tf_op jit(solution)/shard_map/ppermute | solution.py:391
  37.0 0.4 %memory_terms.1.refs_1_.terms = f32[2,512,256]{2,1,0:T(8,128)S(1)} custom-call(bf16[512,256]{1,0:T(8,128)(2,1)S(1)} %ordered.2.refs_0_, bf16[512,256]{1,0:T(8,128)(2,1)S(1)} %collective-permute-done.10.refs_1_, bf16[2,512,1024]{2,1,0:T(8,128)(2,1)S(1)} %copy-done), custom_call_target="tpu_custom_call" | custom-call | flops 1024 | bytes 1024 | tf_op jit(solution)/shard_map/memory_terms/pallas_call | solution.py:299
  37.4 1.8 %finish_first.1 = (bf16[1024,1024]{1,0:T(8,128)(2,1)}, f32[3,512,256]{2,1,0:T(8,128)S(1)}) custom-call(s32[1]{0:T(128)} %bitcast.me_ref, bf16[512,256]{1,0:T(8,128)(2,1)S(1)} %ordered.3.refs_0_, bf16[512,256]{1,0:T(8,128)(2,1)S(1)} %collective-permute-done.12.refs_1_, bf16[512,256]{1,0:T(8,128)(2,1)S(1)} %collective-permute-done.13.refs_2_, ...), custom_call_target="tpu_custom_call" | custom-call | flops 1024 | bytes 1024 | tf_op jit(solution)/shard_map/finish_first/pallas_call | solution.py:280
  39.3 0.4 collective-permute-done.14.b
  39.7 0.3 collective-permute-start.15
  40.0 0.9 %collective-permute-done.15 = f32[8,8,128]{2,1,0:T(8,128)S(1)} collective-permute-done((f32[8,8,128]{2,1,0:T(8,128)S(1)}, f32[8,8,128]{2,1,0:T(8,128)S(1)}, u32[]{:S(2)}, u32[]{:S(2)}) %collective-permute-start.15) | collective-permute-done | bytes 32800 | tf_op jit(solution)/shard_map/ppermute | solution.py:391
  40.9 2.6 %finish_second.1 = (bf16[1024,1024]{1,0:T(8,128)(2,1)}, bf16[1024,1024]{1,0:T(8,128)(2,1)}) custom-call(s32[1]{0:T(128)} %bitcast.me_ref, bf16[512,256]{1,0:T(8,128)(2,1)S(1)} %collective-permute-done.9.last, f32[512,256]{1,0:T(8,128)S(1)} %get-tuple-element.24.term_own, ...), custom_call_target="tpu_custom_call", output_to_operand_aliasing={{0}: (9, {})} | custom-call | flops 1024 | bytes 1024 | tf_op jit(solution)/shard_map/finish_second/pallas_call | solution.py:366
  (25 shorter events, 0.4 us)
Async XLA Ops:
  5.3 2.1 %collective-permute-start.3 = (bf16[2,512,256]{2,1,0:T(8,128)(2,1)S(1)}, bf16[2,512,256]{2,1,0:T(8,128)(2,1)S(1)}, u32[]{:S(2)}, u32[]{:S(2)}) collective-permute-start(bf16[2,512,256]{2,1,0:T(8,128)(2,1)S(1)} %get-tuple-element.19), channel_id=1, source_target_pairs={{0,4},{4,0},{8,12},{12,8},{16,20},{20,16},{24,28},{28,24},{1,5},{5... | collective-permute-start | bytes 1572872 | tf_op jit(solution)/shard_map/ppermute | solution.py:391
  7.2 3.2 %collective-permute-start = (bf16[2,512,256]{2,1,0:T(8,128)(2,1)S(1)}, bf16[2,512,256]{2,1,0:T(8,128)(2,1)S(1)}, u32[]{:S(2)}, u32[]{:S(2)}) collective-permute-start(bf16[2,512,256]{2,1,0:T(8,128)(2,1)S(1)} %memory_product.2), channel_id=1, source_target_pairs={{0,4},{4,0},{8,12},{12,8},{16,20},{20,16},{24,28},{28,24},{1,5},{5... | collective-permute-start | bytes 1572872 | tf_op jit(solution)/shard_map/ppermute | solution.py:391
  7.5 7.2 %collective-permute-start.4 = (bf16[512,256]{1,0:T(8,128)(2,1)S(1)}, bf16[512,256]{1,0:T(8,128)(2,1)S(1)}, u32[]{:S(2)}, u32[]{:S(2)}) collective-permute-start(bf16[512,256]{1,0:T(8,128)(2,1)S(1)} %fusion.4), channel_id=1, source_target_pairs={{0,8},{4,20},{8,0},{12,28},{16,24},{20,4},{24,16},{28,12},{1,9},{5... | collective-permute-start | bytes 786440 | tf_op jit(solution)/shard_map/ppermute | solution.py:391
  11.6 9.6 %copy-start = (bf16[2,512,1024]{2,1,0:T(8,128)(2,1)S(1)}, bf16[2,512,1024]{2,1,0:T(8,128)(2,1)}, u32[]{:S(2)}) copy-start(bf16[2,512,1024]{2,1,0:T(8,128)(2,1)} %w.5) | copy-start | bytes 6291460
  11.6 9.6 %copy-start.1 = (bf16[512,1024]{1,0:T(8,128)(2,1)S(1)}, bf16[512,1024]{1,0:T(8,128)(2,1)}, u32[]{:S(2)}) copy-start(bf16[512,1024]{1,0:T(8,128)(2,1)} %refs_5_.1) | copy-start | bytes 3145732
  11.7 9.6 %copy-start.2 = (f32[32,1024]{1,0:T(8,128)S(1)}, f32[32,1024]{1,0:T(8,128)}, u32[]{:S(2)}) copy-start(f32[32,1024]{1,0:T(8,128)} %coupling.5) | copy-start | bytes 393220
  11.7 7.5 %collective-permute-start.1 = (bf16[512,256]{1,0:T(8,128)(2,1)S(1)}, bf16[512,256]{1,0:T(8,128)(2,1)S(1)}, u32[]{:S(2)}, u32[]{:S(2)}) collective-permute-start(bf16[512,256]{1,0:T(8,128)(2,1)S(1)} %fusion.5._), channel_id=1, source_target_pairs={{0,8},{4,20},{8,0},{12,28},{16,24},{20,4},{24,16},{28,12},{1,9},{5... | collective-permute-start | bytes 786440 | tf_op jit(solution)/shard_map/ppermute | solution.py:391
  14.8 6.5 %collective-permute-start.5 = (bf16[512,256]{1,0:T(8,128)(2,1)S(1)}, bf16[512,256]{1,0:T(8,128)(2,1)S(1)}, u32[]{:S(2)}, u32[]{:S(2)}) collective-permute-start(bf16[512,256]{1,0:T(8,128)(2,1)S(1)} %combined.1.mine), channel_id=1, source_target_pairs={{0,16},{4,12},{8,24},{12,4},{16,0},{20,28},{24,8},{28,20},{1,17},{... | collective-permute-start | bytes 786440 | tf_op jit(solution)/shard_map/ppermute | solution.py:391
  19.3 7.2 %collective-permute-start.2 = (bf16[512,256]{1,0:T(8,128)(2,1)S(1)}, bf16[512,256]{1,0:T(8,128)(2,1)S(1)}, u32[]{:S(2)}, u32[]{:S(2)}) collective-permute-start(bf16[512,256]{1,0:T(8,128)(2,1)S(1)} %fusion.3._.mine), channel_id=1, source_target_pairs={{0,16},{4,12},{8,24},{12,4},{16,0},{20,28},{24,8},{28,20},{1,17},{... | collective-permute-start | bytes 786440 | tf_op jit(solution)/shard_map/ppermute | solution.py:391
  22.4 9.3 %collective-permute-start.11 = (bf16[512,256]{1,0:T(8,128)(2,1)S(1)}, bf16[512,256]{1,0:T(8,128)(2,1)S(1)}, u32[]{:S(2)}, u32[]{:S(2)}) collective-permute-start(bf16[512,256]{1,0:T(8,128)(2,1)S(1)} %get-tuple-element.26), channel_id=1, source_target_pairs={{0,8},{4,20},{8,0},{12,28},{16,24},{20,4},{24,16},{28,12},{1,9},{5... | collective-permute-start | bytes 786440 | tf_op jit(solution)/shard_map/ppermute | solution.py:391
  27.2 4.6 %collective-permute-start.7 = (f32[1,8,128]{2,1,0:T(8,128)S(1)}, f32[1,8,128]{2,1,0:T(8,128)S(1)}, u32[]{:S(2)}, u32[]{:S(2)}) collective-permute-start(f32[1,8,128]{2,1,0:T(8,128)S(1)} %get-tuple-element.23), channel_id=1, source_target_pairs={{0,2},{1,3},{2,0},{3,1},{4,6},{5,7},{6,4},{7,5},{8,10},{9,11},{10,... | collective-permute-start | bytes 12296 | tf_op jit(solution)/shard_map/ppermute | solution.py:405
  29.4 6.4 %collective-permute-start.6 = (bf16[512,256]{1,0:T(8,128)(2,1)S(1)}, bf16[512,256]{1,0:T(8,128)(2,1)S(1)}, u32[]{:S(2)}, u32[]{:S(2)}) collective-permute-start(bf16[512,256]{1,0:T(8,128)(2,1)S(1)} %get-tuple-element.22), channel_id=1, source_target_pairs={{0,8},{4,20},{8,0},{12,28},{16,24},{20,4},{24,16},{28,12},{1,9},{5... | collective-permute-start | bytes 786440 | tf_op jit(solution)/shard_map/ppermute | solution.py:391
  30.4 6.5 %collective-permute-start.10 = (bf16[512,256]{1,0:T(8,128)(2,1)S(1)}, bf16[512,256]{1,0:T(8,128)(2,1)S(1)}, u32[]{:S(2)}, u32[]{:S(2)}) collective-permute-start(bf16[512,256]{1,0:T(8,128)(2,1)S(1)} %get-tuple-element.22), channel_id=1, source_target_pairs={{0,4},{4,0},{8,12},{12,8},{16,20},{20,16},{24,28},{28,24},{1,5},{5... | collective-permute-start | bytes 786440 | tf_op jit(solution)/shard_map/ppermute | solution.py:391
  30.4 7.0 %collective-permute-start.12 = (bf16[512,256]{1,0:T(8,128)(2,1)S(1)}, bf16[512,256]{1,0:T(8,128)(2,1)S(1)}, u32[]{:S(2)}, u32[]{:S(2)}) collective-permute-start(bf16[512,256]{1,0:T(8,128)(2,1)S(1)} %get-tuple-element.26), channel_id=1, source_target_pairs={{0,4},{4,0},{8,12},{12,8},{16,20},{20,16},{24,28},{28,24},{1,5},{5... | collective-permute-start | bytes 786440 | tf_op jit(solution)/shard_map/ppermute | solution.py:391
  31.8 5.7 %collective-permute-start.13 = (bf16[512,256]{1,0:T(8,128)(2,1)S(1)}, bf16[512,256]{1,0:T(8,128)(2,1)S(1)}, u32[]{:S(2)}, u32[]{:S(2)}) collective-permute-start(bf16[512,256]{1,0:T(8,128)(2,1)S(1)} %ordered.3.refs_0_), channel_id=1, source_target_pairs={{0,4},{4,0},{8,12},{12,8},{16,20},{20,16},{24,28},{28,24},{1,5},{5... | collective-permute-start | bytes 786440 | tf_op jit(solution)/shard_map/ppermute | solution.py:391
  31.8 3.7 %collective-permute-start.8 = (f32[2,8,128]{2,1,0:T(8,128)S(1)}, f32[2,8,128]{2,1,0:T(8,128)S(1)}, u32[]{:S(2)}, u32[]{:S(2)}) collective-permute-start(f32[2,8,128]{2,1,0:T(8,128)S(1)} %get-tuple-element.30._), channel_id=1, source_target_pairs={{0,1},{1,0},{2,3},{3,2},{4,5},{5,4},{6,7},{7,6},{8,9},{9,8},{10,11... | collective-permute-start | bytes 24584 | tf_op jit(solution)/shard_map/ppermute | solution.py:405
  35.8 5.1 %collective-permute-start.9 = (bf16[512,256]{1,0:T(8,128)(2,1)S(1)}, bf16[512,256]{1,0:T(8,128)(2,1)S(1)}, u32[]{:S(2)}, u32[]{:S(2)}) collective-permute-start(bf16[512,256]{1,0:T(8,128)(2,1)S(1)} %ordered.2.refs_0_), channel_id=1, source_target_pairs={{0,4},{4,0},{8,12},{12,8},{16,20},{20,16},{24,28},{28,24},{1,5},{5... | collective-permute-start | bytes 786440 | tf_op jit(solution)/shard_map/ppermute | solution.py:391
  35.9 3.8 %collective-permute-start.14 = (f32[4,8,128]{2,1,0:T(8,128)S(1)}, f32[4,8,128]{2,1,0:T(8,128)S(1)}, u32[]{:S(2)}, u32[]{:S(2)}) collective-permute-start(f32[4,8,128]{2,1,0:T(8,128)S(1)} %constant_dynamic-update-slice_fusion.2._.a), channel_id=1, source_target_pairs={{0,8},{4,20},{8,0},{12,28},{16,24},{20,4},{24,16},{28,12},{1,9},{5... | collective-permute-start | bytes 49160 | tf_op jit(solution)/shard_map/ppermute | solution.py:391
  39.7 1.2 %collective-permute-start.15 = (f32[8,8,128]{2,1,0:T(8,128)S(1)}, f32[8,8,128]{2,1,0:T(8,128)S(1)}, u32[]{:S(2)}, u32[]{:S(2)}) collective-permute-start(f32[8,8,128]{2,1,0:T(8,128)S(1)} %joined.1), channel_id=1, source_target_pairs={{0,4},{4,0},{8,12},{12,8},{16,20},{20,16},{24,28},{28,24},{1,5},{5... | collective-permute-start | bytes 98312 | tf_op jit(solution)/shard_map/ppermute | solution.py:391

commit v13 on v12

--- a/solution.py
+++ b/solution.py
@@ -70,7 +70,7 @@
     half = columns // 2
     parts = 4
     eighth = depth // 8
-    chunks = [(0, eighth), (eighth, 3 * eighth), (4 * eighth, 4 * eighth)]
+    chunks = [(0, 2 * eighth), (2 * eighth, 3 * eighth), (5 * eighth, 3 * eighth)]
 
     def kernel(me_ref, sigma_ref, g_ref, sent, kept, sigma_next, g, sigma, total, sems):
         started = []
@@ -305,17 +305,21 @@
     )(*pieces, volterra)
 
 
-def joined(a, b, *after):
-    size = a.shape[0]
-
-    def kernel(a, b, *refs):
+def joined(parts, after=()):
+    size = parts[0].shape[0]
+
+    def kernel(*refs):
         out = refs[-1]
-        out[:size] = a[...]
-        out[size:] = b[...]
-
-    shape = (2 * size,) + a.shape[1:]
-    in_specs = [WHOLE] * 2 + [FAR] * len(after)
-    return call(kernel, "joined", in_specs=in_specs, out_specs=WHOLE, out_shape=near(shape, F32))(a, b, *after)
+        for i in range(len(parts)):
+            out[i * size : (i + 1) * size] = refs[i][...]
+
+    return call(
+        kernel,
+        "joined",
+        in_specs=[WHOLE] * len(parts) + [FAR] * len(after),
+        out_specs=WHOLE,
+        out_shape=near((len(parts) * size,) + parts[0].shape[1:], F32),
+    )(*parts, *after)
 
 
 def ordered(x, after):
@@ -401,6 +405,10 @@
     def passed_on(kept, arrived):
         return (kept[0] + arrived[0].astype(F32)).astype(BF16)
 
+    def from_far(x):
+        flip = [d ^ 1 ^ (1 << (even if d % 2 else odd)[1]) for d in range(past)]
+        return lax.ppermute(x, "past", [(flip[d], d) for d in range(past)])
+
     def widened(share, level):
         return lax.ppermute(share, "second", [(z, z ^ (1 << level)) for z in range(second)])
 
@@ -428,8 +436,7 @@
     partner = ordered(swap(own_1, 1), share)
     terms = memory_terms([partner, swap(own_1, 0)], volterra)
     last = swap(partner, 0)
-    share = joined(share, swap(share, 1), cubic, terms)
-    shares = jnp.concatenate([share, swap(share, 0)])
+    shares = joined([share, swap(share, 0), swap(share, 1), from_far(share)], [cubic, terms])
     results = finish_second(
         me, last, term_own, terms, volterra, cubic_own, cubic, shares, coupling, g_first, bits
     )

time: 43.6 us -> 43.4 us (level)
  waiting for transfers between devices: 11.4 us -> 10.7 us
  starting transfers between devices: 17 us -> 17.6 us
    ppermute x0 -> x1, starting transfers between devices: none -> 1.17 us  [from_far(): return lax.ppermute(x, 'past', [(flip[d], d) for d in range(past)])]
    ppermute x14, waiting for transfers between devices: 8.14 us -> 7.49 us  [swap(): return lax.ppermute(x, 'past', pairs)]
    ppermute x14, starting transfers between devices: 13.6 us -> 13.1 us  [swap(): return lax.ppermute(x, 'past', pairs)]
  transfers between devices with their start and end apart: 16 -> 17, of which waited for: 10 -> 9; matrix products, arithmetic and copies ran while one was open for 0% -> 0% of each run, Pallas kernels for 16% -> 16%
where the time goes in v13:
time: 43.4 us; the launch traced here: 43.2 us
  starting transfers between devices  17.6 us (41%)
  Pallas kernels  13.8 us (32%)
  waiting for transfers between devices  10.7 us (25%)
  between operations  0.8 us (2%)
    ppermute x14, starting transfers between devices, swap(): return lax.ppermute(x, 'past', pairs)  13.1 us
    ppermute x14, waiting for transfers between devices, swap(): return lax.ppermute(x, 'past', pairs)  7.49 us
    pallas_call x1, Pallas kernels, first_products(): call(kernel, 'first_products', in_specs=[SCALAR, HBM, HBM], out_specs=[WH...  4.5 us
    ppermute x2, starting transfers between devices, widened(): lax.ppermute(share, 'second', [(z, z ^ 1 << level) for z in range(second)])  3.32 us
    ppermute x2, waiting for transfers between devices, widened(): lax.ppermute(share, 'second', [(z, z ^ 1 << level) for z in range(second)])  3.21 us
    pallas_call x1, Pallas kernels, finish_second(): call(kernel, 'finish_second', in_specs=[SCALAR] + [WHOLE] * 8 + [HBM], ou...  2.57 us
    pallas_call x2, Pallas kernels, product(): call(kernel, 'memory_product', in_specs=[SCALAR, WHOLE, WHOLE] + [FAR] *...  2.56 us
    pallas_call x1, Pallas kernels, finish_first(): call(kernel, 'finish_first', in_specs=[SCALAR] + [WHOLE] * 7, out_specs=[...  1.85 us
  transfers between devices with their start and end apart: 17, of which 9 were waited for; matrix products, arithmetic and copies ran while one was open for 0% of the time, Pallas kernels for 16%

profile of v13, /device:TPU:0, one launch (start us, length us, event | category | flops | bytes accessed | tf_op | source)
XLA Modules:
  0.0 43.2 jit_solution(7658710150098570437)
XLA Ops:
  0.6 4.5 %first_products.1 = (bf16[2,512,256]{2,1,0:T(8,128)(2,1)S(1)}, f32[2,512,256]{2,1,0:T(8,128)S(1)}, bf16[512,2048]{1,0:T(8,128)(2,1)S(1)}, bf16[2048,1024]{1,0:T(8,128)(2,1)S(1)}) custom-call(s32[1]{0:T(128)} %bitcast.me_ref, bf16[1024,2048]{1,0:T(8,128)(2,1)} %sigma_ref.1, bf16[2048,1024]{1,0:T(8,128)(2,1)} %g_ref.1), custom_call_target="tpu_custom_call" | custom-call | flops 1024 | bytes 1024 | tf_op jit(solution)/shard_map/first_products/pallas_call | solution.py:113
  5.1 0.6 %collective-permute-start.3 = (bf16[2,512,256]{2,1,0:T(8,128)(2,1)S(1)}, bf16[2,512,256]{2,1,0:T(8,128)(2,1)S(1)}, u32[]{:S(2)}, u32[]{:S(2)}) collective-permute-start(bf16[2,512,256]{2,1,0:T(8,128)(2,1)S(1)} %get-tuple-element.19), channel_id=1, source_target_pairs={{0,4},{4,0},{8,12},{12,8},{16,20},{20,16},{24,28},{28,24},{1,5},{5... | collective-permute-start | bytes 1572872 | tf_op jit(solution)/shard_map/ppermute | solution.py:395
  5.7 1.3 %memory_product.2 = bf16[2,512,256]{2,1,0:T(8,128)(2,1)S(1)} custom-call(s32[1]{0:T(128)} %bitcast.me_ref, bf16[512,2048]{1,0:T(8,128)(2,1)S(1)} %get-tuple-element.16.sigma, bf16[2048,1024]{1,0:T(8,128)(2,1)S(1)} %get-tuple-element.17.g), custom_call_target="tpu_custom_call" | custom-call | flops 1024 | bytes 1024 | tf_op jit(solution)/shard_map/memory_product/pallas_call | solution.py:146
  7.0 0.1 collective-permute-start
  7.1 0.2 collective-permute-done.3.arrived
  7.3 2.8 %collective-permute-start.4 = (bf16[512,256]{1,0:T(8,128)(2,1)S(1)}, bf16[512,256]{1,0:T(8,128)(2,1)S(1)}, u32[]{:S(2)}, u32[]{:S(2)}) collective-permute-start(bf16[512,256]{1,0:T(8,128)(2,1)S(1)} %fusion.4), channel_id=1, source_target_pairs={{0,8},{4,20},{8,0},{12,28},{16,24},{20,4},{24,16},{28,12},{1,9},{5... | collective-permute-start | bytes 786440 | tf_op jit(solution)/shard_map/ppermute | solution.py:395
  10.2 1.3 %memory_product.3 = f32[2,512,256]{2,1,0:T(8,128)S(1)} custom-call(s32[1]{0:T(128)} %bitcast.me_ref, bf16[512,2048]{1,0:T(8,128)(2,1)S(1)} %get-tuple-element.16.sigma, bf16[2048,1024]{1,0:T(8,128)(2,1)S(1)} %get-tuple-element.17.g, bf16[2,512,256]{2,1,0:T(8,128)(2,1)S(1)} %collective-permute-done.refs_0_), custom_call_target="tpu_custom_call" | custom-call | flops 1024 | bytes 1024 | tf_op jit(solution)/shard_map/memory_product/pallas_call | solution.py:146
  11.6 1.4 %collective-permute-start.1 = (bf16[512,256]{1,0:T(8,128)(2,1)S(1)}, bf16[512,256]{1,0:T(8,128)(2,1)S(1)}, u32[]{:S(2)}, u32[]{:S(2)}) collective-permute-start(bf16[512,256]{1,0:T(8,128)(2,1)S(1)} %fusion.5._), channel_id=1, source_target_pairs={{0,8},{4,20},{8,0},{12,28},{16,24},{20,4},{24,16},{28,12},{1,9},{5... | collective-permute-start | bytes 786440 | tf_op jit(solution)/shard_map/ppermute | solution.py:395
  13.0 1.5 %collective-permute-done.4.more = bf16[512,256]{1,0:T(8,128)(2,1)S(1)} collective-permute-done((bf16[512,256]{1,0:T(8,128)(2,1)S(1)}, bf16[512,256]{1,0:T(8,128)(2,1)S(1)}, u32[]{:S(2)}, u32[]{:S(2)}) %collective-permute-start.4) | collective-permute-done | bytes 262176 | tf_op jit(solution)/shard_map/ppermute | solution.py:395
  14.5 0.1 combined.1.mine
  14.6 2.1 %collective-permute-start.5 = (bf16[512,256]{1,0:T(8,128)(2,1)S(1)}, bf16[512,256]{1,0:T(8,128)(2,1)S(1)}, u32[]{:S(2)}, u32[]{:S(2)}) collective-permute-start(bf16[512,256]{1,0:T(8,128)(2,1)S(1)} %combined.1.mine), channel_id=1, source_target_pairs={{0,16},{4,12},{8,24},{12,4},{16,0},{20,28},{24,8},{28,20},{1,17},{... | collective-permute-start | bytes 786440 | tf_op jit(solution)/shard_map/ppermute | solution.py:395
  16.7 2.3 %collective-permute-done.1 = bf16[512,256]{1,0:T(8,128)(2,1)S(1)} collective-permute-done((bf16[512,256]{1,0:T(8,128)(2,1)S(1)}, bf16[512,256]{1,0:T(8,128)(2,1)S(1)}, u32[]{:S(2)}, u32[]{:S(2)}) %collective-permute-start.1) | collective-permute-done | bytes 262176 | tf_op jit(solution)/shard_map/ppermute | solution.py:395
  19.1 0.1 fusion.3._.mine
  19.2 1.4 %collective-permute-start.2 = (bf16[512,256]{1,0:T(8,128)(2,1)S(1)}, bf16[512,256]{1,0:T(8,128)(2,1)S(1)}, u32[]{:S(2)}, u32[]{:S(2)}) collective-permute-start(bf16[512,256]{1,0:T(8,128)(2,1)S(1)} %fusion.3._.mine), channel_id=1, source_target_pairs={{0,16},{4,12},{8,24},{12,4},{16,0},{20,28},{24,8},{28,20},{1,17},{... | collective-permute-start | bytes 786440 | tf_op jit(solution)/shard_map/ppermute | solution.py:395
  20.5 0.6 %collective-permute-done.5.theirs = bf16[512,256]{1,0:T(8,128)(2,1)S(1)} collective-permute-done((bf16[512,256]{1,0:T(8,128)(2,1)S(1)}, bf16[512,256]{1,0:T(8,128)(2,1)S(1)}, u32[]{:S(2)}, u32[]{:S(2)}) %collective-permute-start.5) | collective-permute-done | bytes 262176 | tf_op jit(solution)/shard_map/ppermute | solution.py:395
  21.1 1.2 %own_first.1 = (bf16[512,256]{1,0:T(8,128)(2,1)S(1)}, f32[512,256]{1,0:T(8,128)S(1)}, f32[1,128]{1,0:T(1,128)S(1)}, bf16[512,256]{1,0:T(8,128)(2,1)S(1)}, f32[512,256]{1,0:T(8,128)S(1)}) custom-call(s32[1]{0:T(128)} %bitcast.me_ref, bf16[512,256]{1,0:T(8,128)(2,1)S(1)} %combined.1.mine, bf16[512,256]{1,0:T(8,128)(2,1)S(1)} %collective-permute-done.5.theirs, ...), custom_call_target="tpu_custom_call" | custom-call | flops 1024 | bytes 1024 | tf_op jit(solution)/shard_map/own_first/pallas_call | solution.py:208
  22.3 2.1 %collective-permute-start.11 = (bf16[512,256]{1,0:T(8,128)(2,1)S(1)}, bf16[512,256]{1,0:T(8,128)(2,1)S(1)}, u32[]{:S(2)}, u32[]{:S(2)}) collective-permute-start(bf16[512,256]{1,0:T(8,128)(2,1)S(1)} %get-tuple-element.26), channel_id=1, source_target_pairs={{0,8},{4,20},{8,0},{12,28},{16,24},{20,4},{24,16},{28,12},{1,9},{5... | collective-permute-start | bytes 786440 | tf_op jit(solution)/shard_map/ppermute | solution.py:395
  24.3 2.0 %collective-permute-done.2.theirs = bf16[512,256]{1,0:T(8,128)(2,1)S(1)} collective-permute-done((bf16[512,256]{1,0:T(8,128)(2,1)S(1)}, bf16[512,256]{1,0:T(8,128)(2,1)S(1)}, u32[]{:S(2)}, u32[]{:S(2)}) %collective-permute-start.2) | collective-permute-done | bytes 262176 | tf_op jit(solution)/shard_map/ppermute | solution.py:395
  26.4 0.6 %own_second.1 = (bf16[512,256]{1,0:T(8,128)(2,1)S(1)}, f32[1,8,128]{2,1,0:T(8,128)S(1)}, f32[512,256]{1,0:T(8,128)S(1)}) custom-call(s32[1]{0:T(128)} %bitcast.me_ref, bf16[512,256]{1,0:T(8,128)(2,1)S(1)} %fusion.3._.mine, bf16[512,256]{1,0:T(8,128)(2,1)S(1)} %collective-permute-done.2.theirs, bf16[2,512,1024]{2,1,0:T(8,128)(2,1)S(1)} %copy-done, ...), custom_call_target="tpu_custom_call" | custom-call | flops 1024 | bytes 1024 | tf_op jit(solution)/shard_map/own_second/pallas_call | solution.py:246
  27.0 2.2 %collective-permute-start.7 = (f32[1,8,128]{2,1,0:T(8,128)S(1)}, f32[1,8,128]{2,1,0:T(8,128)S(1)}, u32[]{:S(2)}, u32[]{:S(2)}) collective-permute-start(f32[1,8,128]{2,1,0:T(8,128)S(1)} %get-tuple-element.23), channel_id=1, source_target_pairs={{0,2},{1,3},{2,0},{3,1},{4,6},{5,7},{6,4},{7,5},{8,10},{9,11},{10,... | collective-permute-start | bytes 12296 | tf_op jit(solution)/shard_map/ppermute | solution.py:413
  29.2 1.1 %collective-permute-start.6 = (bf16[512,256]{1,0:T(8,128)(2,1)S(1)}, bf16[512,256]{1,0:T(8,128)(2,1)S(1)}, u32[]{:S(2)}, u32[]{:S(2)}) collective-permute-start(bf16[512,256]{1,0:T(8,128)(2,1)S(1)} %get-tuple-element.22), channel_id=1, source_target_pairs={{0,8},{4,20},{8,0},{12,28},{16,24},{20,4},{24,16},{28,12},{1,9},{5... | collective-permute-start | bytes 786440 | tf_op jit(solution)/shard_map/ppermute | solution.py:395
  30.3 1.3 %collective-permute-done.7 = f32[1,8,128]{2,1,0:T(8,128)S(1)} collective-permute-done((f32[1,8,128]{2,1,0:T(8,128)S(1)}, f32[1,8,128]{2,1,0:T(8,128)S(1)}, u32[]{:S(2)}, u32[]{:S(2)}) %collective-permute-start.7) | collective-permute-done | bytes 4128 | tf_op jit(solution)/shard_map/ppermute | solution.py:413
  31.6 1.1 %collective-permute-start.8 = (f32[2,8,128]{2,1,0:T(8,128)S(1)}, f32[2,8,128]{2,1,0:T(8,128)S(1)}, u32[]{:S(2)}, u32[]{:S(2)}) collective-permute-start(f32[2,8,128]{2,1,0:T(8,128)S(1)} %get-tuple-element.30._), channel_id=1, source_target_pairs={{0,1},{1,0},{2,3},{3,2},{4,5},{5,4},{6,7},{7,6},{8,9},{9,8},{10,11... | collective-permute-start | bytes 24584 | tf_op jit(solution)/shard_map/ppermute | solution.py:413
  32.7 0.5 %collective-permute-start.12 = (bf16[512,256]{1,0:T(8,128)(2,1)S(1)}, bf16[512,256]{1,0:T(8,128)(2,1)S(1)}, u32[]{:S(2)}, u32[]{:S(2)}) collective-permute-start(bf16[512,256]{1,0:T(8,128)(2,1)S(1)} %get-tuple-element.26), channel_id=1, source_target_pairs={{0,4},{4,0},{8,12},{12,8},{16,20},{20,16},{24,28},{28,24},{1,5},{5... | collective-permute-start | bytes 786440 | tf_op jit(solution)/shard_map/ppermute | solution.py:395
  33.3 1.9 %collective-permute-done.8 = f32[2,8,128]{2,1,0:T(8,128)S(1)} collective-permute-done((f32[2,8,128]{2,1,0:T(8,128)S(1)}, f32[2,8,128]{2,1,0:T(8,128)S(1)}, u32[]{:S(2)}, u32[]{:S(2)}) %collective-permute-start.8) | collective-permute-done | bytes 8224 | tf_op jit(solution)/shard_map/ppermute | solution.py:413
  35.2 0.4 collective-permute-done.6.x
  35.7 1.2 %collective-permute-start.16 = (f32[4,8,128]{2,1,0:T(8,128)S(1)}, f32[4,8,128]{2,1,0:T(8,128)S(1)}, u32[]{:S(2)}, u32[]{:S(2)}) collective-permute-start(f32[4,8,128]{2,1,0:T(8,128)S(1)} %constant_dynamic-update-slice_fusion.2._.refs_0_), channel_id=1, source_target_pairs={{20,0},{8,4},{28,8},{0,12},{4,16},{24,20},{12,24},{16,28},{21,1},{... | collective-permute-start | bytes 49160 | tf_op jit(solution)/shard_map/ppermute | solution.py:410
  36.9 1.0 %collective-permute-start.15 = (f32[4,8,128]{2,1,0:T(8,128)S(1)}, f32[4,8,128]{2,1,0:T(8,128)S(1)}, u32[]{:S(2)}, u32[]{:S(2)}) collective-permute-start(f32[4,8,128]{2,1,0:T(8,128)S(1)} %constant_dynamic-update-slice_fusion.2._.refs_0_), channel_id=1, source_target_pairs={{0,8},{4,20},{8,0},{12,28},{16,24},{20,4},{24,16},{28,12},{1,9},{5... | collective-permute-start | bytes 49160 | tf_op jit(solution)/shard_map/ppermute | solution.py:395
  37.8 0.4 %memory_terms.1.refs_5_.terms = f32[2,512,256]{2,1,0:T(8,128)S(1)} custom-call(bf16[512,256]{1,0:T(8,128)(2,1)S(1)} %ordered.2.refs_0_, bf16[512,256]{1,0:T(8,128)(2,1)S(1)} %collective-permute-done.10.refs_1_, bf16[2,512,1024]{2,1,0:T(8,128)(2,1)S(1)} %copy-done), custom_call_target="tpu_custom_call" | custom-call | flops 1024 | bytes 1024 | tf_op jit(solution)/shard_map/memory_terms/pallas_call | solution.py:299
  38.3 1.8 %finish_first.1 = (bf16[1024,1024]{1,0:T(8,128)(2,1)}, f32[3,512,256]{2,1,0:T(8,128)S(1)}) custom-call(s32[1]{0:T(128)} %bitcast.me_ref, bf16[512,256]{1,0:T(8,128)(2,1)S(1)} %ordered.3.refs_0_, bf16[512,256]{1,0:T(8,128)(2,1)S(1)} %collective-permute-done.12.refs_1_, bf16[512,256]{1,0:T(8,128)(2,1)S(1)} %collective-permute-done.13.refs_2_, ...), custom_call_target="tpu_custom_call" | custom-call | flops 1024 | bytes 1024 | tf_op jit(solution)/shard_map/finish_first/pallas_call | solution.py:280
  40.2 0.5 %collective-permute-done.15.refs_2_ = f32[4,8,128]{2,1,0:T(8,128)S(1)} collective-permute-done((f32[4,8,128]{2,1,0:T(8,128)S(1)}, f32[4,8,128]{2,1,0:T(8,128)S(1)}, u32[]{:S(2)}, u32[]{:S(2)}) %collective-permute-start.15) | collective-permute-done | bytes 16416 | tf_op jit(solution)/shard_map/ppermute | solution.py:395
  40.6 2.6 %finish_second.1 = (bf16[1024,1024]{1,0:T(8,128)(2,1)}, bf16[1024,1024]{1,0:T(8,128)(2,1)}) custom-call(s32[1]{0:T(128)} %bitcast.me_ref, bf16[512,256]{1,0:T(8,128)(2,1)S(1)} %collective-permute-done.9.last, f32[512,256]{1,0:T(8,128)S(1)} %get-tuple-element.24.term_own, ...), custom_call_target="tpu_custom_call", output_to_operand_aliasing={{0}: (9, {})} | custom-call | flops 1024 | bytes 1024 | tf_op jit(solution)/shard_map/finish_second/pallas_call | solution.py:370
  (26 shorter events, 0.4 us)
Async XLA Ops:
  5.1 2.1 %collective-permute-start.3 = (bf16[2,512,256]{2,1,0:T(8,128)(2,1)S(1)}, bf16[2,512,256]{2,1,0:T(8,128)(2,1)S(1)}, u32[]{:S(2)}, u32[]{:S(2)}) collective-permute-start(bf16[2,512,256]{2,1,0:T(8,128)(2,1)S(1)} %get-tuple-element.19), channel_id=1, source_target_pairs={{0,4},{4,0},{8,12},{12,8},{16,20},{20,16},{24,28},{28,24},{1,5},{5... | collective-permute-start | bytes 1572872 | tf_op jit(solution)/shard_map/ppermute | solution.py:395
  7.0 3.2 %collective-permute-start = (bf16[2,512,256]{2,1,0:T(8,128)(2,1)S(1)}, bf16[2,512,256]{2,1,0:T(8,128)(2,1)S(1)}, u32[]{:S(2)}, u32[]{:S(2)}) collective-permute-start(bf16[2,512,256]{2,1,0:T(8,128)(2,1)S(1)} %memory_product.2), channel_id=1, source_target_pairs={{0,4},{4,0},{8,12},{12,8},{16,20},{20,16},{24,28},{28,24},{1,5},{5... | collective-permute-start | bytes 1572872 | tf_op jit(solution)/shard_map/ppermute | solution.py:395
  7.3 7.2 %collective-permute-start.4 = (bf16[512,256]{1,0:T(8,128)(2,1)S(1)}, bf16[512,256]{1,0:T(8,128)(2,1)S(1)}, u32[]{:S(2)}, u32[]{:S(2)}) collective-permute-start(bf16[512,256]{1,0:T(8,128)(2,1)S(1)} %fusion.4), channel_id=1, source_target_pairs={{0,8},{4,20},{8,0},{12,28},{16,24},{20,4},{24,16},{28,12},{1,9},{5... | collective-permute-start | bytes 786440 | tf_op jit(solution)/shard_map/ppermute | solution.py:395
  11.5 9.6 %copy-start = (bf16[2,512,1024]{2,1,0:T(8,128)(2,1)S(1)}, bf16[2,512,1024]{2,1,0:T(8,128)(2,1)}, u32[]{:S(2)}) copy-start(bf16[2,512,1024]{2,1,0:T(8,128)(2,1)} %w.5) | copy-start | bytes 6291460
  11.5 9.6 %copy-start.1 = (bf16[512,1024]{1,0:T(8,128)(2,1)S(1)}, bf16[512,1024]{1,0:T(8,128)(2,1)}, u32[]{:S(2)}) copy-start(bf16[512,1024]{1,0:T(8,128)(2,1)} %refs_5_.1) | copy-start | bytes 3145732
  11.5 9.6 %copy-start.2 = (f32[32,1024]{1,0:T(8,128)S(1)}, f32[32,1024]{1,0:T(8,128)}, u32[]{:S(2)}) copy-start(f32[32,1024]{1,0:T(8,128)} %coupling.5) | copy-start | bytes 393220
  11.6 7.5 %collective-permute-start.1 = (bf16[512,256]{1,0:T(8,128)(2,1)S(1)}, bf16[512,256]{1,0:T(8,128)(2,1)S(1)}, u32[]{:S(2)}, u32[]{:S(2)}) collective-permute-start(bf16[512,256]{1,0:T(8,128)(2,1)S(1)} %fusion.5._), channel_id=1, source_target_pairs={{0,8},{4,20},{8,0},{12,28},{16,24},{20,4},{24,16},{28,12},{1,9},{5... | collective-permute-start | bytes 786440 | tf_op jit(solution)/shard_map/ppermute | solution.py:395
  14.6 6.5 %collective-permute-start.5 = (bf16[512,256]{1,0:T(8,128)(2,1)S(1)}, bf16[512,256]{1,0:T(8,128)(2,1)S(1)}, u32[]{:S(2)}, u32[]{:S(2)}) collective-permute-start(bf16[512,256]{1,0:T(8,128)(2,1)S(1)} %combined.1.mine), channel_id=1, source_target_pairs={{0,16},{4,12},{8,24},{12,4},{16,0},{20,28},{24,8},{28,20},{1,17},{... | collective-permute-start | bytes 786440 | tf_op jit(solution)/shard_map/ppermute | solution.py:395
  19.2 7.2 %collective-permute-start.2 = (bf16[512,256]{1,0:T(8,128)(2,1)S(1)}, bf16[512,256]{1,0:T(8,128)(2,1)S(1)}, u32[]{:S(2)}, u32[]{:S(2)}) collective-permute-start(bf16[512,256]{1,0:T(8,128)(2,1)S(1)} %fusion.3._.mine), channel_id=1, source_target_pairs={{0,16},{4,12},{8,24},{12,4},{16,0},{20,28},{24,8},{28,20},{1,17},{... | collective-permute-start | bytes 786440 | tf_op jit(solution)/shard_map/ppermute | solution.py:395
  22.3 10.9 %collective-permute-start.11 = (bf16[512,256]{1,0:T(8,128)(2,1)S(1)}, bf16[512,256]{1,0:T(8,128)(2,1)S(1)}, u32[]{:S(2)}, u32[]{:S(2)}) collective-permute-start(bf16[512,256]{1,0:T(8,128)(2,1)S(1)} %get-tuple-element.26), channel_id=1, source_target_pairs={{0,8},{4,20},{8,0},{12,28},{16,24},{20,4},{24,16},{28,12},{1,9},{5... | collective-permute-start | bytes 786440 | tf_op jit(solution)/shard_map/ppermute | solution.py:395
  27.0 4.6 %collective-permute-start.7 = (f32[1,8,128]{2,1,0:T(8,128)S(1)}, f32[1,8,128]{2,1,0:T(8,128)S(1)}, u32[]{:S(2)}, u32[]{:S(2)}) collective-permute-start(f32[1,8,128]{2,1,0:T(8,128)S(1)} %get-tuple-element.23), channel_id=1, source_target_pairs={{0,2},{1,3},{2,0},{3,1},{4,6},{5,7},{6,4},{7,5},{8,10},{9,11},{10,... | collective-permute-start | bytes 12296 | tf_op jit(solution)/shard_map/ppermute | solution.py:413
  29.2 6.4 %collective-permute-start.6 = (bf16[512,256]{1,0:T(8,128)(2,1)S(1)}, bf16[512,256]{1,0:T(8,128)(2,1)S(1)}, u32[]{:S(2)}, u32[]{:S(2)}) collective-permute-start(bf16[512,256]{1,0:T(8,128)(2,1)S(1)} %get-tuple-element.22), channel_id=1, source_target_pairs={{0,8},{4,20},{8,0},{12,28},{16,24},{20,4},{24,16},{28,12},{1,9},{5... | collective-permute-start | bytes 786440 | tf_op jit(solution)/shard_map/ppermute | solution.py:395
  31.6 3.7 %collective-permute-start.8 = (f32[2,8,128]{2,1,0:T(8,128)S(1)}, f32[2,8,128]{2,1,0:T(8,128)S(1)}, u32[]{:S(2)}, u32[]{:S(2)}) collective-permute-start(f32[2,8,128]{2,1,0:T(8,128)S(1)} %get-tuple-element.30._), channel_id=1, source_target_pairs={{0,1},{1,0},{2,3},{3,2},{4,5},{5,4},{6,7},{7,6},{8,9},{9,8},{10,11... | collective-permute-start | bytes 24584 | tf_op jit(solution)/shard_map/ppermute | solution.py:413
  32.7 4.2 %collective-permute-start.10 = (bf16[512,256]{1,0:T(8,128)(2,1)S(1)}, bf16[512,256]{1,0:T(8,128)(2,1)S(1)}, u32[]{:S(2)}, u32[]{:S(2)}) collective-permute-start(bf16[512,256]{1,0:T(8,128)(2,1)S(1)} %get-tuple-element.22), channel_id=1, source_target_pairs={{0,4},{4,0},{8,12},{12,8},{16,20},{20,16},{24,28},{28,24},{1,5},{5... | collective-permute-start | bytes 786440 | tf_op jit(solution)/shard_map/ppermute | solution.py:395
  32.7 5.1 %collective-permute-start.12 = (bf16[512,256]{1,0:T(8,128)(2,1)S(1)}, bf16[512,256]{1,0:T(8,128)(2,1)S(1)}, u32[]{:S(2)}, u32[]{:S(2)}) collective-permute-start(bf16[512,256]{1,0:T(8,128)(2,1)S(1)} %get-tuple-element.26), channel_id=1, source_target_pairs={{0,4},{4,0},{8,12},{12,8},{16,20},{20,16},{24,28},{28,24},{1,5},{5... | collective-permute-start | bytes 786440 | tf_op jit(solution)/shard_map/ppermute | solution.py:395
  33.2 5.1 %collective-permute-start.13 = (bf16[512,256]{1,0:T(8,128)(2,1)S(1)}, bf16[512,256]{1,0:T(8,128)(2,1)S(1)}, u32[]{:S(2)}, u32[]{:S(2)}) collective-permute-start(bf16[512,256]{1,0:T(8,128)(2,1)S(1)} %ordered.3.refs_0_), channel_id=1, source_target_pairs={{0,4},{4,0},{8,12},{12,8},{16,20},{20,16},{24,28},{28,24},{1,5},{5... | collective-permute-start | bytes 786440 | tf_op jit(solution)/shard_map/ppermute | solution.py:395
  35.6 5.0 %collective-permute-start.9 = (bf16[512,256]{1,0:T(8,128)(2,1)S(1)}, bf16[512,256]{1,0:T(8,128)(2,1)S(1)}, u32[]{:S(2)}, u32[]{:S(2)}) collective-permute-start(bf16[512,256]{1,0:T(8,128)(2,1)S(1)} %ordered.2.refs_0_), channel_id=1, source_target_pairs={{0,4},{4,0},{8,12},{12,8},{16,20},{20,16},{24,28},{28,24},{1,5},{5... | collective-permute-start | bytes 786440 | tf_op jit(solution)/shard_map/ppermute | solution.py:395
  35.7 4.4 %collective-permute-start.16 = (f32[4,8,128]{2,1,0:T(8,128)S(1)}, f32[4,8,128]{2,1,0:T(8,128)S(1)}, u32[]{:S(2)}, u32[]{:S(2)}) collective-permute-start(f32[4,8,128]{2,1,0:T(8,128)S(1)} %constant_dynamic-update-slice_fusion.2._.refs_0_), channel_id=1, source_target_pairs={{20,0},{8,4},{28,8},{0,12},{4,16},{24,20},{12,24},{16,28},{21,1},{... | collective-permute-start | bytes 49160 | tf_op jit(solution)/shard_map/ppermute | solution.py:410
  36.9 3.7 %collective-permute-start.15 = (f32[4,8,128]{2,1,0:T(8,128)S(1)}, f32[4,8,128]{2,1,0:T(8,128)S(1)}, u32[]{:S(2)}, u32[]{:S(2)}) collective-permute-start(f32[4,8,128]{2,1,0:T(8,128)S(1)} %constant_dynamic-update-slice_fusion.2._.refs_0_), channel_id=1, source_target_pairs={{0,8},{4,20},{8,0},{12,28},{16,24},{20,4},{24,16},{28,12},{1,9},{5... | collective-permute-start | bytes 49160 | tf_op jit(solution)/shard_map/ppermute | solution.py:395
  37.8 2.8 %collective-permute-start.14 = (f32[4,8,128]{2,1,0:T(8,128)S(1)}, f32[4,8,128]{2,1,0:T(8,128)S(1)}, u32[]{:S(2)}, u32[]{:S(2)}) collective-permute-start(f32[4,8,128]{2,1,0:T(8,128)S(1)} %constant_dynamic-update-slice_fusion.2._.refs_0_), channel_id=1, source_target_pairs={{0,4},{4,0},{8,12},{12,8},{16,20},{20,16},{24,28},{28,24},{1,5},{5... | collective-permute-start | bytes 49160 | tf_op jit(solution)/shard_map/ppermute | solution.py:395

commit v14 on v13

--- a/solution.py
+++ b/solution.py
@@ -252,12 +252,31 @@
     )(me, mine, theirs, volterra, response, squares, coupling)
 
 
-def finish_first(me, pieces, g_own, volterra, edge, coupling, bits):
+def finish_other(me, piece, volterra, edge, coupling, bits):
+    rows, width = piece.shape
+
+    def kernel(me_ref, piece, w, edge, coupling, g_out, cubic):
+        at = columns_of(Place(me_ref[0], bits).quarter_of(2), width)
+        g = jnp.dot(w[0, :, :rows], piece[...], preferred_element_type=F32)
+        g += jnp.dot(w[0, :, rows:], edge[:, at], preferred_element_type=F32)
+        g_out[...] = g.astype(BF16)
+        cubic[...] = cubed(g, coupling[:, at])
+
+    return call(
+        kernel,
+        "finish_other",
+        in_specs=[SCALAR] + [WHOLE] * 4,
+        out_specs=[WHOLE] * 2,
+        out_shape=[near((rows, width), BF16), near((rows, width), F32)],
+    )(me, piece, volterra, edge, coupling)
+
+
+def finish_first(me, pieces, g_own, g_other, volterra, edge, coupling, bits):
     rows, width = pieces[0].shape
     columns = coupling.shape[1]
 
     def kernel(me_ref, *refs):
-        pieces, (g_own, w, edge, coupling, g_out, cubic, held, sems) = refs[:3], refs[3:]
+        pieces, (g_own, g_other, w, edge, coupling, g_out, cubic, held, sems) = refs[:2], refs[2:]
         place = Place(me_ref[0], bits)
 
         def write(source, slot):
@@ -267,12 +286,13 @@
 
         copies = []
         write(g_own, 0)
-        for i in range(3):
-            at = columns_of(place.quarter_of(i + 1), width)
+        write(g_other, 2)
+        for i, slot in enumerate((1, 3)):
+            at = columns_of(place.quarter_of(slot), width)
             g = jnp.dot(w[0, :, :rows], pieces[i][...], preferred_element_type=F32)
             g += jnp.dot(w[0, :, rows:], edge[:, at], preferred_element_type=F32)
             held[i] = g.astype(BF16)
-            write(held.at[i], i + 1)
+            write(held.at[i], slot)
             cubic[i] = cubed(g, coupling[:, at])
         for copy in copies:
             copy.wait()
@@ -282,9 +302,9 @@
         "finish_first",
         in_specs=[SCALAR] + [WHOLE] * 7,
         out_specs=[HBM, WHOLE],
-        out_shape=[jax.ShapeDtypeStruct((2 * rows, columns), BF16), near((3, rows, width), F32)],
-        scratch_shapes=[pltpu.VMEM((3, rows, width), BF16), pltpu.SemaphoreType.DMA((4,))],
-    )(me, *pieces, g_own, volterra, edge, coupling)
+        out_shape=[jax.ShapeDtypeStruct((2 * rows, columns), BF16), near((2, rows, width), F32)],
+        scratch_shapes=[pltpu.VMEM((2, rows, width), BF16), pltpu.SemaphoreType.DMA((4,))],
+    )(me, *pieces, g_own, g_other, volterra, edge, coupling)
 
 
 def memory_terms(pieces, volterra):
@@ -322,19 +342,22 @@
     )(*parts, *after)
 
 
-def ordered(x, after):
-    def kernel(x, _, out):
-        out[...] = x[...]
-
-    return call(kernel, "ordered", in_specs=[WHOLE, FAR], out_specs=WHOLE, out_shape=near(x.shape, x.dtype))(x, after)
-
-
-def finish_second(me, last, term_own, terms, volterra, cubic_own, cubic, shares, coupling, g_first, bits):
+def ordered(x, *after):
+    def kernel(x, *refs):
+        refs[-1][...] = x[...]
+
+    in_specs = [WHOLE] + [FAR] * len(after)
+    return call(kernel, "ordered", in_specs=in_specs, out_specs=WHOLE, out_shape=near(x.shape, x.dtype))(x, *after)
+
+
+def finish_second(me, last, term_own, terms, volterra, cubic_own, cubic_other, cubic, shares, coupling, g_first, bits):
     rows, width = last.shape
     columns = coupling.shape[1]
     everyone = shares.shape[0]
 
-    def kernel(me_ref, last, term_own, terms, w, cubic_own, cubic, shares, coupling, _, g_out, sigma, g_held, s_held, sems):
+    def kernel(me_ref, *refs):
+        last, term_own, terms, w, cubic_own, cubic_other, cubic, shares, coupling, _ = refs[:10]
+        g_out, sigma, g_held, s_held, sems = refs[10:]
         place = Place(me_ref[0], bits)
         last_term = jnp.dot(w[1, :, :rows], last[...], preferred_element_type=F32)
         sums = jnp.sum(shares[...], axis=2, keepdims=True)
@@ -356,9 +379,10 @@
             copies.append(pltpu.make_async_copy(held.at[slot], out.at[pl.ds(block * rows, rows), at], sem))
             copies[-1].start()
 
+        cubic_at = [cubic_own, cubic.at[0], cubic_other, cubic.at[1]]
         for slot in (3, 0, 1, 2):
             at = columns_of(place.quarter_of(slot), width)
-            before = ((cubic[slot - 1] if slot else cubic_own[...]) * scale_0).astype(BF16)
+            before = (cubic_at[slot][...] * scale_0).astype(BF16)
             write(before, s_held, slot, sigma, 0, at)
             g = last_term if slot == 3 else terms[slot - 1] if slot else term_own[...]
             g += jnp.dot(w[1, :, rows:], before, preferred_element_type=F32)
@@ -370,7 +394,7 @@
     return call(
         kernel,
         "finish_second",
-        in_specs=[SCALAR] + [WHOLE] * 8 + [HBM],
+        in_specs=[SCALAR] + [WHOLE] * 9 + [HBM],
         out_specs=[HBM, HBM],
         out_shape=[jax.ShapeDtypeStruct((2 * rows, columns), BF16)] * 2,
         scratch_shapes=[
@@ -378,8 +402,8 @@
             pltpu.VMEM((8, rows, width), BF16),
             pltpu.SemaphoreType.DMA((12,)),
         ],
-        input_output_aliases={9: 0},
-    )(me, last, term_own, terms, volterra, cubic_own, cubic, shares, coupling, g_first)
+        input_output_aliases={10: 0},
+    )(me, last, term_own, terms, volterra, cubic_own, cubic_other, cubic, shares, coupling, g_first)
 
 
 def per_device(past, second, g_hist, sigma_hist, volterra, sigma_edge, coupling):
@@ -425,20 +449,21 @@
         me, mine, theirs, volterra, sigma_edge, coupling, bits, after=mine_1
     )
     own_1, share, term_own = own_second(me, mine_1, theirs_1, volterra, response, squares, coupling, bits)
+    g_other, cubic_other = finish_other(me, swap(own_0, 0), volterra, sigma_edge, coupling, bits)
 
     rounds = log2(second)
-    share = jnp.concatenate([share, widened(share, rounds - 1)])
-    partner = ordered(swap(own_0, 1), share)
-    pieces = [partner, swap(own_0, 0), swap(partner, 0)]
-    g_first, cubic = finish_first(me, pieces, g_own, volterra, sigma_edge, coupling, bits)
-    for level in reversed(range(rounds - 1)):
+    share = jnp.concatenate([share, widened(share, 0)])
+    partner = ordered(swap(own_0, 1), share, cubic_other)
+    pieces = [partner, swap(partner, 0)]
+    g_first, cubic = finish_first(me, pieces, g_own, g_other, volterra, sigma_edge, coupling, bits)
+    for level in range(1, rounds):
         share = jnp.concatenate([share, widened(share, level)])
     partner = ordered(swap(own_1, 1), share)
     terms = memory_terms([partner, swap(own_1, 0)], volterra)
     last = swap(partner, 0)
     shares = joined([share, swap(share, 0), swap(share, 1), from_far(share)], [cubic, terms])
     results = finish_second(
-        me, last, term_own, terms, volterra, cubic_own, cubic, shares, coupling, g_first, bits
+        me, last, term_own, terms, volterra, cubic_own, cubic_other, cubic, shares, coupling, g_first, bits
     )
     return tuple(results)
 

time: 43.4 us -> 42.1 us (0.970)
  waiting for transfers between devices: 10.7 us -> 8.6 us
  starting transfers between devices: 17.6 us -> 18.3 us
    ppermute x2, waiting for transfers between devices: 3.21 us -> 2.15 us  [widened(): lax.ppermute(share, 'second', [(z, z ^ 1 << level) for z in range(second)])]
    ppermute x14, waiting for transfers between devices: 7.49 us -> 6.45 us  [swap(): return lax.ppermute(x, 'past', pairs)]
    ppermute x2, starting transfers between devices: 3.32 us -> 3.78 us  [widened(): lax.ppermute(share, 'second', [(z, z ^ 1 << level) for z in range(second)])]
    pallas_call x3 -> x4, Pallas kernels: 2.61 us -> 3.06 us  [the longest x1 2.56 us: finish_second(): call(kernel, 'finish_second', in_specs=[SCALAR] + [WHOLE] * 9 + [HBM], ou...]
  transfers between devices with their start and end apart: 17 -> 17, of which waited for: 9 -> 8; matrix products, arithmetic and copies ran while one was open for 0% -> 0% of each run, Pallas kernels for 16% -> 17%
where the time goes in v14:
time: 42.1 us; the launch traced here: 42 us
  starting transfers between devices  18.3 us (43%)
  Pallas kernels  14 us (33%)
  waiting for transfers between devices  8.6 us (20%)
  between operations  0.82 us (2%)
    ppermute x14, starting transfers between devices, swap(): return lax.ppermute(x, 'past', pairs)  13.4 us
    ppermute x14, waiting for transfers between devices, swap(): return lax.ppermute(x, 'past', pairs)  6.45 us
    pallas_call x1, Pallas kernels, first_products(): call(kernel, 'first_products', in_specs=[SCALAR, HBM, HBM], out_specs=[WH...  4.5 us
    ppermute x2, starting transfers between devices, widened(): lax.ppermute(share, 'second', [(z, z ^ 1 << level) for z in range(second)])  3.78 us
    pallas_call x2, Pallas kernels, product(): call(kernel, 'memory_product', in_specs=[SCALAR, WHOLE, WHOLE] + [FAR] *...  2.56 us
    pallas_call x1, Pallas kernels, finish_second(): call(kernel, 'finish_second', in_specs=[SCALAR] + [WHOLE] * 9 + [HBM], ou...  2.56 us
    ppermute x2, waiting for transfers between devices, widened(): lax.ppermute(share, 'second', [(z, z ^ 1 << level) for z in range(second)])  2.15 us
    pallas_call x1, Pallas kernels, finish_first(): call(kernel, 'finish_first', in_specs=[SCALAR] + [WHOLE] * 7, out_specs=[...  1.6 us
  transfers between devices with their start and end apart: 17, of which 8 were waited for; matrix products, arithmetic and copies ran while one was open for 0% of the time, Pallas kernels for 17%

profile of v14, /device:TPU:0, one launch (start us, length us, event | category | flops | bytes accessed | tf_op | source)
XLA Modules:
  0.0 42.0 jit_solution(3044876098646942883)
XLA Ops:
  0.6 4.5 %first_products.1 = (bf16[2,512,256]{2,1,0:T(8,128)(2,1)S(1)}, f32[2,512,256]{2,1,0:T(8,128)S(1)}, bf16[512,2048]{1,0:T(8,128)(2,1)S(1)}, bf16[2048,1024]{1,0:T(8,128)(2,1)S(1)}) custom-call(s32[1]{0:T(128)} %bitcast.me_ref, bf16[1024,2048]{1,0:T(8,128)(2,1)} %sigma_ref.1, bf16[2048,1024]{1,0:T(8,128)(2,1)} %g_ref.1), custom_call_target="tpu_custom_call" | custom-call | flops 1024 | bytes 1024 | tf_op jit(solution)/shard_map/first_products/pallas_call | solution.py:113
  5.1 0.6 %collective-permute-start.3 = (bf16[2,512,256]{2,1,0:T(8,128)(2,1)S(1)}, bf16[2,512,256]{2,1,0:T(8,128)(2,1)S(1)}, u32[]{:S(2)}, u32[]{:S(2)}) collective-permute-start(bf16[2,512,256]{2,1,0:T(8,128)(2,1)S(1)} %get-tuple-element.21), channel_id=1, source_target_pairs={{0,4},{4,0},{8,12},{12,8},{16,20},{20,16},{24,28},{28,24},{1,5},{5... | collective-permute-start | bytes 1572872 | tf_op jit(solution)/shard_map/ppermute | solution.py:419
  5.7 1.3 %memory_product.2 = bf16[2,512,256]{2,1,0:T(8,128)(2,1)S(1)} custom-call(s32[1]{0:T(128)} %bitcast.me_ref, bf16[512,2048]{1,0:T(8,128)(2,1)S(1)} %get-tuple-element.18.sigma, bf16[2048,1024]{1,0:T(8,128)(2,1)S(1)} %get-tuple-element.19.g), custom_call_target="tpu_custom_call" | custom-call | flops 1024 | bytes 1024 | tf_op jit(solution)/shard_map/memory_product/pallas_call | solution.py:146
  7.0 0.1 collective-permute-start
  7.1 0.2 collective-permute-done.3.arrived
  7.3 2.8 %collective-permute-start.4 = (bf16[512,256]{1,0:T(8,128)(2,1)S(1)}, bf16[512,256]{1,0:T(8,128)(2,1)S(1)}, u32[]{:S(2)}, u32[]{:S(2)}) collective-permute-start(bf16[512,256]{1,0:T(8,128)(2,1)S(1)} %fusion.4), channel_id=1, source_target_pairs={{0,8},{4,20},{8,0},{12,28},{16,24},{20,4},{24,16},{28,12},{1,9},{5... | collective-permute-start | bytes 786440 | tf_op jit(solution)/shard_map/ppermute | solution.py:419
  10.2 1.3 %memory_product.3 = f32[2,512,256]{2,1,0:T(8,128)S(1)} custom-call(s32[1]{0:T(128)} %bitcast.me_ref, bf16[512,2048]{1,0:T(8,128)(2,1)S(1)} %get-tuple-element.18.sigma, bf16[2048,1024]{1,0:T(8,128)(2,1)S(1)} %get-tuple-element.19.g, bf16[2,512,256]{2,1,0:T(8,128)(2,1)S(1)} %collective-permute-done.refs_0_), custom_call_target="tpu_custom_call" | custom-call | flops 1024 | bytes 1024 | tf_op jit(solution)/shard_map/memory_product/pallas_call | solution.py:146
  11.6 1.4 %collective-permute-start.1 = (bf16[512,256]{1,0:T(8,128)(2,1)S(1)}, bf16[512,256]{1,0:T(8,128)(2,1)S(1)}, u32[]{:S(2)}, u32[]{:S(2)}) collective-permute-start(bf16[512,256]{1,0:T(8,128)(2,1)S(1)} %fusion.5._), channel_id=1, source_target_pairs={{0,8},{4,20},{8,0},{12,28},{16,24},{20,4},{24,16},{28,12},{1,9},{5... | collective-permute-start | bytes 786440 | tf_op jit(solution)/shard_map/ppermute | solution.py:419
  13.0 1.5 %collective-permute-done.4.more = bf16[512,256]{1,0:T(8,128)(2,1)S(1)} collective-permute-done((bf16[512,256]{1,0:T(8,128)(2,1)S(1)}, bf16[512,256]{1,0:T(8,128)(2,1)S(1)}, u32[]{:S(2)}, u32[]{:S(2)}) %collective-permute-start.4) | collective-permute-done | bytes 262176 | tf_op jit(solution)/shard_map/ppermute | solution.py:419
  14.5 0.1 combined.1.mine
  14.6 2.1 %collective-permute-start.5 = (bf16[512,256]{1,0:T(8,128)(2,1)S(1)}, bf16[512,256]{1,0:T(8,128)(2,1)S(1)}, u32[]{:S(2)}, u32[]{:S(2)}) collective-permute-start(bf16[512,256]{1,0:T(8,128)(2,1)S(1)} %combined.1.mine), channel_id=1, source_target_pairs={{0,16},{4,12},{8,24},{12,4},{16,0},{20,28},{24,8},{28,20},{1,17},{... | collective-permute-start | bytes 786440 | tf_op jit(solution)/shard_map/ppermute | solution.py:419
  16.7 2.3 %collective-permute-done.1 = bf16[512,256]{1,0:T(8,128)(2,1)S(1)} collective-permute-done((bf16[512,256]{1,0:T(8,128)(2,1)S(1)}, bf16[512,256]{1,0:T(8,128)(2,1)S(1)}, u32[]{:S(2)}, u32[]{:S(2)}) %collective-permute-start.1) | collective-permute-done | bytes 262176 | tf_op jit(solution)/shard_map/ppermute | solution.py:419
  19.1 0.1 fusion.3._.mine
  19.2 1.4 %collective-permute-start.2 = (bf16[512,256]{1,0:T(8,128)(2,1)S(1)}, bf16[512,256]{1,0:T(8,128)(2,1)S(1)}, u32[]{:S(2)}, u32[]{:S(2)}) collective-permute-start(bf16[512,256]{1,0:T(8,128)(2,1)S(1)} %fusion.3._.mine), channel_id=1, source_target_pairs={{0,16},{4,12},{8,24},{12,4},{16,0},{20,28},{24,8},{28,20},{1,17},{... | collective-permute-start | bytes 786440 | tf_op jit(solution)/shard_map/ppermute | solution.py:419
  20.5 0.6 %collective-permute-done.5.theirs = bf16[512,256]{1,0:T(8,128)(2,1)S(1)} collective-permute-done((bf16[512,256]{1,0:T(8,128)(2,1)S(1)}, bf16[512,256]{1,0:T(8,128)(2,1)S(1)}, u32[]{:S(2)}, u32[]{:S(2)}) %collective-permute-start.5) | collective-permute-done | bytes 262176 | tf_op jit(solution)/shard_map/ppermute | solution.py:419
  21.1 1.2 %own_first.1 = (bf16[512,256]{1,0:T(8,128)(2,1)S(1)}, f32[512,256]{1,0:T(8,128)S(1)}, f32[1,128]{1,0:T(1,128)S(1)}, bf16[512,256]{1,0:T(8,128)(2,1)S(1)}, f32[512,256]{1,0:T(8,128)S(1)}) custom-call(s32[1]{0:T(128)} %bitcast.me_ref, bf16[512,256]{1,0:T(8,128)(2,1)S(1)} %combined.1.mine, bf16[512,256]{1,0:T(8,128)(2,1)S(1)} %collective-permute-done.5.theirs, ...), custom_call_target="tpu_custom_call" | custom-call | flops 1024 | bytes 1024 | tf_op jit(solution)/shard_map/own_first/pallas_call | solution.py:208
  22.3 2.1 %collective-permute-start.12 = (bf16[512,256]{1,0:T(8,128)(2,1)S(1)}, bf16[512,256]{1,0:T(8,128)(2,1)S(1)}, u32[]{:S(2)}, u32[]{:S(2)}) collective-permute-start(bf16[512,256]{1,0:T(8,128)(2,1)S(1)} %get-tuple-element.28), channel_id=1, source_target_pairs={{0,8},{4,20},{8,0},{12,28},{16,24},{20,4},{24,16},{28,12},{1,9},{5... | collective-permute-start | bytes 786440 | tf_op jit(solution)/shard_map/ppermute | solution.py:419
  24.4 1.2 %collective-permute-done.2.theirs = bf16[512,256]{1,0:T(8,128)(2,1)S(1)} collective-permute-done((bf16[512,256]{1,0:T(8,128)(2,1)S(1)}, bf16[512,256]{1,0:T(8,128)(2,1)S(1)}, u32[]{:S(2)}, u32[]{:S(2)}) %collective-permute-start.2) | collective-permute-done | bytes 262176 | tf_op jit(solution)/shard_map/ppermute | solution.py:419
  25.6 0.6 %own_second.1 = (bf16[512,256]{1,0:T(8,128)(2,1)S(1)}, f32[1,8,128]{2,1,0:T(8,128)S(1)}, f32[512,256]{1,0:T(8,128)S(1)}) custom-call(s32[1]{0:T(128)} %bitcast.me_ref, bf16[512,256]{1,0:T(8,128)(2,1)S(1)} %fusion.3._.mine, bf16[512,256]{1,0:T(8,128)(2,1)S(1)} %collective-permute-done.2.theirs, bf16[2,512,1024]{2,1,0:T(8,128)(2,1)S(1)} %copy-done, ...), custom_call_target="tpu_custom_call" | custom-call | flops 1024 | bytes 1024 | tf_op jit(solution)/shard_map/own_second/pallas_call | solution.py:246
  26.2 1.4 %collective-permute-start.7 = (f32[1,8,128]{2,1,0:T(8,128)S(1)}, f32[1,8,128]{2,1,0:T(8,128)S(1)}, u32[]{:S(2)}, u32[]{:S(2)}) collective-permute-start(f32[1,8,128]{2,1,0:T(8,128)S(1)} %get-tuple-element.25), channel_id=1, source_target_pairs={{0,1},{1,0},{2,3},{3,2},{4,5},{5,4},{6,7},{7,6},{8,9},{9,8},{10,11... | collective-permute-start | bytes 12296 | tf_op jit(solution)/shard_map/ppermute | solution.py:437
  27.7 1.2 %collective-permute-start.6 = (bf16[512,256]{1,0:T(8,128)(2,1)S(1)}, bf16[512,256]{1,0:T(8,128)(2,1)S(1)}, u32[]{:S(2)}, u32[]{:S(2)}) collective-permute-start(bf16[512,256]{1,0:T(8,128)(2,1)S(1)} %get-tuple-element.24), channel_id=1, source_target_pairs={{0,8},{4,20},{8,0},{12,28},{16,24},{20,4},{24,16},{28,12},{1,9},{5... | collective-permute-start | bytes 786440 | tf_op jit(solution)/shard_map/ppermute | solution.py:419
  28.9 1.0 %collective-permute-done.7 = f32[1,8,128]{2,1,0:T(8,128)S(1)} collective-permute-done((f32[1,8,128]{2,1,0:T(8,128)S(1)}, f32[1,8,128]{2,1,0:T(8,128)S(1)}, u32[]{:S(2)}, u32[]{:S(2)}) %collective-permute-start.7) | collective-permute-done | bytes 4128 | tf_op jit(solution)/shard_map/ppermute | solution.py:437
  29.9 2.4 %collective-permute-start.8 = (f32[2,8,128]{2,1,0:T(8,128)S(1)}, f32[2,8,128]{2,1,0:T(8,128)S(1)}, u32[]{:S(2)}, u32[]{:S(2)}) collective-permute-start(f32[2,8,128]{2,1,0:T(8,128)S(1)} %get-tuple-element.34.refs_0_), channel_id=1, source_target_pairs={{0,2},{1,3},{2,0},{3,1},{4,6},{5,7},{6,4},{7,5},{8,10},{9,11},{10,... | collective-permute-start | bytes 24584 | tf_op jit(solution)/shard_map/ppermute | solution.py:437
  32.3 0.5 %finish_other.1 = (bf16[512,256]{1,0:T(8,128)(2,1)S(1)}, f32[512,256]{1,0:T(8,128)S(1)}) custom-call(s32[1]{0:T(128)} %bitcast.me_ref, bf16[512,256]{1,0:T(8,128)(2,1)S(1)} %collective-permute-done.11.piece, bf16[2,512,1024]{2,1,0:T(8,128)(2,1)S(1)} %copy-done, bf16[512,1024]{1,0:T(8,128)(2,1)S(1)} %copy-done.1, f32[32,1024]{1,0:T(8,128)S(1)} %copy-done.2), custom_call_target="tpu_custom_call" | custom-call | flops 1024 | bytes 1024 | tf_op jit(solution)/shard_map/finish_other/pallas_call | solution.py:265
  32.8 0.6 %collective-permute-start.13 = (bf16[512,256]{1,0:T(8,128)(2,1)S(1)}, bf16[512,256]{1,0:T(8,128)(2,1)S(1)}, u32[]{:S(2)}, u32[]{:S(2)}) collective-permute-start(bf16[512,256]{1,0:T(8,128)(2,1)S(1)} %ordered.3.refs_0_), channel_id=1, source_target_pairs={{0,4},{4,0},{8,12},{12,8},{16,20},{20,16},{24,28},{28,24},{1,5},{5... | collective-permute-start | bytes 786440 | tf_op jit(solution)/shard_map/ppermute | solution.py:419
  33.4 1.1 %collective-permute-done.8 = f32[2,8,128]{2,1,0:T(8,128)S(1)} collective-permute-done((f32[2,8,128]{2,1,0:T(8,128)S(1)}, f32[2,8,128]{2,1,0:T(8,128)S(1)}, u32[]{:S(2)}, u32[]{:S(2)}) %collective-permute-start.8) | collective-permute-done | bytes 8224 | tf_op jit(solution)/shard_map/ppermute | solution.py:437
  34.6 1.1 %collective-permute-start.16 = (f32[4,8,128]{2,1,0:T(8,128)S(1)}, f32[4,8,128]{2,1,0:T(8,128)S(1)}, u32[]{:S(2)}, u32[]{:S(2)}) collective-permute-start(f32[4,8,128]{2,1,0:T(8,128)S(1)} %constant_dynamic-update-slice_fusion.2.refs_0_), channel_id=1, source_target_pairs={{20,0},{8,4},{28,8},{0,12},{4,16},{24,20},{12,24},{16,28},{21,1},{... | collective-permute-start | bytes 49160 | tf_op jit(solution)/shard_map/ppermute | solution.py:434
  35.7 1.0 %collective-permute-start.15 = (f32[4,8,128]{2,1,0:T(8,128)S(1)}, f32[4,8,128]{2,1,0:T(8,128)S(1)}, u32[]{:S(2)}, u32[]{:S(2)}) collective-permute-start(f32[4,8,128]{2,1,0:T(8,128)S(1)} %constant_dynamic-update-slice_fusion.2.refs_0_), channel_id=1, source_target_pairs={{0,8},{4,20},{8,0},{12,28},{16,24},{20,4},{24,16},{28,12},{1,9},{5... | collective-permute-start | bytes 49160 | tf_op jit(solution)/shard_map/ppermute | solution.py:419
  36.7 0.4 %memory_terms.1.refs_5_.refs_2_ = f32[2,512,256]{2,1,0:T(8,128)S(1)} custom-call(bf16[512,256]{1,0:T(8,128)(2,1)S(1)} %ordered.2.refs_0_, bf16[512,256]{1,0:T(8,128)(2,1)S(1)} %collective-permute-done.10.refs_1_, bf16[2,512,1024]{2,1,0:T(8,128)(2,1)S(1)} %copy-done), custom_call_target="tpu_custom_call" | custom-call | flops 1024 | bytes 1024 | tf_op jit(solution)/shard_map/memory_terms/pallas_call | solution.py:319
  37.2 1.6 %finish_first.1 = (bf16[1024,1024]{1,0:T(8,128)(2,1)}, f32[2,512,256]{2,1,0:T(8,128)S(1)}) custom-call(s32[1]{0:T(128)} %bitcast.me_ref, bf16[512,256]{1,0:T(8,128)(2,1)S(1)} %ordered.3.refs_0_, bf16[512,256]{1,0:T(8,128)(2,1)S(1)} %collective-permute-done.13.refs_1_, bf16[512,256]{1,0:T(8,128)(2,1)S(1)} %get-tuple-element.30.refs_2_, ...), custom_call_target="tpu_custom_call" | custom-call | flops 1024 | bytes 1024 | tf_op jit(solution)/shard_map/finish_first/pallas_call | solution.py:300
  38.8 0.6 %collective-permute-done.15.refs_2_ = f32[4,8,128]{2,1,0:T(8,128)S(1)} collective-permute-done((f32[4,8,128]{2,1,0:T(8,128)S(1)}, f32[4,8,128]{2,1,0:T(8,128)S(1)}, u32[]{:S(2)}, u32[]{:S(2)}) %collective-permute-start.15) | collective-permute-done | bytes 16416 | tf_op jit(solution)/shard_map/ppermute | solution.py:419
  39.4 2.6 %finish_second.1 = (bf16[1024,1024]{1,0:T(8,128)(2,1)}, bf16[1024,1024]{1,0:T(8,128)(2,1)}) custom-call(s32[1]{0:T(128)} %bitcast.me_ref, bf16[512,256]{1,0:T(8,128)(2,1)S(1)} %collective-permute-done.9.refs_0_, f32[512,256]{1,0:T(8,128)S(1)} %get-tuple-element.26.refs_1_, ...), custom_call_target="tpu_custom_call", output_to_operand_aliasing={{0}: (10, {})} | custom-call | flops 1024 | bytes 1024 | tf_op jit(solution)/shard_map/finish_second/pallas_call | solution.py:394
  (27 shorter events, 0.4 us)
Async XLA Ops:
  5.1 2.1 %collective-permute-start.3 = (bf16[2,512,256]{2,1,0:T(8,128)(2,1)S(1)}, bf16[2,512,256]{2,1,0:T(8,128)(2,1)S(1)}, u32[]{:S(2)}, u32[]{:S(2)}) collective-permute-start(bf16[2,512,256]{2,1,0:T(8,128)(2,1)S(1)} %get-tuple-element.21), channel_id=1, source_target_pairs={{0,4},{4,0},{8,12},{12,8},{16,20},{20,16},{24,28},{28,24},{1,5},{5... | collective-permute-start | bytes 1572872 | tf_op jit(solution)/shard_map/ppermute | solution.py:419
  7.0 3.2 %collective-permute-start = (bf16[2,512,256]{2,1,0:T(8,128)(2,1)S(1)}, bf16[2,512,256]{2,1,0:T(8,128)(2,1)S(1)}, u32[]{:S(2)}, u32[]{:S(2)}) collective-permute-start(bf16[2,512,256]{2,1,0:T(8,128)(2,1)S(1)} %memory_product.2), channel_id=1, source_target_pairs={{0,4},{4,0},{8,12},{12,8},{16,20},{20,16},{24,28},{28,24},{1,5},{5... | collective-permute-start | bytes 1572872 | tf_op jit(solution)/shard_map/ppermute | solution.py:419
  7.3 7.2 %collective-permute-start.4 = (bf16[512,256]{1,0:T(8,128)(2,1)S(1)}, bf16[512,256]{1,0:T(8,128)(2,1)S(1)}, u32[]{:S(2)}, u32[]{:S(2)}) collective-permute-start(bf16[512,256]{1,0:T(8,128)(2,1)S(1)} %fusion.4), channel_id=1, source_target_pairs={{0,8},{4,20},{8,0},{12,28},{16,24},{20,4},{24,16},{28,12},{1,9},{5... | collective-permute-start | bytes 786440 | tf_op jit(solution)/shard_map/ppermute | solution.py:419
  11.5 9.6 %copy-start = (bf16[2,512,1024]{2,1,0:T(8,128)(2,1)S(1)}, bf16[2,512,1024]{2,1,0:T(8,128)(2,1)}, u32[]{:S(2)}) copy-start(bf16[2,512,1024]{2,1,0:T(8,128)(2,1)} %refs_3_.1) | copy-start | bytes 6291460
  11.5 9.6 %copy-start.1 = (bf16[512,1024]{1,0:T(8,128)(2,1)S(1)}, bf16[512,1024]{1,0:T(8,128)(2,1)}, u32[]{:S(2)}) copy-start(bf16[512,1024]{1,0:T(8,128)(2,1)} %refs_5_.1) | copy-start | bytes 3145732
  11.5 9.6 %copy-start.2 = (f32[32,1024]{1,0:T(8,128)S(1)}, f32[32,1024]{1,0:T(8,128)}, u32[]{:S(2)}) copy-start(f32[32,1024]{1,0:T(8,128)} %refs_8_.1) | copy-start | bytes 393220
  11.6 7.5 %collective-permute-start.1 = (bf16[512,256]{1,0:T(8,128)(2,1)S(1)}, bf16[512,256]{1,0:T(8,128)(2,1)S(1)}, u32[]{:S(2)}, u32[]{:S(2)}) collective-permute-start(bf16[512,256]{1,0:T(8,128)(2,1)S(1)} %fusion.5._), channel_id=1, source_target_pairs={{0,8},{4,20},{8,0},{12,28},{16,24},{20,4},{24,16},{28,12},{1,9},{5... | collective-permute-start | bytes 786440 | tf_op jit(solution)/shard_map/ppermute | solution.py:419
  14.6 6.5 %collective-permute-start.5 = (bf16[512,256]{1,0:T(8,128)(2,1)S(1)}, bf16[512,256]{1,0:T(8,128)(2,1)S(1)}, u32[]{:S(2)}, u32[]{:S(2)}) collective-permute-start(bf16[512,256]{1,0:T(8,128)(2,1)S(1)} %combined.1.mine), channel_id=1, source_target_pairs={{0,16},{4,12},{8,24},{12,4},{16,0},{20,28},{24,8},{28,20},{1,17},{... | collective-permute-start | bytes 786440 | tf_op jit(solution)/shard_map/ppermute | solution.py:419
  19.2 6.4 %collective-permute-start.2 = (bf16[512,256]{1,0:T(8,128)(2,1)S(1)}, bf16[512,256]{1,0:T(8,128)(2,1)S(1)}, u32[]{:S(2)}, u32[]{:S(2)}) collective-permute-start(bf16[512,256]{1,0:T(8,128)(2,1)S(1)} %fusion.3._.mine), channel_id=1, source_target_pairs={{0,16},{4,12},{8,24},{12,4},{16,0},{20,28},{24,8},{28,20},{1,17},{... | collective-permute-start | bytes 786440 | tf_op jit(solution)/shard_map/ppermute | solution.py:419
  22.3 10.0 %collective-permute-start.11 = (bf16[512,256]{1,0:T(8,128)(2,1)S(1)}, bf16[512,256]{1,0:T(8,128)(2,1)S(1)}, u32[]{:S(2)}, u32[]{:S(2)}) collective-permute-start(bf16[512,256]{1,0:T(8,128)(2,1)S(1)} %get-tuple-element.28), channel_id=1, source_target_pairs={{0,4},{4,0},{8,12},{12,8},{16,20},{20,16},{24,28},{28,24},{1,5},{5... | collective-permute-start | bytes 786440 | tf_op jit(solution)/shard_map/ppermute | solution.py:419
  22.3 10.4 %collective-permute-start.12 = (bf16[512,256]{1,0:T(8,128)(2,1)S(1)}, bf16[512,256]{1,0:T(8,128)(2,1)S(1)}, u32[]{:S(2)}, u32[]{:S(2)}) collective-permute-start(bf16[512,256]{1,0:T(8,128)(2,1)S(1)} %get-tuple-element.28), channel_id=1, source_target_pairs={{0,8},{4,20},{8,0},{12,28},{16,24},{20,4},{24,16},{28,12},{1,9},{5... | collective-permute-start | bytes 786440 | tf_op jit(solution)/shard_map/ppermute | solution.py:419
  26.2 3.7 %collective-permute-start.7 = (f32[1,8,128]{2,1,0:T(8,128)S(1)}, f32[1,8,128]{2,1,0:T(8,128)S(1)}, u32[]{:S(2)}, u32[]{:S(2)}) collective-permute-start(f32[1,8,128]{2,1,0:T(8,128)S(1)} %get-tuple-element.25), channel_id=1, source_target_pairs={{0,1},{1,0},{2,3},{3,2},{4,5},{5,4},{6,7},{7,6},{8,9},{9,8},{10,11... | collective-permute-start | bytes 12296 | tf_op jit(solution)/shard_map/ppermute | solution.py:437
  27.7 6.8 %collective-permute-start.6 = (bf16[512,256]{1,0:T(8,128)(2,1)S(1)}, bf16[512,256]{1,0:T(8,128)(2,1)S(1)}, u32[]{:S(2)}, u32[]{:S(2)}) collective-permute-start(bf16[512,256]{1,0:T(8,128)(2,1)S(1)} %get-tuple-element.24), channel_id=1, source_target_pairs={{0,8},{4,20},{8,0},{12,28},{16,24},{20,4},{24,16},{28,12},{1,9},{5... | collective-permute-start | bytes 786440 | tf_op jit(solution)/shard_map/ppermute | solution.py:419
  29.9 4.5 %collective-permute-start.8 = (f32[2,8,128]{2,1,0:T(8,128)S(1)}, f32[2,8,128]{2,1,0:T(8,128)S(1)}, u32[]{:S(2)}, u32[]{:S(2)}) collective-permute-start(f32[2,8,128]{2,1,0:T(8,128)S(1)} %get-tuple-element.34.refs_0_), channel_id=1, source_target_pairs={{0,2},{1,3},{2,0},{3,1},{4,6},{5,7},{6,4},{7,5},{8,10},{9,11},{10,... | collective-permute-start | bytes 24584 | tf_op jit(solution)/shard_map/ppermute | solution.py:437
  32.3 4.4 %collective-permute-start.10 = (bf16[512,256]{1,0:T(8,128)(2,1)S(1)}, bf16[512,256]{1,0:T(8,128)(2,1)S(1)}, u32[]{:S(2)}, u32[]{:S(2)}) collective-permute-start(bf16[512,256]{1,0:T(8,128)(2,1)S(1)} %get-tuple-element.24), channel_id=1, source_target_pairs={{0,4},{4,0},{8,12},{12,8},{16,20},{20,16},{24,28},{28,24},{1,5},{5... | collective-permute-start | bytes 786440 | tf_op jit(solution)/shard_map/ppermute | solution.py:419
  32.8 4.4 %collective-permute-start.13 = (bf16[512,256]{1,0:T(8,128)(2,1)S(1)}, bf16[512,256]{1,0:T(8,128)(2,1)S(1)}, u32[]{:S(2)}, u32[]{:S(2)}) collective-permute-start(bf16[512,256]{1,0:T(8,128)(2,1)S(1)} %ordered.3.refs_0_), channel_id=1, source_target_pairs={{0,4},{4,0},{8,12},{12,8},{16,20},{20,16},{24,28},{28,24},{1,5},{5... | collective-permute-start | bytes 786440 | tf_op jit(solution)/shard_map/ppermute | solution.py:419
  34.5 4.9 %collective-permute-start.9 = (bf16[512,256]{1,0:T(8,128)(2,1)S(1)}, bf16[512,256]{1,0:T(8,128)(2,1)S(1)}, u32[]{:S(2)}, u32[]{:S(2)}) collective-permute-start(bf16[512,256]{1,0:T(8,128)(2,1)S(1)} %ordered.2.refs_0_), channel_id=1, source_target_pairs={{0,4},{4,0},{8,12},{12,8},{16,20},{20,16},{24,28},{28,24},{1,5},{5... | collective-permute-start | bytes 786440 | tf_op jit(solution)/shard_map/ppermute | solution.py:419
  34.6 4.2 %collective-permute-start.16 = (f32[4,8,128]{2,1,0:T(8,128)S(1)}, f32[4,8,128]{2,1,0:T(8,128)S(1)}, u32[]{:S(2)}, u32[]{:S(2)}) collective-permute-start(f32[4,8,128]{2,1,0:T(8,128)S(1)} %constant_dynamic-update-slice_fusion.2.refs_0_), channel_id=1, source_target_pairs={{20,0},{8,4},{28,8},{0,12},{4,16},{24,20},{12,24},{16,28},{21,1},{... | collective-permute-start | bytes 49160 | tf_op jit(solution)/shard_map/ppermute | solution.py:434
  35.7 3.7 %collective-permute-start.15 = (f32[4,8,128]{2,1,0:T(8,128)S(1)}, f32[4,8,128]{2,1,0:T(8,128)S(1)}, u32[]{:S(2)}, u32[]{:S(2)}) collective-permute-start(f32[4,8,128]{2,1,0:T(8,128)S(1)} %constant_dynamic-update-slice_fusion.2.refs_0_), channel_id=1, source_target_pairs={{0,8},{4,20},{8,0},{12,28},{16,24},{20,4},{24,16},{28,12},{1,9},{5... | collective-permute-start | bytes 49160 | tf_op jit(solution)/shard_map/ppermute | solution.py:419
  36.7 2.7 %collective-permute-start.14 = (f32[4,8,128]{2,1,0:T(8,128)S(1)}, f32[4,8,128]{2,1,0:T(8,128)S(1)}, u32[]{:S(2)}, u32[]{:S(2)}) collective-permute-start(f32[4,8,128]{2,1,0:T(8,128)S(1)} %constant_dynamic-update-slice_fusion.2.refs_0_), channel_id=1, source_target_pairs={{0,4},{4,0},{8,12},{12,8},{16,20},{20,16},{24,28},{28,24},{1,5},{5... | collective-permute-start | bytes 49160 | tf_op jit(solution)/shard_map/ppermute | solution.py:419

commit v15 on v14

--- a/solution.py
+++ b/solution.py
@@ -69,8 +69,11 @@
     depth, columns = g_hist.shape
     half = columns // 2
     parts = 4
-    eighth = depth // 8
-    chunks = [(0, 2 * eighth), (2 * eighth, 3 * eighth), (5 * eighth, 3 * eighth)]
+    unit = depth // 16
+    chunks, start = [], 0
+    for units in (2, 3, 4, 4, 3):
+        chunks.append((start * unit, units * unit))
+        start += units
 
     def kernel(me_ref, sigma_ref, g_ref, sent, kept, sigma_next, g, sigma, total, sems):
         started = []
@@ -380,14 +383,20 @@
             copies[-1].start()
 
         cubic_at = [cubic_own, cubic.at[0], cubic_other, cubic.at[1]]
-        for slot in (3, 0, 1, 2):
+        def response(slot):
+            before = (cubic_at[slot][...] * scale_0).astype(BF16)
+            write(before, s_held, slot, sigma, 0, columns_of(place.quarter_of(slot), width))
+            g = last_term if slot == 3 else terms[slot - 1] if slot else term_own[...]
+            return g + jnp.dot(w[1, :, rows:], before, preferred_element_type=F32)
+
+        slots = (3, 0, 1, 2)
+        g = response(slots[0])
+        for i, slot in enumerate(slots):
+            following = response(slots[i + 1]) if i + 1 < len(slots) else None
             at = columns_of(place.quarter_of(slot), width)
-            before = (cubic_at[slot][...] * scale_0).astype(BF16)
-            write(before, s_held, slot, sigma, 0, at)
-            g = last_term if slot == 3 else terms[slot - 1] if slot else term_own[...]
-            g += jnp.dot(w[1, :, rows:], before, preferred_element_type=F32)
             write(g.astype(BF16), g_held, slot, g_out, 1, at)
             write(cubed(g, coupling[:, at] * scale_1).astype(BF16), s_held, 4 + slot, sigma, 1, at)
+            g = following
         for copy in copies:
             copy.wait()
 

time: 42.1 us -> 42.3 us (level)
  no operation moved by 1% of the time
where the time goes in v15:
time: 42.3 us; the launch traced here: 42.2 us
  starting transfers between devices  18.3 us (43%)
  Pallas kernels  14.3 us (34%)
  waiting for transfers between devices  8.59 us (20%)
  between operations  0.82 us (2%)
    ppermute x14, starting transfers between devices, swap(): return lax.ppermute(x, 'past', pairs)  13.4 us
    ppermute x14, waiting for transfers between devices, swap(): return lax.ppermute(x, 'past', pairs)  6.44 us
    pallas_call x1, Pallas kernels, first_products(): call(kernel, 'first_products', in_specs=[SCALAR, HBM, HBM], out_specs=[WH...  4.76 us
    ppermute x2, starting transfers between devices, widened(): lax.ppermute(share, 'second', [(z, z ^ 1 << level) for z in range(second)])  3.78 us
    pallas_call x2, Pallas kernels, product(): call(kernel, 'memory_product', in_specs=[SCALAR, WHOLE, WHOLE] + [FAR] *...  2.56 us
    pallas_call x1, Pallas kernels, finish_second(): call(kernel, 'finish_second', in_specs=[SCALAR] + [WHOLE] * 9 + [HBM], ou...  2.51 us
    ppermute x2, waiting for transfers between devices, widened(): lax.ppermute(share, 'second', [(z, z ^ 1 << level) for z in range(second)])  2.15 us
    pallas_call x1, Pallas kernels, finish_first(): call(kernel, 'finish_first', in_specs=[SCALAR] + [WHOLE] * 7, out_specs=[...  1.6 us
  transfers between devices with their start and end apart: 17, of which 8 were waited for; matrix products, arithmetic and copies ran while one was open for 0% of the time, Pallas kernels for 17%

profile of v15, /device:TPU:0, one launch (start us, length us, event | category | flops | bytes accessed | tf_op | source)
XLA Modules:
  0.0 42.2 jit_solution(10725476007289162267)
XLA Ops:
  0.6 4.8 %first_products.1 = (bf16[2,512,256]{2,1,0:T(8,128)(2,1)S(1)}, f32[2,512,256]{2,1,0:T(8,128)S(1)}, bf16[512,2048]{1,0:T(8,128)(2,1)S(1)}, bf16[2048,1024]{1,0:T(8,128)(2,1)S(1)}) custom-call(s32[1]{0:T(128)} %bitcast.me_ref, bf16[1024,2048]{1,0:T(8,128)(2,1)} %sigma_ref.1, bf16[2048,1024]{1,0:T(8,128)(2,1)} %g_ref.1), custom_call_target="tpu_custom_call" | custom-call | flops 1024 | bytes 1024 | tf_op jit(solution)/shard_map/first_products/pallas_call | solution.py:116
  5.4 0.6 %collective-permute-start.3 = (bf16[2,512,256]{2,1,0:T(8,128)(2,1)S(1)}, bf16[2,512,256]{2,1,0:T(8,128)(2,1)S(1)}, u32[]{:S(2)}, u32[]{:S(2)}) collective-permute-start(bf16[2,512,256]{2,1,0:T(8,128)(2,1)S(1)} %get-tuple-element.21), channel_id=1, source_target_pairs={{0,4},{4,0},{8,12},{12,8},{16,20},{20,16},{24,28},{28,24},{1,5},{5... | collective-permute-start | bytes 1572872 | tf_op jit(solution)/shard_map/ppermute | solution.py:428
  6.0 1.3 %memory_product.2 = bf16[2,512,256]{2,1,0:T(8,128)(2,1)S(1)} custom-call(s32[1]{0:T(128)} %bitcast.me_ref, bf16[512,2048]{1,0:T(8,128)(2,1)S(1)} %get-tuple-element.18.sigma, bf16[2048,1024]{1,0:T(8,128)(2,1)S(1)} %get-tuple-element.19.g), custom_call_target="tpu_custom_call" | custom-call | flops 1024 | bytes 1024 | tf_op jit(solution)/shard_map/memory_product/pallas_call | solution.py:149
  7.3 0.1 collective-permute-start
  7.4 0.2 collective-permute-done.3.arrived
  7.6 2.8 %collective-permute-start.4 = (bf16[512,256]{1,0:T(8,128)(2,1)S(1)}, bf16[512,256]{1,0:T(8,128)(2,1)S(1)}, u32[]{:S(2)}, u32[]{:S(2)}) collective-permute-start(bf16[512,256]{1,0:T(8,128)(2,1)S(1)} %fusion.4), channel_id=1, source_target_pairs={{0,8},{4,20},{8,0},{12,28},{16,24},{20,4},{24,16},{28,12},{1,9},{5... | collective-permute-start | bytes 786440 | tf_op jit(solution)/shard_map/ppermute | solution.py:428
  10.4 1.3 %memory_product.3 = f32[2,512,256]{2,1,0:T(8,128)S(1)} custom-call(s32[1]{0:T(128)} %bitcast.me_ref, bf16[512,2048]{1,0:T(8,128)(2,1)S(1)} %get-tuple-element.18.sigma, bf16[2048,1024]{1,0:T(8,128)(2,1)S(1)} %get-tuple-element.19.g, bf16[2,512,256]{2,1,0:T(8,128)(2,1)S(1)} %collective-permute-done.refs_0_), custom_call_target="tpu_custom_call" | custom-call | flops 1024 | bytes 1024 | tf_op jit(solution)/shard_map/memory_product/pallas_call | solution.py:149
  11.8 1.4 %collective-permute-start.1 = (bf16[512,256]{1,0:T(8,128)(2,1)S(1)}, bf16[512,256]{1,0:T(8,128)(2,1)S(1)}, u32[]{:S(2)}, u32[]{:S(2)}) collective-permute-start(bf16[512,256]{1,0:T(8,128)(2,1)S(1)} %fusion.5._), channel_id=1, source_target_pairs={{0,8},{4,20},{8,0},{12,28},{16,24},{20,4},{24,16},{28,12},{1,9},{5... | collective-permute-start | bytes 786440 | tf_op jit(solution)/shard_map/ppermute | solution.py:428
  13.2 1.5 %collective-permute-done.4.more = bf16[512,256]{1,0:T(8,128)(2,1)S(1)} collective-permute-done((bf16[512,256]{1,0:T(8,128)(2,1)S(1)}, bf16[512,256]{1,0:T(8,128)(2,1)S(1)}, u32[]{:S(2)}, u32[]{:S(2)}) %collective-permute-start.4) | collective-permute-done | bytes 262176 | tf_op jit(solution)/shard_map/ppermute | solution.py:428
  14.8 0.1 combined.1.mine
  14.9 2.1 %collective-permute-start.5 = (bf16[512,256]{1,0:T(8,128)(2,1)S(1)}, bf16[512,256]{1,0:T(8,128)(2,1)S(1)}, u32[]{:S(2)}, u32[]{:S(2)}) collective-permute-start(bf16[512,256]{1,0:T(8,128)(2,1)S(1)} %combined.1.mine), channel_id=1, source_target_pairs={{0,16},{4,12},{8,24},{12,4},{16,0},{20,28},{24,8},{28,20},{1,17},{... | collective-permute-start | bytes 786440 | tf_op jit(solution)/shard_map/ppermute | solution.py:428
  17.0 2.3 %collective-permute-done.1 = bf16[512,256]{1,0:T(8,128)(2,1)S(1)} collective-permute-done((bf16[512,256]{1,0:T(8,128)(2,1)S(1)}, bf16[512,256]{1,0:T(8,128)(2,1)S(1)}, u32[]{:S(2)}, u32[]{:S(2)}) %collective-permute-start.1) | collective-permute-done | bytes 262176 | tf_op jit(solution)/shard_map/ppermute | solution.py:428
  19.3 0.1 fusion.3._.mine
  19.4 1.4 %collective-permute-start.2 = (bf16[512,256]{1,0:T(8,128)(2,1)S(1)}, bf16[512,256]{1,0:T(8,128)(2,1)S(1)}, u32[]{:S(2)}, u32[]{:S(2)}) collective-permute-start(bf16[512,256]{1,0:T(8,128)(2,1)S(1)} %fusion.3._.mine), channel_id=1, source_target_pairs={{0,16},{4,12},{8,24},{12,4},{16,0},{20,28},{24,8},{28,20},{1,17},{... | collective-permute-start | bytes 786440 | tf_op jit(solution)/shard_map/ppermute | solution.py:428
  20.8 0.5 %collective-permute-done.5.theirs = bf16[512,256]{1,0:T(8,128)(2,1)S(1)} collective-permute-done((bf16[512,256]{1,0:T(8,128)(2,1)S(1)}, bf16[512,256]{1,0:T(8,128)(2,1)S(1)}, u32[]{:S(2)}, u32[]{:S(2)}) %collective-permute-start.5) | collective-permute-done | bytes 262176 | tf_op jit(solution)/shard_map/ppermute | solution.py:428
  21.4 1.2 %own_first.1 = (bf16[512,256]{1,0:T(8,128)(2,1)S(1)}, f32[512,256]{1,0:T(8,128)S(1)}, f32[1,128]{1,0:T(1,128)S(1)}, bf16[512,256]{1,0:T(8,128)(2,1)S(1)}, f32[512,256]{1,0:T(8,128)S(1)}) custom-call(s32[1]{0:T(128)} %bitcast.me_ref, bf16[512,256]{1,0:T(8,128)(2,1)S(1)} %combined.1.mine, bf16[512,256]{1,0:T(8,128)(2,1)S(1)} %collective-permute-done.5.theirs, ...), custom_call_target="tpu_custom_call" | custom-call | flops 1024 | bytes 1024 | tf_op jit(solution)/shard_map/own_first/pallas_call | solution.py:211
  22.6 2.1 %collective-permute-start.12 = (bf16[512,256]{1,0:T(8,128)(2,1)S(1)}, bf16[512,256]{1,0:T(8,128)(2,1)S(1)}, u32[]{:S(2)}, u32[]{:S(2)}) collective-permute-start(bf16[512,256]{1,0:T(8,128)(2,1)S(1)} %get-tuple-element.28), channel_id=1, source_target_pairs={{0,8},{4,20},{8,0},{12,28},{16,24},{20,4},{24,16},{28,12},{1,9},{5... | collective-permute-start | bytes 786440 | tf_op jit(solution)/shard_map/ppermute | solution.py:428
  24.7 1.2 %collective-permute-done.2.theirs = bf16[512,256]{1,0:T(8,128)(2,1)S(1)} collective-permute-done((bf16[512,256]{1,0:T(8,128)(2,1)S(1)}, bf16[512,256]{1,0:T(8,128)(2,1)S(1)}, u32[]{:S(2)}, u32[]{:S(2)}) %collective-permute-start.2) | collective-permute-done | bytes 262176 | tf_op jit(solution)/shard_map/ppermute | solution.py:428
  25.9 0.6 %own_second.1 = (bf16[512,256]{1,0:T(8,128)(2,1)S(1)}, f32[1,8,128]{2,1,0:T(8,128)S(1)}, f32[512,256]{1,0:T(8,128)S(1)}) custom-call(s32[1]{0:T(128)} %bitcast.me_ref, bf16[512,256]{1,0:T(8,128)(2,1)S(1)} %fusion.3._.mine, bf16[512,256]{1,0:T(8,128)(2,1)S(1)} %collective-permute-done.2.theirs, bf16[2,512,1024]{2,1,0:T(8,128)(2,1)S(1)} %copy-done, ...), custom_call_target="tpu_custom_call" | custom-call | flops 1024 | bytes 1024 | tf_op jit(solution)/shard_map/own_second/pallas_call | solution.py:249
  26.5 1.4 %collective-permute-start.7 = (f32[1,8,128]{2,1,0:T(8,128)S(1)}, f32[1,8,128]{2,1,0:T(8,128)S(1)}, u32[]{:S(2)}, u32[]{:S(2)}) collective-permute-start(f32[1,8,128]{2,1,0:T(8,128)S(1)} %get-tuple-element.25), channel_id=1, source_target_pairs={{0,1},{1,0},{2,3},{3,2},{4,5},{5,4},{6,7},{7,6},{8,9},{9,8},{10,11... | collective-permute-start | bytes 12296 | tf_op jit(solution)/shard_map/ppermute | solution.py:446
  27.9 1.2 %collective-permute-start.6 = (bf16[512,256]{1,0:T(8,128)(2,1)S(1)}, bf16[512,256]{1,0:T(8,128)(2,1)S(1)}, u32[]{:S(2)}, u32[]{:S(2)}) collective-permute-start(bf16[512,256]{1,0:T(8,128)(2,1)S(1)} %get-tuple-element.24), channel_id=1, source_target_pairs={{0,8},{4,20},{8,0},{12,28},{16,24},{20,4},{24,16},{28,12},{1,9},{5... | collective-permute-start | bytes 786440 | tf_op jit(solution)/shard_map/ppermute | solution.py:428
  29.1 1.0 %collective-permute-done.7 = f32[1,8,128]{2,1,0:T(8,128)S(1)} collective-permute-done((f32[1,8,128]{2,1,0:T(8,128)S(1)}, f32[1,8,128]{2,1,0:T(8,128)S(1)}, u32[]{:S(2)}, u32[]{:S(2)}) %collective-permute-start.7) | collective-permute-done | bytes 4128 | tf_op jit(solution)/shard_map/ppermute | solution.py:446
  30.2 2.4 %collective-permute-start.8 = (f32[2,8,128]{2,1,0:T(8,128)S(1)}, f32[2,8,128]{2,1,0:T(8,128)S(1)}, u32[]{:S(2)}, u32[]{:S(2)}) collective-permute-start(f32[2,8,128]{2,1,0:T(8,128)S(1)} %get-tuple-element.34.refs_0_), channel_id=1, source_target_pairs={{0,2},{1,3},{2,0},{3,1},{4,6},{5,7},{6,4},{7,5},{8,10},{9,11},{10,... | collective-permute-start | bytes 24584 | tf_op jit(solution)/shard_map/ppermute | solution.py:446
  32.6 0.5 %finish_other.1 = (bf16[512,256]{1,0:T(8,128)(2,1)S(1)}, f32[512,256]{1,0:T(8,128)S(1)}) custom-call(s32[1]{0:T(128)} %bitcast.me_ref, bf16[512,256]{1,0:T(8,128)(2,1)S(1)} %collective-permute-done.11.piece, bf16[2,512,1024]{2,1,0:T(8,128)(2,1)S(1)} %copy-done, bf16[512,1024]{1,0:T(8,128)(2,1)S(1)} %copy-done.1, f32[32,1024]{1,0:T(8,128)S(1)} %copy-done.2), custom_call_target="tpu_custom_call" | custom-call | flops 1024 | bytes 1024 | tf_op jit(solution)/shard_map/finish_other/pallas_call | solution.py:268
  33.1 0.6 %collective-permute-start.13 = (bf16[512,256]{1,0:T(8,128)(2,1)S(1)}, bf16[512,256]{1,0:T(8,128)(2,1)S(1)}, u32[]{:S(2)}, u32[]{:S(2)}) collective-permute-start(bf16[512,256]{1,0:T(8,128)(2,1)S(1)} %ordered.3.refs_0_), channel_id=1, source_target_pairs={{0,4},{4,0},{8,12},{12,8},{16,20},{20,16},{24,28},{28,24},{1,5},{5... | collective-permute-start | bytes 786440 | tf_op jit(solution)/shard_map/ppermute | solution.py:428
  33.6 1.1 %collective-permute-done.8 = f32[2,8,128]{2,1,0:T(8,128)S(1)} collective-permute-done((f32[2,8,128]{2,1,0:T(8,128)S(1)}, f32[2,8,128]{2,1,0:T(8,128)S(1)}, u32[]{:S(2)}, u32[]{:S(2)}) %collective-permute-start.8) | collective-permute-done | bytes 8224 | tf_op jit(solution)/shard_map/ppermute | solution.py:446
  34.8 1.1 %collective-permute-start.16 = (f32[4,8,128]{2,1,0:T(8,128)S(1)}, f32[4,8,128]{2,1,0:T(8,128)S(1)}, u32[]{:S(2)}, u32[]{:S(2)}) collective-permute-start(f32[4,8,128]{2,1,0:T(8,128)S(1)} %constant_dynamic-update-slice_fusion.2.refs_0_), channel_id=1, source_target_pairs={{20,0},{8,4},{28,8},{0,12},{4,16},{24,20},{12,24},{16,28},{21,1},{... | collective-permute-start | bytes 49160 | tf_op jit(solution)/shard_map/ppermute | solution.py:443
  35.9 1.0 %collective-permute-start.15 = (f32[4,8,128]{2,1,0:T(8,128)S(1)}, f32[4,8,128]{2,1,0:T(8,128)S(1)}, u32[]{:S(2)}, u32[]{:S(2)}) collective-permute-start(f32[4,8,128]{2,1,0:T(8,128)S(1)} %constant_dynamic-update-slice_fusion.2.refs_0_), channel_id=1, source_target_pairs={{0,8},{4,20},{8,0},{12,28},{16,24},{20,4},{24,16},{28,12},{1,9},{5... | collective-permute-start | bytes 49160 | tf_op jit(solution)/shard_map/ppermute | solution.py:428
  37.0 0.4 %memory_terms.1.refs_5_.refs_2_ = f32[2,512,256]{2,1,0:T(8,128)S(1)} custom-call(bf16[512,256]{1,0:T(8,128)(2,1)S(1)} %ordered.2.refs_0_, bf16[512,256]{1,0:T(8,128)(2,1)S(1)} %collective-permute-done.10.refs_1_, bf16[2,512,1024]{2,1,0:T(8,128)(2,1)S(1)} %copy-done), custom_call_target="tpu_custom_call" | custom-call | flops 1024 | bytes 1024 | tf_op jit(solution)/shard_map/memory_terms/pallas_call | solution.py:322
  37.4 1.6 %finish_first.1 = (bf16[1024,1024]{1,0:T(8,128)(2,1)}, f32[2,512,256]{2,1,0:T(8,128)S(1)}) custom-call(s32[1]{0:T(128)} %bitcast.me_ref, bf16[512,256]{1,0:T(8,128)(2,1)S(1)} %ordered.3.refs_0_, bf16[512,256]{1,0:T(8,128)(2,1)S(1)} %collective-permute-done.13.refs_1_, bf16[512,256]{1,0:T(8,128)(2,1)S(1)} %get-tuple-element.30.refs_2_, ...), custom_call_target="tpu_custom_call" | custom-call | flops 1024 | bytes 1024 | tf_op jit(solution)/shard_map/finish_first/pallas_call | solution.py:303
  39.1 0.6 %collective-permute-done.15.refs_2_ = f32[4,8,128]{2,1,0:T(8,128)S(1)} collective-permute-done((f32[4,8,128]{2,1,0:T(8,128)S(1)}, f32[4,8,128]{2,1,0:T(8,128)S(1)}, u32[]{:S(2)}, u32[]{:S(2)}) %collective-permute-start.15) | collective-permute-done | bytes 16416 | tf_op jit(solution)/shard_map/ppermute | solution.py:428
  39.7 2.5 %finish_second.1 = (bf16[1024,1024]{1,0:T(8,128)(2,1)}, bf16[1024,1024]{1,0:T(8,128)(2,1)}) custom-call(s32[1]{0:T(128)} %bitcast.me_ref, bf16[512,256]{1,0:T(8,128)(2,1)S(1)} %collective-permute-done.9.refs_0_, f32[512,256]{1,0:T(8,128)S(1)} %get-tuple-element.26.refs_1_, ...), custom_call_target="tpu_custom_call", output_to_operand_aliasing={{0}: (10, {})} | custom-call | flops 1024 | bytes 1024 | tf_op jit(solution)/shard_map/finish_second/pallas_call | solution.py:403
  (27 shorter events, 0.4 us)
Async XLA Ops:
  5.4 2.1 %collective-permute-start.3 = (bf16[2,512,256]{2,1,0:T(8,128)(2,1)S(1)}, bf16[2,512,256]{2,1,0:T(8,128)(2,1)S(1)}, u32[]{:S(2)}, u32[]{:S(2)}) collective-permute-start(bf16[2,512,256]{2,1,0:T(8,128)(2,1)S(1)} %get-tuple-element.21), channel_id=1, source_target_pairs={{0,4},{4,0},{8,12},{12,8},{16,20},{20,16},{24,28},{28,24},{1,5},{5... | collective-permute-start | bytes 1572872 | tf_op jit(solution)/shard_map/ppermute | solution.py:428
  7.3 3.2 %collective-permute-start = (bf16[2,512,256]{2,1,0:T(8,128)(2,1)S(1)}, bf16[2,512,256]{2,1,0:T(8,128)(2,1)S(1)}, u32[]{:S(2)}, u32[]{:S(2)}) collective-permute-start(bf16[2,512,256]{2,1,0:T(8,128)(2,1)S(1)} %memory_product.2), channel_id=1, source_target_pairs={{0,4},{4,0},{8,12},{12,8},{16,20},{20,16},{24,28},{28,24},{1,5},{5... | collective-permute-start | bytes 1572872 | tf_op jit(solution)/shard_map/ppermute | solution.py:428
  7.6 7.2 %collective-permute-start.4 = (bf16[512,256]{1,0:T(8,128)(2,1)S(1)}, bf16[512,256]{1,0:T(8,128)(2,1)S(1)}, u32[]{:S(2)}, u32[]{:S(2)}) collective-permute-start(bf16[512,256]{1,0:T(8,128)(2,1)S(1)} %fusion.4), channel_id=1, source_target_pairs={{0,8},{4,20},{8,0},{12,28},{16,24},{20,4},{24,16},{28,12},{1,9},{5... | collective-permute-start | bytes 786440 | tf_op jit(solution)/shard_map/ppermute | solution.py:428
  11.7 9.6 %copy-start = (bf16[2,512,1024]{2,1,0:T(8,128)(2,1)S(1)}, bf16[2,512,1024]{2,1,0:T(8,128)(2,1)}, u32[]{:S(2)}) copy-start(bf16[2,512,1024]{2,1,0:T(8,128)(2,1)} %refs_3_.1) | copy-start | bytes 6291460
  11.7 9.6 %copy-start.1 = (bf16[512,1024]{1,0:T(8,128)(2,1)S(1)}, bf16[512,1024]{1,0:T(8,128)(2,1)}, u32[]{:S(2)}) copy-start(bf16[512,1024]{1,0:T(8,128)(2,1)} %refs_5_.1) | copy-start | bytes 3145732
  11.8 9.6 %copy-start.2 = (f32[32,1024]{1,0:T(8,128)S(1)}, f32[32,1024]{1,0:T(8,128)}, u32[]{:S(2)}) copy-start(f32[32,1024]{1,0:T(8,128)} %refs_8_.1) | copy-start | bytes 393220
  11.8 7.5 %collective-permute-start.1 = (bf16[512,256]{1,0:T(8,128)(2,1)S(1)}, bf16[512,256]{1,0:T(8,128)(2,1)S(1)}, u32[]{:S(2)}, u32[]{:S(2)}) collective-permute-start(bf16[512,256]{1,0:T(8,128)(2,1)S(1)} %fusion.5._), channel_id=1, source_target_pairs={{0,8},{4,20},{8,0},{12,28},{16,24},{20,4},{24,16},{28,12},{1,9},{5... | collective-permute-start | bytes 786440 | tf_op jit(solution)/shard_map/ppermute | solution.py:428
  14.9 6.5 %collective-permute-start.5 = (bf16[512,256]{1,0:T(8,128)(2,1)S(1)}, bf16[512,256]{1,0:T(8,128)(2,1)S(1)}, u32[]{:S(2)}, u32[]{:S(2)}) collective-permute-start(bf16[512,256]{1,0:T(8,128)(2,1)S(1)} %combined.1.mine), channel_id=1, source_target_pairs={{0,16},{4,12},{8,24},{12,4},{16,0},{20,28},{24,8},{28,20},{1,17},{... | collective-permute-start | bytes 786440 | tf_op jit(solution)/shard_map/ppermute | solution.py:428
  19.4 6.4 %collective-permute-start.2 = (bf16[512,256]{1,0:T(8,128)(2,1)S(1)}, bf16[512,256]{1,0:T(8,128)(2,1)S(1)}, u32[]{:S(2)}, u32[]{:S(2)}) collective-permute-start(bf16[512,256]{1,0:T(8,128)(2,1)S(1)} %fusion.3._.mine), channel_id=1, source_target_pairs={{0,16},{4,12},{8,24},{12,4},{16,0},{20,28},{24,8},{28,20},{1,17},{... | collective-permute-start | bytes 786440 | tf_op jit(solution)/shard_map/ppermute | solution.py:428
  22.5 10.0 %collective-permute-start.11 = (bf16[512,256]{1,0:T(8,128)(2,1)S(1)}, bf16[512,256]{1,0:T(8,128)(2,1)S(1)}, u32[]{:S(2)}, u32[]{:S(2)}) collective-permute-start(bf16[512,256]{1,0:T(8,128)(2,1)S(1)} %get-tuple-element.28), channel_id=1, source_target_pairs={{0,4},{4,0},{8,12},{12,8},{16,20},{20,16},{24,28},{28,24},{1,5},{5... | collective-permute-start | bytes 786440 | tf_op jit(solution)/shard_map/ppermute | solution.py:428
  22.6 10.4 %collective-permute-start.12 = (bf16[512,256]{1,0:T(8,128)(2,1)S(1)}, bf16[512,256]{1,0:T(8,128)(2,1)S(1)}, u32[]{:S(2)}, u32[]{:S(2)}) collective-permute-start(bf16[512,256]{1,0:T(8,128)(2,1)S(1)} %get-tuple-element.28), channel_id=1, source_target_pairs={{0,8},{4,20},{8,0},{12,28},{16,24},{20,4},{24,16},{28,12},{1,9},{5... | collective-permute-start | bytes 786440 | tf_op jit(solution)/shard_map/ppermute | solution.py:428
  26.5 3.7 %collective-permute-start.7 = (f32[1,8,128]{2,1,0:T(8,128)S(1)}, f32[1,8,128]{2,1,0:T(8,128)S(1)}, u32[]{:S(2)}, u32[]{:S(2)}) collective-permute-start(f32[1,8,128]{2,1,0:T(8,128)S(1)} %get-tuple-element.25), channel_id=1, source_target_pairs={{0,1},{1,0},{2,3},{3,2},{4,5},{5,4},{6,7},{7,6},{8,9},{9,8},{10,11... | collective-permute-start | bytes 12296 | tf_op jit(solution)/shard_map/ppermute | solution.py:446
  27.9 6.8 %collective-permute-start.6 = (bf16[512,256]{1,0:T(8,128)(2,1)S(1)}, bf16[512,256]{1,0:T(8,128)(2,1)S(1)}, u32[]{:S(2)}, u32[]{:S(2)}) collective-permute-start(bf16[512,256]{1,0:T(8,128)(2,1)S(1)} %get-tuple-element.24), channel_id=1, source_target_pairs={{0,8},{4,20},{8,0},{12,28},{16,24},{20,4},{24,16},{28,12},{1,9},{5... | collective-permute-start | bytes 786440 | tf_op jit(solution)/shard_map/ppermute | solution.py:428
  30.2 4.5 %collective-permute-start.8 = (f32[2,8,128]{2,1,0:T(8,128)S(1)}, f32[2,8,128]{2,1,0:T(8,128)S(1)}, u32[]{:S(2)}, u32[]{:S(2)}) collective-permute-start(f32[2,8,128]{2,1,0:T(8,128)S(1)} %get-tuple-element.34.refs_0_), channel_id=1, source_target_pairs={{0,2},{1,3},{2,0},{3,1},{4,6},{5,7},{6,4},{7,5},{8,10},{9,11},{10,... | collective-permute-start | bytes 24584 | tf_op jit(solution)/shard_map/ppermute | solution.py:446
  32.5 4.4 %collective-permute-start.10 = (bf16[512,256]{1,0:T(8,128)(2,1)S(1)}, bf16[512,256]{1,0:T(8,128)(2,1)S(1)}, u32[]{:S(2)}, u32[]{:S(2)}) collective-permute-start(bf16[512,256]{1,0:T(8,128)(2,1)S(1)} %get-tuple-element.24), channel_id=1, source_target_pairs={{0,4},{4,0},{8,12},{12,8},{16,20},{20,16},{24,28},{28,24},{1,5},{5... | collective-permute-start | bytes 786440 | tf_op jit(solution)/shard_map/ppermute | solution.py:428
  33.1 4.4 %collective-permute-start.13 = (bf16[512,256]{1,0:T(8,128)(2,1)S(1)}, bf16[512,256]{1,0:T(8,128)(2,1)S(1)}, u32[]{:S(2)}, u32[]{:S(2)}) collective-permute-start(bf16[512,256]{1,0:T(8,128)(2,1)S(1)} %ordered.3.refs_0_), channel_id=1, source_target_pairs={{0,4},{4,0},{8,12},{12,8},{16,20},{20,16},{24,28},{28,24},{1,5},{5... | collective-permute-start | bytes 786440 | tf_op jit(solution)/shard_map/ppermute | solution.py:428
  34.8 4.9 %collective-permute-start.9 = (bf16[512,256]{1,0:T(8,128)(2,1)S(1)}, bf16[512,256]{1,0:T(8,128)(2,1)S(1)}, u32[]{:S(2)}, u32[]{:S(2)}) collective-permute-start(bf16[512,256]{1,0:T(8,128)(2,1)S(1)} %ordered.2.refs_0_), channel_id=1, source_target_pairs={{0,4},{4,0},{8,12},{12,8},{16,20},{20,16},{24,28},{28,24},{1,5},{5... | collective-permute-start | bytes 786440 | tf_op jit(solution)/shard_map/ppermute | solution.py:428
  34.8 4.2 %collective-permute-start.16 = (f32[4,8,128]{2,1,0:T(8,128)S(1)}, f32[4,8,128]{2,1,0:T(8,128)S(1)}, u32[]{:S(2)}, u32[]{:S(2)}) collective-permute-start(f32[4,8,128]{2,1,0:T(8,128)S(1)} %constant_dynamic-update-slice_fusion.2.refs_0_), channel_id=1, source_target_pairs={{20,0},{8,4},{28,8},{0,12},{4,16},{24,20},{12,24},{16,28},{21,1},{... | collective-permute-start | bytes 49160 | tf_op jit(solution)/shard_map/ppermute | solution.py:443
  35.9 3.7 %collective-permute-start.15 = (f32[4,8,128]{2,1,0:T(8,128)S(1)}, f32[4,8,128]{2,1,0:T(8,128)S(1)}, u32[]{:S(2)}, u32[]{:S(2)}) collective-permute-start(f32[4,8,128]{2,1,0:T(8,128)S(1)} %constant_dynamic-update-slice_fusion.2.refs_0_), channel_id=1, source_target_pairs={{0,8},{4,20},{8,0},{12,28},{16,24},{20,4},{24,16},{28,12},{1,9},{5... | collective-permute-start | bytes 49160 | tf_op jit(solution)/shard_map/ppermute | solution.py:428
  37.0 2.7 %collective-permute-start.14 = (f32[4,8,128]{2,1,0:T(8,128)S(1)}, f32[4,8,128]{2,1,0:T(8,128)S(1)}, u32[]{:S(2)}, u32[]{:S(2)}) collective-permute-start(f32[4,8,128]{2,1,0:T(8,128)S(1)} %constant_dynamic-update-slice_fusion.2.refs_0_), channel_id=1, source_target_pairs={{0,4},{4,0},{8,12},{12,8},{16,20},{20,16},{24,28},{28,24},{1,5},{5... | collective-permute-start | bytes 49160 | tf_op jit(solution)/shard_map/ppermute | solution.py:428

commit v16 on v15

--- a/solution.py
+++ b/solution.py
@@ -69,39 +69,45 @@
     depth, columns = g_hist.shape
     half = columns // 2
     parts = 4
-    unit = depth // 16
-    chunks, start = [], 0
-    for units in (2, 3, 4, 4, 3):
-        chunks.append((start * unit, units * unit))
-        start += units
+    eighth = depth // 8
+    chunks = [(0, 2 * eighth), (2 * eighth, 3 * eighth), (5 * eighth, 3 * eighth)]
 
     def kernel(me_ref, sigma_ref, g_ref, sent, kept, sigma_next, g, sigma, total, sems):
-        started = []
-
-        def load(source, target):
-            started.append(pltpu.make_async_copy(source, target, sems.at[len(started)]))
-            started[-1].start()
-            return started[-1]
-
-        pieces = []
-        for start, size in chunks:
-            piece = []
+        def piece(k):
+            start, size = chunks[k]
+            copies, deep = [], pl.ds(start, size)
             for i in range(parts):
                 here = pl.ds(i * (rows // parts), rows // parts)
-                deep = pl.ds(start, size)
-                piece.append(load(sigma_ref.at[here, deep], sigma.at[here, deep]))
+                copies.append((sigma_ref.at[here, deep], sigma.at[here, deep]))
                 here = pl.ds(start + i * (size // parts), size // parts)
-                piece.append(load(g_ref.at[here, :], g.at[here, :]))
-            pieces.append(piece)
-        ahead = []
-        for i in range(2 * parts):
-            here = pl.ds(i * (rows // (2 * parts)), rows // (2 * parts))
-            there = pl.ds(rows + i * (rows // (2 * parts)), rows // (2 * parts))
-            ahead.append(load(sigma_ref.at[there, :], sigma_next.at[here, :]))
-        for k, (start, size) in enumerate(chunks):
-            for copy in pieces[k]:
+                copies.append((g_ref.at[here, :], g.at[here, :]))
+            return copies
+
+        def next_rows():
+            copies, part = [], rows // (2 * parts)
+            for i in range(2 * parts):
+                here = pl.ds(i * part, part)
+                copies.append((sigma_ref.at[pl.ds(rows + i * part, part), :], sigma_next.at[here, :]))
+            return copies
+
+        def start(copies, group):
+            copies = [
+                pltpu.make_async_copy(source, target, sems.at[2 * parts * group + i])
+                for i, (source, target) in enumerate(copies)
+            ]
+            for copy in copies:
+                copy.start()
+            return copies
+
+        loads = [start(piece(0), 0), start(piece(1), 1)]
+        for k, (first, size) in enumerate(chunks):
+            for copy in loads[k]:
                 copy.wait()
-            deep = pl.ds(start, size)
+            if k + 2 < len(chunks):
+                loads.append(start(piece(k + 2), k + 2))
+            if k + 3 == len(chunks):
+                loads.append(start(next_rows(), len(chunks)))
+            deep = pl.ds(first, size)
             term = jnp.dot(sigma[:, deep], g[deep, :], preferred_element_type=F32)
             if k == 0:
                 total[...] = term
@@ -110,7 +116,7 @@
         place = Place(me_ref[0], bits)
         halves_to(sent, total[:, half_of(place.core ^ 1, half)], place.other_side)
         halves_to(kept, total[:, half_of(place.core, half)], place.side)
-        for copy in ahead:
+        for copy in loads[-1]:
             copy.wait()
 
     return call(

time: 42.3 us -> 42.3 us (level)
  no operation moved by 1% of the time
where the time goes in v16:
time: 42.3 us; the launch traced here: 42.1 us
  starting transfers between devices  18.3 us (43%)
  Pallas kernels  14.2 us (34%)
  waiting for transfers between devices  8.61 us (20%)
  between operations  0.82 us (2%)
    ppermute x14, starting transfers between devices, swap(): return lax.ppermute(x, 'past', pairs)  13.4 us
    ppermute x14, waiting for transfers between devices, swap(): return lax.ppermute(x, 'past', pairs)  6.45 us
    pallas_call x1, Pallas kernels, first_products(): call(kernel, 'first_products', in_specs=[SCALAR, HBM, HBM], out_specs=[WH...  4.65 us
    ppermute x2, starting transfers between devices, widened(): lax.ppermute(share, 'second', [(z, z ^ 1 << level) for z in range(second)])  3.79 us
    pallas_call x2, Pallas kernels, product(): call(kernel, 'memory_product', in_specs=[SCALAR, WHOLE, WHOLE] + [FAR] *...  2.56 us
    pallas_call x1, Pallas kernels, finish_second(): call(kernel, 'finish_second', in_specs=[SCALAR] + [WHOLE] * 9 + [HBM], ou...  2.52 us
    ppermute x2, waiting for transfers between devices, widened(): lax.ppermute(share, 'second', [(z, z ^ 1 << level) for z in range(second)])  2.16 us
    pallas_call x1, Pallas kernels, finish_first(): call(kernel, 'finish_first', in_specs=[SCALAR] + [WHOLE] * 7, out_specs=[...  1.61 us
  transfers between devices with their start and end apart: 17, of which 8 were waited for; matrix products, arithmetic and copies ran while one was open for 0% of the time, Pallas kernels for 17%

profile of v16, /device:TPU:0, one launch (start us, length us, event | category | flops | bytes accessed | tf_op | source)
XLA Modules:
  0.0 42.1 jit_solution(11183138834712041994)
XLA Ops:
  0.6 4.6 %first_products.1 = (bf16[2,512,256]{2,1,0:T(8,128)(2,1)S(1)}, f32[2,512,256]{2,1,0:T(8,128)S(1)}, bf16[512,2048]{1,0:T(8,128)(2,1)S(1)}, bf16[2048,1024]{1,0:T(8,128)(2,1)S(1)}) custom-call(s32[1]{0:T(128)} %bitcast.me_ref, bf16[1024,2048]{1,0:T(8,128)(2,1)} %sigma_ref.1, bf16[2048,1024]{1,0:T(8,128)(2,1)} %g_ref.1), custom_call_target="tpu_custom_call" | custom-call | flops 1024 | bytes 1024 | tf_op jit(solution)/shard_map/first_products/pallas_call | solution.py:122
  5.3 0.6 %collective-permute-start.3 = (bf16[2,512,256]{2,1,0:T(8,128)(2,1)S(1)}, bf16[2,512,256]{2,1,0:T(8,128)(2,1)S(1)}, u32[]{:S(2)}, u32[]{:S(2)}) collective-permute-start(bf16[2,512,256]{2,1,0:T(8,128)(2,1)S(1)} %get-tuple-element.21), channel_id=1, source_target_pairs={{0,4},{4,0},{8,12},{12,8},{16,20},{20,16},{24,28},{28,24},{1,5},{5... | collective-permute-start | bytes 1572872 | tf_op jit(solution)/shard_map/ppermute | solution.py:434
  5.9 1.3 %memory_product.2 = bf16[2,512,256]{2,1,0:T(8,128)(2,1)S(1)} custom-call(s32[1]{0:T(128)} %bitcast.me_ref, bf16[512,2048]{1,0:T(8,128)(2,1)S(1)} %get-tuple-element.18.sigma, bf16[2048,1024]{1,0:T(8,128)(2,1)S(1)} %get-tuple-element.19.g), custom_call_target="tpu_custom_call" | custom-call | flops 1024 | bytes 1024 | tf_op jit(solution)/shard_map/memory_product/pallas_call | solution.py:155
  7.3 0.2 collective-permute-done.3.arrived
  7.5 2.8 %collective-permute-start.4 = (bf16[512,256]{1,0:T(8,128)(2,1)S(1)}, bf16[512,256]{1,0:T(8,128)(2,1)S(1)}, u32[]{:S(2)}, u32[]{:S(2)}) collective-permute-start(bf16[512,256]{1,0:T(8,128)(2,1)S(1)} %fusion.4), channel_id=1, source_target_pairs={{0,8},{4,20},{8,0},{12,28},{16,24},{20,4},{24,16},{28,12},{1,9},{5... | collective-permute-start | bytes 786440 | tf_op jit(solution)/shard_map/ppermute | solution.py:434
  10.3 1.3 %memory_product.3 = f32[2,512,256]{2,1,0:T(8,128)S(1)} custom-call(s32[1]{0:T(128)} %bitcast.me_ref, bf16[512,2048]{1,0:T(8,128)(2,1)S(1)} %get-tuple-element.18.sigma, bf16[2048,1024]{1,0:T(8,128)(2,1)S(1)} %get-tuple-element.19.g, bf16[2,512,256]{2,1,0:T(8,128)(2,1)S(1)} %collective-permute-done.refs_0_), custom_call_target="tpu_custom_call" | custom-call | flops 1024 | bytes 1024 | tf_op jit(solution)/shard_map/memory_product/pallas_call | solution.py:155
  11.7 1.4 %collective-permute-start.1 = (bf16[512,256]{1,0:T(8,128)(2,1)S(1)}, bf16[512,256]{1,0:T(8,128)(2,1)S(1)}, u32[]{:S(2)}, u32[]{:S(2)}) collective-permute-start(bf16[512,256]{1,0:T(8,128)(2,1)S(1)} %fusion.5._), channel_id=1, source_target_pairs={{0,8},{4,20},{8,0},{12,28},{16,24},{20,4},{24,16},{28,12},{1,9},{5... | collective-permute-start | bytes 786440 | tf_op jit(solution)/shard_map/ppermute | solution.py:434
  13.1 1.5 %collective-permute-done.4.more = bf16[512,256]{1,0:T(8,128)(2,1)S(1)} collective-permute-done((bf16[512,256]{1,0:T(8,128)(2,1)S(1)}, bf16[512,256]{1,0:T(8,128)(2,1)S(1)}, u32[]{:S(2)}, u32[]{:S(2)}) %collective-permute-start.4) | collective-permute-done | bytes 262176 | tf_op jit(solution)/shard_map/ppermute | solution.py:434
  14.7 0.1 combined.1.mine
  14.8 2.1 %collective-permute-start.5 = (bf16[512,256]{1,0:T(8,128)(2,1)S(1)}, bf16[512,256]{1,0:T(8,128)(2,1)S(1)}, u32[]{:S(2)}, u32[]{:S(2)}) collective-permute-start(bf16[512,256]{1,0:T(8,128)(2,1)S(1)} %combined.1.mine), channel_id=1, source_target_pairs={{0,16},{4,12},{8,24},{12,4},{16,0},{20,28},{24,8},{28,20},{1,17},{... | collective-permute-start | bytes 786440 | tf_op jit(solution)/shard_map/ppermute | solution.py:434
  16.9 2.3 %collective-permute-done.1 = bf16[512,256]{1,0:T(8,128)(2,1)S(1)} collective-permute-done((bf16[512,256]{1,0:T(8,128)(2,1)S(1)}, bf16[512,256]{1,0:T(8,128)(2,1)S(1)}, u32[]{:S(2)}, u32[]{:S(2)}) %collective-permute-start.1) | collective-permute-done | bytes 262176 | tf_op jit(solution)/shard_map/ppermute | solution.py:434
  19.2 0.1 fusion.3._.mine
  19.3 1.4 %collective-permute-start.2 = (bf16[512,256]{1,0:T(8,128)(2,1)S(1)}, bf16[512,256]{1,0:T(8,128)(2,1)S(1)}, u32[]{:S(2)}, u32[]{:S(2)}) collective-permute-start(bf16[512,256]{1,0:T(8,128)(2,1)S(1)} %fusion.3._.mine), channel_id=1, source_target_pairs={{0,16},{4,12},{8,24},{12,4},{16,0},{20,28},{24,8},{28,20},{1,17},{... | collective-permute-start | bytes 786440 | tf_op jit(solution)/shard_map/ppermute | solution.py:434
  20.7 0.6 %collective-permute-done.5.theirs = bf16[512,256]{1,0:T(8,128)(2,1)S(1)} collective-permute-done((bf16[512,256]{1,0:T(8,128)(2,1)S(1)}, bf16[512,256]{1,0:T(8,128)(2,1)S(1)}, u32[]{:S(2)}, u32[]{:S(2)}) %collective-permute-start.5) | collective-permute-done | bytes 262176 | tf_op jit(solution)/shard_map/ppermute | solution.py:434
  21.3 1.2 %own_first.1 = (bf16[512,256]{1,0:T(8,128)(2,1)S(1)}, f32[512,256]{1,0:T(8,128)S(1)}, f32[1,128]{1,0:T(1,128)S(1)}, bf16[512,256]{1,0:T(8,128)(2,1)S(1)}, f32[512,256]{1,0:T(8,128)S(1)}) custom-call(s32[1]{0:T(128)} %bitcast.me_ref, bf16[512,256]{1,0:T(8,128)(2,1)S(1)} %combined.1.mine, bf16[512,256]{1,0:T(8,128)(2,1)S(1)} %collective-permute-done.5.theirs, ...), custom_call_target="tpu_custom_call" | custom-call | flops 1024 | bytes 1024 | tf_op jit(solution)/shard_map/own_first/pallas_call | solution.py:217
  22.4 0.1 collective-permute-start.11
  22.5 2.1 %collective-permute-start.12 = (bf16[512,256]{1,0:T(8,128)(2,1)S(1)}, bf16[512,256]{1,0:T(8,128)(2,1)S(1)}, u32[]{:S(2)}, u32[]{:S(2)}) collective-permute-start(bf16[512,256]{1,0:T(8,128)(2,1)S(1)} %get-tuple-element.28), channel_id=1, source_target_pairs={{0,8},{4,20},{8,0},{12,28},{16,24},{20,4},{24,16},{28,12},{1,9},{5... | collective-permute-start | bytes 786440 | tf_op jit(solution)/shard_map/ppermute | solution.py:434
  24.6 1.2 %collective-permute-done.2.theirs = bf16[512,256]{1,0:T(8,128)(2,1)S(1)} collective-permute-done((bf16[512,256]{1,0:T(8,128)(2,1)S(1)}, bf16[512,256]{1,0:T(8,128)(2,1)S(1)}, u32[]{:S(2)}, u32[]{:S(2)}) %collective-permute-start.2) | collective-permute-done | bytes 262176 | tf_op jit(solution)/shard_map/ppermute | solution.py:434
  25.8 0.6 %own_second.1 = (bf16[512,256]{1,0:T(8,128)(2,1)S(1)}, f32[1,8,128]{2,1,0:T(8,128)S(1)}, f32[512,256]{1,0:T(8,128)S(1)}) custom-call(s32[1]{0:T(128)} %bitcast.me_ref, bf16[512,256]{1,0:T(8,128)(2,1)S(1)} %fusion.3._.mine, bf16[512,256]{1,0:T(8,128)(2,1)S(1)} %collective-permute-done.2.theirs, bf16[2,512,1024]{2,1,0:T(8,128)(2,1)S(1)} %copy-done, ...), custom_call_target="tpu_custom_call" | custom-call | flops 1024 | bytes 1024 | tf_op jit(solution)/shard_map/own_second/pallas_call | solution.py:255
  26.4 1.4 %collective-permute-start.7 = (f32[1,8,128]{2,1,0:T(8,128)S(1)}, f32[1,8,128]{2,1,0:T(8,128)S(1)}, u32[]{:S(2)}, u32[]{:S(2)}) collective-permute-start(f32[1,8,128]{2,1,0:T(8,128)S(1)} %get-tuple-element.25), channel_id=1, source_target_pairs={{0,1},{1,0},{2,3},{3,2},{4,5},{5,4},{6,7},{7,6},{8,9},{9,8},{10,11... | collective-permute-start | bytes 12296 | tf_op jit(solution)/shard_map/ppermute | solution.py:452
  27.8 1.2 %collective-permute-start.6 = (bf16[512,256]{1,0:T(8,128)(2,1)S(1)}, bf16[512,256]{1,0:T(8,128)(2,1)S(1)}, u32[]{:S(2)}, u32[]{:S(2)}) collective-permute-start(bf16[512,256]{1,0:T(8,128)(2,1)S(1)} %get-tuple-element.24), channel_id=1, source_target_pairs={{0,8},{4,20},{8,0},{12,28},{16,24},{20,4},{24,16},{28,12},{1,9},{5... | collective-permute-start | bytes 786440 | tf_op jit(solution)/shard_map/ppermute | solution.py:434
  29.0 1.0 %collective-permute-done.7 = f32[1,8,128]{2,1,0:T(8,128)S(1)} collective-permute-done((f32[1,8,128]{2,1,0:T(8,128)S(1)}, f32[1,8,128]{2,1,0:T(8,128)S(1)}, u32[]{:S(2)}, u32[]{:S(2)}) %collective-permute-start.7) | collective-permute-done | bytes 4128 | tf_op jit(solution)/shard_map/ppermute | solution.py:452
  30.1 2.4 %collective-permute-start.8 = (f32[2,8,128]{2,1,0:T(8,128)S(1)}, f32[2,8,128]{2,1,0:T(8,128)S(1)}, u32[]{:S(2)}, u32[]{:S(2)}) collective-permute-start(f32[2,8,128]{2,1,0:T(8,128)S(1)} %get-tuple-element.34.refs_0_), channel_id=1, source_target_pairs={{0,2},{1,3},{2,0},{3,1},{4,6},{5,7},{6,4},{7,5},{8,10},{9,11},{10,... | collective-permute-start | bytes 24584 | tf_op jit(solution)/shard_map/ppermute | solution.py:452
  32.4 0.5 %finish_other.1 = (bf16[512,256]{1,0:T(8,128)(2,1)S(1)}, f32[512,256]{1,0:T(8,128)S(1)}) custom-call(s32[1]{0:T(128)} %bitcast.me_ref, bf16[512,256]{1,0:T(8,128)(2,1)S(1)} %collective-permute-done.11.piece, bf16[2,512,1024]{2,1,0:T(8,128)(2,1)S(1)} %copy-done, bf16[512,1024]{1,0:T(8,128)(2,1)S(1)} %copy-done.1, f32[32,1024]{1,0:T(8,128)S(1)} %copy-done.2), custom_call_target="tpu_custom_call" | custom-call | flops 1024 | bytes 1024 | tf_op jit(solution)/shard_map/finish_other/pallas_call | solution.py:274
  33.0 0.6 %collective-permute-start.13 = (bf16[512,256]{1,0:T(8,128)(2,1)S(1)}, bf16[512,256]{1,0:T(8,128)(2,1)S(1)}, u32[]{:S(2)}, u32[]{:S(2)}) collective-permute-start(bf16[512,256]{1,0:T(8,128)(2,1)S(1)} %ordered.3.refs_0_), channel_id=1, source_target_pairs={{0,4},{4,0},{8,12},{12,8},{16,20},{20,16},{24,28},{28,24},{1,5},{5... | collective-permute-start | bytes 786440 | tf_op jit(solution)/shard_map/ppermute | solution.py:434
  33.5 1.1 %collective-permute-done.8 = f32[2,8,128]{2,1,0:T(8,128)S(1)} collective-permute-done((f32[2,8,128]{2,1,0:T(8,128)S(1)}, f32[2,8,128]{2,1,0:T(8,128)S(1)}, u32[]{:S(2)}, u32[]{:S(2)}) %collective-permute-start.8) | collective-permute-done | bytes 8224 | tf_op jit(solution)/shard_map/ppermute | solution.py:452
  34.7 1.1 %collective-permute-start.16 = (f32[4,8,128]{2,1,0:T(8,128)S(1)}, f32[4,8,128]{2,1,0:T(8,128)S(1)}, u32[]{:S(2)}, u32[]{:S(2)}) collective-permute-start(f32[4,8,128]{2,1,0:T(8,128)S(1)} %constant_dynamic-update-slice_fusion.2.refs_0_), channel_id=1, source_target_pairs={{20,0},{8,4},{28,8},{0,12},{4,16},{24,20},{12,24},{16,28},{21,1},{... | collective-permute-start | bytes 49160 | tf_op jit(solution)/shard_map/ppermute | solution.py:449
  35.8 1.0 %collective-permute-start.15 = (f32[4,8,128]{2,1,0:T(8,128)S(1)}, f32[4,8,128]{2,1,0:T(8,128)S(1)}, u32[]{:S(2)}, u32[]{:S(2)}) collective-permute-start(f32[4,8,128]{2,1,0:T(8,128)S(1)} %constant_dynamic-update-slice_fusion.2.refs_0_), channel_id=1, source_target_pairs={{0,8},{4,20},{8,0},{12,28},{16,24},{20,4},{24,16},{28,12},{1,9},{5... | collective-permute-start | bytes 49160 | tf_op jit(solution)/shard_map/ppermute | solution.py:434
  36.9 0.4 %memory_terms.1.refs_5_.refs_2_ = f32[2,512,256]{2,1,0:T(8,128)S(1)} custom-call(bf16[512,256]{1,0:T(8,128)(2,1)S(1)} %ordered.2.refs_0_, bf16[512,256]{1,0:T(8,128)(2,1)S(1)} %collective-permute-done.10.refs_1_, bf16[2,512,1024]{2,1,0:T(8,128)(2,1)S(1)} %copy-done), custom_call_target="tpu_custom_call" | custom-call | flops 1024 | bytes 1024 | tf_op jit(solution)/shard_map/memory_terms/pallas_call | solution.py:328
  37.3 1.6 %finish_first.1 = (bf16[1024,1024]{1,0:T(8,128)(2,1)}, f32[2,512,256]{2,1,0:T(8,128)S(1)}) custom-call(s32[1]{0:T(128)} %bitcast.me_ref, bf16[512,256]{1,0:T(8,128)(2,1)S(1)} %ordered.3.refs_0_, bf16[512,256]{1,0:T(8,128)(2,1)S(1)} %collective-permute-done.13.refs_1_, bf16[512,256]{1,0:T(8,128)(2,1)S(1)} %get-tuple-element.30.refs_2_, ...), custom_call_target="tpu_custom_call" | custom-call | flops 1024 | bytes 1024 | tf_op jit(solution)/shard_map/finish_first/pallas_call | solution.py:309
  38.9 0.6 %collective-permute-done.15.refs_2_ = f32[4,8,128]{2,1,0:T(8,128)S(1)} collective-permute-done((f32[4,8,128]{2,1,0:T(8,128)S(1)}, f32[4,8,128]{2,1,0:T(8,128)S(1)}, u32[]{:S(2)}, u32[]{:S(2)}) %collective-permute-start.15) | collective-permute-done | bytes 16416 | tf_op jit(solution)/shard_map/ppermute | solution.py:434
  39.6 2.5 %finish_second.1 = (bf16[1024,1024]{1,0:T(8,128)(2,1)}, bf16[1024,1024]{1,0:T(8,128)(2,1)}) custom-call(s32[1]{0:T(128)} %bitcast.me_ref, bf16[512,256]{1,0:T(8,128)(2,1)S(1)} %collective-permute-done.9.refs_0_, f32[512,256]{1,0:T(8,128)S(1)} %get-tuple-element.26.refs_1_, ...), custom_call_target="tpu_custom_call", output_to_operand_aliasing={{0}: (10, {})} | custom-call | flops 1024 | bytes 1024 | tf_op jit(solution)/shard_map/finish_second/pallas_call | solution.py:409
  (27 shorter events, 0.4 us)
Async XLA Ops:
  5.3 2.1 %collective-permute-start.3 = (bf16[2,512,256]{2,1,0:T(8,128)(2,1)S(1)}, bf16[2,512,256]{2,1,0:T(8,128)(2,1)S(1)}, u32[]{:S(2)}, u32[]{:S(2)}) collective-permute-start(bf16[2,512,256]{2,1,0:T(8,128)(2,1)S(1)} %get-tuple-element.21), channel_id=1, source_target_pairs={{0,4},{4,0},{8,12},{12,8},{16,20},{20,16},{24,28},{28,24},{1,5},{5... | collective-permute-start | bytes 1572872 | tf_op jit(solution)/shard_map/ppermute | solution.py:434
  7.2 3.2 %collective-permute-start = (bf16[2,512,256]{2,1,0:T(8,128)(2,1)S(1)}, bf16[2,512,256]{2,1,0:T(8,128)(2,1)S(1)}, u32[]{:S(2)}, u32[]{:S(2)}) collective-permute-start(bf16[2,512,256]{2,1,0:T(8,128)(2,1)S(1)} %memory_product.2), channel_id=1, source_target_pairs={{0,4},{4,0},{8,12},{12,8},{16,20},{20,16},{24,28},{28,24},{1,5},{5... | collective-permute-start | bytes 1572872 | tf_op jit(solution)/shard_map/ppermute | solution.py:434
  7.5 7.2 %collective-permute-start.4 = (bf16[512,256]{1,0:T(8,128)(2,1)S(1)}, bf16[512,256]{1,0:T(8,128)(2,1)S(1)}, u32[]{:S(2)}, u32[]{:S(2)}) collective-permute-start(bf16[512,256]{1,0:T(8,128)(2,1)S(1)} %fusion.4), channel_id=1, source_target_pairs={{0,8},{4,20},{8,0},{12,28},{16,24},{20,4},{24,16},{28,12},{1,9},{5... | collective-permute-start | bytes 786440 | tf_op jit(solution)/shard_map/ppermute | solution.py:434
  11.6 9.6 %copy-start = (bf16[2,512,1024]{2,1,0:T(8,128)(2,1)S(1)}, bf16[2,512,1024]{2,1,0:T(8,128)(2,1)}, u32[]{:S(2)}) copy-start(bf16[2,512,1024]{2,1,0:T(8,128)(2,1)} %refs_3_.1) | copy-start | bytes 6291460
  11.6 9.6 %copy-start.1 = (bf16[512,1024]{1,0:T(8,128)(2,1)S(1)}, bf16[512,1024]{1,0:T(8,128)(2,1)}, u32[]{:S(2)}) copy-start(bf16[512,1024]{1,0:T(8,128)(2,1)} %refs_5_.1) | copy-start | bytes 3145732
  11.7 9.6 %copy-start.2 = (f32[32,1024]{1,0:T(8,128)S(1)}, f32[32,1024]{1,0:T(8,128)}, u32[]{:S(2)}) copy-start(f32[32,1024]{1,0:T(8,128)} %refs_8_.1) | copy-start | bytes 393220
  11.7 7.5 %collective-permute-start.1 = (bf16[512,256]{1,0:T(8,128)(2,1)S(1)}, bf16[512,256]{1,0:T(8,128)(2,1)S(1)}, u32[]{:S(2)}, u32[]{:S(2)}) collective-permute-start(bf16[512,256]{1,0:T(8,128)(2,1)S(1)} %fusion.5._), channel_id=1, source_target_pairs={{0,8},{4,20},{8,0},{12,28},{16,24},{20,4},{24,16},{28,12},{1,9},{5... | collective-permute-start | bytes 786440 | tf_op jit(solution)/shard_map/ppermute | solution.py:434
  14.8 6.5 %collective-permute-start.5 = (bf16[512,256]{1,0:T(8,128)(2,1)S(1)}, bf16[512,256]{1,0:T(8,128)(2,1)S(1)}, u32[]{:S(2)}, u32[]{:S(2)}) collective-permute-start(bf16[512,256]{1,0:T(8,128)(2,1)S(1)} %combined.1.mine), channel_id=1, source_target_pairs={{0,16},{4,12},{8,24},{12,4},{16,0},{20,28},{24,8},{28,20},{1,17},{... | collective-permute-start | bytes 786440 | tf_op jit(solution)/shard_map/ppermute | solution.py:434
  19.3 6.4 %collective-permute-start.2 = (bf16[512,256]{1,0:T(8,128)(2,1)S(1)}, bf16[512,256]{1,0:T(8,128)(2,1)S(1)}, u32[]{:S(2)}, u32[]{:S(2)}) collective-permute-start(bf16[512,256]{1,0:T(8,128)(2,1)S(1)} %fusion.3._.mine), channel_id=1, source_target_pairs={{0,16},{4,12},{8,24},{12,4},{16,0},{20,28},{24,8},{28,20},{1,17},{... | collective-permute-start | bytes 786440 | tf_op jit(solution)/shard_map/ppermute | solution.py:434
  22.4 10.0 %collective-permute-start.11 = (bf16[512,256]{1,0:T(8,128)(2,1)S(1)}, bf16[512,256]{1,0:T(8,128)(2,1)S(1)}, u32[]{:S(2)}, u32[]{:S(2)}) collective-permute-start(bf16[512,256]{1,0:T(8,128)(2,1)S(1)} %get-tuple-element.28), channel_id=1, source_target_pairs={{0,4},{4,0},{8,12},{12,8},{16,20},{20,16},{24,28},{28,24},{1,5},{5... | collective-permute-start | bytes 786440 | tf_op jit(solution)/shard_map/ppermute | solution.py:434
  22.5 10.4 %collective-permute-start.12 = (bf16[512,256]{1,0:T(8,128)(2,1)S(1)}, bf16[512,256]{1,0:T(8,128)(2,1)S(1)}, u32[]{:S(2)}, u32[]{:S(2)}) collective-permute-start(bf16[512,256]{1,0:T(8,128)(2,1)S(1)} %get-tuple-element.28), channel_id=1, source_target_pairs={{0,8},{4,20},{8,0},{12,28},{16,24},{20,4},{24,16},{28,12},{1,9},{5... | collective-permute-start | bytes 786440 | tf_op jit(solution)/shard_map/ppermute | solution.py:434
  26.4 3.7 %collective-permute-start.7 = (f32[1,8,128]{2,1,0:T(8,128)S(1)}, f32[1,8,128]{2,1,0:T(8,128)S(1)}, u32[]{:S(2)}, u32[]{:S(2)}) collective-permute-start(f32[1,8,128]{2,1,0:T(8,128)S(1)} %get-tuple-element.25), channel_id=1, source_target_pairs={{0,1},{1,0},{2,3},{3,2},{4,5},{5,4},{6,7},{7,6},{8,9},{9,8},{10,11... | collective-permute-start | bytes 12296 | tf_op jit(solution)/shard_map/ppermute | solution.py:452
  27.8 6.8 %collective-permute-start.6 = (bf16[512,256]{1,0:T(8,128)(2,1)S(1)}, bf16[512,256]{1,0:T(8,128)(2,1)S(1)}, u32[]{:S(2)}, u32[]{:S(2)}) collective-permute-start(bf16[512,256]{1,0:T(8,128)(2,1)S(1)} %get-tuple-element.24), channel_id=1, source_target_pairs={{0,8},{4,20},{8,0},{12,28},{16,24},{20,4},{24,16},{28,12},{1,9},{5... | collective-permute-start | bytes 786440 | tf_op jit(solution)/shard_map/ppermute | solution.py:434
  30.1 4.5 %collective-permute-start.8 = (f32[2,8,128]{2,1,0:T(8,128)S(1)}, f32[2,8,128]{2,1,0:T(8,128)S(1)}, u32[]{:S(2)}, u32[]{:S(2)}) collective-permute-start(f32[2,8,128]{2,1,0:T(8,128)S(1)} %get-tuple-element.34.refs_0_), channel_id=1, source_target_pairs={{0,2},{1,3},{2,0},{3,1},{4,6},{5,7},{6,4},{7,5},{8,10},{9,11},{10,... | collective-permute-start | bytes 24584 | tf_op jit(solution)/shard_map/ppermute | solution.py:452
  32.4 4.4 %collective-permute-start.10 = (bf16[512,256]{1,0:T(8,128)(2,1)S(1)}, bf16[512,256]{1,0:T(8,128)(2,1)S(1)}, u32[]{:S(2)}, u32[]{:S(2)}) collective-permute-start(bf16[512,256]{1,0:T(8,128)(2,1)S(1)} %get-tuple-element.24), channel_id=1, source_target_pairs={{0,4},{4,0},{8,12},{12,8},{16,20},{20,16},{24,28},{28,24},{1,5},{5... | collective-permute-start | bytes 786440 | tf_op jit(solution)/shard_map/ppermute | solution.py:434
  33.0 4.4 %collective-permute-start.13 = (bf16[512,256]{1,0:T(8,128)(2,1)S(1)}, bf16[512,256]{1,0:T(8,128)(2,1)S(1)}, u32[]{:S(2)}, u32[]{:S(2)}) collective-permute-start(bf16[512,256]{1,0:T(8,128)(2,1)S(1)} %ordered.3.refs_0_), channel_id=1, source_target_pairs={{0,4},{4,0},{8,12},{12,8},{16,20},{20,16},{24,28},{28,24},{1,5},{5... | collective-permute-start | bytes 786440 | tf_op jit(solution)/shard_map/ppermute | solution.py:434
  34.7 4.9 %collective-permute-start.9 = (bf16[512,256]{1,0:T(8,128)(2,1)S(1)}, bf16[512,256]{1,0:T(8,128)(2,1)S(1)}, u32[]{:S(2)}, u32[]{:S(2)}) collective-permute-start(bf16[512,256]{1,0:T(8,128)(2,1)S(1)} %ordered.2.refs_0_), channel_id=1, source_target_pairs={{0,4},{4,0},{8,12},{12,8},{16,20},{20,16},{24,28},{28,24},{1,5},{5... | collective-permute-start | bytes 786440 | tf_op jit(solution)/shard_map/ppermute | solution.py:434
  34.7 4.2 %collective-permute-start.16 = (f32[4,8,128]{2,1,0:T(8,128)S(1)}, f32[4,8,128]{2,1,0:T(8,128)S(1)}, u32[]{:S(2)}, u32[]{:S(2)}) collective-permute-start(f32[4,8,128]{2,1,0:T(8,128)S(1)} %constant_dynamic-update-slice_fusion.2.refs_0_), channel_id=1, source_target_pairs={{20,0},{8,4},{28,8},{0,12},{4,16},{24,20},{12,24},{16,28},{21,1},{... | collective-permute-start | bytes 49160 | tf_op jit(solution)/shard_map/ppermute | solution.py:449
  35.8 3.7 %collective-permute-start.15 = (f32[4,8,128]{2,1,0:T(8,128)S(1)}, f32[4,8,128]{2,1,0:T(8,128)S(1)}, u32[]{:S(2)}, u32[]{:S(2)}) collective-permute-start(f32[4,8,128]{2,1,0:T(8,128)S(1)} %constant_dynamic-update-slice_fusion.2.refs_0_), channel_id=1, source_target_pairs={{0,8},{4,20},{8,0},{12,28},{16,24},{20,4},{24,16},{28,12},{1,9},{5... | collective-permute-start | bytes 49160 | tf_op jit(solution)/shard_map/ppermute | solution.py:434
  36.9 2.7 %collective-permute-start.14 = (f32[4,8,128]{2,1,0:T(8,128)S(1)}, f32[4,8,128]{2,1,0:T(8,128)S(1)}, u32[]{:S(2)}, u32[]{:S(2)}) collective-permute-start(f32[4,8,128]{2,1,0:T(8,128)S(1)} %constant_dynamic-update-slice_fusion.2.refs_0_), channel_id=1, source_target_pairs={{0,4},{4,0},{8,12},{12,8},{16,20},{20,16},{24,28},{28,24},{1,5},{5... | collective-permute-start | bytes 49160 | tf_op jit(solution)/shard_map/ppermute | solution.py:434

commit v17 on v15

--- a/solution.py
+++ b/solution.py
@@ -69,11 +69,8 @@
     depth, columns = g_hist.shape
     half = columns // 2
     parts = 4
-    unit = depth // 16
-    chunks, start = [], 0
-    for units in (2, 3, 4, 4, 3):
-        chunks.append((start * unit, units * unit))
-        start += units
+    eighth = depth // 8
+    chunks = [(0, 2 * eighth), (2 * eighth, 3 * eighth), (5 * eighth, 3 * eighth)]
 
     def kernel(me_ref, sigma_ref, g_ref, sent, kept, sigma_next, g, sigma, total, sems):
         started = []

time: 42.3 us -> 42.1 us (level)
  no operation moved by 1% of the time
where the time goes in v17:
time: 42.1 us; the launch traced here: 42 us
  starting transfers between devices  18.3 us (43%)
  Pallas kernels  14 us (33%)
  waiting for transfers between devices  8.6 us (20%)
  between operations  0.82 us (2%)
    ppermute x14, starting transfers between devices, swap(): return lax.ppermute(x, 'past', pairs)  13.4 us
    ppermute x14, waiting for transfers between devices, swap(): return lax.ppermute(x, 'past', pairs)  6.45 us
    pallas_call x1, Pallas kernels, first_products(): call(kernel, 'first_products', in_specs=[SCALAR, HBM, HBM], out_specs=[WH...  4.5 us
    ppermute x2, starting transfers between devices, widened(): lax.ppermute(share, 'second', [(z, z ^ 1 << level) for z in range(second)])  3.78 us
    pallas_call x2, Pallas kernels, product(): call(kernel, 'memory_product', in_specs=[SCALAR, WHOLE, WHOLE] + [FAR] *...  2.56 us
    pallas_call x1, Pallas kernels, finish_second(): call(kernel, 'finish_second', in_specs=[SCALAR] + [WHOLE] * 9 + [HBM], ou...  2.52 us
    ppermute x2, waiting for transfers between devices, widened(): lax.ppermute(share, 'second', [(z, z ^ 1 << level) for z in range(second)])  2.15 us
    pallas_call x1, Pallas kernels, finish_first(): call(kernel, 'finish_first', in_specs=[SCALAR] + [WHOLE] * 7, out_specs=[...  1.6 us
  transfers between devices with their start and end apart: 17, of which 8 were waited for; matrix products, arithmetic and copies ran while one was open for 0% of the time, Pallas kernels for 17%

profile of v17, /device:TPU:0, one launch (start us, length us, event | category | flops | bytes accessed | tf_op | source)
XLA Modules:
  0.0 42.0 jit_solution(2542895629991685810)
XLA Ops:
  0.6 4.5 %first_products.1 = (bf16[2,512,256]{2,1,0:T(8,128)(2,1)S(1)}, f32[2,512,256]{2,1,0:T(8,128)S(1)}, bf16[512,2048]{1,0:T(8,128)(2,1)S(1)}, bf16[2048,1024]{1,0:T(8,128)(2,1)S(1)}) custom-call(s32[1]{0:T(128)} %bitcast.me_ref, bf16[1024,2048]{1,0:T(8,128)(2,1)} %sigma_ref.1, bf16[2048,1024]{1,0:T(8,128)(2,1)} %g_ref.1), custom_call_target="tpu_custom_call" | custom-call | flops 1024 | bytes 1024 | tf_op jit(solution)/shard_map/first_products/pallas_call | solution.py:113
  5.1 0.6 %collective-permute-start.3 = (bf16[2,512,256]{2,1,0:T(8,128)(2,1)S(1)}, bf16[2,512,256]{2,1,0:T(8,128)(2,1)S(1)}, u32[]{:S(2)}, u32[]{:S(2)}) collective-permute-start(bf16[2,512,256]{2,1,0:T(8,128)(2,1)S(1)} %get-tuple-element.21), channel_id=1, source_target_pairs={{0,4},{4,0},{8,12},{12,8},{16,20},{20,16},{24,28},{28,24},{1,5},{5... | collective-permute-start | bytes 1572872 | tf_op jit(solution)/shard_map/ppermute | solution.py:425
  5.7 1.3 %memory_product.2 = bf16[2,512,256]{2,1,0:T(8,128)(2,1)S(1)} custom-call(s32[1]{0:T(128)} %bitcast.me_ref, bf16[512,2048]{1,0:T(8,128)(2,1)S(1)} %get-tuple-element.18.sigma, bf16[2048,1024]{1,0:T(8,128)(2,1)S(1)} %get-tuple-element.19.g), custom_call_target="tpu_custom_call" | custom-call | flops 1024 | bytes 1024 | tf_op jit(solution)/shard_map/memory_product/pallas_call | solution.py:146
  7.1 0.2 collective-permute-done.3.arrived
  7.3 2.8 %collective-permute-start.4 = (bf16[512,256]{1,0:T(8,128)(2,1)S(1)}, bf16[512,256]{1,0:T(8,128)(2,1)S(1)}, u32[]{:S(2)}, u32[]{:S(2)}) collective-permute-start(bf16[512,256]{1,0:T(8,128)(2,1)S(1)} %fusion.4), channel_id=1, source_target_pairs={{0,8},{4,20},{8,0},{12,28},{16,24},{20,4},{24,16},{28,12},{1,9},{5... | collective-permute-start | bytes 786440 | tf_op jit(solution)/shard_map/ppermute | solution.py:425
  10.2 1.3 %memory_product.3 = f32[2,512,256]{2,1,0:T(8,128)S(1)} custom-call(s32[1]{0:T(128)} %bitcast.me_ref, bf16[512,2048]{1,0:T(8,128)(2,1)S(1)} %get-tuple-element.18.sigma, bf16[2048,1024]{1,0:T(8,128)(2,1)S(1)} %get-tuple-element.19.g, bf16[2,512,256]{2,1,0:T(8,128)(2,1)S(1)} %collective-permute-done.refs_0_), custom_call_target="tpu_custom_call" | custom-call | flops 1024 | bytes 1024 | tf_op jit(solution)/shard_map/memory_product/pallas_call | solution.py:146
  11.6 1.4 %collective-permute-start.1 = (bf16[512,256]{1,0:T(8,128)(2,1)S(1)}, bf16[512,256]{1,0:T(8,128)(2,1)S(1)}, u32[]{:S(2)}, u32[]{:S(2)}) collective-permute-start(bf16[512,256]{1,0:T(8,128)(2,1)S(1)} %fusion.5._), channel_id=1, source_target_pairs={{0,8},{4,20},{8,0},{12,28},{16,24},{20,4},{24,16},{28,12},{1,9},{5... | collective-permute-start | bytes 786440 | tf_op jit(solution)/shard_map/ppermute | solution.py:425
  13.0 1.5 %collective-permute-done.4.more = bf16[512,256]{1,0:T(8,128)(2,1)S(1)} collective-permute-done((bf16[512,256]{1,0:T(8,128)(2,1)S(1)}, bf16[512,256]{1,0:T(8,128)(2,1)S(1)}, u32[]{:S(2)}, u32[]{:S(2)}) %collective-permute-start.4) | collective-permute-done | bytes 262176 | tf_op jit(solution)/shard_map/ppermute | solution.py:425
  14.5 0.1 combined.1.mine
  14.6 2.1 %collective-permute-start.5 = (bf16[512,256]{1,0:T(8,128)(2,1)S(1)}, bf16[512,256]{1,0:T(8,128)(2,1)S(1)}, u32[]{:S(2)}, u32[]{:S(2)}) collective-permute-start(bf16[512,256]{1,0:T(8,128)(2,1)S(1)} %combined.1.mine), channel_id=1, source_target_pairs={{0,16},{4,12},{8,24},{12,4},{16,0},{20,28},{24,8},{28,20},{1,17},{... | collective-permute-start | bytes 786440 | tf_op jit(solution)/shard_map/ppermute | solution.py:425
  16.7 2.3 %collective-permute-done.1 = bf16[512,256]{1,0:T(8,128)(2,1)S(1)} collective-permute-done((bf16[512,256]{1,0:T(8,128)(2,1)S(1)}, bf16[512,256]{1,0:T(8,128)(2,1)S(1)}, u32[]{:S(2)}, u32[]{:S(2)}) %collective-permute-start.1) | collective-permute-done | bytes 262176 | tf_op jit(solution)/shard_map/ppermute | solution.py:425
  19.1 0.1 fusion.3._.mine
  19.2 1.4 %collective-permute-start.2 = (bf16[512,256]{1,0:T(8,128)(2,1)S(1)}, bf16[512,256]{1,0:T(8,128)(2,1)S(1)}, u32[]{:S(2)}, u32[]{:S(2)}) collective-permute-start(bf16[512,256]{1,0:T(8,128)(2,1)S(1)} %fusion.3._.mine), channel_id=1, source_target_pairs={{0,16},{4,12},{8,24},{12,4},{16,0},{20,28},{24,8},{28,20},{1,17},{... | collective-permute-start | bytes 786440 | tf_op jit(solution)/shard_map/ppermute | solution.py:425
  20.5 0.6 %collective-permute-done.5.theirs = bf16[512,256]{1,0:T(8,128)(2,1)S(1)} collective-permute-done((bf16[512,256]{1,0:T(8,128)(2,1)S(1)}, bf16[512,256]{1,0:T(8,128)(2,1)S(1)}, u32[]{:S(2)}, u32[]{:S(2)}) %collective-permute-start.5) | collective-permute-done | bytes 262176 | tf_op jit(solution)/shard_map/ppermute | solution.py:425
  21.1 1.2 %own_first.1 = (bf16[512,256]{1,0:T(8,128)(2,1)S(1)}, f32[512,256]{1,0:T(8,128)S(1)}, f32[1,128]{1,0:T(1,128)S(1)}, bf16[512,256]{1,0:T(8,128)(2,1)S(1)}, f32[512,256]{1,0:T(8,128)S(1)}) custom-call(s32[1]{0:T(128)} %bitcast.me_ref, bf16[512,256]{1,0:T(8,128)(2,1)S(1)} %combined.1.mine, bf16[512,256]{1,0:T(8,128)(2,1)S(1)} %collective-permute-done.5.theirs, ...), custom_call_target="tpu_custom_call" | custom-call | flops 1024 | bytes 1024 | tf_op jit(solution)/shard_map/own_first/pallas_call | solution.py:208
  22.3 2.1 %collective-permute-start.12 = (bf16[512,256]{1,0:T(8,128)(2,1)S(1)}, bf16[512,256]{1,0:T(8,128)(2,1)S(1)}, u32[]{:S(2)}, u32[]{:S(2)}) collective-permute-start(bf16[512,256]{1,0:T(8,128)(2,1)S(1)} %get-tuple-element.28), channel_id=1, source_target_pairs={{0,8},{4,20},{8,0},{12,28},{16,24},{20,4},{24,16},{28,12},{1,9},{5... | collective-permute-start | bytes 786440 | tf_op jit(solution)/shard_map/ppermute | solution.py:425
  24.4 1.2 %collective-permute-done.2.theirs = bf16[512,256]{1,0:T(8,128)(2,1)S(1)} collective-permute-done((bf16[512,256]{1,0:T(8,128)(2,1)S(1)}, bf16[512,256]{1,0:T(8,128)(2,1)S(1)}, u32[]{:S(2)}, u32[]{:S(2)}) %collective-permute-start.2) | collective-permute-done | bytes 262176 | tf_op jit(solution)/shard_map/ppermute | solution.py:425
  25.6 0.6 %own_second.1 = (bf16[512,256]{1,0:T(8,128)(2,1)S(1)}, f32[1,8,128]{2,1,0:T(8,128)S(1)}, f32[512,256]{1,0:T(8,128)S(1)}) custom-call(s32[1]{0:T(128)} %bitcast.me_ref, bf16[512,256]{1,0:T(8,128)(2,1)S(1)} %fusion.3._.mine, bf16[512,256]{1,0:T(8,128)(2,1)S(1)} %collective-permute-done.2.theirs, bf16[2,512,1024]{2,1,0:T(8,128)(2,1)S(1)} %copy-done, ...), custom_call_target="tpu_custom_call" | custom-call | flops 1024 | bytes 1024 | tf_op jit(solution)/shard_map/own_second/pallas_call | solution.py:246
  26.2 1.4 %collective-permute-start.7 = (f32[1,8,128]{2,1,0:T(8,128)S(1)}, f32[1,8,128]{2,1,0:T(8,128)S(1)}, u32[]{:S(2)}, u32[]{:S(2)}) collective-permute-start(f32[1,8,128]{2,1,0:T(8,128)S(1)} %get-tuple-element.25), channel_id=1, source_target_pairs={{0,1},{1,0},{2,3},{3,2},{4,5},{5,4},{6,7},{7,6},{8,9},{9,8},{10,11... | collective-permute-start | bytes 12296 | tf_op jit(solution)/shard_map/ppermute | solution.py:443
  27.7 1.2 %collective-permute-start.6 = (bf16[512,256]{1,0:T(8,128)(2,1)S(1)}, bf16[512,256]{1,0:T(8,128)(2,1)S(1)}, u32[]{:S(2)}, u32[]{:S(2)}) collective-permute-start(bf16[512,256]{1,0:T(8,128)(2,1)S(1)} %get-tuple-element.24), channel_id=1, source_target_pairs={{0,8},{4,20},{8,0},{12,28},{16,24},{20,4},{24,16},{28,12},{1,9},{5... | collective-permute-start | bytes 786440 | tf_op jit(solution)/shard_map/ppermute | solution.py:425
  28.9 1.0 %collective-permute-done.7 = f32[1,8,128]{2,1,0:T(8,128)S(1)} collective-permute-done((f32[1,8,128]{2,1,0:T(8,128)S(1)}, f32[1,8,128]{2,1,0:T(8,128)S(1)}, u32[]{:S(2)}, u32[]{:S(2)}) %collective-permute-start.7) | collective-permute-done | bytes 4128 | tf_op jit(solution)/shard_map/ppermute | solution.py:443
  29.9 2.4 %collective-permute-start.8 = (f32[2,8,128]{2,1,0:T(8,128)S(1)}, f32[2,8,128]{2,1,0:T(8,128)S(1)}, u32[]{:S(2)}, u32[]{:S(2)}) collective-permute-start(f32[2,8,128]{2,1,0:T(8,128)S(1)} %get-tuple-element.34.refs_0_), channel_id=1, source_target_pairs={{0,2},{1,3},{2,0},{3,1},{4,6},{5,7},{6,4},{7,5},{8,10},{9,11},{10,... | collective-permute-start | bytes 24584 | tf_op jit(solution)/shard_map/ppermute | solution.py:443
  32.3 0.5 %finish_other.1 = (bf16[512,256]{1,0:T(8,128)(2,1)S(1)}, f32[512,256]{1,0:T(8,128)S(1)}) custom-call(s32[1]{0:T(128)} %bitcast.me_ref, bf16[512,256]{1,0:T(8,128)(2,1)S(1)} %collective-permute-done.11.piece, bf16[2,512,1024]{2,1,0:T(8,128)(2,1)S(1)} %copy-done, bf16[512,1024]{1,0:T(8,128)(2,1)S(1)} %copy-done.1, f32[32,1024]{1,0:T(8,128)S(1)} %copy-done.2), custom_call_target="tpu_custom_call" | custom-call | flops 1024 | bytes 1024 | tf_op jit(solution)/shard_map/finish_other/pallas_call | solution.py:265
  32.8 0.6 %collective-permute-start.13 = (bf16[512,256]{1,0:T(8,128)(2,1)S(1)}, bf16[512,256]{1,0:T(8,128)(2,1)S(1)}, u32[]{:S(2)}, u32[]{:S(2)}) collective-permute-start(bf16[512,256]{1,0:T(8,128)(2,1)S(1)} %ordered.3.refs_0_), channel_id=1, source_target_pairs={{0,4},{4,0},{8,12},{12,8},{16,20},{20,16},{24,28},{28,24},{1,5},{5... | collective-permute-start | bytes 786440 | tf_op jit(solution)/shard_map/ppermute | solution.py:425
  33.4 1.1 %collective-permute-done.8 = f32[2,8,128]{2,1,0:T(8,128)S(1)} collective-permute-done((f32[2,8,128]{2,1,0:T(8,128)S(1)}, f32[2,8,128]{2,1,0:T(8,128)S(1)}, u32[]{:S(2)}, u32[]{:S(2)}) %collective-permute-start.8) | collective-permute-done | bytes 8224 | tf_op jit(solution)/shard_map/ppermute | solution.py:443
  34.5 0.1 collective-permute-start.9
  34.6 1.1 %collective-permute-start.16 = (f32[4,8,128]{2,1,0:T(8,128)S(1)}, f32[4,8,128]{2,1,0:T(8,128)S(1)}, u32[]{:S(2)}, u32[]{:S(2)}) collective-permute-start(f32[4,8,128]{2,1,0:T(8,128)S(1)} %constant_dynamic-update-slice_fusion.2.refs_0_), channel_id=1, source_target_pairs={{20,0},{8,4},{28,8},{0,12},{4,16},{24,20},{12,24},{16,28},{21,1},{... | collective-permute-start | bytes 49160 | tf_op jit(solution)/shard_map/ppermute | solution.py:440
  35.7 1.0 %collective-permute-start.15 = (f32[4,8,128]{2,1,0:T(8,128)S(1)}, f32[4,8,128]{2,1,0:T(8,128)S(1)}, u32[]{:S(2)}, u32[]{:S(2)}) collective-permute-start(f32[4,8,128]{2,1,0:T(8,128)S(1)} %constant_dynamic-update-slice_fusion.2.refs_0_), channel_id=1, source_target_pairs={{0,8},{4,20},{8,0},{12,28},{16,24},{20,4},{24,16},{28,12},{1,9},{5... | collective-permute-start | bytes 49160 | tf_op jit(solution)/shard_map/ppermute | solution.py:425
  36.7 0.4 %memory_terms.1.refs_5_.refs_2_ = f32[2,512,256]{2,1,0:T(8,128)S(1)} custom-call(bf16[512,256]{1,0:T(8,128)(2,1)S(1)} %ordered.2.refs_0_, bf16[512,256]{1,0:T(8,128)(2,1)S(1)} %collective-permute-done.10.refs_1_, bf16[2,512,1024]{2,1,0:T(8,128)(2,1)S(1)} %copy-done), custom_call_target="tpu_custom_call" | custom-call | flops 1024 | bytes 1024 | tf_op jit(solution)/shard_map/memory_terms/pallas_call | solution.py:319
  37.2 1.6 %finish_first.1 = (bf16[1024,1024]{1,0:T(8,128)(2,1)}, f32[2,512,256]{2,1,0:T(8,128)S(1)}) custom-call(s32[1]{0:T(128)} %bitcast.me_ref, bf16[512,256]{1,0:T(8,128)(2,1)S(1)} %ordered.3.refs_0_, bf16[512,256]{1,0:T(8,128)(2,1)S(1)} %collective-permute-done.13.refs_1_, bf16[512,256]{1,0:T(8,128)(2,1)S(1)} %get-tuple-element.30.refs_2_, ...), custom_call_target="tpu_custom_call" | custom-call | flops 1024 | bytes 1024 | tf_op jit(solution)/shard_map/finish_first/pallas_call | solution.py:300
  38.8 0.6 %collective-permute-done.15.refs_2_ = f32[4,8,128]{2,1,0:T(8,128)S(1)} collective-permute-done((f32[4,8,128]{2,1,0:T(8,128)S(1)}, f32[4,8,128]{2,1,0:T(8,128)S(1)}, u32[]{:S(2)}, u32[]{:S(2)}) %collective-permute-start.15) | collective-permute-done | bytes 16416 | tf_op jit(solution)/shard_map/ppermute | solution.py:425
  39.4 2.5 %finish_second.1 = (bf16[1024,1024]{1,0:T(8,128)(2,1)}, bf16[1024,1024]{1,0:T(8,128)(2,1)}) custom-call(s32[1]{0:T(128)} %bitcast.me_ref, bf16[512,256]{1,0:T(8,128)(2,1)S(1)} %collective-permute-done.9.refs_0_, f32[512,256]{1,0:T(8,128)S(1)} %get-tuple-element.26.refs_1_, ...), custom_call_target="tpu_custom_call", output_to_operand_aliasing={{0}: (10, {})} | custom-call | flops 1024 | bytes 1024 | tf_op jit(solution)/shard_map/finish_second/pallas_call | solution.py:400
  (27 shorter events, 0.4 us)
Async XLA Ops:
  5.1 2.1 %collective-permute-start.3 = (bf16[2,512,256]{2,1,0:T(8,128)(2,1)S(1)}, bf16[2,512,256]{2,1,0:T(8,128)(2,1)S(1)}, u32[]{:S(2)}, u32[]{:S(2)}) collective-permute-start(bf16[2,512,256]{2,1,0:T(8,128)(2,1)S(1)} %get-tuple-element.21), channel_id=1, source_target_pairs={{0,4},{4,0},{8,12},{12,8},{16,20},{20,16},{24,28},{28,24},{1,5},{5... | collective-permute-start | bytes 1572872 | tf_op jit(solution)/shard_map/ppermute | solution.py:425
  7.0 3.2 %collective-permute-start = (bf16[2,512,256]{2,1,0:T(8,128)(2,1)S(1)}, bf16[2,512,256]{2,1,0:T(8,128)(2,1)S(1)}, u32[]{:S(2)}, u32[]{:S(2)}) collective-permute-start(bf16[2,512,256]{2,1,0:T(8,128)(2,1)S(1)} %memory_product.2), channel_id=1, source_target_pairs={{0,4},{4,0},{8,12},{12,8},{16,20},{20,16},{24,28},{28,24},{1,5},{5... | collective-permute-start | bytes 1572872 | tf_op jit(solution)/shard_map/ppermute | solution.py:425
  7.3 7.2 %collective-permute-start.4 = (bf16[512,256]{1,0:T(8,128)(2,1)S(1)}, bf16[512,256]{1,0:T(8,128)(2,1)S(1)}, u32[]{:S(2)}, u32[]{:S(2)}) collective-permute-start(bf16[512,256]{1,0:T(8,128)(2,1)S(1)} %fusion.4), channel_id=1, source_target_pairs={{0,8},{4,20},{8,0},{12,28},{16,24},{20,4},{24,16},{28,12},{1,9},{5... | collective-permute-start | bytes 786440 | tf_op jit(solution)/shard_map/ppermute | solution.py:425
  11.5 9.6 %copy-start = (bf16[2,512,1024]{2,1,0:T(8,128)(2,1)S(1)}, bf16[2,512,1024]{2,1,0:T(8,128)(2,1)}, u32[]{:S(2)}) copy-start(bf16[2,512,1024]{2,1,0:T(8,128)(2,1)} %refs_3_.1) | copy-start | bytes 6291460
  11.5 9.6 %copy-start.1 = (bf16[512,1024]{1,0:T(8,128)(2,1)S(1)}, bf16[512,1024]{1,0:T(8,128)(2,1)}, u32[]{:S(2)}) copy-start(bf16[512,1024]{1,0:T(8,128)(2,1)} %refs_5_.1) | copy-start | bytes 3145732
  11.5 9.6 %copy-start.2 = (f32[32,1024]{1,0:T(8,128)S(1)}, f32[32,1024]{1,0:T(8,128)}, u32[]{:S(2)}) copy-start(f32[32,1024]{1,0:T(8,128)} %refs_8_.1) | copy-start | bytes 393220
  11.6 7.5 %collective-permute-start.1 = (bf16[512,256]{1,0:T(8,128)(2,1)S(1)}, bf16[512,256]{1,0:T(8,128)(2,1)S(1)}, u32[]{:S(2)}, u32[]{:S(2)}) collective-permute-start(bf16[512,256]{1,0:T(8,128)(2,1)S(1)} %fusion.5._), channel_id=1, source_target_pairs={{0,8},{4,20},{8,0},{12,28},{16,24},{20,4},{24,16},{28,12},{1,9},{5... | collective-permute-start | bytes 786440 | tf_op jit(solution)/shard_map/ppermute | solution.py:425
  14.6 6.5 %collective-permute-start.5 = (bf16[512,256]{1,0:T(8,128)(2,1)S(1)}, bf16[512,256]{1,0:T(8,128)(2,1)S(1)}, u32[]{:S(2)}, u32[]{:S(2)}) collective-permute-start(bf16[512,256]{1,0:T(8,128)(2,1)S(1)} %combined.1.mine), channel_id=1, source_target_pairs={{0,16},{4,12},{8,24},{12,4},{16,0},{20,28},{24,8},{28,20},{1,17},{... | collective-permute-start | bytes 786440 | tf_op jit(solution)/shard_map/ppermute | solution.py:425
  19.2 6.4 %collective-permute-start.2 = (bf16[512,256]{1,0:T(8,128)(2,1)S(1)}, bf16[512,256]{1,0:T(8,128)(2,1)S(1)}, u32[]{:S(2)}, u32[]{:S(2)}) collective-permute-start(bf16[512,256]{1,0:T(8,128)(2,1)S(1)} %fusion.3._.mine), channel_id=1, source_target_pairs={{0,16},{4,12},{8,24},{12,4},{16,0},{20,28},{24,8},{28,20},{1,17},{... | collective-permute-start | bytes 786440 | tf_op jit(solution)/shard_map/ppermute | solution.py:425
  22.3 10.0 %collective-permute-start.11 = (bf16[512,256]{1,0:T(8,128)(2,1)S(1)}, bf16[512,256]{1,0:T(8,128)(2,1)S(1)}, u32[]{:S(2)}, u32[]{:S(2)}) collective-permute-start(bf16[512,256]{1,0:T(8,128)(2,1)S(1)} %get-tuple-element.28), channel_id=1, source_target_pairs={{0,4},{4,0},{8,12},{12,8},{16,20},{20,16},{24,28},{28,24},{1,5},{5... | collective-permute-start | bytes 786440 | tf_op jit(solution)/shard_map/ppermute | solution.py:425
  22.3 10.4 %collective-permute-start.12 = (bf16[512,256]{1,0:T(8,128)(2,1)S(1)}, bf16[512,256]{1,0:T(8,128)(2,1)S(1)}, u32[]{:S(2)}, u32[]{:S(2)}) collective-permute-start(bf16[512,256]{1,0:T(8,128)(2,1)S(1)} %get-tuple-element.28), channel_id=1, source_target_pairs={{0,8},{4,20},{8,0},{12,28},{16,24},{20,4},{24,16},{28,12},{1,9},{5... | collective-permute-start | bytes 786440 | tf_op jit(solution)/shard_map/ppermute | solution.py:425
  26.2 3.7 %collective-permute-start.7 = (f32[1,8,128]{2,1,0:T(8,128)S(1)}, f32[1,8,128]{2,1,0:T(8,128)S(1)}, u32[]{:S(2)}, u32[]{:S(2)}) collective-permute-start(f32[1,8,128]{2,1,0:T(8,128)S(1)} %get-tuple-element.25), channel_id=1, source_target_pairs={{0,1},{1,0},{2,3},{3,2},{4,5},{5,4},{6,7},{7,6},{8,9},{9,8},{10,11... | collective-permute-start | bytes 12296 | tf_op jit(solution)/shard_map/ppermute | solution.py:443
  27.7 6.8 %collective-permute-start.6 = (bf16[512,256]{1,0:T(8,128)(2,1)S(1)}, bf16[512,256]{1,0:T(8,128)(2,1)S(1)}, u32[]{:S(2)}, u32[]{:S(2)}) collective-permute-start(bf16[512,256]{1,0:T(8,128)(2,1)S(1)} %get-tuple-element.24), channel_id=1, source_target_pairs={{0,8},{4,20},{8,0},{12,28},{16,24},{20,4},{24,16},{28,12},{1,9},{5... | collective-permute-start | bytes 786440 | tf_op jit(solution)/shard_map/ppermute | solution.py:425
  29.9 4.5 %collective-permute-start.8 = (f32[2,8,128]{2,1,0:T(8,128)S(1)}, f32[2,8,128]{2,1,0:T(8,128)S(1)}, u32[]{:S(2)}, u32[]{:S(2)}) collective-permute-start(f32[2,8,128]{2,1,0:T(8,128)S(1)} %get-tuple-element.34.refs_0_), channel_id=1, source_target_pairs={{0,2},{1,3},{2,0},{3,1},{4,6},{5,7},{6,4},{7,5},{8,10},{9,11},{10,... | collective-permute-start | bytes 24584 | tf_op jit(solution)/shard_map/ppermute | solution.py:443
  32.3 4.4 %collective-permute-start.10 = (bf16[512,256]{1,0:T(8,128)(2,1)S(1)}, bf16[512,256]{1,0:T(8,128)(2,1)S(1)}, u32[]{:S(2)}, u32[]{:S(2)}) collective-permute-start(bf16[512,256]{1,0:T(8,128)(2,1)S(1)} %get-tuple-element.24), channel_id=1, source_target_pairs={{0,4},{4,0},{8,12},{12,8},{16,20},{20,16},{24,28},{28,24},{1,5},{5... | collective-permute-start | bytes 786440 | tf_op jit(solution)/shard_map/ppermute | solution.py:425
  32.8 4.4 %collective-permute-start.13 = (bf16[512,256]{1,0:T(8,128)(2,1)S(1)}, bf16[512,256]{1,0:T(8,128)(2,1)S(1)}, u32[]{:S(2)}, u32[]{:S(2)}) collective-permute-start(bf16[512,256]{1,0:T(8,128)(2,1)S(1)} %ordered.3.refs_0_), channel_id=1, source_target_pairs={{0,4},{4,0},{8,12},{12,8},{16,20},{20,16},{24,28},{28,24},{1,5},{5... | collective-permute-start | bytes 786440 | tf_op jit(solution)/shard_map/ppermute | solution.py:425
  34.5 4.9 %collective-permute-start.9 = (bf16[512,256]{1,0:T(8,128)(2,1)S(1)}, bf16[512,256]{1,0:T(8,128)(2,1)S(1)}, u32[]{:S(2)}, u32[]{:S(2)}) collective-permute-start(bf16[512,256]{1,0:T(8,128)(2,1)S(1)} %ordered.2.refs_0_), channel_id=1, source_target_pairs={{0,4},{4,0},{8,12},{12,8},{16,20},{20,16},{24,28},{28,24},{1,5},{5... | collective-permute-start | bytes 786440 | tf_op jit(solution)/shard_map/ppermute | solution.py:425
  34.6 4.2 %collective-permute-start.16 = (f32[4,8,128]{2,1,0:T(8,128)S(1)}, f32[4,8,128]{2,1,0:T(8,128)S(1)}, u32[]{:S(2)}, u32[]{:S(2)}) collective-permute-start(f32[4,8,128]{2,1,0:T(8,128)S(1)} %constant_dynamic-update-slice_fusion.2.refs_0_), channel_id=1, source_target_pairs={{20,0},{8,4},{28,8},{0,12},{4,16},{24,20},{12,24},{16,28},{21,1},{... | collective-permute-start | bytes 49160 | tf_op jit(solution)/shard_map/ppermute | solution.py:440
  35.7 3.7 %collective-permute-start.15 = (f32[4,8,128]{2,1,0:T(8,128)S(1)}, f32[4,8,128]{2,1,0:T(8,128)S(1)}, u32[]{:S(2)}, u32[]{:S(2)}) collective-permute-start(f32[4,8,128]{2,1,0:T(8,128)S(1)} %constant_dynamic-update-slice_fusion.2.refs_0_), channel_id=1, source_target_pairs={{0,8},{4,20},{8,0},{12,28},{16,24},{20,4},{24,16},{28,12},{1,9},{5... | collective-permute-start | bytes 49160 | tf_op jit(solution)/shard_map/ppermute | solution.py:425
  36.7 2.7 %collective-permute-start.14 = (f32[4,8,128]{2,1,0:T(8,128)S(1)}, f32[4,8,128]{2,1,0:T(8,128)S(1)}, u32[]{:S(2)}, u32[]{:S(2)}) collective-permute-start(f32[4,8,128]{2,1,0:T(8,128)S(1)} %constant_dynamic-update-slice_fusion.2.refs_0_), channel_id=1, source_target_pairs={{0,4},{4,0},{8,12},{12,8},{16,20},{20,16},{24,28},{28,24},{1,5},{5... | collective-permute-start | bytes 49160 | tf_op jit(solution)/shard_map/ppermute | solution.py:425

commit v18 on v17

--- a/solution.py
+++ b/solution.py
@@ -68,11 +68,14 @@
 def first_products(me, sigma_hist, g_hist, rows, bits):
     depth, columns = g_hist.shape
     half = columns // 2
+    tall = sigma_hist.shape[0]
     parts = 4
     eighth = depth // 8
     chunks = [(0, 2 * eighth), (2 * eighth, 3 * eighth), (5 * eighth, 3 * eighth)]
 
-    def kernel(me_ref, sigma_ref, g_ref, sent, kept, sigma_next, g, sigma, total, sems):
+    def kernel(me_ref, sigma_ref, g_ref, sent_0, sent_1, sigma, g_kept, g_sent, total, sems):
+        place = Place(me_ref[0], bits)
+        sent_at, kept_at = half_of(place.core ^ 1, half), half_of(place.core, half)
         started = []
 
         def load(source, target):
@@ -84,29 +87,29 @@
         for start, size in chunks:
             piece = []
             for i in range(parts):
-                here = pl.ds(i * (rows // parts), rows // parts)
+                here = pl.ds(i * (tall // parts), tall // parts)
                 deep = pl.ds(start, size)
                 piece.append(load(sigma_ref.at[here, deep], sigma.at[here, deep]))
                 here = pl.ds(start + i * (size // parts), size // parts)
-                piece.append(load(g_ref.at[here, :], g.at[here, :]))
+                piece.append(load(g_ref.at[here, sent_at], g_sent.at[here, :]))
             pieces.append(piece)
         ahead = []
         for i in range(2 * parts):
-            here = pl.ds(i * (rows // (2 * parts)), rows // (2 * parts))
-            there = pl.ds(rows + i * (rows // (2 * parts)), rows // (2 * parts))
-            ahead.append(load(sigma_ref.at[there, :], sigma_next.at[here, :]))
+            here = pl.ds(i * (depth // (2 * parts)), depth // (2 * parts))
+            ahead.append(load(g_ref.at[here, kept_at], g_kept.at[here, :]))
         for k, (start, size) in enumerate(chunks):
             for copy in pieces[k]:
                 copy.wait()
             deep = pl.ds(start, size)
-            term = jnp.dot(sigma[:, deep], g[deep, :], preferred_element_type=F32)
+            term = jnp.dot(sigma[:, deep], g_sent[deep, :], preferred_element_type=F32)
             if k == 0:
                 total[...] = term
+            elif k < len(chunks) - 1:
+                total[...] += term
             else:
-                total[...] += term
-        place = Place(me_ref[0], bits)
-        halves_to(sent, total[:, half_of(place.core ^ 1, half)], place.other_side)
-        halves_to(kept, total[:, half_of(place.core, half)], place.side)
+                term += total[...]
+                halves_to(sent_0, term[:rows], place.other_side)
+                halves_to(sent_1, term[rows:], place.other_side)
         for copy in ahead:
             copy.wait()
 
@@ -115,15 +118,10 @@
         "first_products",
         in_specs=[SCALAR, HBM, HBM],
         out_specs=[WHOLE] * 4,
-        out_shape=[
-            near((2, rows, half // 2), BF16),
-            near((2, rows, half // 2), F32),
-            near((rows, depth), BF16),
-            near((depth, columns), BF16),
-        ],
+        out_shape=[near((2, rows, half // 2), BF16)] * 2 + [near((tall, depth), BF16), near((depth, half), BF16)],
         scratch_shapes=[
-            pltpu.VMEM((rows, depth), BF16),
-            pltpu.VMEM((rows, columns), F32),
+            pltpu.VMEM((depth, half), BF16),
+            pltpu.VMEM((tall, half), F32),
             pltpu.SemaphoreType.DMA((2 * parts * (len(chunks) + 1),)),
         ],
     )(me, far(sigma_hist), far(g_hist))
@@ -133,14 +131,12 @@
     return pl.ds(pl.multiple_of(core * half, half), half)
 
 
-def product(me, sigma, g, bits, send, after=None):
-    rows, half = sigma.shape[0], g.shape[1] // 2
+def product(me, sigma, g, block, rows, bits, after=None):
+    half = g.shape[1]
 
     def kernel(me_ref, sigma, g, *refs):
-        place = Place(me_ref[0], bits)
-        columns = half_of(place.core ^ int(send), half)
-        term = jnp.dot(sigma[...], g[:, columns], preferred_element_type=F32)
-        halves_to(refs[-1], term, place.other_side if send else place.side)
+        term = jnp.dot(sigma[block * rows : (block + 1) * rows], g[...], preferred_element_type=F32)
+        halves_to(refs[-1], term, Place(me_ref[0], bits).side)
 
     extra = [] if after is None else [after]
     return call(
@@ -148,7 +144,7 @@
         "memory_product",
         in_specs=[SCALAR, WHOLE, WHOLE] + [FAR] * len(extra),
         out_specs=WHOLE,
-        out_shape=near((2, rows, half // 2), BF16 if send else F32),
+        out_shape=near((2, rows, half // 2), F32),
     )(me, sigma, g, *extra)
 
 
@@ -442,11 +438,11 @@
     def widened(share, level):
         return lax.ppermute(share, "second", [(z, z ^ (1 << level)) for z in range(second)])
 
-    send, kept_0, sigma_1, g_near = first_products(me, sigma_hist, g_hist, rows, bits)
-    arrived_0 = swap(send, 0)
-    arrived_1 = swap(product(me, sigma_1, g_near, bits, True), 0)
+    send_0, send_1, sigma, g_kept = first_products(me, sigma_hist, g_hist, rows, bits)
+    arrived_0, arrived_1 = swap(send_0, 0), swap(send_1, 0)
+    kept_0 = product(me, sigma, g_kept, 0, rows, bits)
     sent_0 = passed_on(kept_0, arrived_0)
-    kept_1 = product(me, sigma_1, g_near, bits, False, after=arrived_1)
+    kept_1 = product(me, sigma, g_kept, 1, rows, bits, after=arrived_1)
     sent_1 = passed_on(kept_1, arrived_1)
 
     mine, theirs = exchanged(kept_0, arrived_0, sent_0, after=sent_1)

time: 42.1 us -> 41.9 us (level)
  waiting for transfers between devices: 8.6 us -> 9.34 us
  starting transfers between devices: 18.3 us -> 17.6 us
    ppermute x14, waiting for transfers between devices: 6.45 us -> 7.21 us  [swap(): return lax.ppermute(x, 'past', pairs)]
    ppermute x14, starting transfers between devices: 13.4 us -> 12.7 us  [swap(): return lax.ppermute(x, 'past', pairs)]
where the time goes in v18:
time: 41.9 us; the launch traced here: 41.8 us
  starting transfers between devices  17.6 us (42%)
  Pallas kernels  13.8 us (33%)
  waiting for transfers between devices  9.34 us (22%)
  between operations  0.81 us (2%)
    ppermute x14, starting transfers between devices, swap(): return lax.ppermute(x, 'past', pairs)  12.7 us
    ppermute x14, waiting for transfers between devices, swap(): return lax.ppermute(x, 'past', pairs)  7.21 us
    pallas_call x1, Pallas kernels, first_products(): call(kernel, 'first_products', in_specs=[SCALAR, HBM, HBM], out_specs=[WH...  4.31 us
    ppermute x2, starting transfers between devices, widened(): lax.ppermute(share, 'second', [(z, z ^ 1 << level) for z in range(second)])  3.8 us
    pallas_call x2, Pallas kernels, product(): call(kernel, 'memory_product', in_specs=[SCALAR, WHOLE, WHOLE] + [FAR] *...  2.55 us
    pallas_call x1, Pallas kernels, finish_second(): call(kernel, 'finish_second', in_specs=[SCALAR] + [WHOLE] * 9 + [HBM], ou...  2.51 us
    ppermute x2, waiting for transfers between devices, widened(): lax.ppermute(share, 'second', [(z, z ^ 1 << level) for z in range(second)])  2.12 us
    pallas_call x1, Pallas kernels, finish_first(): call(kernel, 'finish_first', in_specs=[SCALAR] + [WHOLE] * 7, out_specs=[...  1.6 us
  transfers between devices with their start and end apart: 17, of which 8 were waited for; matrix products, arithmetic and copies ran while one was open for 0% of the time, Pallas kernels for 17%

profile of v18, /device:TPU:0, one launch (start us, length us, event | category | flops | bytes accessed | tf_op | source)
XLA Modules:
  0.0 41.8 jit_solution(16830859644436760655)
XLA Ops:
  0.6 4.3 %first_products.1 = (bf16[2,512,256]{2,1,0:T(8,128)(2,1)S(1)}, bf16[2,512,256]{2,1,0:T(8,128)(2,1)S(1)}, bf16[1024,2048]{1,0:T(8,128)(2,1)S(1)}, bf16[2048,512]{1,0:T(8,128)(2,1)S(1)}) custom-call(s32[1]{0:T(128)} %bitcast.me_ref, bf16[1024,2048]{1,0:T(8,128)(2,1)} %sigma_ref.1, bf16[2048,1024]{1,0:T(8,128)(2,1)} %g_ref.1), custom_call_target="tpu_custom_call" | custom-call | flops 1024 | bytes 1024 | tf_op jit(solution)/shard_map/first_products/pallas_call | solution.py:116
  4.9 0.5 %collective-permute-start.3 = (bf16[2,512,256]{2,1,0:T(8,128)(2,1)S(1)}, bf16[2,512,256]{2,1,0:T(8,128)(2,1)S(1)}, u32[]{:S(2)}, u32[]{:S(2)}) collective-permute-start(bf16[2,512,256]{2,1,0:T(8,128)(2,1)S(1)} %get-tuple-element.21), channel_id=1, source_target_pairs={{0,4},{4,0},{8,12},{12,8},{16,20},{20,16},{24,28},{28,24},{1,5},{5... | collective-permute-start | bytes 1572872 | tf_op jit(solution)/shard_map/ppermute | solution.py:421
  5.4 0.1 collective-permute-start
  5.5 1.3 %memory_product.3.kept = f32[2,512,256]{2,1,0:T(8,128)S(1)} custom-call(s32[1]{0:T(128)} %bitcast.me_ref, bf16[1024,2048]{1,0:T(8,128)(2,1)S(1)} %get-tuple-element.18.sigma, bf16[2048,512]{1,0:T(8,128)(2,1)S(1)} %get-tuple-element.19.g), custom_call_target="tpu_custom_call" | custom-call | flops 1024 | bytes 1024 | tf_op jit(solution)/shard_map/memory_product/pallas_call | solution.py:142
  6.8 0.2 collective-permute-done.3.arrived
  7.0 3.0 %collective-permute-start.4 = (bf16[512,256]{1,0:T(8,128)(2,1)S(1)}, bf16[512,256]{1,0:T(8,128)(2,1)S(1)}, u32[]{:S(2)}, u32[]{:S(2)}) collective-permute-start(bf16[512,256]{1,0:T(8,128)(2,1)S(1)} %fusion.6), channel_id=1, source_target_pairs={{0,8},{4,20},{8,0},{12,28},{16,24},{20,4},{24,16},{28,12},{1,9},{5... | collective-permute-start | bytes 786440 | tf_op jit(solution)/shard_map/ppermute | solution.py:421
  10.0 1.3 %memory_product.2 = f32[2,512,256]{2,1,0:T(8,128)S(1)} custom-call(s32[1]{0:T(128)} %bitcast.me_ref, bf16[1024,2048]{1,0:T(8,128)(2,1)S(1)} %get-tuple-element.18.sigma, bf16[2048,512]{1,0:T(8,128)(2,1)S(1)} %get-tuple-element.19.g, bf16[2,512,256]{2,1,0:T(8,128)(2,1)S(1)} %collective-permute-done.refs_0_), custom_call_target="tpu_custom_call" | custom-call | flops 1024 | bytes 1024 | tf_op jit(solution)/shard_map/memory_product/pallas_call | solution.py:142
  11.4 0.7 %collective-permute-start.1 = (bf16[512,256]{1,0:T(8,128)(2,1)S(1)}, bf16[512,256]{1,0:T(8,128)(2,1)S(1)}, u32[]{:S(2)}, u32[]{:S(2)}) collective-permute-start(bf16[512,256]{1,0:T(8,128)(2,1)S(1)} %fusion.5._), channel_id=1, source_target_pairs={{0,8},{4,20},{8,0},{12,28},{16,24},{20,4},{24,16},{28,12},{1,9},{5... | collective-permute-start | bytes 786440 | tf_op jit(solution)/shard_map/ppermute | solution.py:421
  12.1 2.3 %collective-permute-done.4.more = bf16[512,256]{1,0:T(8,128)(2,1)S(1)} collective-permute-done((bf16[512,256]{1,0:T(8,128)(2,1)S(1)}, bf16[512,256]{1,0:T(8,128)(2,1)S(1)}, u32[]{:S(2)}, u32[]{:S(2)}) %collective-permute-start.4) | collective-permute-done | bytes 262176 | tf_op jit(solution)/shard_map/ppermute | solution.py:421
  14.3 0.1 combined.1.mine
  14.4 2.1 %collective-permute-start.5 = (bf16[512,256]{1,0:T(8,128)(2,1)S(1)}, bf16[512,256]{1,0:T(8,128)(2,1)S(1)}, u32[]{:S(2)}, u32[]{:S(2)}) collective-permute-start(bf16[512,256]{1,0:T(8,128)(2,1)S(1)} %combined.1.mine), channel_id=1, source_target_pairs={{0,16},{4,12},{8,24},{12,4},{16,0},{20,28},{24,8},{28,20},{1,17},{... | collective-permute-start | bytes 786440 | tf_op jit(solution)/shard_map/ppermute | solution.py:421
  16.5 2.4 %collective-permute-done.1 = bf16[512,256]{1,0:T(8,128)(2,1)S(1)} collective-permute-done((bf16[512,256]{1,0:T(8,128)(2,1)S(1)}, bf16[512,256]{1,0:T(8,128)(2,1)S(1)}, u32[]{:S(2)}, u32[]{:S(2)}) %collective-permute-start.1) | collective-permute-done | bytes 262176 | tf_op jit(solution)/shard_map/ppermute | solution.py:421
  18.9 0.1 fusion.4._.mine
  19.0 1.4 %collective-permute-start.2 = (bf16[512,256]{1,0:T(8,128)(2,1)S(1)}, bf16[512,256]{1,0:T(8,128)(2,1)S(1)}, u32[]{:S(2)}, u32[]{:S(2)}) collective-permute-start(bf16[512,256]{1,0:T(8,128)(2,1)S(1)} %fusion.4._.mine), channel_id=1, source_target_pairs={{0,16},{4,12},{8,24},{12,4},{16,0},{20,28},{24,8},{28,20},{1,17},{... | collective-permute-start | bytes 786440 | tf_op jit(solution)/shard_map/ppermute | solution.py:421
  20.3 0.6 %collective-permute-done.5.theirs = bf16[512,256]{1,0:T(8,128)(2,1)S(1)} collective-permute-done((bf16[512,256]{1,0:T(8,128)(2,1)S(1)}, bf16[512,256]{1,0:T(8,128)(2,1)S(1)}, u32[]{:S(2)}, u32[]{:S(2)}) %collective-permute-start.5) | collective-permute-done | bytes 262176 | tf_op jit(solution)/shard_map/ppermute | solution.py:421
  20.9 1.2 %own_first.1 = (bf16[512,256]{1,0:T(8,128)(2,1)S(1)}, f32[512,256]{1,0:T(8,128)S(1)}, f32[1,128]{1,0:T(1,128)S(1)}, bf16[512,256]{1,0:T(8,128)(2,1)S(1)}, f32[512,256]{1,0:T(8,128)S(1)}) custom-call(s32[1]{0:T(128)} %bitcast.me_ref, bf16[512,256]{1,0:T(8,128)(2,1)S(1)} %combined.1.mine, bf16[512,256]{1,0:T(8,128)(2,1)S(1)} %collective-permute-done.5.theirs, ...), custom_call_target="tpu_custom_call" | custom-call | flops 1024 | bytes 1024 | tf_op jit(solution)/shard_map/own_first/pallas_call | solution.py:204
  22.1 2.1 %collective-permute-start.12 = (bf16[512,256]{1,0:T(8,128)(2,1)S(1)}, bf16[512,256]{1,0:T(8,128)(2,1)S(1)}, u32[]{:S(2)}, u32[]{:S(2)}) collective-permute-start(bf16[512,256]{1,0:T(8,128)(2,1)S(1)} %get-tuple-element.28), channel_id=1, source_target_pairs={{0,8},{4,20},{8,0},{12,28},{16,24},{20,4},{24,16},{28,12},{1,9},{5... | collective-permute-start | bytes 786440 | tf_op jit(solution)/shard_map/ppermute | solution.py:421
  24.2 1.2 %collective-permute-done.2.theirs = bf16[512,256]{1,0:T(8,128)(2,1)S(1)} collective-permute-done((bf16[512,256]{1,0:T(8,128)(2,1)S(1)}, bf16[512,256]{1,0:T(8,128)(2,1)S(1)}, u32[]{:S(2)}, u32[]{:S(2)}) %collective-permute-start.2) | collective-permute-done | bytes 262176 | tf_op jit(solution)/shard_map/ppermute | solution.py:421
  25.4 0.6 %own_second.1 = (bf16[512,256]{1,0:T(8,128)(2,1)S(1)}, f32[1,8,128]{2,1,0:T(8,128)S(1)}, f32[512,256]{1,0:T(8,128)S(1)}) custom-call(s32[1]{0:T(128)} %bitcast.me_ref, bf16[512,256]{1,0:T(8,128)(2,1)S(1)} %fusion.4._.mine, bf16[512,256]{1,0:T(8,128)(2,1)S(1)} %collective-permute-done.2.theirs, bf16[2,512,1024]{2,1,0:T(8,128)(2,1)S(1)} %copy-done, ...), custom_call_target="tpu_custom_call" | custom-call | flops 1024 | bytes 1024 | tf_op jit(solution)/shard_map/own_second/pallas_call | solution.py:242
  26.1 1.4 %collective-permute-start.7 = (f32[1,8,128]{2,1,0:T(8,128)S(1)}, f32[1,8,128]{2,1,0:T(8,128)S(1)}, u32[]{:S(2)}, u32[]{:S(2)}) collective-permute-start(f32[1,8,128]{2,1,0:T(8,128)S(1)} %get-tuple-element.25), channel_id=1, source_target_pairs={{0,1},{1,0},{2,3},{3,2},{4,5},{5,4},{6,7},{7,6},{8,9},{9,8},{10,11... | collective-permute-start | bytes 12296 | tf_op jit(solution)/shard_map/ppermute | solution.py:439
  27.5 1.2 %collective-permute-start.6 = (bf16[512,256]{1,0:T(8,128)(2,1)S(1)}, bf16[512,256]{1,0:T(8,128)(2,1)S(1)}, u32[]{:S(2)}, u32[]{:S(2)}) collective-permute-start(bf16[512,256]{1,0:T(8,128)(2,1)S(1)} %get-tuple-element.24), channel_id=1, source_target_pairs={{0,8},{4,20},{8,0},{12,28},{16,24},{20,4},{24,16},{28,12},{1,9},{5... | collective-permute-start | bytes 786440 | tf_op jit(solution)/shard_map/ppermute | solution.py:421
  28.7 1.0 %collective-permute-done.7 = f32[1,8,128]{2,1,0:T(8,128)S(1)} collective-permute-done((f32[1,8,128]{2,1,0:T(8,128)S(1)}, f32[1,8,128]{2,1,0:T(8,128)S(1)}, u32[]{:S(2)}, u32[]{:S(2)}) %collective-permute-start.7) | collective-permute-done | bytes 4128 | tf_op jit(solution)/shard_map/ppermute | solution.py:439
  29.7 2.4 %collective-permute-start.8 = (f32[2,8,128]{2,1,0:T(8,128)S(1)}, f32[2,8,128]{2,1,0:T(8,128)S(1)}, u32[]{:S(2)}, u32[]{:S(2)}) collective-permute-start(f32[2,8,128]{2,1,0:T(8,128)S(1)} %get-tuple-element.34.refs_0_), channel_id=1, source_target_pairs={{0,2},{1,3},{2,0},{3,1},{4,6},{5,7},{6,4},{7,5},{8,10},{9,11},{10,... | collective-permute-start | bytes 24584 | tf_op jit(solution)/shard_map/ppermute | solution.py:439
  32.1 0.5 %finish_other.1 = (bf16[512,256]{1,0:T(8,128)(2,1)S(1)}, f32[512,256]{1,0:T(8,128)S(1)}) custom-call(s32[1]{0:T(128)} %bitcast.me_ref, bf16[512,256]{1,0:T(8,128)(2,1)S(1)} %collective-permute-done.11.piece, bf16[2,512,1024]{2,1,0:T(8,128)(2,1)S(1)} %copy-done, bf16[512,1024]{1,0:T(8,128)(2,1)S(1)} %copy-done.1, f32[32,1024]{1,0:T(8,128)S(1)} %copy-done.2), custom_call_target="tpu_custom_call" | custom-call | flops 1024 | bytes 1024 | tf_op jit(solution)/shard_map/finish_other/pallas_call | solution.py:261
  32.6 0.6 %collective-permute-start.13 = (bf16[512,256]{1,0:T(8,128)(2,1)S(1)}, bf16[512,256]{1,0:T(8,128)(2,1)S(1)}, u32[]{:S(2)}, u32[]{:S(2)}) collective-permute-start(bf16[512,256]{1,0:T(8,128)(2,1)S(1)} %ordered.3.refs_0_), channel_id=1, source_target_pairs={{0,4},{4,0},{8,12},{12,8},{16,20},{20,16},{24,28},{28,24},{1,5},{5... | collective-permute-start | bytes 786440 | tf_op jit(solution)/shard_map/ppermute | solution.py:421
  33.2 1.1 %collective-permute-done.8 = f32[2,8,128]{2,1,0:T(8,128)S(1)} collective-permute-done((f32[2,8,128]{2,1,0:T(8,128)S(1)}, f32[2,8,128]{2,1,0:T(8,128)S(1)}, u32[]{:S(2)}, u32[]{:S(2)}) %collective-permute-start.8) | collective-permute-done | bytes 8224 | tf_op jit(solution)/shard_map/ppermute | solution.py:439
  34.4 1.1 %collective-permute-start.16 = (f32[4,8,128]{2,1,0:T(8,128)S(1)}, f32[4,8,128]{2,1,0:T(8,128)S(1)}, u32[]{:S(2)}, u32[]{:S(2)}) collective-permute-start(f32[4,8,128]{2,1,0:T(8,128)S(1)} %constant_dynamic-update-slice_fusion.2.refs_0_), channel_id=1, source_target_pairs={{20,0},{8,4},{28,8},{0,12},{4,16},{24,20},{12,24},{16,28},{21,1},{... | collective-permute-start | bytes 49160 | tf_op jit(solution)/shard_map/ppermute | solution.py:436
  35.5 1.0 %collective-permute-start.15 = (f32[4,8,128]{2,1,0:T(8,128)S(1)}, f32[4,8,128]{2,1,0:T(8,128)S(1)}, u32[]{:S(2)}, u32[]{:S(2)}) collective-permute-start(f32[4,8,128]{2,1,0:T(8,128)S(1)} %constant_dynamic-update-slice_fusion.2.refs_0_), channel_id=1, source_target_pairs={{0,8},{4,20},{8,0},{12,28},{16,24},{20,4},{24,16},{28,12},{1,9},{5... | collective-permute-start | bytes 49160 | tf_op jit(solution)/shard_map/ppermute | solution.py:421
  36.5 0.4 %memory_terms.1.refs_5_.refs_2_ = f32[2,512,256]{2,1,0:T(8,128)S(1)} custom-call(bf16[512,256]{1,0:T(8,128)(2,1)S(1)} %ordered.2.refs_0_, bf16[512,256]{1,0:T(8,128)(2,1)S(1)} %collective-permute-done.10.refs_1_, bf16[2,512,1024]{2,1,0:T(8,128)(2,1)S(1)} %copy-done), custom_call_target="tpu_custom_call" | custom-call | flops 1024 | bytes 1024 | tf_op jit(solution)/shard_map/memory_terms/pallas_call | solution.py:315
  37.0 1.6 %finish_first.1 = (bf16[1024,1024]{1,0:T(8,128)(2,1)}, f32[2,512,256]{2,1,0:T(8,128)S(1)}) custom-call(s32[1]{0:T(128)} %bitcast.me_ref, bf16[512,256]{1,0:T(8,128)(2,1)S(1)} %ordered.3.refs_0_, bf16[512,256]{1,0:T(8,128)(2,1)S(1)} %collective-permute-done.13.refs_1_, bf16[512,256]{1,0:T(8,128)(2,1)S(1)} %get-tuple-element.30.refs_2_, ...), custom_call_target="tpu_custom_call" | custom-call | flops 1024 | bytes 1024 | tf_op jit(solution)/shard_map/finish_first/pallas_call | solution.py:296
  38.6 0.6 %collective-permute-done.15.refs_2_ = f32[4,8,128]{2,1,0:T(8,128)S(1)} collective-permute-done((f32[4,8,128]{2,1,0:T(8,128)S(1)}, f32[4,8,128]{2,1,0:T(8,128)S(1)}, u32[]{:S(2)}, u32[]{:S(2)}) %collective-permute-start.15) | collective-permute-done | bytes 16416 | tf_op jit(solution)/shard_map/ppermute | solution.py:421
  39.2 2.5 %finish_second.1 = (bf16[1024,1024]{1,0:T(8,128)(2,1)}, bf16[1024,1024]{1,0:T(8,128)(2,1)}) custom-call(s32[1]{0:T(128)} %bitcast.me_ref, bf16[512,256]{1,0:T(8,128)(2,1)S(1)} %collective-permute-done.9.refs_0_, f32[512,256]{1,0:T(8,128)S(1)} %get-tuple-element.26.refs_1_, ...), custom_call_target="tpu_custom_call", output_to_operand_aliasing={{0}: (10, {})} | custom-call | flops 1024 | bytes 1024 | tf_op jit(solution)/shard_map/finish_second/pallas_call | solution.py:396
  (27 shorter events, 0.4 us)
Async XLA Ops:
  4.9 2.0 %collective-permute-start.3 = (bf16[2,512,256]{2,1,0:T(8,128)(2,1)S(1)}, bf16[2,512,256]{2,1,0:T(8,128)(2,1)S(1)}, u32[]{:S(2)}, u32[]{:S(2)}) collective-permute-start(bf16[2,512,256]{2,1,0:T(8,128)(2,1)S(1)} %get-tuple-element.21), channel_id=1, source_target_pairs={{0,4},{4,0},{8,12},{12,8},{16,20},{20,16},{24,28},{28,24},{1,5},{5... | collective-permute-start | bytes 1572872 | tf_op jit(solution)/shard_map/ppermute | solution.py:421
  5.4 4.6 %collective-permute-start = (bf16[2,512,256]{2,1,0:T(8,128)(2,1)S(1)}, bf16[2,512,256]{2,1,0:T(8,128)(2,1)S(1)}, u32[]{:S(2)}, u32[]{:S(2)}) collective-permute-start(bf16[2,512,256]{2,1,0:T(8,128)(2,1)S(1)} %get-tuple-element.20), channel_id=1, source_target_pairs={{0,4},{4,0},{8,12},{12,8},{16,20},{20,16},{24,28},{28,24},{1,5},{5... | collective-permute-start | bytes 1572872 | tf_op jit(solution)/shard_map/ppermute | solution.py:421
  7.0 7.3 %collective-permute-start.4 = (bf16[512,256]{1,0:T(8,128)(2,1)S(1)}, bf16[512,256]{1,0:T(8,128)(2,1)S(1)}, u32[]{:S(2)}, u32[]{:S(2)}) collective-permute-start(bf16[512,256]{1,0:T(8,128)(2,1)S(1)} %fusion.6), channel_id=1, source_target_pairs={{0,8},{4,20},{8,0},{12,28},{16,24},{20,4},{24,16},{28,12},{1,9},{5... | collective-permute-start | bytes 786440 | tf_op jit(solution)/shard_map/ppermute | solution.py:421
  11.3 9.6 %copy-start = (bf16[2,512,1024]{2,1,0:T(8,128)(2,1)S(1)}, bf16[2,512,1024]{2,1,0:T(8,128)(2,1)}, u32[]{:S(2)}) copy-start(bf16[2,512,1024]{2,1,0:T(8,128)(2,1)} %refs_3_.1) | copy-start | bytes 6291460
  11.4 9.5 %copy-start.1 = (bf16[512,1024]{1,0:T(8,128)(2,1)S(1)}, bf16[512,1024]{1,0:T(8,128)(2,1)}, u32[]{:S(2)}) copy-start(bf16[512,1024]{1,0:T(8,128)(2,1)} %refs_5_.1) | copy-start | bytes 3145732
  11.4 9.5 %copy-start.2 = (f32[32,1024]{1,0:T(8,128)S(1)}, f32[32,1024]{1,0:T(8,128)}, u32[]{:S(2)}) copy-start(f32[32,1024]{1,0:T(8,128)} %refs_8_.1) | copy-start | bytes 393220
  11.4 7.5 %collective-permute-start.1 = (bf16[512,256]{1,0:T(8,128)(2,1)S(1)}, bf16[512,256]{1,0:T(8,128)(2,1)S(1)}, u32[]{:S(2)}, u32[]{:S(2)}) collective-permute-start(bf16[512,256]{1,0:T(8,128)(2,1)S(1)} %fusion.5._), channel_id=1, source_target_pairs={{0,8},{4,20},{8,0},{12,28},{16,24},{20,4},{24,16},{28,12},{1,9},{5... | collective-permute-start | bytes 786440 | tf_op jit(solution)/shard_map/ppermute | solution.py:421
  14.4 6.5 %collective-permute-start.5 = (bf16[512,256]{1,0:T(8,128)(2,1)S(1)}, bf16[512,256]{1,0:T(8,128)(2,1)S(1)}, u32[]{:S(2)}, u32[]{:S(2)}) collective-permute-start(bf16[512,256]{1,0:T(8,128)(2,1)S(1)} %combined.1.mine), channel_id=1, source_target_pairs={{0,16},{4,12},{8,24},{12,4},{16,0},{20,28},{24,8},{28,20},{1,17},{... | collective-permute-start | bytes 786440 | tf_op jit(solution)/shard_map/ppermute | solution.py:421
  19.0 6.4 %collective-permute-start.2 = (bf16[512,256]{1,0:T(8,128)(2,1)S(1)}, bf16[512,256]{1,0:T(8,128)(2,1)S(1)}, u32[]{:S(2)}, u32[]{:S(2)}) collective-permute-start(bf16[512,256]{1,0:T(8,128)(2,1)S(1)} %fusion.4._.mine), channel_id=1, source_target_pairs={{0,16},{4,12},{8,24},{12,4},{16,0},{20,28},{24,8},{28,20},{1,17},{... | collective-permute-start | bytes 786440 | tf_op jit(solution)/shard_map/ppermute | solution.py:421
  22.1 10.1 %collective-permute-start.11 = (bf16[512,256]{1,0:T(8,128)(2,1)S(1)}, bf16[512,256]{1,0:T(8,128)(2,1)S(1)}, u32[]{:S(2)}, u32[]{:S(2)}) collective-permute-start(bf16[512,256]{1,0:T(8,128)(2,1)S(1)} %get-tuple-element.28), channel_id=1, source_target_pairs={{0,4},{4,0},{8,12},{12,8},{16,20},{20,16},{24,28},{28,24},{1,5},{5... | collective-permute-start | bytes 786440 | tf_op jit(solution)/shard_map/ppermute | solution.py:421
  22.1 10.4 %collective-permute-start.12 = (bf16[512,256]{1,0:T(8,128)(2,1)S(1)}, bf16[512,256]{1,0:T(8,128)(2,1)S(1)}, u32[]{:S(2)}, u32[]{:S(2)}) collective-permute-start(bf16[512,256]{1,0:T(8,128)(2,1)S(1)} %get-tuple-element.28), channel_id=1, source_target_pairs={{0,8},{4,20},{8,0},{12,28},{16,24},{20,4},{24,16},{28,12},{1,9},{5... | collective-permute-start | bytes 786440 | tf_op jit(solution)/shard_map/ppermute | solution.py:421
  26.1 3.7 %collective-permute-start.7 = (f32[1,8,128]{2,1,0:T(8,128)S(1)}, f32[1,8,128]{2,1,0:T(8,128)S(1)}, u32[]{:S(2)}, u32[]{:S(2)}) collective-permute-start(f32[1,8,128]{2,1,0:T(8,128)S(1)} %get-tuple-element.25), channel_id=1, source_target_pairs={{0,1},{1,0},{2,3},{3,2},{4,5},{5,4},{6,7},{7,6},{8,9},{9,8},{10,11... | collective-permute-start | bytes 12296 | tf_op jit(solution)/shard_map/ppermute | solution.py:439
  27.5 6.8 %collective-permute-start.6 = (bf16[512,256]{1,0:T(8,128)(2,1)S(1)}, bf16[512,256]{1,0:T(8,128)(2,1)S(1)}, u32[]{:S(2)}, u32[]{:S(2)}) collective-permute-start(bf16[512,256]{1,0:T(8,128)(2,1)S(1)} %get-tuple-element.24), channel_id=1, source_target_pairs={{0,8},{4,20},{8,0},{12,28},{16,24},{20,4},{24,16},{28,12},{1,9},{5... | collective-permute-start | bytes 786440 | tf_op jit(solution)/shard_map/ppermute | solution.py:421
  29.7 4.5 %collective-permute-start.8 = (f32[2,8,128]{2,1,0:T(8,128)S(1)}, f32[2,8,128]{2,1,0:T(8,128)S(1)}, u32[]{:S(2)}, u32[]{:S(2)}) collective-permute-start(f32[2,8,128]{2,1,0:T(8,128)S(1)} %get-tuple-element.34.refs_0_), channel_id=1, source_target_pairs={{0,2},{1,3},{2,0},{3,1},{4,6},{5,7},{6,4},{7,5},{8,10},{9,11},{10,... | collective-permute-start | bytes 24584 | tf_op jit(solution)/shard_map/ppermute | solution.py:439
  32.1 4.4 %collective-permute-start.10 = (bf16[512,256]{1,0:T(8,128)(2,1)S(1)}, bf16[512,256]{1,0:T(8,128)(2,1)S(1)}, u32[]{:S(2)}, u32[]{:S(2)}) collective-permute-start(bf16[512,256]{1,0:T(8,128)(2,1)S(1)} %get-tuple-element.24), channel_id=1, source_target_pairs={{0,4},{4,0},{8,12},{12,8},{16,20},{20,16},{24,28},{28,24},{1,5},{5... | collective-permute-start | bytes 786440 | tf_op jit(solution)/shard_map/ppermute | solution.py:421
  32.6 4.3 %collective-permute-start.13 = (bf16[512,256]{1,0:T(8,128)(2,1)S(1)}, bf16[512,256]{1,0:T(8,128)(2,1)S(1)}, u32[]{:S(2)}, u32[]{:S(2)}) collective-permute-start(bf16[512,256]{1,0:T(8,128)(2,1)S(1)} %ordered.3.refs_0_), channel_id=1, source_target_pairs={{0,4},{4,0},{8,12},{12,8},{16,20},{20,16},{24,28},{28,24},{1,5},{5... | collective-permute-start | bytes 786440 | tf_op jit(solution)/shard_map/ppermute | solution.py:421
  34.3 4.9 %collective-permute-start.9 = (bf16[512,256]{1,0:T(8,128)(2,1)S(1)}, bf16[512,256]{1,0:T(8,128)(2,1)S(1)}, u32[]{:S(2)}, u32[]{:S(2)}) collective-permute-start(bf16[512,256]{1,0:T(8,128)(2,1)S(1)} %ordered.2.refs_0_), channel_id=1, source_target_pairs={{0,4},{4,0},{8,12},{12,8},{16,20},{20,16},{24,28},{28,24},{1,5},{5... | collective-permute-start | bytes 786440 | tf_op jit(solution)/shard_map/ppermute | solution.py:421
  34.4 4.2 %collective-permute-start.16 = (f32[4,8,128]{2,1,0:T(8,128)S(1)}, f32[4,8,128]{2,1,0:T(8,128)S(1)}, u32[]{:S(2)}, u32[]{:S(2)}) collective-permute-start(f32[4,8,128]{2,1,0:T(8,128)S(1)} %constant_dynamic-update-slice_fusion.2.refs_0_), channel_id=1, source_target_pairs={{20,0},{8,4},{28,8},{0,12},{4,16},{24,20},{12,24},{16,28},{21,1},{... | collective-permute-start | bytes 49160 | tf_op jit(solution)/shard_map/ppermute | solution.py:436
  35.5 3.7 %collective-permute-start.15 = (f32[4,8,128]{2,1,0:T(8,128)S(1)}, f32[4,8,128]{2,1,0:T(8,128)S(1)}, u32[]{:S(2)}, u32[]{:S(2)}) collective-permute-start(f32[4,8,128]{2,1,0:T(8,128)S(1)} %constant_dynamic-update-slice_fusion.2.refs_0_), channel_id=1, source_target_pairs={{0,8},{4,20},{8,0},{12,28},{16,24},{20,4},{24,16},{28,12},{1,9},{5... | collective-permute-start | bytes 49160 | tf_op jit(solution)/shard_map/ppermute | solution.py:421
  36.5 2.7 %collective-permute-start.14 = (f32[4,8,128]{2,1,0:T(8,128)S(1)}, f32[4,8,128]{2,1,0:T(8,128)S(1)}, u32[]{:S(2)}, u32[]{:S(2)}) collective-permute-start(f32[4,8,128]{2,1,0:T(8,128)S(1)} %constant_dynamic-update-slice_fusion.2.refs_0_), channel_id=1, source_target_pairs={{0,4},{4,0},{8,12},{12,8},{16,20},{20,16},{24,28},{28,24},{1,5},{5... | collective-permute-start | bytes 49160 | tf_op jit(solution)/shard_map/ppermute | solution.py:421

commit v19 on v18

--- a/solution.py
+++ b/solution.py
@@ -73,7 +73,7 @@
     eighth = depth // 8
     chunks = [(0, 2 * eighth), (2 * eighth, 3 * eighth), (5 * eighth, 3 * eighth)]
 
-    def kernel(me_ref, sigma_ref, g_ref, sent_0, sent_1, sigma, g_kept, g_sent, total, sems):
+    def kernel(me_ref, sigma_ref, g_ref, on_0, on_1, kept_0, kept_1, sigma, g_kept, g_sent, total, sems):
         place = Place(me_ref[0], bits)
         sent_at, kept_at = half_of(place.core ^ 1, half), half_of(place.core, half)
         started = []
@@ -108,8 +108,11 @@
                 total[...] += term
             else:
                 term += total[...]
-                halves_to(sent_0, term[:rows], place.other_side)
-                halves_to(sent_1, term[rows:], place.other_side)
+                left, right = term[:, : half // 2], term[:, half // 2 :]
+                on = jnp.where(place.other_side == 0, right, left).astype(BF16)
+                on_0[...], on_1[...] = on[:rows], on[rows:]
+                keep = jnp.where(place.other_side == 0, left, right)
+                kept_0[...], kept_1[...] = keep[:rows], keep[rows:]
         for copy in ahead:
             copy.wait()
 
@@ -117,8 +120,10 @@
         kernel,
         "first_products",
         in_specs=[SCALAR, HBM, HBM],
-        out_specs=[WHOLE] * 4,
-        out_shape=[near((2, rows, half // 2), BF16)] * 2 + [near((tall, depth), BF16), near((depth, half), BF16)],
+        out_specs=[WHOLE] * 6,
+        out_shape=[near((rows, half // 2), BF16)] * 2
+        + [near((rows, half // 2), F32)] * 2
+        + [near((tall, depth), BF16), near((depth, half), BF16)],
         scratch_shapes=[
             pltpu.VMEM((depth, half), BF16),
             pltpu.VMEM((tall, half), F32),
@@ -151,10 +156,10 @@
 def combined(kept, arrived, more, after):
     rows, width = more.shape
     if after is None:
-        return (kept[1] + arrived[1].astype(F32) + more.astype(F32)).astype(BF16)
+        return (kept[1] + arrived + more.astype(F32)).astype(BF16)
 
     def kernel(kept, arrived, more, _, out):
-        out[...] = (kept[1] + arrived[1].astype(F32) + more[...].astype(F32)).astype(BF16)
+        out[...] = (kept[1] + arrived[...] + more[...].astype(F32)).astype(BF16)
 
     return call(
         kernel, "combined", in_specs=[WHOLE] * 3 + [FAR], out_specs=WHOLE, out_shape=near((rows, width), BF16)
@@ -429,7 +434,7 @@
         return mine, theirs
 
     def passed_on(kept, arrived):
-        return (kept[0] + arrived[0].astype(F32)).astype(BF16)
+        return (kept[0] + arrived.astype(F32)).astype(BF16)
 
     def from_far(x):
         flip = [d ^ 1 ^ (1 << (even if d % 2 else odd)[1]) for d in range(past)]
@@ -438,12 +443,13 @@
     def widened(share, level):
         return lax.ppermute(share, "second", [(z, z ^ (1 << level)) for z in range(second)])
 
-    send_0, send_1, sigma, g_kept = first_products(me, sigma_hist, g_hist, rows, bits)
-    arrived_0, arrived_1 = swap(send_0, 0), swap(send_1, 0)
+    on_0, on_1, keep_0, keep_1, sigma, g_kept = first_products(me, sigma_hist, g_hist, rows, bits)
+    arrived_on_1 = swap(on_1, 0)
     kept_0 = product(me, sigma, g_kept, 0, rows, bits)
-    sent_0 = passed_on(kept_0, arrived_0)
-    kept_1 = product(me, sigma, g_kept, 1, rows, bits, after=arrived_1)
-    sent_1 = passed_on(kept_1, arrived_1)
+    sent_0 = passed_on(kept_0, swap(on_0, 0))
+    kept_1 = product(me, sigma, g_kept, 1, rows, bits, after=arrived_on_1)
+    sent_1 = passed_on(kept_1, arrived_on_1)
+    arrived_0, arrived_1 = swap(keep_0, 0), swap(keep_1, 0)
 
     mine, theirs = exchanged(kept_0, arrived_0, sent_0, after=sent_1)
     mine_1, theirs_1 = exchanged(kept_1, arrived_1, sent_1)

time: 41.9 us -> 42.4 us (1.012)
  waiting for transfers between devices: 9.34 us -> 9.84 us
    ppermute x14 -> x16, waiting for transfers between devices: 7.21 us -> 7.7 us  [swap(): return lax.ppermute(x, 'past', pairs)]
    ppermute x14 -> x16, starting transfers between devices: 12.7 us -> 12.7 us  [swap(): return lax.ppermute(x, 'past', pairs)]
  transfers between devices with their start and end apart: 17 -> 19, of which waited for: 8 -> 7; matrix products, arithmetic and copies ran while one was open for 0% -> 1% of each run, Pallas kernels for 17% -> 16%
where the time goes in v19:
time: 42.4 us; the launch traced here: 42.2 us
  starting transfers between devices  17.6 us (42%)
  Pallas kernels  13.8 us (33%)
  waiting for transfers between devices  9.84 us (23%)
  between operations  0.82 us (2%)
    ppermute x16, starting transfers between devices, swap(): return lax.ppermute(x, 'past', pairs)  12.7 us
    ppermute x16, waiting for transfers between devices, swap(): return lax.ppermute(x, 'past', pairs)  7.7 us
    pallas_call x1, Pallas kernels, first_products(): call(kernel, 'first_products', in_specs=[SCALAR, HBM, HBM], out_specs=[WH...  4.28 us
    ppermute x2, starting transfers between devices, widened(): lax.ppermute(share, 'second', [(z, z ^ 1 << level) for z in range(second)])  3.8 us
    pallas_call x2, Pallas kernels, product(): call(kernel, 'memory_product', in_specs=[SCALAR, WHOLE, WHOLE] + [FAR] *...  2.55 us
    pallas_call x1, Pallas kernels, finish_second(): call(kernel, 'finish_second', in_specs=[SCALAR] + [WHOLE] * 9 + [HBM], ou...  2.52 us
    ppermute x2, waiting for transfers between devices, widened(): lax.ppermute(share, 'second', [(z, z ^ 1 << level) for z in range(second)])  2.13 us
    pallas_call x1, Pallas kernels, finish_first(): call(kernel, 'finish_first', in_specs=[SCALAR] + [WHOLE] * 7, out_specs=[...  1.6 us
  transfers between devices with their start and end apart: 19, of which 7 were waited for; matrix products, arithmetic and copies ran while one was open for 1% of the time, Pallas kernels for 16%

profile of v19, /device:TPU:0, one launch (start us, length us, event | category | flops | bytes accessed | tf_op | source)
XLA Modules:
  0.0 42.2 jit_solution(11755873405620830629)
XLA Ops:
  0.6 4.3 %first_products.1 = (bf16[512,256]{1,0:T(8,128)(2,1)S(1)}, bf16[512,256]{1,0:T(8,128)(2,1)S(1)}, f32[512,256]{1,0:T(8,128)S(1)}, f32[512,256]{1,0:T(8,128)S(1)},...) custom-call(s32[1]{0:T(128)} %bitcast.me_ref, bf16[1024,2048]{1,0:T(8,128)(2,1)} %sigma_ref.1, ...), custom_call_target="tpu_custom_call" | custom-call | flops 1024 | bytes 1024 | tf_op jit(solution)/shard_map/first_products/pallas_call | solution.py:119
  4.9 0.5 %collective-permute-start.5 = (bf16[512,256]{1,0:T(8,128)(2,1)S(1)}, bf16[512,256]{1,0:T(8,128)(2,1)S(1)}, u32[]{:S(2)}, u32[]{:S(2)}) collective-permute-start(bf16[512,256]{1,0:T(8,128)(2,1)S(1)} %get-tuple-element.25), channel_id=1, source_target_pairs={{0,4},{4,0},{8,12},{12,8},{16,20},{20,16},{24,28},{28,24},{1,5},{5... | collective-permute-start | bytes 786440 | tf_op jit(solution)/shard_map/ppermute | solution.py:426
  5.4 0.1 collective-permute-start
  5.5 0.4 %collective-permute-start.1 = (f32[512,256]{1,0:T(8,128)S(1)}, f32[512,256]{1,0:T(8,128)S(1)}, u32[]{:S(2)}, u32[]{:S(2)}) collective-permute-start(f32[512,256]{1,0:T(8,128)S(1)} %get-tuple-element.23), channel_id=1, source_target_pairs={{0,4},{4,0},{8,12},{12,8},{16,20},{20,16},{24,28},{28,24},{1,5},{5... | collective-permute-start | bytes 1572872 | tf_op jit(solution)/shard_map/ppermute | solution.py:426
  5.9 0.1 collective-permute-start.4
  6.0 1.3 %memory_product.3.kept = f32[2,512,256]{2,1,0:T(8,128)S(1)} custom-call(s32[1]{0:T(128)} %bitcast.me_ref, bf16[1024,2048]{1,0:T(8,128)(2,1)S(1)} %get-tuple-element.20.sigma, bf16[2048,512]{1,0:T(8,128)(2,1)S(1)} %get-tuple-element.21.g), custom_call_target="tpu_custom_call" | custom-call | flops 1024 | bytes 1024 | tf_op jit(solution)/shard_map/memory_product/pallas_call | solution.py:147
  7.4 3.0 %collective-permute-start.6 = (bf16[512,256]{1,0:T(8,128)(2,1)S(1)}, bf16[512,256]{1,0:T(8,128)(2,1)S(1)}, u32[]{:S(2)}, u32[]{:S(2)}) collective-permute-start(bf16[512,256]{1,0:T(8,128)(2,1)S(1)} %fusion.1), channel_id=1, source_target_pairs={{0,8},{4,20},{8,0},{12,28},{16,24},{20,4},{24,16},{28,12},{1,9},{5... | collective-permute-start | bytes 786440 | tf_op jit(solution)/shard_map/ppermute | solution.py:426
  10.4 1.3 %memory_product.2 = f32[2,512,256]{2,1,0:T(8,128)S(1)} custom-call(s32[1]{0:T(128)} %bitcast.me_ref, bf16[1024,2048]{1,0:T(8,128)(2,1)S(1)} %get-tuple-element.20.sigma, bf16[2048,512]{1,0:T(8,128)(2,1)S(1)} %get-tuple-element.21.g, bf16[512,256]{1,0:T(8,128)(2,1)S(1)} %collective-permute-done.refs_0_), custom_call_target="tpu_custom_call" | custom-call | flops 1024 | bytes 1024 | tf_op jit(solution)/shard_map/memory_product/pallas_call | solution.py:147
  11.8 0.1 collective-permute-start.2
  11.8 2.9 %collective-permute-done.6.more = bf16[512,256]{1,0:T(8,128)(2,1)S(1)} collective-permute-done((bf16[512,256]{1,0:T(8,128)(2,1)S(1)}, bf16[512,256]{1,0:T(8,128)(2,1)S(1)}, u32[]{:S(2)}, u32[]{:S(2)}) %collective-permute-start.6) | collective-permute-done | bytes 262176 | tf_op jit(solution)/shard_map/ppermute | solution.py:426
  14.8 2.1 %collective-permute-start.7 = (bf16[512,256]{1,0:T(8,128)(2,1)S(1)}, bf16[512,256]{1,0:T(8,128)(2,1)S(1)}, u32[]{:S(2)}, u32[]{:S(2)}) collective-permute-start(bf16[512,256]{1,0:T(8,128)(2,1)S(1)} %combined.1.mine), channel_id=1, source_target_pairs={{0,16},{4,12},{8,24},{12,4},{16,0},{20,28},{24,8},{28,20},{1,17},{... | collective-permute-start | bytes 786440 | tf_op jit(solution)/shard_map/ppermute | solution.py:426
  16.9 2.4 %collective-permute-done.2 = bf16[512,256]{1,0:T(8,128)(2,1)S(1)} collective-permute-done((bf16[512,256]{1,0:T(8,128)(2,1)S(1)}, bf16[512,256]{1,0:T(8,128)(2,1)S(1)}, u32[]{:S(2)}, u32[]{:S(2)}) %collective-permute-start.2) | collective-permute-done | bytes 262176 | tf_op jit(solution)/shard_map/ppermute | solution.py:426
  19.3 0.1 fusion.6._.mine
  19.4 1.4 %collective-permute-start.3 = (bf16[512,256]{1,0:T(8,128)(2,1)S(1)}, bf16[512,256]{1,0:T(8,128)(2,1)S(1)}, u32[]{:S(2)}, u32[]{:S(2)}) collective-permute-start(bf16[512,256]{1,0:T(8,128)(2,1)S(1)} %fusion.6._.mine), channel_id=1, source_target_pairs={{0,16},{4,12},{8,24},{12,4},{16,0},{20,28},{24,8},{28,20},{1,17},{... | collective-permute-start | bytes 786440 | tf_op jit(solution)/shard_map/ppermute | solution.py:426
  20.8 0.5 %collective-permute-done.7.theirs = bf16[512,256]{1,0:T(8,128)(2,1)S(1)} collective-permute-done((bf16[512,256]{1,0:T(8,128)(2,1)S(1)}, bf16[512,256]{1,0:T(8,128)(2,1)S(1)}, u32[]{:S(2)}, u32[]{:S(2)}) %collective-permute-start.7) | collective-permute-done | bytes 262176 | tf_op jit(solution)/shard_map/ppermute | solution.py:426
  21.3 1.2 %own_first.1 = (bf16[512,256]{1,0:T(8,128)(2,1)S(1)}, f32[512,256]{1,0:T(8,128)S(1)}, f32[1,128]{1,0:T(1,128)S(1)}, bf16[512,256]{1,0:T(8,128)(2,1)S(1)}, f32[512,256]{1,0:T(8,128)S(1)}) custom-call(s32[1]{0:T(128)} %bitcast.me_ref, bf16[512,256]{1,0:T(8,128)(2,1)S(1)} %combined.1.mine, bf16[512,256]{1,0:T(8,128)(2,1)S(1)} %collective-permute-done.7.theirs, ...), custom_call_target="tpu_custom_call" | custom-call | flops 1024 | bytes 1024 | tf_op jit(solution)/shard_map/own_first/pallas_call | solution.py:209
  22.5 2.1 %collective-permute-start.14 = (bf16[512,256]{1,0:T(8,128)(2,1)S(1)}, bf16[512,256]{1,0:T(8,128)(2,1)S(1)}, u32[]{:S(2)}, u32[]{:S(2)}) collective-permute-start(bf16[512,256]{1,0:T(8,128)(2,1)S(1)} %get-tuple-element.32), channel_id=1, source_target_pairs={{0,8},{4,20},{8,0},{12,28},{16,24},{20,4},{24,16},{28,12},{1,9},{5... | collective-permute-start | bytes 786440 | tf_op jit(solution)/shard_map/ppermute | solution.py:426
  24.6 1.3 %collective-permute-done.3.theirs = bf16[512,256]{1,0:T(8,128)(2,1)S(1)} collective-permute-done((bf16[512,256]{1,0:T(8,128)(2,1)S(1)}, bf16[512,256]{1,0:T(8,128)(2,1)S(1)}, u32[]{:S(2)}, u32[]{:S(2)}) %collective-permute-start.3) | collective-permute-done | bytes 262176 | tf_op jit(solution)/shard_map/ppermute | solution.py:426
  25.9 0.6 %own_second.1 = (bf16[512,256]{1,0:T(8,128)(2,1)S(1)}, f32[1,8,128]{2,1,0:T(8,128)S(1)}, f32[512,256]{1,0:T(8,128)S(1)}) custom-call(s32[1]{0:T(128)} %bitcast.me_ref, bf16[512,256]{1,0:T(8,128)(2,1)S(1)} %fusion.6._.mine, bf16[512,256]{1,0:T(8,128)(2,1)S(1)} %collective-permute-done.3.theirs, bf16[2,512,1024]{2,1,0:T(8,128)(2,1)S(1)} %copy-done, ...), custom_call_target="tpu_custom_call" | custom-call | flops 1024 | bytes 1024 | tf_op jit(solution)/shard_map/own_second/pallas_call | solution.py:247
  26.5 1.4 %collective-permute-start.9 = (f32[1,8,128]{2,1,0:T(8,128)S(1)}, f32[1,8,128]{2,1,0:T(8,128)S(1)}, u32[]{:S(2)}, u32[]{:S(2)}) collective-permute-start(f32[1,8,128]{2,1,0:T(8,128)S(1)} %get-tuple-element.29), channel_id=1, source_target_pairs={{0,1},{1,0},{2,3},{3,2},{4,5},{5,4},{6,7},{7,6},{8,9},{9,8},{10,11... | collective-permute-start | bytes 12296 | tf_op jit(solution)/shard_map/ppermute | solution.py:444
  27.9 1.2 %collective-permute-start.8 = (bf16[512,256]{1,0:T(8,128)(2,1)S(1)}, bf16[512,256]{1,0:T(8,128)(2,1)S(1)}, u32[]{:S(2)}, u32[]{:S(2)}) collective-permute-start(bf16[512,256]{1,0:T(8,128)(2,1)S(1)} %get-tuple-element.28), channel_id=1, source_target_pairs={{0,8},{4,20},{8,0},{12,28},{16,24},{20,4},{24,16},{28,12},{1,9},{5... | collective-permute-start | bytes 786440 | tf_op jit(solution)/shard_map/ppermute | solution.py:426
  29.1 1.0 %collective-permute-done.9 = f32[1,8,128]{2,1,0:T(8,128)S(1)} collective-permute-done((f32[1,8,128]{2,1,0:T(8,128)S(1)}, f32[1,8,128]{2,1,0:T(8,128)S(1)}, u32[]{:S(2)}, u32[]{:S(2)}) %collective-permute-start.9) | collective-permute-done | bytes 4128 | tf_op jit(solution)/shard_map/ppermute | solution.py:444
  30.2 2.4 %collective-permute-start.10 = (f32[2,8,128]{2,1,0:T(8,128)S(1)}, f32[2,8,128]{2,1,0:T(8,128)S(1)}, u32[]{:S(2)}, u32[]{:S(2)}) collective-permute-start(f32[2,8,128]{2,1,0:T(8,128)S(1)} %get-tuple-element.38.refs_0_), channel_id=1, source_target_pairs={{0,2},{1,3},{2,0},{3,1},{4,6},{5,7},{6,4},{7,5},{8,10},{9,11},{10,... | collective-permute-start | bytes 24584 | tf_op jit(solution)/shard_map/ppermute | solution.py:444
  32.6 0.5 %finish_other.1 = (bf16[512,256]{1,0:T(8,128)(2,1)S(1)}, f32[512,256]{1,0:T(8,128)S(1)}) custom-call(s32[1]{0:T(128)} %bitcast.me_ref, bf16[512,256]{1,0:T(8,128)(2,1)S(1)} %collective-permute-done.13.piece, bf16[2,512,1024]{2,1,0:T(8,128)(2,1)S(1)} %copy-done, bf16[512,1024]{1,0:T(8,128)(2,1)S(1)} %copy-done.1, f32[32,1024]{1,0:T(8,128)S(1)} %copy-done.2), custom_call_target="tpu_custom_call" | custom-call | flops 1024 | bytes 1024 | tf_op jit(solution)/shard_map/finish_other/pallas_call | solution.py:266
  33.1 0.6 %collective-permute-start.15 = (bf16[512,256]{1,0:T(8,128)(2,1)S(1)}, bf16[512,256]{1,0:T(8,128)(2,1)S(1)}, u32[]{:S(2)}, u32[]{:S(2)}) collective-permute-start(bf16[512,256]{1,0:T(8,128)(2,1)S(1)} %ordered.3.refs_0_), channel_id=1, source_target_pairs={{0,4},{4,0},{8,12},{12,8},{16,20},{20,16},{24,28},{28,24},{1,5},{5... | collective-permute-start | bytes 786440 | tf_op jit(solution)/shard_map/ppermute | solution.py:426
  33.6 1.1 %collective-permute-done.10 = f32[2,8,128]{2,1,0:T(8,128)S(1)} collective-permute-done((f32[2,8,128]{2,1,0:T(8,128)S(1)}, f32[2,8,128]{2,1,0:T(8,128)S(1)}, u32[]{:S(2)}, u32[]{:S(2)}) %collective-permute-start.10) | collective-permute-done | bytes 8224 | tf_op jit(solution)/shard_map/ppermute | solution.py:444
  34.8 1.1 %collective-permute-start.18 = (f32[4,8,128]{2,1,0:T(8,128)S(1)}, f32[4,8,128]{2,1,0:T(8,128)S(1)}, u32[]{:S(2)}, u32[]{:S(2)}) collective-permute-start(f32[4,8,128]{2,1,0:T(8,128)S(1)} %constant_dynamic-update-slice_fusion.2.refs_0_), channel_id=1, source_target_pairs={{20,0},{8,4},{28,8},{0,12},{4,16},{24,20},{12,24},{16,28},{21,1},{... | collective-permute-start | bytes 49160 | tf_op jit(solution)/shard_map/ppermute | solution.py:441
  35.9 1.0 %collective-permute-start.17 = (f32[4,8,128]{2,1,0:T(8,128)S(1)}, f32[4,8,128]{2,1,0:T(8,128)S(1)}, u32[]{:S(2)}, u32[]{:S(2)}) collective-permute-start(f32[4,8,128]{2,1,0:T(8,128)S(1)} %constant_dynamic-update-slice_fusion.2.refs_0_), channel_id=1, source_target_pairs={{0,8},{4,20},{8,0},{12,28},{16,24},{20,4},{24,16},{28,12},{1,9},{5... | collective-permute-start | bytes 49160 | tf_op jit(solution)/shard_map/ppermute | solution.py:426
  37.0 0.4 %memory_terms.1.refs_5_.refs_2_ = f32[2,512,256]{2,1,0:T(8,128)S(1)} custom-call(bf16[512,256]{1,0:T(8,128)(2,1)S(1)} %ordered.2.refs_0_, bf16[512,256]{1,0:T(8,128)(2,1)S(1)} %collective-permute-done.12.refs_1_, bf16[2,512,1024]{2,1,0:T(8,128)(2,1)S(1)} %copy-done), custom_call_target="tpu_custom_call" | custom-call | flops 1024 | bytes 1024 | tf_op jit(solution)/shard_map/memory_terms/pallas_call | solution.py:320
  37.4 1.6 %finish_first.1 = (bf16[1024,1024]{1,0:T(8,128)(2,1)}, f32[2,512,256]{2,1,0:T(8,128)S(1)}) custom-call(s32[1]{0:T(128)} %bitcast.me_ref, bf16[512,256]{1,0:T(8,128)(2,1)S(1)} %ordered.3.refs_0_, bf16[512,256]{1,0:T(8,128)(2,1)S(1)} %collective-permute-done.15.refs_1_, bf16[512,256]{1,0:T(8,128)(2,1)S(1)} %get-tuple-element.34.refs_2_, ...), custom_call_target="tpu_custom_call" | custom-call | flops 1024 | bytes 1024 | tf_op jit(solution)/shard_map/finish_first/pallas_call | solution.py:301
  39.0 0.6 %collective-permute-done.17.refs_2_ = f32[4,8,128]{2,1,0:T(8,128)S(1)} collective-permute-done((f32[4,8,128]{2,1,0:T(8,128)S(1)}, f32[4,8,128]{2,1,0:T(8,128)S(1)}, u32[]{:S(2)}, u32[]{:S(2)}) %collective-permute-start.17) | collective-permute-done | bytes 16416 | tf_op jit(solution)/shard_map/ppermute | solution.py:426
  39.7 2.5 %finish_second.1 = (bf16[1024,1024]{1,0:T(8,128)(2,1)}, bf16[1024,1024]{1,0:T(8,128)(2,1)}) custom-call(s32[1]{0:T(128)} %bitcast.me_ref, bf16[512,256]{1,0:T(8,128)(2,1)S(1)} %collective-permute-done.11.refs_0_, f32[512,256]{1,0:T(8,128)S(1)} %get-tuple-element.30.refs_1_, ...), custom_call_target="tpu_custom_call", output_to_operand_aliasing={{0}: (10, {})} | custom-call | flops 1024 | bytes 1024 | tf_op jit(solution)/shard_map/finish_second/pallas_call | solution.py:401
  (31 shorter events, 0.4 us)
Async XLA Ops:
  4.9 2.4 %collective-permute-start.5 = (bf16[512,256]{1,0:T(8,128)(2,1)S(1)}, bf16[512,256]{1,0:T(8,128)(2,1)S(1)}, u32[]{:S(2)}, u32[]{:S(2)}) collective-permute-start(bf16[512,256]{1,0:T(8,128)(2,1)S(1)} %get-tuple-element.25), channel_id=1, source_target_pairs={{0,4},{4,0},{8,12},{12,8},{16,20},{20,16},{24,28},{28,24},{1,5},{5... | collective-permute-start | bytes 786440 | tf_op jit(solution)/shard_map/ppermute | solution.py:426
  5.4 5.0 %collective-permute-start = (bf16[512,256]{1,0:T(8,128)(2,1)S(1)}, bf16[512,256]{1,0:T(8,128)(2,1)S(1)}, u32[]{:S(2)}, u32[]{:S(2)}) collective-permute-start(bf16[512,256]{1,0:T(8,128)(2,1)S(1)} %get-tuple-element.22), channel_id=1, source_target_pairs={{0,4},{4,0},{8,12},{12,8},{16,20},{20,16},{24,28},{28,24},{1,5},{5... | collective-permute-start | bytes 786440 | tf_op jit(solution)/shard_map/ppermute | solution.py:426
  5.5 11.4 %collective-permute-start.1 = (f32[512,256]{1,0:T(8,128)S(1)}, f32[512,256]{1,0:T(8,128)S(1)}, u32[]{:S(2)}, u32[]{:S(2)}) collective-permute-start(f32[512,256]{1,0:T(8,128)S(1)} %get-tuple-element.23), channel_id=1, source_target_pairs={{0,4},{4,0},{8,12},{12,8},{16,20},{20,16},{24,28},{28,24},{1,5},{5... | collective-permute-start | bytes 1572872 | tf_op jit(solution)/shard_map/ppermute | solution.py:426
  5.9 5.9 %collective-permute-start.4 = (f32[512,256]{1,0:T(8,128)S(1)}, f32[512,256]{1,0:T(8,128)S(1)}, u32[]{:S(2)}, u32[]{:S(2)}) collective-permute-start(f32[512,256]{1,0:T(8,128)S(1)} %get-tuple-element.24), channel_id=1, source_target_pairs={{0,4},{4,0},{8,12},{12,8},{16,20},{20,16},{24,28},{28,24},{1,5},{5... | collective-permute-start | bytes 1572872 | tf_op jit(solution)/shard_map/ppermute | solution.py:426
  7.4 7.4 %collective-permute-start.6 = (bf16[512,256]{1,0:T(8,128)(2,1)S(1)}, bf16[512,256]{1,0:T(8,128)(2,1)S(1)}, u32[]{:S(2)}, u32[]{:S(2)}) collective-permute-start(bf16[512,256]{1,0:T(8,128)(2,1)S(1)} %fusion.1), channel_id=1, source_target_pairs={{0,8},{4,20},{8,0},{12,28},{16,24},{20,4},{24,16},{28,12},{1,9},{5... | collective-permute-start | bytes 786440 | tf_op jit(solution)/shard_map/ppermute | solution.py:426
  11.7 9.5 %copy-start = (bf16[2,512,1024]{2,1,0:T(8,128)(2,1)S(1)}, bf16[2,512,1024]{2,1,0:T(8,128)(2,1)}, u32[]{:S(2)}) copy-start(bf16[2,512,1024]{2,1,0:T(8,128)(2,1)} %refs_3_.1) | copy-start | bytes 6291460
  11.7 9.5 %copy-start.1 = (bf16[512,1024]{1,0:T(8,128)(2,1)S(1)}, bf16[512,1024]{1,0:T(8,128)(2,1)}, u32[]{:S(2)}) copy-start(bf16[512,1024]{1,0:T(8,128)(2,1)} %refs_5_.1) | copy-start | bytes 3145732
  11.7 9.5 %copy-start.2 = (f32[32,1024]{1,0:T(8,128)S(1)}, f32[32,1024]{1,0:T(8,128)}, u32[]{:S(2)}) copy-start(f32[32,1024]{1,0:T(8,128)} %refs_8_.1) | copy-start | bytes 393220
  11.8 7.6 %collective-permute-start.2 = (bf16[512,256]{1,0:T(8,128)(2,1)S(1)}, bf16[512,256]{1,0:T(8,128)(2,1)S(1)}, u32[]{:S(2)}, u32[]{:S(2)}) collective-permute-start(bf16[512,256]{1,0:T(8,128)(2,1)S(1)} %fusion.3._), channel_id=1, source_target_pairs={{0,8},{4,20},{8,0},{12,28},{16,24},{20,4},{24,16},{28,12},{1,9},{5... | collective-permute-start | bytes 786440 | tf_op jit(solution)/shard_map/ppermute | solution.py:426
  14.8 6.5 %collective-permute-start.7 = (bf16[512,256]{1,0:T(8,128)(2,1)S(1)}, bf16[512,256]{1,0:T(8,128)(2,1)S(1)}, u32[]{:S(2)}, u32[]{:S(2)}) collective-permute-start(bf16[512,256]{1,0:T(8,128)(2,1)S(1)} %combined.1.mine), channel_id=1, source_target_pairs={{0,16},{4,12},{8,24},{12,4},{16,0},{20,28},{24,8},{28,20},{1,17},{... | collective-permute-start | bytes 786440 | tf_op jit(solution)/shard_map/ppermute | solution.py:426
  19.4 6.4 %collective-permute-start.3 = (bf16[512,256]{1,0:T(8,128)(2,1)S(1)}, bf16[512,256]{1,0:T(8,128)(2,1)S(1)}, u32[]{:S(2)}, u32[]{:S(2)}) collective-permute-start(bf16[512,256]{1,0:T(8,128)(2,1)S(1)} %fusion.6._.mine), channel_id=1, source_target_pairs={{0,16},{4,12},{8,24},{12,4},{16,0},{20,28},{24,8},{28,20},{1,17},{... | collective-permute-start | bytes 786440 | tf_op jit(solution)/shard_map/ppermute | solution.py:426
  22.4 10.1 %collective-permute-start.13 = (bf16[512,256]{1,0:T(8,128)(2,1)S(1)}, bf16[512,256]{1,0:T(8,128)(2,1)S(1)}, u32[]{:S(2)}, u32[]{:S(2)}) collective-permute-start(bf16[512,256]{1,0:T(8,128)(2,1)S(1)} %get-tuple-element.32), channel_id=1, source_target_pairs={{0,4},{4,0},{8,12},{12,8},{16,20},{20,16},{24,28},{28,24},{1,5},{5... | collective-permute-start | bytes 786440 | tf_op jit(solution)/shard_map/ppermute | solution.py:426
  22.5 10.5 %collective-permute-start.14 = (bf16[512,256]{1,0:T(8,128)(2,1)S(1)}, bf16[512,256]{1,0:T(8,128)(2,1)S(1)}, u32[]{:S(2)}, u32[]{:S(2)}) collective-permute-start(bf16[512,256]{1,0:T(8,128)(2,1)S(1)} %get-tuple-element.32), channel_id=1, source_target_pairs={{0,8},{4,20},{8,0},{12,28},{16,24},{20,4},{24,16},{28,12},{1,9},{5... | collective-permute-start | bytes 786440 | tf_op jit(solution)/shard_map/ppermute | solution.py:426
  26.5 3.7 %collective-permute-start.9 = (f32[1,8,128]{2,1,0:T(8,128)S(1)}, f32[1,8,128]{2,1,0:T(8,128)S(1)}, u32[]{:S(2)}, u32[]{:S(2)}) collective-permute-start(f32[1,8,128]{2,1,0:T(8,128)S(1)} %get-tuple-element.29), channel_id=1, source_target_pairs={{0,1},{1,0},{2,3},{3,2},{4,5},{5,4},{6,7},{7,6},{8,9},{9,8},{10,11... | collective-permute-start | bytes 12296 | tf_op jit(solution)/shard_map/ppermute | solution.py:444
  27.9 6.8 %collective-permute-start.8 = (bf16[512,256]{1,0:T(8,128)(2,1)S(1)}, bf16[512,256]{1,0:T(8,128)(2,1)S(1)}, u32[]{:S(2)}, u32[]{:S(2)}) collective-permute-start(bf16[512,256]{1,0:T(8,128)(2,1)S(1)} %get-tuple-element.28), channel_id=1, source_target_pairs={{0,8},{4,20},{8,0},{12,28},{16,24},{20,4},{24,16},{28,12},{1,9},{5... | collective-permute-start | bytes 786440 | tf_op jit(solution)/shard_map/ppermute | solution.py:426
  30.2 4.5 %collective-permute-start.10 = (f32[2,8,128]{2,1,0:T(8,128)S(1)}, f32[2,8,128]{2,1,0:T(8,128)S(1)}, u32[]{:S(2)}, u32[]{:S(2)}) collective-permute-start(f32[2,8,128]{2,1,0:T(8,128)S(1)} %get-tuple-element.38.refs_0_), channel_id=1, source_target_pairs={{0,2},{1,3},{2,0},{3,1},{4,6},{5,7},{6,4},{7,5},{8,10},{9,11},{10,... | collective-permute-start | bytes 24584 | tf_op jit(solution)/shard_map/ppermute | solution.py:444
  32.5 4.4 %collective-permute-start.12 = (bf16[512,256]{1,0:T(8,128)(2,1)S(1)}, bf16[512,256]{1,0:T(8,128)(2,1)S(1)}, u32[]{:S(2)}, u32[]{:S(2)}) collective-permute-start(bf16[512,256]{1,0:T(8,128)(2,1)S(1)} %get-tuple-element.28), channel_id=1, source_target_pairs={{0,4},{4,0},{8,12},{12,8},{16,20},{20,16},{24,28},{28,24},{1,5},{5... | collective-permute-start | bytes 786440 | tf_op jit(solution)/shard_map/ppermute | solution.py:426
  33.1 4.4 %collective-permute-start.15 = (bf16[512,256]{1,0:T(8,128)(2,1)S(1)}, bf16[512,256]{1,0:T(8,128)(2,1)S(1)}, u32[]{:S(2)}, u32[]{:S(2)}) collective-permute-start(bf16[512,256]{1,0:T(8,128)(2,1)S(1)} %ordered.3.refs_0_), channel_id=1, source_target_pairs={{0,4},{4,0},{8,12},{12,8},{16,20},{20,16},{24,28},{28,24},{1,5},{5... | collective-permute-start | bytes 786440 | tf_op jit(solution)/shard_map/ppermute | solution.py:426
  34.8 4.9 %collective-permute-start.11 = (bf16[512,256]{1,0:T(8,128)(2,1)S(1)}, bf16[512,256]{1,0:T(8,128)(2,1)S(1)}, u32[]{:S(2)}, u32[]{:S(2)}) collective-permute-start(bf16[512,256]{1,0:T(8,128)(2,1)S(1)} %ordered.2.refs_0_), channel_id=1, source_target_pairs={{0,4},{4,0},{8,12},{12,8},{16,20},{20,16},{24,28},{28,24},{1,5},{5... | collective-permute-start | bytes 786440 | tf_op jit(solution)/shard_map/ppermute | solution.py:426
  34.8 4.2 %collective-permute-start.18 = (f32[4,8,128]{2,1,0:T(8,128)S(1)}, f32[4,8,128]{2,1,0:T(8,128)S(1)}, u32[]{:S(2)}, u32[]{:S(2)}) collective-permute-start(f32[4,8,128]{2,1,0:T(8,128)S(1)} %constant_dynamic-update-slice_fusion.2.refs_0_), channel_id=1, source_target_pairs={{20,0},{8,4},{28,8},{0,12},{4,16},{24,20},{12,24},{16,28},{21,1},{... | collective-permute-start | bytes 49160 | tf_op jit(solution)/shard_map/ppermute | solution.py:441
  35.9 3.7 %collective-permute-start.17 = (f32[4,8,128]{2,1,0:T(8,128)S(1)}, f32[4,8,128]{2,1,0:T(8,128)S(1)}, u32[]{:S(2)}, u32[]{:S(2)}) collective-permute-start(f32[4,8,128]{2,1,0:T(8,128)S(1)} %constant_dynamic-update-slice_fusion.2.refs_0_), channel_id=1, source_target_pairs={{0,8},{4,20},{8,0},{12,28},{16,24},{20,4},{24,16},{28,12},{1,9},{5... | collective-permute-start | bytes 49160 | tf_op jit(solution)/shard_map/ppermute | solution.py:426
  37.0 2.7 %collective-permute-start.16 = (f32[4,8,128]{2,1,0:T(8,128)S(1)}, f32[4,8,128]{2,1,0:T(8,128)S(1)}, u32[]{:S(2)}, u32[]{:S(2)}) collective-permute-start(f32[4,8,128]{2,1,0:T(8,128)S(1)} %constant_dynamic-update-slice_fusion.2.refs_0_), channel_id=1, source_target_pairs={{0,4},{4,0},{8,12},{12,8},{16,20},{20,16},{24,28},{28,24},{1,5},{5... | collective-permute-start | bytes 49160 | tf_op jit(solution)/shard_map/ppermute | solution.py:426
